TPU v7x, 32 devices: a whole 2x2x4 slice. The times are simulated.
32 devices in a mesh: band: 8 (over z, y), grid: 2 (over x), ham: 2 (over core).
Axes of the slice: x: 2, y: 2, z: 4, core: 2. Of those that a mesh axis runs over, the one named last changes fastest.
Arguments:
- orbitals: bfloat16 [128, 64, 192], P('band', ('grid', 'ham')), may hold values from -6 to 6
- coulomb: float32 [64, 192], P(('grid', 'ham')), may hold values from 0.1 to 10
- occupied: int32 [8], replicated, may hold values from 1 to 16
- owners: int32 [128, 1], P('band'), may hold values from 0 to 3; in each aligned block of 16 rows (0 to 15, 16 to 31, ...) at most 8 rows name the same one
Outputs:
- projectors: bfloat16 [8, 4, 8, 64, 192], P('band', ('grid', 'ham'))
- intersection: float32 [8, 16, 16], P('band')
Inputs may be any that keep to these rules, and one draw needn't show every extreme that they name: `owners`: among the 16 bands of one block at most 8 name the same owner; in some blocks one owner is named by exactly 8.
All inputs are finite; a program needn't handle non-finite values.
Results may differ from a plain program's by a relative error of at most 0.0038.
Values may be sent and summed in bfloat16 or wider, within the bound.
No kernel may reach another device: no remote copies, remote signals or barrier semaphores. Data moves between devices by JAX's collectives and lax.ppermute only.
A program may use at most 64 MiB of HBM per device.

v0:
```python
import math

import jax
import jax.numpy as jnp
from jax import lax
from jax.sharding import PartitionSpec as P

CAP = 8


HIGHEST = lax.Precision.HIGHEST


def shifted(value, axis, steps):
    count = lax.axis_size(axis)
    pairs = [(source, (source + steps) % count) for source in range(count)]
    return lax.ppermute(value, axis, pairs)


def spectral_tables(points):
    midpoint = points // 2
    row_ids = jnp.arange(points)
    frequency = jnp.where(row_ids <= midpoint, row_ids, row_ids - midpoint)
    phases = row_ids[:, None] * frequency[None, :] % points
    angles = phases.astype(jnp.float32) * (2.0 * math.pi / points)
    cosine_cols = (row_ids <= midpoint)[None, :]
    forward_t = jnp.where(cosine_cols, jnp.cos(angles), jnp.sin(angles))
    single = (frequency == 0) | (row_ids == midpoint)
    scaling = jnp.where(single, 1.0, 2.0) / points
    inverse_t = forward_t.T * scaling[:, None]
    return (forward_t.astype(jnp.bfloat16), inverse_t.astype(jnp.bfloat16))


def potential(native, guests, tables):
    multiplier, forward_t, inverse_t = tables
    members, line_count, points = native.shape
    visiting = guests.shape[0]
    density = (native[:, None].astype(jnp.float32) * guests[None].astype(jnp.float32)).astype(
        jnp.bfloat16
    )
    density = density.reshape(members * visiting * line_count, points)
    spectrum = jnp.dot(density, forward_t, preferred_element_type=jnp.float32).reshape(
        members, visiting, line_count, points
    )
    spectrum = (spectrum * multiplier[None, None]).astype(jnp.bfloat16)
    field = jnp.dot(
        spectrum.reshape(members * visiting * line_count, points),
        inverse_t,
        preferred_element_type=jnp.float32,
    )
    return field.astype(jnp.bfloat16).reshape(members, visiting, line_count, points)


def accumulate_one(native, visitor, weights, running, tables):
    field = potential(native, visitor, tables)
    weighted = visitor * weights.astype(jnp.bfloat16)[:, None, None]
    return running + jnp.einsum(
        "igLx,gLx->iLx", field, weighted, preferred_element_type=jnp.float32
    )


def neighbours(orbitals, toward):
    arrivals = []
    carried = orbitals
    for distance in (1, 2):
        carried = shifted(carried, "band", toward)
        arrivals.append(carried)
    return arrivals


def local(orbitals, coulomb, occupied, owners):
    members, line_count, points = orbitals.shape
    band_count = lax.axis_size("band")
    position = lax.axis_index("band")
    groups_total = lax.axis_size("grid") * lax.axis_size("ham")
    forward_t, inverse_t = spectral_tables(points)
    mirrored = jnp.roll(coulomb[:, ::-1], 1, axis=1)
    kernel = 0.5 * (coulomb + mirrored)
    midpoint = points // 2
    multiplier = jnp.concatenate([kernel[:, : midpoint + 1], kernel[:, 1:midpoint]], axis=1)
    tables = (multiplier, forward_t, inverse_t)
    member_ids = jnp.arange(members)

    def mask_of(offset):
        return (member_ids < occupied[(position + offset) % band_count]).astype(jnp.float32)

    native_weights = mask_of(0)
    accrued = accumulate_one(
        orbitals, orbitals, native_weights, jnp.zeros(orbitals.shape, jnp.float32), tables
    )
    for toward in (1, -1):
        for distance, visitor in zip((1, 2), neighbours(orbitals, toward)):
            accrued = accumulate_one(
                orbitals, visitor, mask_of(-toward * distance), accrued, tables
            )
    partial_value = jnp.einsum(
        "ilx,klx->ik", orbitals.astype(jnp.float32), accrued, precision=HIGHEST
    )
    intersection = lax.psum(partial_value, ("grid", "ham")) / (line_count * groups_total * points)
    factor = jnp.linalg.cholesky(intersection)
    compressed = lax.linalg.triangular_solve(
        factor, accrued.reshape(members, line_count * points), left_side=True, lower=True
    ).astype(jnp.bfloat16)
    owner_ids = owners[:, 0]
    onehot = (owner_ids[:, None] == jnp.arange(groups_total)[None, :]).astype(jnp.int32)
    ranking = jnp.sum(jnp.cumsum(onehot, axis=0) * onehot, axis=1) - 1
    target = owner_ids * CAP + ranking
    placement = (jnp.arange(groups_total * CAP)[:, None] == target[None, :]).astype(jnp.bfloat16)
    outgoing = jnp.dot(placement, compressed, preferred_element_type=jnp.float32).astype(
        jnp.bfloat16
    )
    outgoing = outgoing.reshape(groups_total, CAP, line_count, points)
    arrived = lax.all_to_all(outgoing, ("grid", "ham"), split_axis=0, concat_axis=2, tiled=True)
    return (arrived.reshape(1, 1, CAP, groups_total * line_count, points), intersection[None])


def solution(mesh):
    in_specs = (P("band", ("grid", "ham"), None), P(("grid", "ham"), None), P(), P("band", None))
    out_specs = (P("band", ("grid", "ham"), None, None, None), P("band", None, None))
    return jax.shard_map(local, mesh=mesh, in_specs=in_specs, out_specs=out_specs, check_vma=False)
```

profile of v0, /device:TPU:0, one launch (start us, length us, event | category | flops | bytes accessed | tf_op | source)
XLA Modules:
  0.0 95.4 jit_solution(9165857274942863637)
XLA Ops:
  0.6 6.1 %collective-permute-start.2 = (bf16[16,16,192]{2,1,0:T(8,128)(2,1)}, bf16[16,16,192]{2,1,0:T(8,128)(2,1)}, u32[]{:S(2)}, u32[]{:S(2)}) collective-permute-start(bf16[16,16,192]{2,1,0:T(8,128)(2,1)} %param.4), channel_id=1, source_target_pairs={{0,28},{4,0},{8,4},{12,8},{16,12},{20,16},{24,20},{28,24},{1,29},{... | collective-permute-start | bytes 294920 | tf_op jit(solution)/shard_map/ppermute | solution.py:17
  9.3 1.5 %fusion.86 = (s32[1]{0:T(128)}, s32[1]{0:T(128)}, s32[1]{0:T(128)}, s32[1]{0:T(128)}, s32[1]{0:T(128)}) fusion(s32[8]{0:T(128)} %param.6, s32[]{:T(128)S(6)} %select_n.145, s32[]{:T(128)S(6)} %select_n.147, s32[]{:T(128)S(6)} %select_n.137, s32[]{:T(128)S(6)} %select_n.151, s32[]{:T(128)S(6)} %select_n.149), kind=kLoop, calls=%fused_computation.137 | loop fusion | bytes 60 | tf_op jit(solution)/shard_map/dynamic_slice | solution.py:85
  10.9 1.2 %fusion.54 = bf16[16]{0:T(256)(128)(2,1)} fusion(s32[]{:T(128)} %bitcast.34), kind=kLoop, calls=%fused_computation.104 | loop fusion | flops 48 | bytes 36 | tf_op jit(solution)/shard_map/convert_element_type | solution.py:56
  12.7 1.1 %bitcast_convert_fusion.4 = (f32[16,192,16]{1,0,2:T(8,128)S(1)}, f32[16,16,192]{2,1,0:T(8,128)S(1)}) fusion(bf16[16,16,192]{2,1,0:T(8,128)(2,1)} %param.4, bf16[16]{0:T(256)(128)(2,1)S(1)} %fusion.50), kind=kLoop, calls=%fused_computation.55 | loop fusion | flops 147456 | bytes 491552
  14.5 1.1 %fusion.52 = bf16[16]{0:T(256)(128)(2,1)} fusion(s32[]{:T(128)} %bitcast.24), kind=kLoop, calls=%fused_computation.102 | loop fusion | flops 48 | bytes 36 | tf_op jit(solution)/shard_map/convert_element_type | solution.py:56
  15.7 2.2 %multiply_convert_fusion.8 = bf16[16,16,16,192]{3,2,1,0:T(8,128)(2,1)S(1)} fusion(f32[16,192]{1,0:T(8,128)S(1)} %pad_maximum_fusion, f32[16,16,192]{2,1,0:T(8,128)S(1)} %get-tuple-element.9, s32[192]{0:T(256)S(1)} %add_select_fusion.2, pred[192]{0:T(512)(128)(4,1)S(1)} %iota_compare_fusion.5), kind=kOutput, calls=%fused_computation.18 | convolution fusion | flops 305541120 | bytes 1782720 | tf_op jit(solution)/shard_map/dot_general | solution.py:42
  17.9 2.8 %convolution_convert_fusion.4 = bf16[4096,192]{0,1:T(8,128)(2,1)} fusion(bf16[4096,192]{1,0:T(8,128)(2,1)S(1)} %bitcast.89, f32[192]{0:T(256)S(1)} %fusion.49, s32[192]{0:T(256)S(1)} %add_select_fusion.2, pred[192]{0:T(512)(128)(4,1)S(1)} %iota_compare_fusion.5), kind=kOutput, calls=%fused_computation.4 | convolution fusion | flops 303218688 | bytes 3147456 | tf_op jit(solution)/shard_map/dot_general | solution.py:46
  20.7 3.2 %copy.56 = bf16[4096,192]{1,0:T(8,128)(2,1)S(1)} copy(bf16[4096,192]{0,1:T(8,128)(2,1)} %convolution_convert_fusion.4) | data formatting | bytes 3145728
  25.4 1.1 %bitcast_convert_fusion.1 = (f32[16,192,16]{1,0,2:T(8,128)S(1)}, f32[16,16,192]{2,1,0:T(8,128)S(1)}) fusion(bf16[16,16,192]{2,1,0:T(8,128)(2,1)} %collective-permute-done.2, bf16[16]{0:T(256)(128)(2,1)S(1)} %fusion.53), kind=kLoop, calls=%fused_computation.52 | loop fusion | flops 147456 | bytes 491552
  26.5 2.2 %multiply_convert_fusion.2 = bf16[16,16,16,192]{3,2,1,0:T(8,128)(2,1)S(1)} fusion(f32[16,16,192]{2,1,0:T(8,128)S(1)} %get-tuple-element.13, f32[16,192]{1,0:T(8,128)S(1)} %pad_maximum_fusion, f32[16,16,192]{2,1,0:T(8,128)S(1)} %get-tuple-element.9, s32[192]{0:T(256)S(1)} %add_select_fusion.2, pred[192]{0:T(512)(128)(4,1)S(1)} %iota_compare_fusion.5), kind=kOutput, calls=%fused_computation.12 | convolution fusion | flops 305541120 | bytes 1979328 | tf_op jit(solution)/shard_map/dot_general | solution.py:42
  28.7 1.7 %convolution_convert_fusion.1 = bf16[4096,192]{0,1:T(8,128)(2,1)S(1)} fusion(bf16[4096,192]{1,0:T(8,128)(2,1)S(1)} %bitcast.87, f32[192]{0:T(256)S(1)} %fusion.49, s32[192]{0:T(256)S(1)} %add_select_fusion.2, pred[192]{0:T(512)(128)(4,1)S(1)} %iota_compare_fusion.5), kind=kOutput, calls=%fused_computation.1 | convolution fusion | flops 303218688 | bytes 3147456 | tf_op jit(solution)/shard_map/dot_general | solution.py:46
  30.5 2.2 %multiply_convert_fusion.6 = bf16[16,16,16,192]{3,2,1,0:T(8,128)(2,1)S(1)} fusion(f32[16,16,192]{2,1,0:T(8,128)S(1)} %get-tuple-element.7, f32[16,192]{1,0:T(8,128)S(1)} %copy-done.4, f32[16,16,192]{2,1,0:T(8,128)S(1)} %get-tuple-element.9, s32[192]{0:T(256)S(1)} %add_select_fusion.2, pred[192]{0:T(512)(128)(4,1)S(1)} %iota_compare_fusion.5), kind=kOutput, calls=%fused_computation.16 | convolution fusion | flops 305541120 | bytes 1979328 | tf_op jit(solution)/shard_map/dot_general | solution.py:42
  32.8 4.8 %collective-permute-start.3 = (bf16[16,16,192]{2,1,0:T(8,128)(2,1)}, bf16[16,16,192]{2,1,0:T(8,128)(2,1)}, u32[]{:S(2)}, u32[]{:S(2)}) collective-permute-start(bf16[16,16,192]{2,1,0:T(8,128)(2,1)} %collective-permute-done.2), channel_id=1, source_target_pairs={{0,28},{4,0},{8,4},{12,8},{16,12},{20,16},{24,20},{28,24},{1,29},{... | collective-permute-start | bytes 294920 | tf_op jit(solution)/shard_map/ppermute | solution.py:17
  37.5 2.8 %convolution_convert_fusion.3 = bf16[4096,192]{0,1:T(8,128)(2,1)} fusion(bf16[4096,192]{1,0:T(8,128)(2,1)S(1)} %bitcast.86, f32[192]{0:T(256)S(1)} %fusion.49, s32[192]{0:T(256)S(1)} %add_select_fusion.2, pred[192]{0:T(512)(128)(4,1)S(1)} %iota_compare_fusion.5), kind=kOutput, calls=%fused_computation.3 | convolution fusion | flops 303218688 | bytes 3147456 | tf_op jit(solution)/shard_map/dot_general | solution.py:46
  40.3 2.5 %copy.59 = bf16[4096,192]{1,0:T(8,128)(2,1)} copy(bf16[4096,192]{0,1:T(8,128)(2,1)S(1)} %convolution_convert_fusion.1) | data formatting | bytes 3145728
  42.8 3.1 %copy.57 = bf16[4096,192]{1,0:T(8,128)(2,1)S(1)} copy(bf16[4096,192]{0,1:T(8,128)(2,1)} %convolution_convert_fusion.3) | data formatting | bytes 3145728
  46.2 1.1 %bitcast_convert_fusion = (f32[16,192,16]{1,0,2:T(8,128)S(1)}, f32[16,16,192]{2,1,0:T(8,128)S(1)}) fusion(bf16[16,16,192]{2,1,0:T(8,128)(2,1)} %collective-permute-done.3, bf16[16]{0:T(256)(128)(2,1)} %fusion.54), kind=kLoop, calls=%fused_computation.51 | loop fusion | flops 147456 | bytes 491552
  47.3 2.9 %multiply_convert_fusion = bf16[16,16,16,192]{3,2,1,0:T(8,128)(2,1)S(1)} fusion(f32[16,16,192]{2,1,0:T(8,128)S(1)} %get-tuple-element.15, f32[16,192]{1,0:T(8,128)} %copy-done.3, f32[16,16,192]{2,1,0:T(8,128)S(1)} %get-tuple-element.9, s32[192]{0:T(256)S(1)} %add_select_fusion.2, pred[192]{0:T(512)(128)(4,1)S(1)} %iota_compare_fusion.5), kind=kOutput, calls=%fused_computation.10 | convolution fusion | flops 305541120 | bytes 1979328 | tf_op jit(solution)/shard_map/dot_general | solution.py:42
  50.3 2.8 %convolution_convert_fusion = bf16[4096,192]{0,1:T(8,128)(2,1)} fusion(bf16[4096,192]{1,0:T(8,128)(2,1)S(1)} %bitcast.88, f32[192]{0:T(256)S(1)} %fusion.49, s32[192]{0:T(256)S(1)} %add_select_fusion.2, pred[192]{0:T(512)(128)(4,1)S(1)} %iota_compare_fusion.5), kind=kOutput, calls=%fused_computation | convolution fusion | flops 303218688 | bytes 3147456 | tf_op jit(solution)/shard_map/dot_general | solution.py:46
  53.1 3.8 %copy.60 = bf16[4096,192]{1,0:T(8,128)(2,1)} copy(bf16[4096,192]{0,1:T(8,128)(2,1)} %convolution_convert_fusion) | data formatting | bytes 3145728
  56.9 1.1 %bitcast_convert_fusion.2 = (f32[16,192,16]{1,0,2:T(8,128)S(1)}, f32[16,16,192]{2,1,0:T(8,128)S(1)}) fusion(bf16[16,16,192]{2,1,0:T(8,128)(2,1)} %collective-permute-done.1, bf16[16]{0:T(256)(128)(2,1)} %fusion.52), kind=kLoop, calls=%fused_computation.53 | loop fusion | flops 147456 | bytes 491552
  58.0 3.3 %multiply_convert_fusion.4 = bf16[16,16,16,192]{3,2,1,0:T(8,128)(2,1)S(1)} fusion(f32[16,16,192]{2,1,0:T(8,128)S(1)} %get-tuple-element.11, f32[16,192]{1,0:T(8,128)} %copy-done.3, f32[16,16,192]{2,1,0:T(8,128)} %copy-done.2, s32[192]{0:T(256)S(1)} %add_select_fusion.2, pred[192]{0:T(512)(128)(4,1)S(1)} %iota_compare_fusion.5), kind=kOutput, calls=%fused_computation.14 | convolution fusion | flops 305541120 | bytes 1979328 | tf_op jit(solution)/shard_map/dot_general | solution.py:42
  61.3 2.8 %convolution_convert_fusion.2 = bf16[4096,192]{0,1:T(8,128)(2,1)} fusion(bf16[4096,192]{1,0:T(8,128)(2,1)S(1)} %bitcast.85, f32[192]{0:T(256)S(1)} %fusion.49, s32[192]{0:T(256)S(1)} %add_select_fusion.2, pred[192]{0:T(512)(128)(4,1)S(1)} %iota_compare_fusion.5), kind=kOutput, calls=%fused_computation.2 | convolution fusion | flops 303218688 | bytes 3147456 | tf_op jit(solution)/shard_map/dot_general | solution.py:46
  64.1 3.8 %copy.58 = bf16[4096,192]{1,0:T(8,128)(2,1)} copy(bf16[4096,192]{0,1:T(8,128)(2,1)} %convolution_convert_fusion.2) | data formatting | bytes 3145728
  68.0 3.4 %multiply_reduce_fusion = (f32[16,192,16]{1,0,2:T(8,128)S(1)}, f32[16,192,16]{1,0,2:T(8,128)S(1)}) fusion(bf16[16,192,16,16]{1,0,2,3:T(8,128)(2,1)} %bitcast.83, f32[16,192,16]{1,0,2:T(8,128)S(1)} %get-tuple-element.14, bf16[16,192,16,16]{1,0,2,3:T(8,128)(2,1)} %bitcast.82, f32[16,192,16]{1,0,2:T(8,128)S(1)} %get-tuple-element.12), kind=kLoop, calls=%fused_computation.5 | loop fusion | flops 4620288 | bytes 3932160 | tf_op jit(solution)/shard_map/igLx,gLx->iLx/dot_general | solution.py:57
  71.4 1.0 %multiply_reduce_fusion.2 = (f32[16,192,16]{1,0,2:T(8,128)S(1)}, f32[16,192,16]{1,0,2:T(8,128)S(1)}) fusion(bf16[16,192,16,16]{1,0,2,3:T(8,128)(2,1)S(1)} %bitcast.84, f32[16,192,16]{1,0,2:T(8,128)S(1)} %get-tuple-element.10, bf16[16,192,16,16]{1,0,2,3:T(8,128)(2,1)S(1)} %bitcast.81, f32[16,192,16]{1,0,2:T(8,128)S(1)} %get-tuple-element.6), kind=kLoop, calls=%fused_computation.7 | loop fusion | flops 4620288 | bytes 3932160 | tf_op jit(solution)/shard_map/igLx,gLx->iLx/dot_general | solution.py:57
  73.7 5.9 %psum.7 = f32[16,16]{0,1:T(8,128)S(1)} all-reduce(f32[16,16]{0,1:T(8,128)S(1)} %convolution_bitcast_fusion), channel_id=1, replica_groups=mesh['band'=8,'grid'=2,'ham'=2] {'grid','ham'}, use_global_device_ids=true, to_apply=%region_2.3 | all-reduce | flops 256 | bytes 2048 | tf_op jit(solution)/shard_map/psum | solution.py:99
  79.7 1.5 %cholesky.16 = f32[16,16]{1,0:T(8,128)S(1)} custom-call(f32[16,16]{1,0:T(8,128)S(1)} %fusion.46), custom_call_target="Cholesky" | custom-call | tf_op jit(solution)/shard_map/jit(cholesky)/cholesky | solution.py:100
  82.4 1.2 %custom-call.6 = f32[1,16,16]{1,2,0:T(8,128)S(1)} custom-call(f32[1,16,16]{2,1,0:T(8,128)S(1)} %fusion.44), custom_call_target="InvertDiagBlocksLowerTriangular" | custom-call | tf_op jit(solution)/shard_map/triangular_solve | solution.py:101
  84.2 1.0 %reshape.166 = bf16[4,8,16,192]{3,2,1,0:T(8,128)(2,1)} reshape(bf16[32,3072]{1,0:T(8,128)(2,1)S(1)} %convolution_convert_fusion.5) | data formatting | bytes 393216 | tf_op jit(solution)/shard_map/reshape | solution.py:112
  85.3 3.4 %all-to-all-start = ((bf16[4,8,16,192]{3,2,1,0:T(8,128)(2,1)}), bf16[4,8,16,192]{3,2,1,0:T(8,128)(2,1)S(1)}, u32[]{:S(2)}, u32[]{:S(2)}) async-start(bf16[4,8,16,192]{3,2,1,0:T(8,128)(2,1)} %reshape.166), calls=%async_computation | async-start | bytes 524288 | tf_op jit(solution)/shard_map/all_to_all | solution.py:113
  89.3 5.3 %all-to-all-done = bf16[4,8,16,192]{3,2,1,0:T(8,128)(2,1)S(1)} async-done(((bf16[4,8,16,192]{3,2,1,0:T(8,128)(2,1)}), bf16[4,8,16,192]{3,2,1,0:T(8,128)(2,1)S(1)}, u32[]{:S(2)}, u32[]{:S(2)}) %all-to-all-start) | async-done | bytes 196640 | tf_op jit(solution)/shard_map/all_to_all | solution.py:113
  (51 shorter events, 10.5 us)
Async XLA Ops:
  0.6 24.7 %collective-permute-start.2 = (bf16[16,16,192]{2,1,0:T(8,128)(2,1)}, bf16[16,16,192]{2,1,0:T(8,128)(2,1)}, u32[]{:S(2)}, u32[]{:S(2)}) collective-permute-start(bf16[16,16,192]{2,1,0:T(8,128)(2,1)} %param.4), channel_id=1, source_target_pairs={{0,28},{4,0},{8,4},{12,8},{16,12},{20,16},{24,20},{28,24},{1,29},{... | collective-permute-start | bytes 294920 | tf_op jit(solution)/shard_map/ppermute | solution.py:17
  6.7 23.7 %collective-permute-start = (bf16[16,16,192]{2,1,0:T(8,128)(2,1)}, bf16[16,16,192]{2,1,0:T(8,128)(2,1)S(1)}, u32[]{:S(2)}, u32[]{:S(2)}) collective-permute-start(bf16[16,16,192]{2,1,0:T(8,128)(2,1)} %param.4), channel_id=1, source_target_pairs={{0,4},{4,8},{8,12},{12,16},{16,20},{20,24},{24,28},{28,0},{1,5},{5... | collective-permute-start | bytes 294920 | tf_op jit(solution)/shard_map/ppermute | solution.py:17
  13.7 33.6 %copy-start.2 = (f32[16,16,192]{2,1,0:T(8,128)}, f32[16,16,192]{2,1,0:T(8,128)S(1)}, u32[]{:S(2)}) copy-start(f32[16,16,192]{2,1,0:T(8,128)S(1)} %get-tuple-element.9) | copy-start | bytes 589828
  15.7 10.8 %copy-start.3 = (f32[16,192]{1,0:T(8,128)}, f32[16,192]{1,0:T(8,128)S(1)}, u32[]{:S(2)}) copy-start(f32[16,192]{1,0:T(8,128)S(1)} %pad_maximum_fusion) | copy-start | bytes 36868
  20.7 3.2 %copy-start.5 = (s32[16,1]{0,1:T(1,128)S(1)}, s32[16,1]{0,1:T(1,128)}, u32[]{:S(2)}) copy-start(s32[16,1]{0,1:T(1,128)} %param.7) | copy-start | bytes 196
  28.7 1.8 %copy-start.4 = (f32[16,192]{1,0:T(8,128)S(1)}, f32[16,192]{1,0:T(8,128)}, u32[]{:S(2)}) copy-start(f32[16,192]{1,0:T(8,128)} %copy-done.3) | copy-start | bytes 36868
  32.8 13.5 %collective-permute-start.3 = (bf16[16,16,192]{2,1,0:T(8,128)(2,1)}, bf16[16,16,192]{2,1,0:T(8,128)(2,1)}, u32[]{:S(2)}, u32[]{:S(2)}) collective-permute-start(bf16[16,16,192]{2,1,0:T(8,128)(2,1)} %collective-permute-done.2), channel_id=1, source_target_pairs={{0,28},{4,0},{8,4},{12,8},{16,12},{20,16},{24,20},{28,24},{1,29},{... | collective-permute-start | bytes 294920 | tf_op jit(solution)/shard_map/ppermute | solution.py:17
  46.0 11.0 %collective-permute-start.1 = (bf16[16,16,192]{2,1,0:T(8,128)(2,1)S(1)}, bf16[16,16,192]{2,1,0:T(8,128)(2,1)}, u32[]{:S(2)}, u32[]{:S(2)}) collective-permute-start(bf16[16,16,192]{2,1,0:T(8,128)(2,1)S(1)} %collective-permute-done), channel_id=1, source_target_pairs={{0,4},{4,8},{8,12},{12,16},{16,20},{20,24},{24,28},{28,0},{1,5},{5... | collective-permute-start | bytes 294920 | tf_op jit(solution)/shard_map/ppermute | solution.py:17
  67.9 3.4 %copy-start = (bf16[4096,192]{1,0:T(8,128)(2,1)S(1)}, bf16[4096,192]{1,0:T(8,128)(2,1)}, u32[]{:S(2)}) copy-start(bf16[4096,192]{1,0:T(8,128)(2,1)} %copy.58) | copy-start | bytes 4718596
  72.3 0.9 copy-start.1
  85.3 9.4 %all-to-all-start = ((bf16[4,8,16,192]{3,2,1,0:T(8,128)(2,1)}), bf16[4,8,16,192]{3,2,1,0:T(8,128)(2,1)S(1)}, u32[]{:S(2)}, u32[]{:S(2)}) async-start(bf16[4,8,16,192]{3,2,1,0:T(8,128)(2,1)} %reshape.166), calls=%async_computation | async-start | bytes 524288 | tf_op jit(solution)/shard_map/all_to_all | solution.py:113
where the time goes:
time: 96.2 us; the launch traced here: 95.4 us
  matrix products  26.9 us (28%)
  local copies, waits for them, and re-layouts  23.1 us (24%)
  other arithmetic  18.8 us (20%)
  starting transfers between devices  14.5 us (15%)
  blocking collectives  5.88 us (6%)
  waiting for transfers between devices  5.34 us (6%)
    unnamed x20, local copies, waits for them, and re-layouts  18 us
    dot_general x5, matrix products, potential(): jnp.dot(spectrum.reshape(members * visiting * line_count, points), invers...  13 us
    dot_general x5, matrix products, potential(): jnp.dot(density, forward_t, preferred_element_type=jnp.float32)  12.9 us
    ppermute x4, starting transfers between devices, shifted(): return lax.ppermute(value, axis, pairs)  11.1 us
    psum x1, blocking collectives, local(): lax.psum(partial_value, ('grid', 'ham'))  5.88 us
    all_to_all x1, waiting for transfers between devices, local(): lax.all_to_all(outgoing, ('grid', 'ham'), split_axis=0, concat_axis=2, ti...  5.33 us
    dot_general x3, other arithmetic, accumulate_one(): jnp.einsum('igLx,gLx->iLx', field, weighted, preferred_element_type=jnp.f...  4.84 us
    unnamed x5, other arithmetic  4.36 us
  transfers between devices with their start and end apart: 5, of which 1 were waited for; matrix products, arithmetic and copies ran while one was open for 45% of the time, Pallas kernels for 0%

commit v1 on v0

v1 whole, which is shorter than its diff:
```python
import math

import jax
import jax.numpy as jnp
import numpy as np
from jax import lax
from jax.experimental import pallas as pl
from jax.experimental.pallas import tpu as pltpu
from jax.sharding import PartitionSpec as P

CAP = 8
REACH = 2
LANES = 128
HIGHEST = lax.Precision.HIGHEST
VMEM_LIMIT = 48 * 1024 * 1024


def shifted(value, axis, steps):
    count = lax.axis_size(axis)
    pairs = [(source, (source + steps) % count) for source in range(count)]
    return lax.ppermute(value, axis, pairs)


def swapped(value, flip):
    count = lax.axis_size("grid") * lax.axis_size("ham")
    pairs = [(source, source ^ flip) for source in range(count)]
    return lax.ppermute(value, ("grid", "ham"), pairs)


def spectral_tables(points):
    midpoint = points // 2
    ids = np.arange(points)
    frequency = np.where(ids <= midpoint, ids, ids - midpoint)
    angles = (ids[:, None] * frequency[None, :] % points) * (2.0 * math.pi / points)
    forward = np.where((ids <= midpoint)[None, :], np.cos(angles), np.sin(angles))
    single = (frequency == 0) | (ids == midpoint)
    inverse = forward.T * (np.where(single, 1.0, 2.0) / points)[:, None]
    mirror = np.zeros((points, points))
    mirror[frequency, ids] += 0.5
    mirror[(points - frequency) % points, ids] += 0.5
    return tuple(jnp.asarray(t.astype(np.float32)).astype(jnp.bfloat16) for t in (forward, inverse, mirror))


def halves(value):
    high = value.astype(jnp.bfloat16)
    return high, (value - high.astype(jnp.float32)).astype(jnp.bfloat16)


def dot32(a, b, contract=((1,), (0,))):
    return lax.dot_general(a, b, (contract, ((), ())), preferred_element_type=jnp.float32)


def dot_exact(a, b, contract=((1,), (0,))):
    return lax.dot_general(
        a, b, (contract, ((), ())), precision=HIGHEST, preferred_element_type=jnp.float32
    )


def response_kernel(coulomb_ref, forward_ref, inverse_ref, mirror_ref, out_ref):
    points = coulomb_ref.shape[1]
    multiplier = dot_exact(coulomb_ref[...], mirror_ref[...].astype(jnp.float32))
    forward = forward_ref[...].astype(jnp.float32)
    inverse = inverse_ref[...]
    for line in range(coulomb_ref.shape[0]):
        high, low = halves(forward * multiplier[line : line + 1, :])
        out_ref[line, :, :points] = dot32(high, inverse) + dot32(low, inverse)
        out_ref[line, :, points:] = jnp.zeros((points, out_ref.shape[2] - points), jnp.float32)


def image_kernel(occupied_ref, *refs):
    blocks, (response_ref, wide_ref, narrow_ref, overlap_ref, rows, images) = refs[:-6], refs[-6:]
    members, lines, points = blocks[0].shape
    size = members * lines
    tiles = rows.shape[0]
    spans = [(t, t * LANES, min(LANES, points - t * LANES)) for t in range(tiles)]
    position = lax.axis_index("band")
    total = lax.axis_size("band")
    member_ids = lax.broadcasted_iota(jnp.int32, (members, LANES), 0)
    rows[tiles - 1] = jnp.zeros(rows.shape[1:], jnp.float32)
    masks = []
    for place, block in enumerate(blocks):
        flat = block[...].reshape(size, points).astype(jnp.float32)
        for tile, start, width in spans:
            rows[tile, place * size : (place + 1) * size, :width] = flat[:, start : start + width]
        offset = 0 if place == 0 else OFFSETS[place - 1]
        filled = occupied_ref[lax.rem(position + (offset + total), total)]
        masks.append((member_ids < filled).astype(jnp.float32))
    mask = jnp.concatenate(masks, axis=0)
    overlap = jnp.zeros((members, members), jnp.float32)
    for line in range(lines):
        picked = [
            rows[tile, pl.ds(line, len(blocks) * members, stride=lines), :]
            for tile in range(tiles)
        ]
        masked = jnp.concatenate([(p * mask).astype(jnp.bfloat16) for p in picked], axis=1)
        window = jnp.concatenate([p.astype(jnp.bfloat16) for p in picked], axis=1)
        native = window[:members]
        gram = dot32(masked[:, :points], window, ((0,), (0,)))
        high, low = halves(gram * response_ref[line])
        image = dot32(native[:, :points], high) + dot32(native[:, :points], low)
        for tile in range(tiles):
            images[tile, pl.ds(line, members, stride=lines), :] = image[
                :, tile * LANES : (tile + 1) * LANES
            ]
        high, low = halves(image)
        across = ((1,), (1,))
        overlap = overlap + (dot32(native, high, across) + dot32(native, low, across))
    overlap_ref[...] = overlap
    for tile, start, width in spans:
        piece = images[tile].reshape(members, lines, LANES)[:, :, :width]
        wide_ref[:, :, start : start + width] = piece
        narrow_ref[:, :, start : start + width] = piece.astype(jnp.bfloat16)


def factor_kernel(cells, owners_ref, *refs):
    parts, (overlap_ref, weights_ref) = refs[:-2], refs[-2:]
    members = owners_ref.shape[0]
    sums = [part[...] for part in parts]
    while len(sums) > 1:
        sums = [a + b for a, b in zip(sums[::2], sums[1::2])]
    overlap = sums[0] * (1.0 / cells)
    overlap_ref[...] = overlap
    square = (members, members)
    row_ids = lax.broadcasted_iota(jnp.int32, square, 0)
    col_ids = lax.broadcasted_iota(jnp.int32, square, 1)
    identity = (row_ids == col_ids).astype(jnp.float32)
    upper = 0.5 * (overlap + dot_exact(overlap, identity, ((0,), (0,))))
    lower = identity
    for k in range(members):
        column = jnp.broadcast_to(upper[:, k : k + 1], square)
        pivot = jnp.broadcast_to(column[k : k + 1, :], square)
        scale = jnp.where(row_ids > k, column / pivot, 0.0)
        upper = upper - scale * upper[k : k + 1, :]
        lower = lower - scale * lower[k : k + 1, :]
    diagonal = jnp.sum(upper * identity, axis=1, keepdims=True)
    inverse = lower / jnp.sqrt(diagonal)
    group = lax.axis_index("grid") * lax.axis_size("ham") + lax.axis_index("ham")
    mine = (owners_ref[...] == group).astype(jnp.float32)
    before = (col_ids < row_ids).astype(jnp.float32)
    ranking = dot_exact(before, jnp.broadcast_to(mine, (members, CAP)))
    slots = lax.broadcasted_iota(jnp.int32, (members, CAP), 1).astype(jnp.float32)
    placement = jnp.where(ranking == slots, 1.0, 0.0) * mine
    chosen = dot_exact(placement, inverse, ((0,), (0,)))
    for k in range(members):
        weights_ref[k * CAP : (k + 1) * CAP, :] = jnp.broadcast_to(
            chosen[:, k : k + 1], (CAP, weights_ref.shape[1])
        )


def route_kernel(weights_ref, *refs):
    parts, out_ref = refs[:-1], refs[-1]
    members, lines, _ = parts[0].shape
    group = lax.axis_index("grid") * lax.axis_size("ham") + lax.axis_index("ham")
    for flip, part in enumerate(parts):
        start = pl.multiple_of((group ^ flip) * lines, lines)
        sums = [None] * CAP
        for k in range(members):
            image = part[k].astype(jnp.float32)
            for slot in range(CAP):
                row = k * CAP + slot
                term = weights_ref[row : row + 1, :] * image
                sums[slot] = term if k == 0 else sums[slot] + term
        for slot in range(CAP):
            out_ref[slot, pl.ds(start, lines), :] = sums[slot].astype(jnp.bfloat16)


OFFSETS = tuple(o for d in range(1, REACH + 1) for o in (d, -d))


def call(kernel, name, shapes, flops, moved, scratch=(), scalars=0, operands=0):
    vmem = pl.BlockSpec(memory_space=pltpu.VMEM)
    smem = pl.BlockSpec(memory_space=pltpu.SMEM)
    return pl.pallas_call(
        kernel,
        name=name,
        out_shape=shapes,
        in_specs=[smem] * scalars + [vmem] * operands,
        out_specs=[vmem] * len(shapes),
        scratch_shapes=list(scratch),
        compiler_params=pltpu.CompilerParams(vmem_limit_bytes=VMEM_LIMIT),
        cost_estimate=pl.CostEstimate(flops=flops, bytes_accessed=moved, transcendentals=0),
    )


def local(orbitals, coulomb, occupied, owners):
    members, lines, points = orbitals.shape
    groups = lax.axis_size("grid") * lax.axis_size("ham")
    tiles = -(-points // LANES)
    f32, bf16 = jnp.float32, jnp.bfloat16
    shape = jax.ShapeDtypeStruct
    guests = [shifted(orbitals, "band", -offset) for offset in OFFSETS]
    forward, inverse, mirror = spectral_tables(points)
    (response,) = call(
        response_kernel,
        "response",
        [shape((lines, points, tiles * LANES), f32)],
        4 * lines * points**3,
        4 * lines * points**2,
        operands=4,
    )(coulomb, forward, inverse, mirror)
    blocks = len(guests) + 1
    wide, narrow, overlap = call(
        image_kernel,
        "image",
        [
            shape((members, lines, points), f32),
            shape((members, lines, points), bf16),
            shape((members, members), f32),
        ],
        2 * lines * points**2 * members * (blocks + 2),
        4 * lines * points**2,
        scratch=[
            pltpu.VMEM((tiles, blocks * members * lines, LANES), f32),
            pltpu.VMEM((tiles, members * lines, LANES), f32),
        ],
        scalars=1,
        operands=blocks + 1,
    )(occupied, orbitals, *guests, response)
    flips = range(1, groups)
    overlaps = [overlap] + [swapped(overlap, flip) for flip in flips]
    near = lax.axis_size("ham")
    images = [wide] + [swapped(wide if flip < near else narrow, flip) for flip in flips]
    cells = lines * groups * points

    def factor(*refs):
        factor_kernel(cells, *refs)

    intersection, weights = call(
        factor,
        "factor",
        [shape((members, members), f32), shape((members * CAP, points), f32)],
        members**3,
        members**2 * 4,
        operands=1 + groups,
    )(owners, *overlaps)
    (routed,) = call(
        route_kernel,
        "route",
        [shape((CAP, groups * lines, points), bf16)],
        2 * CAP * members * groups * lines * points,
        6 * members * groups * lines * points,
        operands=1 + groups,
    )(weights, *images)
    return routed[None, None], intersection[None]


def solution(mesh):
    in_specs = (P("band", ("grid", "ham"), None), P(("grid", "ham"), None), P(), P("band", None))
    out_specs = (P("band", ("grid", "ham"), None, None, None), P("band", None, None))
    return jax.shard_map(local, mesh=mesh, in_specs=in_specs, out_specs=out_specs, check_vma=False)
```

time: 96.2 us -> 35.6 us (0.37)
  the two profiles are of different devices: /device:TPU:0 before, /device:TPU:5 now
where the time goes in v1:
time: 35.6 us; the launch traced here: 35.4 us
  starting transfers between devices  13.8 us (39%)
  Pallas kernels  9.56 us (27%)
  waiting for transfers between devices  7.84 us (22%)
  local copies, waits for them, and re-layouts  3.49 us (10%)
  between operations  0.72 us (2%)
    ppermute x4, starting transfers between devices, shifted(): return lax.ppermute(value, axis, pairs)  7.53 us
    ppermute x6, starting transfers between devices, swapped(): return lax.ppermute(value, ('grid', 'ham'), pairs)  6.25 us
    pallas_call x1, Pallas kernels, local(): call(image_kernel, 'image', [shape((members, lines, points), f32), shape(...  4.5 us
    ppermute x6, waiting for transfers between devices, swapped(): return lax.ppermute(value, ('grid', 'ham'), pairs)  4.38 us
    unnamed x15, local copies, waits for them, and re-layouts  3.49 us
    ppermute x4, waiting for transfers between devices, shifted(): return lax.ppermute(value, axis, pairs)  3.46 us
    pallas_call x1, Pallas kernels, local(): call(factor, 'factor', [shape((members, members), f32), shape((members *...  2.24 us
    pallas_call x1, Pallas kernels, local(): call(route_kernel, 'route', [shape((CAP, groups * lines, points), bf16)],...  1.5 us
  transfers between devices with their start and end apart: 10, of which 3 were waited for; matrix products, arithmetic and copies ran while one was open for 0% of the time, Pallas kernels for 10%

profile of v1, /device:TPU:5, one launch (start us, length us, event | category | flops | bytes accessed | tf_op | source)
XLA Modules:
  0.0 35.4 jit_solution(11367309411144527155)
XLA Ops:
  0.6 0.0 copy-start
  0.6 0.1 collective-permute-start
  0.7 2.4 %collective-permute-start.1 = (bf16[16,16,192]{2,1,0:T(8,128)(2,1)}, bf16[16,16,192]{2,1,0:T(8,128)(2,1)S(1)}, u32[]{:S(2)}, u32[]{:S(2)}) collective-permute-start(bf16[16,16,192]{2,1,0:T(8,128)(2,1)} %refs_0_.2), channel_id=1, source_target_pairs={{0,4},{4,8},{8,12},{12,16},{16,20},{20,24},{24,28},{28,0},{1,5},{5... | collective-permute-start | bytes 294920 | tf_op jit(solution)/shard_map/ppermute | solution.py:21
  3.1 5.1 %collective-permute-start.2 = (bf16[16,16,192]{2,1,0:T(8,128)(2,1)}, bf16[16,16,192]{2,1,0:T(8,128)(2,1)S(1)}, u32[]{:S(2)}, u32[]{:S(2)}) collective-permute-start(bf16[16,16,192]{2,1,0:T(8,128)(2,1)} %refs_0_.2), channel_id=1, source_target_pairs={{0,24},{4,28},{8,0},{12,4},{16,8},{20,12},{24,16},{28,20},{1,25},{... | collective-permute-start | bytes 294920 | tf_op jit(solution)/shard_map/ppermute | solution.py:21
  8.2 0.0 collective-permute-start.3
  8.2 0.9 %copy-done.1 = bf16[192,192]{1,0:T(8,128)(2,1)S(1)} copy-done((bf16[192,192]{1,0:T(8,128)(2,1)S(1)}, bf16[192,192]{1,0:T(8,128)(2,1)}, u32[]{:S(2)}) %copy-start.1) | copy-done | bytes 73752
  9.1 0.9 %copy-done.2 = bf16[192,192]{1,0:T(8,128)(2,1)S(1)} copy-done((bf16[192,192]{1,0:T(8,128)(2,1)S(1)}, bf16[192,192]{1,0:T(8,128)(2,1)}, u32[]{:S(2)}) %copy-start.2) | copy-done | bytes 73752
  10.0 0.9 %copy-done.3 = bf16[192,192]{1,0:T(8,128)(2,1)S(1)} copy-done((bf16[192,192]{1,0:T(8,128)(2,1)S(1)}, bf16[192,192]{1,0:T(8,128)(2,1)}, u32[]{:S(2)}) %copy-start.3) | copy-done | bytes 73752
  10.9 0.7 %copy-done.4 = f32[16,192]{1,0:T(8,128)S(1)} copy-done((f32[16,192]{1,0:T(8,128)S(1)}, f32[16,192]{1,0:T(8,128)}, u32[]{:S(2)}) %copy-start.4) | copy-done | bytes 12312
  11.6 1.3 %response.1.refs_5_ = f32[16,192,256]{2,1,0:T(8,128)S(1)} custom-call(f32[16,192]{1,0:T(8,128)S(1)} %copy-done.4, bf16[192,192]{1,0:T(8,128)(2,1)S(1)} %copy-done.3, bf16[192,192]{1,0:T(8,128)(2,1)S(1)} %copy-done.1, bf16[192,192]{1,0:T(8,128)(2,1)S(1)} %copy-done.2), custom_call_target="tpu_custom_call" | custom-call | flops 452984832 | bytes 2359296 | tf_op jit(solution)/shard_map/response/pallas_call | solution.py:193
  12.9 0.0 collective-permute-done.refs_1_
  12.9 0.0 collective-permute-done.1.refs_2_
  12.9 0.0 collective-permute-done.2.refs_3_
  12.9 3.4 %collective-permute-done.3.refs_4_ = bf16[16,16,192]{2,1,0:T(8,128)(2,1)S(1)} collective-permute-done((bf16[16,16,192]{2,1,0:T(8,128)(2,1)}, bf16[16,16,192]{2,1,0:T(8,128)(2,1)S(1)}, u32[]{:S(2)}, u32[]{:S(2)}) %collective-permute-start.3) | collective-permute-done | bytes 98336 | tf_op jit(solution)/shard_map/ppermute | solution.py:21
  16.4 0.0 copy-done
  16.4 0.0 copy-done.5
  16.4 4.5 %image.1 = (f32[16,16,192]{2,1,0:T(8,128)S(1)}, bf16[16,16,192]{2,1,0:T(8,128)(2,1)S(1)}, f32[16,16]{1,0:T(8,128)S(1)}) custom-call(s32[8]{0:T(128)S(1)} %copy-done.5, bf16[16,16,192]{2,1,0:T(8,128)(2,1)S(1)} %copy-done, bf16[16,16,192]{2,1,0:T(8,128)(2,1)S(1)} %collective-permute-done.refs_1_, bf16[16,16,192]{2,1,0:T(8,128)(2,1)S(1)} %collective-permute-done.1.refs_2_, ...), custom_call_target="tpu_custom_call" | custom-call | flops 132120576 | bytes 2359296 | tf_op jit(solution)/shard_map/image/pallas_call | solution.py:202
  20.9 2.1 %collective-permute-start.7 = (f32[16,16,192]{2,1,0:T(8,128)S(1)}, f32[16,16,192]{2,1,0:T(8,128)S(1)}, u32[]{:S(2)}, u32[]{:S(2)}) collective-permute-start(f32[16,16,192]{2,1,0:T(8,128)S(1)} %get-tuple-element.9.refs_0_), channel_id=1, source_target_pairs={{0,1},{1,0},{2,3},{3,2},{4,5},{5,4},{6,7},{7,6},{8,9},{9,8},{10,11... | collective-permute-start | bytes 589832 | tf_op jit(solution)/shard_map/ppermute | solution.py:27
  23.0 1.2 %collective-permute-start.8 = (bf16[16,16,192]{2,1,0:T(8,128)(2,1)S(1)}, bf16[16,16,192]{2,1,0:T(8,128)(2,1)S(1)}, u32[]{:S(2)}, u32[]{:S(2)}) collective-permute-start(bf16[16,16,192]{2,1,0:T(8,128)(2,1)S(1)} %get-tuple-element.10), channel_id=1, source_target_pairs={{0,2},{1,3},{2,0},{3,1},{4,6},{5,7},{6,4},{7,5},{8,10},{9,11},{10,... | collective-permute-start | bytes 294920 | tf_op jit(solution)/shard_map/ppermute | solution.py:27
  24.2 0.5 %collective-permute-start.9 = (bf16[16,16,192]{2,1,0:T(8,128)(2,1)S(1)}, bf16[16,16,192]{2,1,0:T(8,128)(2,1)S(1)}, u32[]{:S(2)}, u32[]{:S(2)}) collective-permute-start(bf16[16,16,192]{2,1,0:T(8,128)(2,1)S(1)} %get-tuple-element.10), channel_id=1, source_target_pairs={{0,3},{1,2},{2,1},{3,0},{4,7},{5,6},{6,5},{7,4},{8,11},{9,10},{10,... | collective-permute-start | bytes 294920 | tf_op jit(solution)/shard_map/ppermute | solution.py:27
  24.7 0.2 collective-permute-start.4
  24.9 1.2 %collective-permute-start.5 = (f32[16,16]{1,0:T(8,128)S(1)}, f32[16,16]{1,0:T(8,128)S(1)}, u32[]{:S(2)}, u32[]{:S(2)}) collective-permute-start(f32[16,16]{1,0:T(8,128)S(1)} %get-tuple-element.7.refs_1_), channel_id=1, source_target_pairs={{0,2},{1,3},{2,0},{3,1},{4,6},{5,7},{6,4},{7,5},{8,10},{9,11},{10,... | collective-permute-start | bytes 3080 | tf_op jit(solution)/shard_map/ppermute | solution.py:27
  26.1 0.0 collective-permute-done.4.refs_2_
  26.1 1.1 %collective-permute-start.6 = (f32[16,16]{1,0:T(8,128)S(1)}, f32[16,16]{1,0:T(8,128)S(1)}, u32[]{:S(2)}, u32[]{:S(2)}) collective-permute-start(f32[16,16]{1,0:T(8,128)S(1)} %get-tuple-element.7.refs_1_), channel_id=1, source_target_pairs={{0,3},{1,2},{2,1},{3,0},{4,7},{5,6},{6,5},{7,4},{8,11},{9,10},{10,... | collective-permute-start | bytes 3080 | tf_op jit(solution)/shard_map/ppermute | solution.py:27
  27.1 0.1 copy.9.refs_0_
  27.2 3.7 %collective-permute-done.5.refs_3_ = f32[16,16]{1,0:T(8,128)S(1)} collective-permute-done((f32[16,16]{1,0:T(8,128)S(1)}, f32[16,16]{1,0:T(8,128)S(1)}, u32[]{:S(2)}, u32[]{:S(2)}) %collective-permute-start.5) | collective-permute-done | bytes 1056 | tf_op jit(solution)/shard_map/ppermute | solution.py:27
  30.9 0.7 %collective-permute-done.6.refs_4_ = f32[16,16]{1,0:T(8,128)S(1)} collective-permute-done((f32[16,16]{1,0:T(8,128)S(1)}, f32[16,16]{1,0:T(8,128)S(1)}, u32[]{:S(2)}, u32[]{:S(2)}) %collective-permute-start.6) | collective-permute-done | bytes 1056 | tf_op jit(solution)/shard_map/ppermute | solution.py:27
  31.6 2.2 %factor.1 = (f32[16,16]{1,0:T(8,128)}, f32[128,192]{1,0:T(8,128)S(1)}) custom-call(s32[16,1]{1,0:T(8,128)S(1)} %copy.9.refs_0_, f32[16,16]{1,0:T(8,128)S(1)} %get-tuple-element.7.refs_1_, f32[16,16]{1,0:T(8,128)S(1)} %collective-permute-done.4.refs_2_, f32[16,16]{1,0:T(8,128)S(1)} %collective-permute-done.5.refs_3_, f32[16,16]{1,0:T(8,128)S(1)} %collective-permute-done.6.refs_4_), custom_call_target="tpu_custom_call" | custom-call | flops 4096 | bytes 1024 | tf_op jit(solution)/shard_map/factor/pallas_call | solution.py:228
  33.8 0.0 collective-permute-done.8.refs_2_
  33.9 0.0 collective-permute-done.9.refs_3_
  33.9 0.0 collective-permute-done.7.refs_1_
  33.9 1.5 %route.1 = bf16[8,64,192]{2,1,0:T(8,128)(2,1)} custom-call(f32[128,192]{1,0:T(8,128)S(1)} %get-tuple-element.8.weights_ref, f32[16,16,192]{2,1,0:T(8,128)S(1)} %get-tuple-element.9.refs_0_, f32[16,16,192]{2,1,0:T(8,128)S(1)} %collective-permute-done.7.refs_1_, bf16[16,16,192]{2,1,0:T(8,128)(2,1)S(1)} %collective-permute-done.8.refs_2_, ...), custom_call_target="tpu_custom_call" | custom-call | flops 3145728 | bytes 1179648 | tf_op jit(solution)/shard_map/route/pallas_call | solution.py:236
  (7 shorter events, 0.0 us)
Async XLA Ops:
  0.6 15.8 %copy-start = (bf16[16,16,192]{2,1,0:T(8,128)(2,1)S(1)}, bf16[16,16,192]{2,1,0:T(8,128)(2,1)}, u32[]{:S(2)}) copy-start(bf16[16,16,192]{2,1,0:T(8,128)(2,1)} %refs_0_.2) | copy-start | bytes 294916
  0.6 12.3 %collective-permute-start = (bf16[16,16,192]{2,1,0:T(8,128)(2,1)}, bf16[16,16,192]{2,1,0:T(8,128)(2,1)S(1)}, u32[]{:S(2)}, u32[]{:S(2)}) collective-permute-start(bf16[16,16,192]{2,1,0:T(8,128)(2,1)} %refs_0_.2), channel_id=1, source_target_pairs={{0,28},{4,0},{8,4},{12,8},{16,12},{20,16},{24,20},{28,24},{1,29},{... | collective-permute-start | bytes 294920 | tf_op jit(solution)/shard_map/ppermute | solution.py:21
  0.7 12.2 %collective-permute-start.1 = (bf16[16,16,192]{2,1,0:T(8,128)(2,1)}, bf16[16,16,192]{2,1,0:T(8,128)(2,1)S(1)}, u32[]{:S(2)}, u32[]{:S(2)}) collective-permute-start(bf16[16,16,192]{2,1,0:T(8,128)(2,1)} %refs_0_.2), channel_id=1, source_target_pairs={{0,4},{4,8},{8,12},{12,16},{16,20},{20,24},{24,28},{28,0},{1,5},{5... | collective-permute-start | bytes 294920 | tf_op jit(solution)/shard_map/ppermute | solution.py:21
  3.1 9.9 %collective-permute-start.2 = (bf16[16,16,192]{2,1,0:T(8,128)(2,1)}, bf16[16,16,192]{2,1,0:T(8,128)(2,1)S(1)}, u32[]{:S(2)}, u32[]{:S(2)}) collective-permute-start(bf16[16,16,192]{2,1,0:T(8,128)(2,1)} %refs_0_.2), channel_id=1, source_target_pairs={{0,24},{4,28},{8,0},{12,4},{16,8},{20,12},{24,16},{28,20},{1,25},{... | collective-permute-start | bytes 294920 | tf_op jit(solution)/shard_map/ppermute | solution.py:21
  8.2 8.2 %collective-permute-start.3 = (bf16[16,16,192]{2,1,0:T(8,128)(2,1)}, bf16[16,16,192]{2,1,0:T(8,128)(2,1)S(1)}, u32[]{:S(2)}, u32[]{:S(2)}) collective-permute-start(bf16[16,16,192]{2,1,0:T(8,128)(2,1)} %refs_0_.2), channel_id=1, source_target_pairs={{0,8},{4,12},{8,16},{12,20},{16,24},{20,28},{24,0},{28,4},{1,9},{5... | collective-permute-start | bytes 294920 | tf_op jit(solution)/shard_map/ppermute | solution.py:21
  8.2 0.9 %copy-start.1 = (bf16[192,192]{1,0:T(8,128)(2,1)S(1)}, bf16[192,192]{1,0:T(8,128)(2,1)}, u32[]{:S(2)}) copy-start(bf16[192,192]{1,0:T(8,128)(2,1)} %constant.10.inverse_ref) | copy-start | bytes 221188
  9.1 0.9 %copy-start.2 = (bf16[192,192]{1,0:T(8,128)(2,1)S(1)}, bf16[192,192]{1,0:T(8,128)(2,1)}, u32[]{:S(2)}) copy-start(bf16[192,192]{1,0:T(8,128)(2,1)} %constant.11.mirror_ref) | copy-start | bytes 221188
  10.0 0.9 %copy-start.3 = (bf16[192,192]{1,0:T(8,128)(2,1)S(1)}, bf16[192,192]{1,0:T(8,128)(2,1)}, u32[]{:S(2)}) copy-start(bf16[192,192]{1,0:T(8,128)(2,1)} %constant.9.forward_ref) | copy-start | bytes 221188
  10.9 0.7 %copy-start.4 = (f32[16,192]{1,0:T(8,128)S(1)}, f32[16,192]{1,0:T(8,128)}, u32[]{:S(2)}) copy-start(f32[16,192]{1,0:T(8,128)} %coulomb_ref.1) | copy-start | bytes 36868
  11.6 4.8 %copy-start.5 = (s32[8]{0:T(128)S(1)}, s32[8]{0:T(128)}, u32[]{:S(2)}) copy-start(s32[8]{0:T(128)} %occupied_ref.1) | copy-start | bytes 100
  11.6 15.6 %copy-start.6 = (s32[16,1]{0,1:T(1,128)S(1)}, s32[16,1]{0,1:T(1,128)}, u32[]{:S(2)}) copy-start(s32[16,1]{0,1:T(1,128)} %param.10) | copy-start | bytes 196
  20.9 13.0 %collective-permute-start.7 = (f32[16,16,192]{2,1,0:T(8,128)S(1)}, f32[16,16,192]{2,1,0:T(8,128)S(1)}, u32[]{:S(2)}, u32[]{:S(2)}) collective-permute-start(f32[16,16,192]{2,1,0:T(8,128)S(1)} %get-tuple-element.9.refs_0_), channel_id=1, source_target_pairs={{0,1},{1,0},{2,3},{3,2},{4,5},{5,4},{6,7},{7,6},{8,9},{9,8},{10,11... | collective-permute-start | bytes 589832 | tf_op jit(solution)/shard_map/ppermute | solution.py:27
  23.0 10.8 %collective-permute-start.8 = (bf16[16,16,192]{2,1,0:T(8,128)(2,1)S(1)}, bf16[16,16,192]{2,1,0:T(8,128)(2,1)S(1)}, u32[]{:S(2)}, u32[]{:S(2)}) collective-permute-start(bf16[16,16,192]{2,1,0:T(8,128)(2,1)S(1)} %get-tuple-element.10), channel_id=1, source_target_pairs={{0,2},{1,3},{2,0},{3,1},{4,6},{5,7},{6,4},{7,5},{8,10},{9,11},{10,... | collective-permute-start | bytes 294920 | tf_op jit(solution)/shard_map/ppermute | solution.py:27
  24.2 9.6 %collective-permute-start.9 = (bf16[16,16,192]{2,1,0:T(8,128)(2,1)S(1)}, bf16[16,16,192]{2,1,0:T(8,128)(2,1)S(1)}, u32[]{:S(2)}, u32[]{:S(2)}) collective-permute-start(bf16[16,16,192]{2,1,0:T(8,128)(2,1)S(1)} %get-tuple-element.10), channel_id=1, source_target_pairs={{0,3},{1,2},{2,1},{3,0},{4,7},{5,6},{6,5},{7,4},{8,11},{9,10},{10,... | collective-permute-start | bytes 294920 | tf_op jit(solution)/shard_map/ppermute | solution.py:27
  24.7 1.4 %collective-permute-start.4 = (f32[16,16]{1,0:T(8,128)S(1)}, f32[16,16]{1,0:T(8,128)S(1)}, u32[]{:S(2)}, u32[]{:S(2)}) collective-permute-start(f32[16,16]{1,0:T(8,128)S(1)} %get-tuple-element.7.refs_1_), channel_id=1, source_target_pairs={{0,1},{1,0},{2,3},{3,2},{4,5},{5,4},{6,7},{7,6},{8,9},{9,8},{10,11... | collective-permute-start | bytes 3080 | tf_op jit(solution)/shard_map/ppermute | solution.py:27
  24.9 6.0 %collective-permute-start.5 = (f32[16,16]{1,0:T(8,128)S(1)}, f32[16,16]{1,0:T(8,128)S(1)}, u32[]{:S(2)}, u32[]{:S(2)}) collective-permute-start(f32[16,16]{1,0:T(8,128)S(1)} %get-tuple-element.7.refs_1_), channel_id=1, source_target_pairs={{0,2},{1,3},{2,0},{3,1},{4,6},{5,7},{6,4},{7,5},{8,10},{9,11},{10,... | collective-permute-start | bytes 3080 | tf_op jit(solution)/shard_map/ppermute | solution.py:27
  26.1 5.5 %collective-permute-start.6 = (f32[16,16]{1,0:T(8,128)S(1)}, f32[16,16]{1,0:T(8,128)S(1)}, u32[]{:S(2)}, u32[]{:S(2)}) collective-permute-start(f32[16,16]{1,0:T(8,128)S(1)} %get-tuple-element.7.refs_1_), channel_id=1, source_target_pairs={{0,3},{1,2},{2,1},{3,0},{4,7},{5,6},{6,5},{7,4},{8,11},{9,10},{10,... | collective-permute-start | bytes 3080 | tf_op jit(solution)/shard_map/ppermute | solution.py:27

commit v2 on v1

v2 whole, which is shorter than its diff:
```python
import math

import jax
import jax.numpy as jnp
import numpy as np
from jax import lax
from jax.experimental import pallas as pl
from jax.experimental.pallas import tpu as pltpu
from jax.sharding import PartitionSpec as P

CAP = 8
LANES = 128
HIGHEST = lax.Precision.HIGHEST
VMEM_LIMIT = 48 * 1024 * 1024
NT = ((1,), (1,))
F32, BF16 = jnp.float32, jnp.bfloat16


def partners(block, count):
    even, low = block % 2 == 0, block % 4 < 2
    choose = jnp.where if isinstance(block, jax.Array) else (lambda c, a, b: a if c else b)
    steps = (choose(low, -2, 2), choose(even, -1, 1), choose(even, 1, -1), choose(low, 2, -2))
    return [(block + step + count) % count for step in steps]


def exchanged(value):
    count = lax.axis_size("band")
    assert count % 4 == 0
    tables = [partners(block, count) for block in range(count)]
    return [
        lax.ppermute(value, "band", [(block, row[turn]) for block, row in enumerate(tables)])
        for turn in range(4)
    ]


def swapped(value, flip):
    count = lax.axis_size("grid") * lax.axis_size("ham")
    return lax.ppermute(value, ("grid", "ham"), [(group, group ^ flip) for group in range(count)])


def spectral_tables(points):
    midpoint = points // 2
    ids = np.arange(points)
    frequency = np.where(ids <= midpoint, ids, ids - midpoint)
    angles = (ids[:, None] * frequency[None, :] % points) * (2.0 * math.pi / points)
    forward = np.where((ids <= midpoint)[None, :], np.cos(angles), np.sin(angles))
    single = (frequency == 0) | (ids == midpoint)
    inverse = forward.T * (np.where(single, 1.0, 2.0) / points)[:, None]
    mirror = np.zeros((points, points))
    mirror[frequency, ids] += 0.5
    mirror[(points - frequency) % points, ids] += 0.5
    return jnp.asarray(np.stack([forward.T, inverse.T, mirror]).astype(np.float32)).astype(BF16)


def halves(value):
    high = value.astype(BF16)
    return high, (value - high.astype(F32)).astype(BF16)


def dot32(a, b, contract=((1,), (0,))):
    return lax.dot_general(a, b, (contract, ((), ())), preferred_element_type=F32)


def dot_exact(a, b, contract=((1,), (0,))):
    return lax.dot_general(
        a, b, (contract, ((), ())), precision=HIGHEST, preferred_element_type=F32
    )


def ids(shape, axis):
    return lax.broadcasted_iota(jnp.int32, shape, axis)


def rows_of(block, pack, span):
    members, _, points = block.shape
    part = block[:, pack * span : (pack + 1) * span, :]
    return part.reshape(members * span, points)


def pack_kernel(orbitals_ref, out_ref):
    span = LANES // orbitals_ref.shape[0]
    block = orbitals_ref[...].astype(F32)
    for pack in range(out_ref.shape[0]):
        out_ref[pack] = rows_of(block, pack, span).T.astype(BF16)


def response_kernel(coulomb_ref, tables_ref, out_ref):
    points = coulomb_ref.shape[1]
    multiplier = dot_exact(coulomb_ref[...], tables_ref[2].astype(F32))
    forward = tables_ref[0]
    inverse = tables_ref[1].astype(F32)
    pad = jnp.zeros((points, out_ref.shape[2] - points), F32)
    for line in range(coulomb_ref.shape[0]):
        high, low = halves(inverse * multiplier[line : line + 1, :])
        out_ref[line, :, :points] = dot32(high, forward) + dot32(low, forward)
        out_ref[line, :, points:] = pad


def image_kernel(occupied_ref, orbitals_ref, *refs):
    blocks, (response_ref, wide_ref, narrow_ref, overlap_ref, window, masked) = refs[:-6], refs[-6:]
    members, lines, points = orbitals_ref.shape
    packs, padded, width = window.shape
    span = LANES // members
    total = lax.axis_size("band")
    position = lax.axis_index("band")
    places = [position] + partners(position, total)
    lane = ids((1, LANES), 1)
    filled = [(lane // span < occupied_ref[place]).astype(F32) for place in places]
    for place, block in enumerate(blocks):
        window[:, :points, place * LANES : (place + 1) * LANES] = block[...]
    window[:, points:, :] = jnp.zeros((packs, padded - points, width), BF16)
    natives = orbitals_ref[...].astype(F32)
    square = (LANES, LANES)
    same_line = ids(square, 0) % span == ids(square, 1) % span
    cross = jnp.zeros(square, F32)
    for pack in range(packs):
        whole = window[pack, :points, :]
        for line in range(span):
            chosen = (lane % span == line).astype(F32)
            mask = jnp.concatenate([f * chosen for f in filled], axis=1).astype(BF16)
            masked[line * points : (line + 1) * points, :] = whole * mask
        gram = dot32(masked[...], window[pack], NT)
        response = response_ref[pack * span : (pack + 1) * span].reshape(span * points, padded)
        high, low = halves(gram * response)
        native = window[pack, :, :LANES]
        fields = dot32(high, native) + dot32(low, native)
        image = jnp.zeros((points, LANES), F32)
        for line in range(span):
            field = fields[line * points : (line + 1) * points, :]
            image = jnp.where(lane % span == line, field, image)
        wide_ref[pack] = image
        narrow_ref[pack] = image.astype(BF16)
        high, low = halves(image)
        rows = rows_of(natives, pack, span).astype(BF16)
        cross = cross + (dot32(rows, high) + dot32(rows, low))
    cross = jnp.where(same_line, cross, 0.0).reshape(members, span, LANES).sum(axis=1)
    gather = (ids((LANES, members), 0) // span == ids((LANES, members), 1)).astype(F32)
    overlap_ref[...] = dot_exact(cross, gather)


def factor_kernel(cells, owners_ref, *refs):
    parts, (overlap_ref, weights_ref) = refs[:-2], refs[-2:]
    members = owners_ref.shape[0]
    span = LANES // members
    sums = [part[...] for part in parts]
    while len(sums) > 1:
        sums = [a + b for a, b in zip(sums[::2], sums[1::2])]
    overlap = sums[0] * (1.0 / cells)
    overlap_ref[...] = overlap
    square = (members, members)
    row_ids, col_ids = ids(square, 0), ids(square, 1)
    identity = (row_ids == col_ids).astype(F32)
    upper = 0.5 * (overlap + dot_exact(overlap, identity, ((0,), (0,))))
    lower = identity
    for k in range(members):
        column = jnp.broadcast_to(upper[:, k : k + 1], square)
        pivot = jnp.broadcast_to(column[k : k + 1, :], square)
        scale = jnp.where(row_ids > k, column / pivot, 0.0)
        upper = upper - scale * upper[k : k + 1, :]
        lower = lower - scale * lower[k : k + 1, :]
    diagonal = jnp.sum(upper * identity, axis=1, keepdims=True)
    inverse = lower / jnp.sqrt(diagonal)
    group = lax.axis_index("grid") * lax.axis_size("ham") + lax.axis_index("ham")
    mine = (owners_ref[...] == group).astype(F32)
    before = (col_ids < row_ids).astype(F32)
    ranking = dot_exact(before, jnp.broadcast_to(mine, (members, CAP)))
    slots = ids((members, CAP), 1).astype(F32)
    placement = jnp.where(ranking == slots, 1.0, 0.0) * mine
    chosen = dot_exact(placement, inverse, ((0,), (0,)))
    rows = CAP * span
    spread = (ids((members, LANES), 0) == ids((members, LANES), 1) // span).astype(F32)
    repeat = (ids((rows, CAP), 0) // span == ids((rows, CAP), 1)).astype(F32)
    weights = dot_exact(repeat, dot_exact(chosen, spread))
    same_line = ids((rows, LANES), 0) % span == ids((rows, LANES), 1) % span
    high, low = halves(jnp.where(same_line, weights, 0.0))
    weights_ref[:rows, :] = high
    weights_ref[rows:, :] = low


def route_kernel(weights_ref, *refs):
    parts, out_ref = refs[:-1], refs[-1]
    packs, points, _ = parts[0].shape
    weights = weights_ref[...]
    rows = weights.shape[0] // 2
    span = rows // CAP
    lines = packs * span
    group = lax.axis_index("grid") * lax.axis_size("ham") + lax.axis_index("ham")
    for flip, part in enumerate(parts):
        start = pl.multiple_of((group ^ flip) * lines, lines)
        sums = []
        for pack in range(packs):
            if part.dtype == BF16:
                both = dot32(weights, part[pack], NT)
                result = both[:rows] + both[rows:]
            else:
                high, low = halves(part[pack])
                both = dot32(weights, high, NT)
                result = both[:rows] + (both[rows:] + dot32(weights[:rows], low, NT))
            sums.append(result.reshape(CAP, span, points))
        out_ref[:, pl.ds(start, lines), :] = jnp.concatenate(sums, axis=1).astype(BF16)


def call(kernel, name, shapes, flops, moved, scratch=(), scalars=0, operands=0):
    vmem = pl.BlockSpec(memory_space=pltpu.VMEM)
    smem = pl.BlockSpec(memory_space=pltpu.SMEM)
    return pl.pallas_call(
        kernel,
        name=name,
        out_shape=shapes,
        in_specs=[smem] * scalars + [vmem] * operands,
        out_specs=[vmem] * len(shapes),
        scratch_shapes=list(scratch),
        compiler_params=pltpu.CompilerParams(vmem_limit_bytes=VMEM_LIMIT),
        cost_estimate=pl.CostEstimate(flops=flops, bytes_accessed=moved, transcendentals=0),
    )


def local(orbitals, coulomb, occupied, owners):
    members, lines, points = orbitals.shape
    grids, near = lax.axis_size("grid"), lax.axis_size("ham")
    groups = grids * near
    padded = -(-points // LANES) * LANES
    span = LANES // members
    packs = lines // span
    shape = jax.ShapeDtypeStruct
    (packed,) = call(
        pack_kernel,
        "pack",
        [shape((packs, points, LANES), BF16)],
        orbitals.size,
        4 * orbitals.size,
        operands=1,
    )(orbitals)
    guests = exchanged(packed)
    (response,) = call(
        response_kernel,
        "response",
        [shape((lines, points, padded), F32)],
        4 * lines * points**3,
        4 * lines * points**2,
        operands=2,
    )(coulomb, spectral_tables(points))
    blocks = len(guests) + 1
    width = blocks * LANES
    wide, narrow, overlap = call(
        image_kernel,
        "image",
        [
            shape((packs, points, LANES), F32),
            shape((packs, points, LANES), BF16),
            shape((members, members), F32),
        ],
        2 * lines * points * padded * (width + 2 * LANES),
        4 * lines * points**2,
        scratch=[
            pltpu.VMEM((packs, padded, width), BF16),
            pltpu.VMEM((span * points, width), BF16),
        ],
        scalars=1,
        operands=blocks + 2,
    )(occupied, orbitals, packed, *guests, response)

    def gathered(value, far):
        held = [value] + [swapped(value, flip) for flip in range(1, near)]
        for grid in range(1, grids):
            across = swapped(far, grid * near)
            held += [across] + [swapped(across, flip) for flip in range(1, near)]
        return held

    overlaps = gathered(overlap, overlap)
    images = gathered(wide, narrow)
    cells = lines * groups * points

    def factor(*refs):
        factor_kernel(cells, *refs)

    intersection, weights = call(
        factor,
        "factor",
        [shape((members, members), F32), shape((2 * CAP * span, LANES), BF16)],
        members**3,
        members**2 * 4,
        operands=1 + groups,
    )(owners, *overlaps)
    (routed,) = call(
        route_kernel,
        "route",
        [shape((CAP, groups * lines, points), BF16)],
        2 * CAP * members * groups * lines * points,
        6 * members * groups * lines * points,
        operands=1 + groups,
    )(weights, *images)
    return routed[None, None], intersection[None]


def solution(mesh):
    in_specs = (P("band", ("grid", "ham"), None), P(("grid", "ham"), None), P(), P("band", None))
    out_specs = (P("band", ("grid", "ham"), None, None, None), P("band", None, None))
    return jax.shard_map(local, mesh=mesh, in_specs=in_specs, out_specs=out_specs, check_vma=False)
```

time: 35.6 us -> 33.3 us (0.935)
  the two profiles are of different devices: /device:TPU:5 before, /device:TPU:0 now
where the time goes in v2:
time: 33.3 us; the launch traced here: 33.1 us
  starting transfers between devices  11.3 us (34%)
  Pallas kernels  10.1 us (30%)
  waiting for transfers between devices  8.24 us (25%)
  local copies, waits for them, and re-layouts  2.67 us (8%)
  between operations  0.71 us (2%)
    ppermute x4, starting transfers between devices, exchanged(): lax.ppermute(value, 'band', [(block, row[turn]) for block, row in enumera...  8.1 us
    ppermute x6, waiting for transfers between devices, swapped(): lax.ppermute(value, ('grid', 'ham'), [(group, group ^ flip) for group in...  6.14 us
    pallas_call x1, Pallas kernels, local(): call(image_kernel, 'image', [shape((packs, points, LANES), F32), shape((p...  5.03 us
    ppermute x6, starting transfers between devices, swapped(): lax.ppermute(value, ('grid', 'ham'), [(group, group ^ flip) for group in...  3.23 us
    unnamed x13, local copies, waits for them, and re-layouts  2.67 us
    pallas_call x1, Pallas kernels, local(): call(factor, 'factor', [shape((members, members), F32), shape((2 * CAP *...  2.46 us
    ppermute x4, waiting for transfers between devices, exchanged(): lax.ppermute(value, 'band', [(block, row[turn]) for block, row in enumera...  2.1 us
    pallas_call x1, Pallas kernels, local(): call(response_kernel, 'response', [shape((lines, points, padded), F32)],...  1.31 us
  transfers between devices with their start and end apart: 10, of which 4 were waited for; matrix products, arithmetic and copies ran while one was open for 0% of the time, Pallas kernels for 11%

profile of v2, /device:TPU:0, one launch (start us, length us, event | category | flops | bytes accessed | tf_op | source)
XLA Modules:
  0.0 33.1 jit_solution(16859901216962495289)
XLA Ops:
  0.6 0.0 copy-start.1
  0.6 0.9 %copy-done.1 = bf16[16,16,192]{2,1,0:T(8,128)(2,1)S(1)} copy-done((bf16[16,16,192]{2,1,0:T(8,128)(2,1)S(1)}, bf16[16,16,192]{2,1,0:T(8,128)(2,1)}, u32[]{:S(2)}) %copy-start.1) | copy-done | bytes 98328
  1.5 0.1 pack.1.refs_0_
  1.6 5.1 %collective-permute-start = (bf16[2,192,128]{2,1,0:T(8,128)(2,1)S(1)}, bf16[2,192,128]{2,1,0:T(8,128)(2,1)S(1)}, u32[]{:S(2)}, u32[]{:S(2)}) collective-permute-start(bf16[2,192,128]{2,1,0:T(8,128)(2,1)S(1)} %pack.1.refs_0_), channel_id=1, source_target_pairs={{0,24},{4,28},{8,16},{12,20},{16,8},{20,12},{24,0},{28,4},{1,25},{... | collective-permute-start | bytes 294920 | tf_op jit(solution)/shard_map/ppermute | solution.py:31
  6.8 1.2 %collective-permute-start.1 = (bf16[2,192,128]{2,1,0:T(8,128)(2,1)S(1)}, bf16[2,192,128]{2,1,0:T(8,128)(2,1)S(1)}, u32[]{:S(2)}, u32[]{:S(2)}) collective-permute-start(bf16[2,192,128]{2,1,0:T(8,128)(2,1)S(1)} %pack.1.refs_0_), channel_id=1, source_target_pairs={{0,28},{4,8},{8,4},{12,16},{16,12},{20,24},{24,20},{28,0},{1,29},{... | collective-permute-start | bytes 294920 | tf_op jit(solution)/shard_map/ppermute | solution.py:31
  7.9 0.3 %collective-permute-start.2 = (bf16[2,192,128]{2,1,0:T(8,128)(2,1)S(1)}, bf16[2,192,128]{2,1,0:T(8,128)(2,1)S(1)}, u32[]{:S(2)}, u32[]{:S(2)}) collective-permute-start(bf16[2,192,128]{2,1,0:T(8,128)(2,1)S(1)} %pack.1.refs_0_), channel_id=1, source_target_pairs={{0,4},{4,0},{8,12},{12,8},{16,20},{20,16},{24,28},{28,24},{1,5},{5... | collective-permute-start | bytes 294920 | tf_op jit(solution)/shard_map/ppermute | solution.py:31
  8.3 1.5 %collective-permute-start.3 = (bf16[2,192,128]{2,1,0:T(8,128)(2,1)S(1)}, bf16[2,192,128]{2,1,0:T(8,128)(2,1)S(1)}, u32[]{:S(2)}, u32[]{:S(2)}) collective-permute-start(bf16[2,192,128]{2,1,0:T(8,128)(2,1)S(1)} %pack.1.refs_0_), channel_id=1, source_target_pairs={{0,8},{4,12},{8,0},{12,4},{16,24},{20,28},{24,16},{28,20},{1,9},{5... | collective-permute-start | bytes 294920 | tf_op jit(solution)/shard_map/ppermute | solution.py:31
  9.7 1.0 %copy-done = bf16[3,192,192]{2,1,0:T(8,128)(2,1)S(1)} copy-done((bf16[3,192,192]{2,1,0:T(8,128)(2,1)S(1)}, bf16[3,192,192]{2,1,0:T(8,128)(2,1)}, u32[]{:S(2)}) %copy-start) | copy-done | bytes 221208
  10.7 0.7 %copy-done.3 = f32[16,192]{1,0:T(8,128)S(1)} copy-done((f32[16,192]{1,0:T(8,128)S(1)}, f32[16,192]{1,0:T(8,128)}, u32[]{:S(2)}) %copy-start.3) | copy-done | bytes 12312
  11.4 1.3 %response.1.refs_5_ = f32[16,192,256]{2,1,0:T(8,128)S(1)} custom-call(f32[16,192]{1,0:T(8,128)S(1)} %copy-done.3, bf16[3,192,192]{2,1,0:T(8,128)(2,1)S(1)} %copy-done), custom_call_target="tpu_custom_call" | custom-call | flops 452984832 | bytes 2359296 | tf_op jit(solution)/shard_map/response/pallas_call | solution.py:235
  12.7 0.0 copy-start.5
  12.8 0.0 collective-permute-done.refs_1_
  12.8 2.1 %collective-permute-done.1.refs_2_ = bf16[2,192,128]{2,1,0:T(8,128)(2,1)S(1)} collective-permute-done((bf16[2,192,128]{2,1,0:T(8,128)(2,1)S(1)}, bf16[2,192,128]{2,1,0:T(8,128)(2,1)S(1)}, u32[]{:S(2)}, u32[]{:S(2)}) %collective-permute-start.1) | collective-permute-done | bytes 98336 | tf_op jit(solution)/shard_map/ppermute | solution.py:31
  14.9 0.0 collective-permute-done.2.refs_3_
  14.9 0.0 collective-permute-done.3.refs_4_
  14.9 0.0 copy-done.2
  14.9 5.0 %image.1 = (f32[2,192,128]{2,1,0:T(8,128)S(1)}, bf16[2,192,128]{2,1,0:T(8,128)(2,1)S(1)}, f32[16,16]{1,0:T(8,128)S(1)}) custom-call(s32[8]{0:T(128)S(1)} %copy-done.4, bf16[16,16,192]{2,1,0:T(8,128)(2,1)S(1)} %copy-done.2, bf16[2,192,128]{2,1,0:T(8,128)(2,1)S(1)} %pack.1.refs_0_, bf16[2,192,128]{2,1,0:T(8,128)(2,1)S(1)} %collective-permute-done.refs_1_, ...), custom_call_target="tpu_custom_call" | custom-call | flops 1409286144 | bytes 2359296 | tf_op jit(solution)/shard_map/image/pallas_call | solution.py:245
  19.9 1.5 %collective-permute-start.8 = (bf16[2,192,128]{2,1,0:T(8,128)(2,1)S(1)}, bf16[2,192,128]{2,1,0:T(8,128)(2,1)S(1)}, u32[]{:S(2)}, u32[]{:S(2)}) collective-permute-start(bf16[2,192,128]{2,1,0:T(8,128)(2,1)S(1)} %get-tuple-element.10), channel_id=1, source_target_pairs={{0,2},{1,3},{2,0},{3,1},{4,6},{5,7},{6,4},{7,5},{8,10},{9,11},{10,... | collective-permute-start | bytes 294920 | tf_op jit(solution)/shard_map/ppermute | solution.py:38
  21.4 0.0 collective-permute-start.7
  21.4 3.1 %collective-permute-done.8.refs_2_ = bf16[2,192,128]{2,1,0:T(8,128)(2,1)S(1)} collective-permute-done((bf16[2,192,128]{2,1,0:T(8,128)(2,1)S(1)}, bf16[2,192,128]{2,1,0:T(8,128)(2,1)S(1)}, u32[]{:S(2)}, u32[]{:S(2)}) %collective-permute-start.8) | collective-permute-done | bytes 98336 | tf_op jit(solution)/shard_map/ppermute | solution.py:38
  24.5 0.0 collective-permute-start.9
  24.5 1.5 %collective-permute-start.5 = (f32[16,16]{1,0:T(8,128)S(1)}, f32[16,16]{1,0:T(8,128)S(1)}, u32[]{:S(2)}, u32[]{:S(2)}) collective-permute-start(f32[16,16]{1,0:T(8,128)S(1)} %get-tuple-element.7.refs_1_), channel_id=1, source_target_pairs={{0,2},{1,3},{2,0},{3,1},{4,6},{5,7},{6,4},{7,5},{8,10},{9,11},{10,... | collective-permute-start | bytes 3080 | tf_op jit(solution)/shard_map/ppermute | solution.py:38
  26.0 0.2 collective-permute-start.4
  26.3 1.9 %collective-permute-done.5.refs_3_ = f32[16,16]{1,0:T(8,128)S(1)} collective-permute-done((f32[16,16]{1,0:T(8,128)S(1)}, f32[16,16]{1,0:T(8,128)S(1)}, u32[]{:S(2)}, u32[]{:S(2)}) %collective-permute-start.5) | collective-permute-done | bytes 1056 | tf_op jit(solution)/shard_map/ppermute | solution.py:38
  28.2 0.0 collective-permute-start.6
  28.2 0.1 copy.7.refs_0_
  28.3 0.0 collective-permute-done.4.refs_2_
  28.3 1.1 %collective-permute-done.6.refs_4_ = f32[16,16]{1,0:T(8,128)S(1)} collective-permute-done((f32[16,16]{1,0:T(8,128)S(1)}, f32[16,16]{1,0:T(8,128)S(1)}, u32[]{:S(2)}, u32[]{:S(2)}) %collective-permute-start.6) | collective-permute-done | bytes 1056 | tf_op jit(solution)/shard_map/ppermute | solution.py:38
  29.4 2.5 %factor.1 = (f32[16,16]{1,0:T(8,128)}, bf16[128,128]{1,0:T(8,128)(2,1)S(1)}) custom-call(s32[16,1]{1,0:T(8,128)S(1)} %copy.7.refs_0_, f32[16,16]{1,0:T(8,128)S(1)} %get-tuple-element.7.refs_1_, f32[16,16]{1,0:T(8,128)S(1)} %collective-permute-done.4.refs_2_, f32[16,16]{1,0:T(8,128)S(1)} %collective-permute-done.5.refs_3_, ...), custom_call_target="tpu_custom_call" | custom-call | flops 4096 | bytes 1024 | tf_op jit(solution)/shard_map/factor/pallas_call | solution.py:277
  31.8 0.0 collective-permute-done.9.refs_3_
  31.8 0.0 collective-permute-done.7.refs_1_
  31.9 1.2 %route.1 = bf16[8,64,192]{2,1,0:T(8,128)(2,1)} custom-call(bf16[128,128]{1,0:T(8,128)(2,1)S(1)} %get-tuple-element.8.weights_ref, f32[2,192,128]{2,1,0:T(8,128)S(1)} %get-tuple-element.9.refs_0_, f32[2,192,128]{2,1,0:T(8,128)S(1)} %collective-permute-done.7.refs_1_, bf16[2,192,128]{2,1,0:T(8,128)(2,1)S(1)} %collective-permute-done.8.refs_2_, ...), custom_call_target="tpu_custom_call" | custom-call | flops 3145728 | bytes 1179648 | tf_op jit(solution)/shard_map/route/pallas_call | solution.py:285
  (6 shorter events, 0.0 us)
Async XLA Ops:
  0.6 0.9 %copy-start.1 = (bf16[16,16,192]{2,1,0:T(8,128)(2,1)S(1)}, bf16[16,16,192]{2,1,0:T(8,128)(2,1)}, u32[]{:S(2)}) copy-start(bf16[16,16,192]{2,1,0:T(8,128)(2,1)} %orbitals_ref.3) | copy-start | bytes 294916
  1.5 13.3 %copy-start.2 = (bf16[16,16,192]{2,1,0:T(8,128)(2,1)S(1)}, bf16[16,16,192]{2,1,0:T(8,128)(2,1)}, u32[]{:S(2)}) copy-start(bf16[16,16,192]{2,1,0:T(8,128)(2,1)} %orbitals_ref.3) | copy-start | bytes 294916
  1.5 13.3 %copy-start.4 = (s32[8]{0:T(128)S(1)}, s32[8]{0:T(128)}, u32[]{:S(2)}) copy-start(s32[8]{0:T(128)} %occupied_ref.1) | copy-start | bytes 100
  1.6 11.1 %collective-permute-start = (bf16[2,192,128]{2,1,0:T(8,128)(2,1)S(1)}, bf16[2,192,128]{2,1,0:T(8,128)(2,1)S(1)}, u32[]{:S(2)}, u32[]{:S(2)}) collective-permute-start(bf16[2,192,128]{2,1,0:T(8,128)(2,1)S(1)} %pack.1.refs_0_), channel_id=1, source_target_pairs={{0,24},{4,28},{8,16},{12,20},{16,8},{20,12},{24,0},{28,4},{1,25},{... | collective-permute-start | bytes 294920 | tf_op jit(solution)/shard_map/ppermute | solution.py:31
  6.8 8.1 %collective-permute-start.1 = (bf16[2,192,128]{2,1,0:T(8,128)(2,1)S(1)}, bf16[2,192,128]{2,1,0:T(8,128)(2,1)S(1)}, u32[]{:S(2)}, u32[]{:S(2)}) collective-permute-start(bf16[2,192,128]{2,1,0:T(8,128)(2,1)S(1)} %pack.1.refs_0_), channel_id=1, source_target_pairs={{0,28},{4,8},{8,4},{12,16},{16,12},{20,24},{24,20},{28,0},{1,29},{... | collective-permute-start | bytes 294920 | tf_op jit(solution)/shard_map/ppermute | solution.py:31
  7.9 6.9 %collective-permute-start.2 = (bf16[2,192,128]{2,1,0:T(8,128)(2,1)S(1)}, bf16[2,192,128]{2,1,0:T(8,128)(2,1)S(1)}, u32[]{:S(2)}, u32[]{:S(2)}) collective-permute-start(bf16[2,192,128]{2,1,0:T(8,128)(2,1)S(1)} %pack.1.refs_0_), channel_id=1, source_target_pairs={{0,4},{4,0},{8,12},{12,8},{16,20},{20,16},{24,28},{28,24},{1,5},{5... | collective-permute-start | bytes 294920 | tf_op jit(solution)/shard_map/ppermute | solution.py:31
  8.3 6.6 %collective-permute-start.3 = (bf16[2,192,128]{2,1,0:T(8,128)(2,1)S(1)}, bf16[2,192,128]{2,1,0:T(8,128)(2,1)S(1)}, u32[]{:S(2)}, u32[]{:S(2)}) collective-permute-start(bf16[2,192,128]{2,1,0:T(8,128)(2,1)S(1)} %pack.1.refs_0_), channel_id=1, source_target_pairs={{0,8},{4,12},{8,0},{12,4},{16,24},{20,28},{24,16},{28,20},{1,9},{5... | collective-permute-start | bytes 294920 | tf_op jit(solution)/shard_map/ppermute | solution.py:31
  9.7 1.0 %copy-start = (bf16[3,192,192]{2,1,0:T(8,128)(2,1)S(1)}, bf16[3,192,192]{2,1,0:T(8,128)(2,1)}, u32[]{:S(2)}) copy-start(bf16[3,192,192]{2,1,0:T(8,128)(2,1)} %constant.3.tables_ref) | copy-start | bytes 663556
  10.7 0.7 %copy-start.3 = (f32[16,192]{1,0:T(8,128)S(1)}, f32[16,192]{1,0:T(8,128)}, u32[]{:S(2)}) copy-start(f32[16,192]{1,0:T(8,128)} %coulomb_ref.1) | copy-start | bytes 36868
  12.7 15.5 %copy-start.5 = (s32[16,1]{0,1:T(1,128)S(1)}, s32[16,1]{0,1:T(1,128)}, u32[]{:S(2)}) copy-start(s32[16,1]{0,1:T(1,128)} %param.8) | copy-start | bytes 196
  19.9 4.6 %collective-permute-start.8 = (bf16[2,192,128]{2,1,0:T(8,128)(2,1)S(1)}, bf16[2,192,128]{2,1,0:T(8,128)(2,1)S(1)}, u32[]{:S(2)}, u32[]{:S(2)}) collective-permute-start(bf16[2,192,128]{2,1,0:T(8,128)(2,1)S(1)} %get-tuple-element.10), channel_id=1, source_target_pairs={{0,2},{1,3},{2,0},{3,1},{4,6},{5,7},{6,4},{7,5},{8,10},{9,11},{10,... | collective-permute-start | bytes 294920 | tf_op jit(solution)/shard_map/ppermute | solution.py:38
  21.4 10.4 %collective-permute-start.7 = (f32[2,192,128]{2,1,0:T(8,128)S(1)}, f32[2,192,128]{2,1,0:T(8,128)S(1)}, u32[]{:S(2)}, u32[]{:S(2)}) collective-permute-start(f32[2,192,128]{2,1,0:T(8,128)S(1)} %get-tuple-element.9.refs_0_), channel_id=1, source_target_pairs={{0,1},{1,0},{2,3},{3,2},{4,5},{5,4},{6,7},{7,6},{8,9},{9,8},{10,11... | collective-permute-start | bytes 589832 | tf_op jit(solution)/shard_map/ppermute | solution.py:38
  24.5 7.3 %collective-permute-start.9 = (bf16[2,192,128]{2,1,0:T(8,128)(2,1)S(1)}, bf16[2,192,128]{2,1,0:T(8,128)(2,1)S(1)}, u32[]{:S(2)}, u32[]{:S(2)}) collective-permute-start(bf16[2,192,128]{2,1,0:T(8,128)(2,1)S(1)} %collective-permute-done.8.refs_2_), channel_id=1, source_target_pairs={{0,1},{1,0},{2,3},{3,2},{4,5},{5,4},{6,7},{7,6},{8,9},{9,8},{10,11... | collective-permute-start | bytes 294920 | tf_op jit(solution)/shard_map/ppermute | solution.py:38
  24.5 3.7 %collective-permute-start.5 = (f32[16,16]{1,0:T(8,128)S(1)}, f32[16,16]{1,0:T(8,128)S(1)}, u32[]{:S(2)}, u32[]{:S(2)}) collective-permute-start(f32[16,16]{1,0:T(8,128)S(1)} %get-tuple-element.7.refs_1_), channel_id=1, source_target_pairs={{0,2},{1,3},{2,0},{3,1},{4,6},{5,7},{6,4},{7,5},{8,10},{9,11},{10,... | collective-permute-start | bytes 3080 | tf_op jit(solution)/shard_map/ppermute | solution.py:38
  26.0 2.3 %collective-permute-start.4 = (f32[16,16]{1,0:T(8,128)S(1)}, f32[16,16]{1,0:T(8,128)S(1)}, u32[]{:S(2)}, u32[]{:S(2)}) collective-permute-start(f32[16,16]{1,0:T(8,128)S(1)} %get-tuple-element.7.refs_1_), channel_id=1, source_target_pairs={{0,1},{1,0},{2,3},{3,2},{4,5},{5,4},{6,7},{7,6},{8,9},{9,8},{10,11... | collective-permute-start | bytes 3080 | tf_op jit(solution)/shard_map/ppermute | solution.py:38
  28.2 1.2 %collective-permute-start.6 = (f32[16,16]{1,0:T(8,128)S(1)}, f32[16,16]{1,0:T(8,128)S(1)}, u32[]{:S(2)}, u32[]{:S(2)}) collective-permute-start(f32[16,16]{1,0:T(8,128)S(1)} %collective-permute-done.5.refs_3_), channel_id=1, source_target_pairs={{0,1},{1,0},{2,3},{3,2},{4,5},{5,4},{6,7},{7,6},{8,9},{9,8},{10,11... | collective-permute-start | bytes 3080 | tf_op jit(solution)/shard_map/ppermute | solution.py:38

commit v3 on v2

--- a/solution.py
+++ b/solution.py
@@ -12,6 +12,7 @@
 LANES = 128
 HIGHEST = lax.Precision.HIGHEST
 VMEM_LIMIT = 48 * 1024 * 1024
+FACTOR_COST = 3_000_000_000
 NT = ((1,), (1,))
 F32, BF16 = jnp.float32, jnp.bfloat16
 
@@ -71,6 +72,23 @@
     return lax.broadcasted_iota(jnp.int32, shape, axis)
 
 
+def lane_member(lane, members):
+    return lane % members
+
+
+def lane_quarter(lane, turn):
+    return (lane // (LANES // 4)) ^ turn
+
+
+def lane_line(lane, turn, members):
+    per = LANES // 4 // members
+    return lane_quarter(lane, turn) * per + lane % (LANES // 4) // members
+
+
+def own_turn():
+    return lax.axis_index("band") % 4
+
+
 def rows_of(block, pack, span):
     members, _, points = block.shape
     part = block[:, pack * span : (pack + 1) * span, :]
@@ -78,10 +96,15 @@
 
 
 def pack_kernel(orbitals_ref, out_ref):
-    span = LANES // orbitals_ref.shape[0]
+    members = orbitals_ref.shape[0]
+    span = LANES // members
     block = orbitals_ref[...].astype(F32)
+    row, lane = ids((LANES, LANES), 0), ids((LANES, LANES), 1)
+    source = lane_member(lane, members) * span + lane_line(lane, own_turn(), members)
+    order = (row == source).astype(BF16)
     for pack in range(out_ref.shape[0]):
-        out_ref[pack] = rows_of(block, pack, span).T.astype(BF16)
+        rows = rows_of(block, pack, span).T.astype(BF16)
+        out_ref[pack] = dot32(rows, order).astype(BF16)
 
 
 def response_kernel(coulomb_ref, tables_ref, out_ref):
@@ -97,84 +120,109 @@
 
 
 def image_kernel(occupied_ref, orbitals_ref, *refs):
-    blocks, (response_ref, wide_ref, narrow_ref, overlap_ref, window, masked) = refs[:-6], refs[-6:]
+    blocks, (response_ref, wide_ref, narrow_ref, overlap_ref) = refs[:-4], refs[-4:]
     members, lines, points = orbitals_ref.shape
-    packs, padded, width = window.shape
+    packs = blocks[0].shape[0]
+    padded = response_ref.shape[2]
     span = LANES // members
+    per = span // 4
     total = lax.axis_size("band")
     position = lax.axis_index("band")
     places = [position] + partners(position, total)
+    turns = [place % 4 for place in places]
     lane = ids((1, LANES), 1)
-    filled = [(lane // span < occupied_ref[place]).astype(F32) for place in places]
-    for place, block in enumerate(blocks):
-        window[:, :points, place * LANES : (place + 1) * LANES] = block[...]
-    window[:, points:, :] = jnp.zeros((packs, padded - points, width), BF16)
+    own_line = lane_line(lane, turns[0], members)
+    filled = [lane_member(lane, members) < occupied_ref[place] for place in places]
+    quarters = [lane_quarter(lane, turn) for turn in turns]
+    step = lane % (LANES // 4) // members
+    apart, merged = 1, (0, 2, 3, 4)
     natives = orbitals_ref[...].astype(F32)
     square = (LANES, LANES)
-    same_line = ids(square, 0) % span == ids(square, 1) % span
+    row_line = ids(square, 0) % span
+    same_line = row_line == lane_line(ids(square, 1), turns[0], members)
+    blank = jnp.zeros((padded - points, 2 * LANES), BF16)
     cross = jnp.zeros(square, F32)
     for pack in range(packs):
-        whole = window[pack, :points, :]
-        for line in range(span):
-            chosen = (lane % span == line).astype(F32)
-            mask = jnp.concatenate([f * chosen for f in filled], axis=1).astype(BF16)
-            masked[line * points : (line + 1) * points, :] = whole * mask
-        gram = dot32(masked[...], window[pack], NT)
-        response = response_ref[pack * span : (pack + 1) * span].reshape(span * points, padded)
-        high, low = halves(gram * response)
-        native = window[pack, :, :LANES]
-        fields = dot32(high, native) + dot32(low, native)
+        tiles = [block[pack] for block in blocks]
+        native = jnp.concatenate([tiles[0], blank[:, :LANES]], axis=0)
         image = jnp.zeros((points, LANES), F32)
-        for line in range(span):
-            field = fields[line * points : (line + 1) * points, :]
-            image = jnp.where(lane % span == line, field, image)
+        for quarter in range(4):
+            here = [(q == quarter) for q in quarters]
+            together = sum(tiles[m] * here[m].astype(F32).astype(BF16) for m in merged)
+            window = jnp.concatenate([together, tiles[apart]], axis=1)
+            occupied = sum((here[m] & filled[m]).astype(F32) for m in merged)
+            beside = (here[apart] & filled[apart]).astype(F32)
+            both = jnp.concatenate([occupied, beside], axis=1)
+            steps = jnp.concatenate([step, step], axis=1)
+            masked = jnp.concatenate(
+                [window * jnp.where(steps == k, both, 0.0).astype(BF16) for k in range(per)], axis=0
+            )
+            gram = dot32(masked, jnp.concatenate([window, blank], axis=0), NT)
+            first = pack * span + quarter * per
+            response = response_ref[first : first + per].reshape(per * points, padded)
+            high, low = halves(gram * response)
+            fields = dot32(jnp.concatenate([high, low], axis=0), native)
+            for k in range(per):
+                a, b = k * points, (per + k) * points
+                field = fields[a : a + points] + fields[b : b + points]
+                image = jnp.where(own_line == quarter * per + k, field, image)
         wide_ref[pack] = image
         narrow_ref[pack] = image.astype(BF16)
-        high, low = halves(image)
         rows = rows_of(natives, pack, span).astype(BF16)
-        cross = cross + (dot32(rows, high) + dot32(rows, low))
+        product = dot32(rows, jnp.concatenate(halves(image), axis=1))
+        cross = cross + (product[:, :LANES] + product[:, LANES:])
     cross = jnp.where(same_line, cross, 0.0).reshape(members, span, LANES).sum(axis=1)
-    gather = (ids((LANES, members), 0) // span == ids((LANES, members), 1)).astype(F32)
-    overlap_ref[...] = dot_exact(cross, gather)
+    gather = lane_member(ids((LANES, members), 0), members) == ids((LANES, members), 1)
+    overlap_ref[...] = dot_exact(cross, gather.astype(F32))
 
 
 def factor_kernel(cells, owners_ref, *refs):
     parts, (overlap_ref, weights_ref) = refs[:-2], refs[-2:]
     members = owners_ref.shape[0]
     span = LANES // members
+    turn = own_turn()
     sums = [part[...] for part in parts]
     while len(sums) > 1:
         sums = [a + b for a, b in zip(sums[::2], sums[1::2])]
     overlap = sums[0] * (1.0 / cells)
     overlap_ref[...] = overlap
+    rows = CAP * span
     square = (members, members)
-    row_ids, col_ids = ids(square, 0), ids(square, 1)
-    identity = (row_ids == col_ids).astype(F32)
-    upper = 0.5 * (overlap + dot_exact(overlap, identity, ((0,), (0,))))
-    lower = identity
-    for k in range(members):
-        column = jnp.broadcast_to(upper[:, k : k + 1], square)
-        pivot = jnp.broadcast_to(column[k : k + 1, :], square)
-        scale = jnp.where(row_ids > k, column / pivot, 0.0)
-        upper = upper - scale * upper[k : k + 1, :]
-        lower = lower - scale * lower[k : k + 1, :]
-    diagonal = jnp.sum(upper * identity, axis=1, keepdims=True)
-    inverse = lower / jnp.sqrt(diagonal)
     group = lax.axis_index("grid") * lax.axis_size("ham") + lax.axis_index("ham")
     mine = (owners_ref[...] == group).astype(F32)
-    before = (col_ids < row_ids).astype(F32)
-    ranking = dot_exact(before, jnp.broadcast_to(mine, (members, CAP)))
-    slots = ids((members, CAP), 1).astype(F32)
-    placement = jnp.where(ranking == slots, 1.0, 0.0) * mine
-    chosen = dot_exact(placement, inverse, ((0,), (0,)))
-    rows = CAP * span
-    spread = (ids((members, LANES), 0) == ids((members, LANES), 1) // span).astype(F32)
-    repeat = (ids((rows, CAP), 0) // span == ids((rows, CAP), 1)).astype(F32)
-    weights = dot_exact(repeat, dot_exact(chosen, spread))
-    same_line = ids((rows, LANES), 0) % span == ids((rows, LANES), 1) % span
-    high, low = halves(jnp.where(same_line, weights, 0.0))
-    weights_ref[:rows, :] = high
-    weights_ref[rows:, :] = low
+    eye = (ids(square, 0) == ids(square, 1)).astype(F32)
+    mine_row = jnp.sum(mine * eye, axis=0, keepdims=True)
+    before = (ids(square, 0) < ids(square, 1)).astype(F32)
+    ranking = jnp.sum(mine * before, axis=0, keepdims=True)
+    slot = (ids((rows, members), 0) // span).astype(F32)
+    placed = (jnp.where(slot == ranking, 1.0, 0.0) * mine_row).astype(BF16)
+    wide = (members, LANES)
+    row = ids(wide, 0)
+    upper = 0.5 * (overlap + dot_exact(overlap, eye, ((0,), (0,))))
+    lower = (row == lane_member(ids(wide, 1), members)).astype(F32)
+    for k in range(0, members, 2):
+        first = jnp.broadcast_to(upper[:, k : k + 1], wide)
+        second = jnp.broadcast_to(upper[:, k + 1 : k + 2], wide)
+        a, b, c = first[k : k + 1], first[k + 1 : k + 2], second[k + 1 : k + 2]
+        scale = 1.0 / (a * c - b * b)
+        below = row > k + 1
+        one = jnp.where(below, (first * c - second * b) * scale, 0.0)
+        two = jnp.where(below, (second * a - first * b) * scale, 0.0)
+        lower = lower - (one * lower[k : k + 1] + two * lower[k + 1 : k + 2])
+        one, two = one[:, :members], two[:, :members]
+        upper = upper - (one * upper[k : k + 1] + two * upper[k + 1 : k + 2])
+    diagonal = jnp.sum(upper * eye, axis=1, keepdims=True)
+    beside = (ids(square, 0) == ids(square, 1) + 1) & (ids(square, 0) % 2 == 1)
+    share = jnp.sum(jnp.where(beside, upper, 0.0), axis=1, keepdims=True)
+    previous = jnp.concatenate([diagonal[:1], diagonal[:-1]], axis=0)
+    ratio = share / previous
+    above = jnp.concatenate([lower[:1], lower[:-1]], axis=0)
+    inverse = (lower - ratio * above) / jnp.sqrt(diagonal - ratio * share)
+    high, low = halves(inverse)
+    same_line = ids((rows, LANES), 0) % span == lane_line(ids((rows, LANES), 1), turn, members)
+    for place, half in ((0, high), (rows, low)):
+        chosen = jnp.where(same_line, dot32(placed, half), 0.0)
+        weights_ref[place : place + rows, :] = chosen.astype(BF16)
 
 
 def route_kernel(weights_ref, *refs):
@@ -241,7 +289,6 @@
         operands=2,
     )(coulomb, spectral_tables(points))
     blocks = len(guests) + 1
-    width = blocks * LANES
     wide, narrow, overlap = call(
         image_kernel,
         "image",
@@ -250,25 +297,17 @@
             shape((packs, points, LANES), BF16),
             shape((members, members), F32),
         ],
-        2 * lines * points * padded * (width + 2 * LANES),
+        2 * lines * points * padded * (4 * LANES),
         4 * lines * points**2,
-        scratch=[
-            pltpu.VMEM((packs, padded, width), BF16),
-            pltpu.VMEM((span * points, width), BF16),
-        ],
         scalars=1,
         operands=blocks + 2,
     )(occupied, orbitals, packed, *guests, response)
 
-    def gathered(value, far):
-        held = [value] + [swapped(value, flip) for flip in range(1, near)]
-        for grid in range(1, grids):
-            across = swapped(far, grid * near)
-            held += [across] + [swapped(across, flip) for flip in range(1, near)]
-        return held
-
-    overlaps = gathered(overlap, overlap)
-    images = gathered(wide, narrow)
+    overlaps = [overlap] + [swapped(overlap, flip) for flip in range(1, groups)]
+    images = [wide] + [swapped(wide, flip) for flip in range(1, near)]
+    for grid in range(1, grids):
+        across = swapped(narrow, grid * near)
+        images += [across] + [swapped(across, flip) for flip in range(1, near)]
     cells = lines * groups * points
 
     def factor(*refs):
@@ -278,7 +317,7 @@
         factor,
         "factor",
         [shape((members, members), F32), shape((2 * CAP * span, LANES), BF16)],
-        members**3,
+        FACTOR_COST,
         members**2 * 4,
         operands=1 + groups,
     )(owners, *overlaps)

time: 33.3 us -> 25.9 us (0.78)
  waiting for transfers between devices: 8.24 us -> 3.58 us
  Pallas kernels: 10.1 us -> 6.94 us
  starting transfers between devices: 11.3 us -> 11.7 us
    ppermute x6, waiting for transfers between devices: 6.14 us -> 1.48 us  [swapped(): lax.ppermute(value, ('grid', 'ham'), [(group, group ^ flip) for group in...]
    pallas_call x1, Pallas kernels: 5.03 us -> 2.85 us  [local(): call(image_kernel, 'image', [shape((packs, points, LANES), F32), shape((p...]
    pallas_call x1, Pallas kernels: 2.46 us -> 1.31 us  [local(): call(factor, 'factor', [shape((members, members), F32), shape((2 * CAP *...]
    ppermute x6, starting transfers between devices: 3.23 us -> 3.65 us  [swapped(): lax.ppermute(value, ('grid', 'ham'), [(group, group ^ flip) for group in...]
  transfers between devices with their start and end apart: 10 -> 10, of which waited for: 4 -> 3; matrix products, arithmetic and copies ran while one was open for 0% -> 0% of each run, Pallas kernels for 11% -> 10%
where the time goes in v3:
time: 25.9 us; the launch traced here: 25.7 us
  starting transfers between devices  11.7 us (45%)
  Pallas kernels  6.94 us (27%)
  waiting for transfers between devices  3.58 us (14%)
  local copies, waits for them, and re-layouts  2.67 us (10%)
  between operations  0.71 us (3%)
    ppermute x4, starting transfers between devices, exchanged(): lax.ppermute(value, 'band', [(block, row[turn]) for block, row in enumera...  8.1 us
    ppermute x6, starting transfers between devices, swapped(): lax.ppermute(value, ('grid', 'ham'), [(group, group ^ flip) for group in...  3.65 us
    pallas_call x1, Pallas kernels, local(): call(image_kernel, 'image', [shape((packs, points, LANES), F32), shape((p...  2.85 us
    unnamed x13, local copies, waits for them, and re-layouts  2.67 us
    ppermute x4, waiting for transfers between devices, exchanged(): lax.ppermute(value, 'band', [(block, row[turn]) for block, row in enumera...  2.11 us
    ppermute x6, waiting for transfers between devices, swapped(): lax.ppermute(value, ('grid', 'ham'), [(group, group ^ flip) for group in...  1.48 us
    pallas_call x1, Pallas kernels, local(): call(response_kernel, 'response', [shape((lines, points, padded), F32)],...  1.31 us
    pallas_call x1, Pallas kernels, local(): call(factor, 'factor', [shape((members, members), F32), shape((2 * CAP *...  1.31 us
  transfers between devices with their start and end apart: 10, of which 3 were waited for; matrix products, arithmetic and copies ran while one was open for 0% of the time, Pallas kernels for 10%

profile of v3, /device:TPU:0, one launch (start us, length us, event | category | flops | bytes accessed | tf_op | source)
XLA Modules:
  0.0 25.7 jit_solution(2737739630015876692)
XLA Ops:
  0.6 0.0 copy-start
  0.6 0.9 %copy-done = bf16[16,16,192]{2,1,0:T(8,128)(2,1)S(1)} copy-done((bf16[16,16,192]{2,1,0:T(8,128)(2,1)S(1)}, bf16[16,16,192]{2,1,0:T(8,128)(2,1)}, u32[]{:S(2)}) %copy-start) | copy-done | bytes 98328
  1.5 0.2 pack.1.refs_0_
  1.8 5.1 %collective-permute-start = (bf16[2,192,128]{2,1,0:T(8,128)(2,1)S(1)}, bf16[2,192,128]{2,1,0:T(8,128)(2,1)S(1)}, u32[]{:S(2)}, u32[]{:S(2)}) collective-permute-start(bf16[2,192,128]{2,1,0:T(8,128)(2,1)S(1)} %pack.1.refs_0_), channel_id=1, source_target_pairs={{0,24},{4,28},{8,16},{12,20},{16,8},{20,12},{24,0},{28,4},{1,25},{... | collective-permute-start | bytes 294920 | tf_op jit(solution)/shard_map/ppermute | solution.py:32
  6.9 1.2 %collective-permute-start.1 = (bf16[2,192,128]{2,1,0:T(8,128)(2,1)S(1)}, bf16[2,192,128]{2,1,0:T(8,128)(2,1)S(1)}, u32[]{:S(2)}, u32[]{:S(2)}) collective-permute-start(bf16[2,192,128]{2,1,0:T(8,128)(2,1)S(1)} %pack.1.refs_0_), channel_id=1, source_target_pairs={{0,28},{4,8},{8,4},{12,16},{16,12},{20,24},{24,20},{28,0},{1,29},{... | collective-permute-start | bytes 294920 | tf_op jit(solution)/shard_map/ppermute | solution.py:32
  8.1 0.3 %collective-permute-start.2 = (bf16[2,192,128]{2,1,0:T(8,128)(2,1)S(1)}, bf16[2,192,128]{2,1,0:T(8,128)(2,1)S(1)}, u32[]{:S(2)}, u32[]{:S(2)}) collective-permute-start(bf16[2,192,128]{2,1,0:T(8,128)(2,1)S(1)} %pack.1.refs_0_), channel_id=1, source_target_pairs={{0,4},{4,0},{8,12},{12,8},{16,20},{20,16},{24,28},{28,24},{1,5},{5... | collective-permute-start | bytes 294920 | tf_op jit(solution)/shard_map/ppermute | solution.py:32
  8.4 1.5 %collective-permute-start.3 = (bf16[2,192,128]{2,1,0:T(8,128)(2,1)S(1)}, bf16[2,192,128]{2,1,0:T(8,128)(2,1)S(1)}, u32[]{:S(2)}, u32[]{:S(2)}) collective-permute-start(bf16[2,192,128]{2,1,0:T(8,128)(2,1)S(1)} %pack.1.refs_0_), channel_id=1, source_target_pairs={{0,8},{4,12},{8,0},{12,4},{16,24},{20,28},{24,16},{28,20},{1,9},{5... | collective-permute-start | bytes 294920 | tf_op jit(solution)/shard_map/ppermute | solution.py:32
  9.9 1.0 %copy-done.2 = bf16[3,192,192]{2,1,0:T(8,128)(2,1)S(1)} copy-done((bf16[3,192,192]{2,1,0:T(8,128)(2,1)S(1)}, bf16[3,192,192]{2,1,0:T(8,128)(2,1)}, u32[]{:S(2)}) %copy-start.2) | copy-done | bytes 221208
  10.8 0.7 %copy-done.3 = f32[16,192]{1,0:T(8,128)S(1)} copy-done((f32[16,192]{1,0:T(8,128)S(1)}, f32[16,192]{1,0:T(8,128)}, u32[]{:S(2)}) %copy-start.3) | copy-done | bytes 12312
  11.6 1.3 %response.1.refs_5_ = f32[16,192,256]{2,1,0:T(8,128)S(1)} custom-call(f32[16,192]{1,0:T(8,128)S(1)} %copy-done.3, bf16[3,192,192]{2,1,0:T(8,128)(2,1)S(1)} %copy-done.2), custom_call_target="tpu_custom_call" | custom-call | flops 452984832 | bytes 2359296 | tf_op jit(solution)/shard_map/response/pallas_call | solution.py:283
  12.9 0.0 collective-permute-done.refs_1_
  12.9 2.1 %collective-permute-done.1.refs_2_ = bf16[2,192,128]{2,1,0:T(8,128)(2,1)S(1)} collective-permute-done((bf16[2,192,128]{2,1,0:T(8,128)(2,1)S(1)}, bf16[2,192,128]{2,1,0:T(8,128)(2,1)S(1)}, u32[]{:S(2)}, u32[]{:S(2)}) %collective-permute-start.1) | collective-permute-done | bytes 98336 | tf_op jit(solution)/shard_map/ppermute | solution.py:32
  15.0 0.0 collective-permute-done.2.refs_3_
  15.0 0.0 collective-permute-done.3.refs_4_
  15.0 0.0 copy-done.1
  15.0 0.0 copy-done.4
  15.0 2.9 %image.1 = (f32[2,192,128]{2,1,0:T(8,128)S(1)}, bf16[2,192,128]{2,1,0:T(8,128)(2,1)S(1)}, f32[16,16]{1,0:T(8,128)S(1)}) custom-call(s32[8]{0:T(128)S(1)} %copy-done.4, bf16[16,16,192]{2,1,0:T(8,128)(2,1)S(1)} %copy-done.1, bf16[2,192,128]{2,1,0:T(8,128)(2,1)S(1)} %pack.1.refs_0_, bf16[2,192,128]{2,1,0:T(8,128)(2,1)S(1)} %collective-permute-done.refs_1_, ...), custom_call_target="tpu_custom_call" | custom-call | flops 805306368 | bytes 2359296 | tf_op jit(solution)/shard_map/image/pallas_call | solution.py:292
  17.9 1.5 %collective-permute-start.8 = (bf16[2,192,128]{2,1,0:T(8,128)(2,1)S(1)}, bf16[2,192,128]{2,1,0:T(8,128)(2,1)S(1)}, u32[]{:S(2)}, u32[]{:S(2)}) collective-permute-start(bf16[2,192,128]{2,1,0:T(8,128)(2,1)S(1)} %get-tuple-element.10), channel_id=1, source_target_pairs={{0,2},{1,3},{2,0},{3,1},{4,6},{5,7},{6,4},{7,5},{8,10},{9,11},{10,... | collective-permute-start | bytes 294920 | tf_op jit(solution)/shard_map/ppermute | solution.py:39
  19.4 0.0 collective-permute-start.4
  19.4 0.5 %collective-permute-start.5 = (f32[16,16]{1,0:T(8,128)S(1)}, f32[16,16]{1,0:T(8,128)S(1)}, u32[]{:S(2)}, u32[]{:S(2)}) collective-permute-start(f32[16,16]{1,0:T(8,128)S(1)} %get-tuple-element.7.refs_1_), channel_id=1, source_target_pairs={{0,2},{1,3},{2,0},{3,1},{4,6},{5,7},{6,4},{7,5},{8,10},{9,11},{10,... | collective-permute-start | bytes 3080 | tf_op jit(solution)/shard_map/ppermute | solution.py:39
  19.9 1.3 %collective-permute-start.6 = (f32[16,16]{1,0:T(8,128)S(1)}, f32[16,16]{1,0:T(8,128)S(1)}, u32[]{:S(2)}, u32[]{:S(2)}) collective-permute-start(f32[16,16]{1,0:T(8,128)S(1)} %get-tuple-element.7.refs_1_), channel_id=1, source_target_pairs={{0,3},{1,2},{2,1},{3,0},{4,7},{5,6},{6,5},{7,4},{8,11},{9,10},{10,... | collective-permute-start | bytes 3080 | tf_op jit(solution)/shard_map/ppermute | solution.py:39
  21.2 0.1 copy.7.refs_0_
  21.3 0.3 %collective-permute-start.7 = (f32[2,192,128]{2,1,0:T(8,128)S(1)}, f32[2,192,128]{2,1,0:T(8,128)S(1)}, u32[]{:S(2)}, u32[]{:S(2)}) collective-permute-start(f32[2,192,128]{2,1,0:T(8,128)S(1)} %get-tuple-element.9.refs_0_), channel_id=1, source_target_pairs={{0,1},{1,0},{2,3},{3,2},{4,5},{5,4},{6,7},{7,6},{8,9},{9,8},{10,11... | collective-permute-start | bytes 589832 | tf_op jit(solution)/shard_map/ppermute | solution.py:39
  21.6 0.9 %collective-permute-done.8.refs_2_ = bf16[2,192,128]{2,1,0:T(8,128)(2,1)S(1)} collective-permute-done((bf16[2,192,128]{2,1,0:T(8,128)(2,1)S(1)}, bf16[2,192,128]{2,1,0:T(8,128)(2,1)S(1)}, u32[]{:S(2)}, u32[]{:S(2)}) %collective-permute-start.8) | collective-permute-done | bytes 98336 | tf_op jit(solution)/shard_map/ppermute | solution.py:39
  22.5 0.0 collective-permute-start.9
  22.5 0.0 collective-permute-done.4.refs_2_
  22.5 0.5 %collective-permute-done.5.refs_3_ = f32[16,16]{1,0:T(8,128)S(1)} collective-permute-done((f32[16,16]{1,0:T(8,128)S(1)}, f32[16,16]{1,0:T(8,128)S(1)}, u32[]{:S(2)}, u32[]{:S(2)}) %collective-permute-start.5) | collective-permute-done | bytes 1056 | tf_op jit(solution)/shard_map/ppermute | solution.py:39
  23.1 0.0 collective-permute-done.6.refs_4_
  23.1 1.3 %factor.1 = (f32[16,16]{1,0:T(8,128)}, bf16[128,128]{1,0:T(8,128)(2,1)S(1)}) custom-call(s32[16,1]{1,0:T(8,128)S(1)} %copy.7.refs_0_, f32[16,16]{1,0:T(8,128)S(1)} %get-tuple-element.7.refs_1_, f32[16,16]{1,0:T(8,128)S(1)} %collective-permute-done.4.refs_2_, f32[16,16]{1,0:T(8,128)S(1)} %collective-permute-done.5.refs_3_, ...), custom_call_target="tpu_custom_call" | custom-call | flops 3000000000 | bytes 1024 | tf_op jit(solution)/shard_map/factor/pallas_call | solution.py:316
  24.4 0.0 collective-permute-done.9.refs_3_
  24.4 0.0 collective-permute-done.7.refs_1_
  24.4 1.2 %route.1 = bf16[8,64,192]{2,1,0:T(8,128)(2,1)} custom-call(bf16[128,128]{1,0:T(8,128)(2,1)S(1)} %get-tuple-element.8.weights_ref, f32[2,192,128]{2,1,0:T(8,128)S(1)} %get-tuple-element.9.refs_0_, f32[2,192,128]{2,1,0:T(8,128)S(1)} %collective-permute-done.7.refs_1_, bf16[2,192,128]{2,1,0:T(8,128)(2,1)S(1)} %collective-permute-done.8.refs_2_, ...), custom_call_target="tpu_custom_call" | custom-call | flops 3145728 | bytes 1179648 | tf_op jit(solution)/shard_map/route/pallas_call | solution.py:324
  (6 shorter events, 0.0 us)
Async XLA Ops:
  0.6 0.9 %copy-start = (bf16[16,16,192]{2,1,0:T(8,128)(2,1)S(1)}, bf16[16,16,192]{2,1,0:T(8,128)(2,1)}, u32[]{:S(2)}) copy-start(bf16[16,16,192]{2,1,0:T(8,128)(2,1)} %orbitals_ref.3) | copy-start | bytes 294916
  1.5 13.5 %copy-start.1 = (bf16[16,16,192]{2,1,0:T(8,128)(2,1)S(1)}, bf16[16,16,192]{2,1,0:T(8,128)(2,1)}, u32[]{:S(2)}) copy-start(bf16[16,16,192]{2,1,0:T(8,128)(2,1)} %orbitals_ref.3) | copy-start | bytes 294916
  1.5 13.5 %copy-start.4 = (s32[8]{0:T(128)S(1)}, s32[8]{0:T(128)}, u32[]{:S(2)}) copy-start(s32[8]{0:T(128)} %occupied_ref.1) | copy-start | bytes 100
  1.5 19.7 %copy-start.5 = (s32[16,1]{0,1:T(1,128)S(1)}, s32[16,1]{0,1:T(1,128)}, u32[]{:S(2)}) copy-start(s32[16,1]{0,1:T(1,128)} %param.8) | copy-start | bytes 196
  1.8 11.1 %collective-permute-start = (bf16[2,192,128]{2,1,0:T(8,128)(2,1)S(1)}, bf16[2,192,128]{2,1,0:T(8,128)(2,1)S(1)}, u32[]{:S(2)}, u32[]{:S(2)}) collective-permute-start(bf16[2,192,128]{2,1,0:T(8,128)(2,1)S(1)} %pack.1.refs_0_), channel_id=1, source_target_pairs={{0,24},{4,28},{8,16},{12,20},{16,8},{20,12},{24,0},{28,4},{1,25},{... | collective-permute-start | bytes 294920 | tf_op jit(solution)/shard_map/ppermute | solution.py:32
  6.9 8.1 %collective-permute-start.1 = (bf16[2,192,128]{2,1,0:T(8,128)(2,1)S(1)}, bf16[2,192,128]{2,1,0:T(8,128)(2,1)S(1)}, u32[]{:S(2)}, u32[]{:S(2)}) collective-permute-start(bf16[2,192,128]{2,1,0:T(8,128)(2,1)S(1)} %pack.1.refs_0_), channel_id=1, source_target_pairs={{0,28},{4,8},{8,4},{12,16},{16,12},{20,24},{24,20},{28,0},{1,29},{... | collective-permute-start | bytes 294920 | tf_op jit(solution)/shard_map/ppermute | solution.py:32
  8.1 6.9 %collective-permute-start.2 = (bf16[2,192,128]{2,1,0:T(8,128)(2,1)S(1)}, bf16[2,192,128]{2,1,0:T(8,128)(2,1)S(1)}, u32[]{:S(2)}, u32[]{:S(2)}) collective-permute-start(bf16[2,192,128]{2,1,0:T(8,128)(2,1)S(1)} %pack.1.refs_0_), channel_id=1, source_target_pairs={{0,4},{4,0},{8,12},{12,8},{16,20},{20,16},{24,28},{28,24},{1,5},{5... | collective-permute-start | bytes 294920 | tf_op jit(solution)/shard_map/ppermute | solution.py:32
  8.4 6.6 %collective-permute-start.3 = (bf16[2,192,128]{2,1,0:T(8,128)(2,1)S(1)}, bf16[2,192,128]{2,1,0:T(8,128)(2,1)S(1)}, u32[]{:S(2)}, u32[]{:S(2)}) collective-permute-start(bf16[2,192,128]{2,1,0:T(8,128)(2,1)S(1)} %pack.1.refs_0_), channel_id=1, source_target_pairs={{0,8},{4,12},{8,0},{12,4},{16,24},{20,28},{24,16},{28,20},{1,9},{5... | collective-permute-start | bytes 294920 | tf_op jit(solution)/shard_map/ppermute | solution.py:32
  9.9 1.0 %copy-start.2 = (bf16[3,192,192]{2,1,0:T(8,128)(2,1)S(1)}, bf16[3,192,192]{2,1,0:T(8,128)(2,1)}, u32[]{:S(2)}) copy-start(bf16[3,192,192]{2,1,0:T(8,128)(2,1)} %constant.3.tables_ref) | copy-start | bytes 663556
  10.8 0.7 %copy-start.3 = (f32[16,192]{1,0:T(8,128)S(1)}, f32[16,192]{1,0:T(8,128)}, u32[]{:S(2)}) copy-start(f32[16,192]{1,0:T(8,128)} %coulomb_ref.1) | copy-start | bytes 36868
  17.9 4.7 %collective-permute-start.8 = (bf16[2,192,128]{2,1,0:T(8,128)(2,1)S(1)}, bf16[2,192,128]{2,1,0:T(8,128)(2,1)S(1)}, u32[]{:S(2)}, u32[]{:S(2)}) collective-permute-start(bf16[2,192,128]{2,1,0:T(8,128)(2,1)S(1)} %get-tuple-element.10), channel_id=1, source_target_pairs={{0,2},{1,3},{2,0},{3,1},{4,6},{5,7},{6,4},{7,5},{8,10},{9,11},{10,... | collective-permute-start | bytes 294920 | tf_op jit(solution)/shard_map/ppermute | solution.py:39
  19.4 3.2 %collective-permute-start.4 = (f32[16,16]{1,0:T(8,128)S(1)}, f32[16,16]{1,0:T(8,128)S(1)}, u32[]{:S(2)}, u32[]{:S(2)}) collective-permute-start(f32[16,16]{1,0:T(8,128)S(1)} %get-tuple-element.7.refs_1_), channel_id=1, source_target_pairs={{0,1},{1,0},{2,3},{3,2},{4,5},{5,4},{6,7},{7,6},{8,9},{9,8},{10,11... | collective-permute-start | bytes 3080 | tf_op jit(solution)/shard_map/ppermute | solution.py:39
  19.4 3.7 %collective-permute-start.5 = (f32[16,16]{1,0:T(8,128)S(1)}, f32[16,16]{1,0:T(8,128)S(1)}, u32[]{:S(2)}, u32[]{:S(2)}) collective-permute-start(f32[16,16]{1,0:T(8,128)S(1)} %get-tuple-element.7.refs_1_), channel_id=1, source_target_pairs={{0,2},{1,3},{2,0},{3,1},{4,6},{5,7},{6,4},{7,5},{8,10},{9,11},{10,... | collective-permute-start | bytes 3080 | tf_op jit(solution)/shard_map/ppermute | solution.py:39
  19.9 3.2 %collective-permute-start.6 = (f32[16,16]{1,0:T(8,128)S(1)}, f32[16,16]{1,0:T(8,128)S(1)}, u32[]{:S(2)}, u32[]{:S(2)}) collective-permute-start(f32[16,16]{1,0:T(8,128)S(1)} %get-tuple-element.7.refs_1_), channel_id=1, source_target_pairs={{0,3},{1,2},{2,1},{3,0},{4,7},{5,6},{6,5},{7,4},{8,11},{9,10},{10,... | collective-permute-start | bytes 3080 | tf_op jit(solution)/shard_map/ppermute | solution.py:39
  21.3 3.1 %collective-permute-start.7 = (f32[2,192,128]{2,1,0:T(8,128)S(1)}, f32[2,192,128]{2,1,0:T(8,128)S(1)}, u32[]{:S(2)}, u32[]{:S(2)}) collective-permute-start(f32[2,192,128]{2,1,0:T(8,128)S(1)} %get-tuple-element.9.refs_0_), channel_id=1, source_target_pairs={{0,1},{1,0},{2,3},{3,2},{4,5},{5,4},{6,7},{7,6},{8,9},{9,8},{10,11... | collective-permute-start | bytes 589832 | tf_op jit(solution)/shard_map/ppermute | solution.py:39
  22.5 1.9 %collective-permute-start.9 = (bf16[2,192,128]{2,1,0:T(8,128)(2,1)S(1)}, bf16[2,192,128]{2,1,0:T(8,128)(2,1)S(1)}, u32[]{:S(2)}, u32[]{:S(2)}) collective-permute-start(bf16[2,192,128]{2,1,0:T(8,128)(2,1)S(1)} %collective-permute-done.8.refs_2_), channel_id=1, source_target_pairs={{0,1},{1,0},{2,3},{3,2},{4,5},{5,4},{6,7},{7,6},{8,9},{9,8},{10,11... | collective-permute-start | bytes 294920 | tf_op jit(solution)/shard_map/ppermute | solution.py:39

commit v4 on v3

--- a/solution.py
+++ b/solution.py
@@ -1,3 +1,4 @@
+import functools
 import math
 
 import jax
@@ -17,19 +18,18 @@
 F32, BF16 = jnp.float32, jnp.bfloat16
 
 
-def partners(block, count):
-    even, low = block % 2 == 0, block % 4 < 2
-    choose = jnp.where if isinstance(block, jax.Array) else (lambda c, a, b: a if c else b)
-    steps = (choose(low, -2, 2), choose(even, -1, 1), choose(even, 1, -1), choose(low, 2, -2))
+def sources(block, count):
+    odd = block % 2
+    steps = (-2, 2 * odd - 1, 1 - 2 * odd, 2)
     return [(block + step + count) % count for step in steps]
 
 
 def exchanged(value):
     count = lax.axis_size("band")
     assert count % 4 == 0
-    tables = [partners(block, count) for block in range(count)]
+    tables = [sources(block, count) for block in range(count)]
     return [
-        lax.ppermute(value, "band", [(block, row[turn]) for block, row in enumerate(tables)])
+        lax.ppermute(value, "band", [(row[turn], block) for block, row in enumerate(tables)])
         for turn in range(4)
     ]
 
@@ -53,9 +53,14 @@
     return jnp.asarray(np.stack([forward.T, inverse.T, mirror]).astype(np.float32)).astype(BF16)
 
 
+def split(value):
+    high = value.astype(BF16)
+    return high, value - high.astype(F32)
+
+
 def halves(value):
-    high = value.astype(BF16)
-    return high, (value - high.astype(F32)).astype(BF16)
+    high, rest = split(value)
+    return high, rest.astype(BF16)
 
 
 def dot32(a, b, contract=((1,), (0,))):
@@ -119,16 +124,15 @@
         out_ref[line, :, points:] = pad
 
 
-def image_kernel(occupied_ref, orbitals_ref, *refs):
-    blocks, (response_ref, wide_ref, narrow_ref, overlap_ref) = refs[:-4], refs[-4:]
-    members, lines, points = orbitals_ref.shape
-    packs = blocks[0].shape[0]
+def image_kernel(members, occupied_ref, *refs):
+    blocks, (response_ref, wide_ref, narrow_ref) = refs[:-3], refs[-3:]
+    packs, points, _ = blocks[0].shape
     padded = response_ref.shape[2]
     span = LANES // members
     per = span // 4
     total = lax.axis_size("band")
     position = lax.axis_index("band")
-    places = [position] + partners(position, total)
+    places = [position] + sources(position, total)
     turns = [place % 4 for place in places]
     lane = ids((1, LANES), 1)
     own_line = lane_line(lane, turns[0], members)
@@ -136,12 +140,7 @@
     quarters = [lane_quarter(lane, turn) for turn in turns]
     step = lane % (LANES // 4) // members
     apart, merged = 1, (0, 2, 3, 4)
-    natives = orbitals_ref[...].astype(F32)
-    square = (LANES, LANES)
-    row_line = ids(square, 0) % span
-    same_line = row_line == lane_line(ids(square, 1), turns[0], members)
     blank = jnp.zeros((padded - points, 2 * LANES), BF16)
-    cross = jnp.zeros(square, F32)
     for pack in range(packs):
         tiles = [block[pack] for block in blocks]
         native = jnp.concatenate([tiles[0], blank[:, :LANES]], axis=0)
@@ -168,12 +167,20 @@
                 image = jnp.where(own_line == quarter * per + k, field, image)
         wide_ref[pack] = image
         narrow_ref[pack] = image.astype(BF16)
+
+
+def overlap_kernel(orbitals_ref, image_ref, out_ref):
+    members, _, _ = orbitals_ref.shape
+    span = LANES // members
+    natives = orbitals_ref[...].astype(F32)
+    square = (LANES, LANES)
+    same_line = ids(square, 0) % span == lane_line(ids(square, 1), own_turn(), members)
+    cross = jnp.zeros(square, F32)
+    for pack in range(image_ref.shape[0]):
         rows = rows_of(natives, pack, span).astype(BF16)
-        product = dot32(rows, jnp.concatenate(halves(image), axis=1))
+        product = dot32(rows, jnp.concatenate(halves(image_ref[pack]), axis=1))
         cross = cross + (product[:, :LANES] + product[:, LANES:])
-    cross = jnp.where(same_line, cross, 0.0).reshape(members, span, LANES).sum(axis=1)
-    gather = lane_member(ids((LANES, members), 0), members) == ids((LANES, members), 1)
-    overlap_ref[...] = dot_exact(cross, gather.astype(F32))
+    out_ref[...] = jnp.where(same_line, cross, 0.0).reshape(members, span, LANES).sum(axis=1)
 
 
 def factor_kernel(cells, owners_ref, *refs):
@@ -184,7 +191,12 @@
     sums = [part[...] for part in parts]
     while len(sums) > 1:
         sums = [a + b for a, b in zip(sums[::2], sums[1::2])]
-    overlap = sums[0] * (1.0 / cells)
+    high, rest = split(sums[0])
+    pieces = [high, *halves(rest)]
+    across = (members, LANES)
+    gather = (ids(across, 0) == lane_member(ids(across, 1), members)).astype(BF16)
+    overlap = sum(dot32(piece, gather, NT) for piece in pieces) * (1.0 / cells)
+    flipped = sum(dot32(gather, piece, NT) for piece in pieces) * (1.0 / cells)
     overlap_ref[...] = overlap
     rows = CAP * span
     square = (members, members)
@@ -198,7 +210,7 @@
     placed = (jnp.where(slot == ranking, 1.0, 0.0) * mine_row).astype(BF16)
     wide = (members, LANES)
     row = ids(wide, 0)
-    upper = 0.5 * (overlap + dot_exact(overlap, eye, ((0,), (0,))))
+    upper = 0.5 * (overlap + flipped)
     lower = (row == lane_member(ids(wide, 1), members)).astype(F32)
     for k in range(0, members, 2):
         first = jnp.broadcast_to(upper[:, k : k + 1], wide)
@@ -280,6 +292,7 @@
         operands=1,
     )(orbitals)
     guests = exchanged(packed)
+    tables = spectral_tables(points)
     (response,) = call(
         response_kernel,
         "response",
@@ -287,22 +300,25 @@
         4 * lines * points**3,
         4 * lines * points**2,
         operands=2,
-    )(coulomb, spectral_tables(points))
+    )(coulomb, tables)
     blocks = len(guests) + 1
-    wide, narrow, overlap = call(
-        image_kernel,
+    wide, narrow = call(
+        functools.partial(image_kernel, members),
         "image",
-        [
-            shape((packs, points, LANES), F32),
-            shape((packs, points, LANES), BF16),
-            shape((members, members), F32),
-        ],
+        [shape((packs, points, LANES), F32), shape((packs, points, LANES), BF16)],
         2 * lines * points * padded * (4 * LANES),
         4 * lines * points**2,
         scalars=1,
-        operands=blocks + 2,
-    )(occupied, orbitals, packed, *guests, response)
-
+        operands=blocks + 1,
+    )(occupied, packed, *guests, response)
+    (overlap,) = call(
+        overlap_kernel,
+        "overlap",
+        [shape((members, LANES), F32)],
+        4 * packs * points * LANES**2,
+        8 * orbitals.size,
+        operands=2,
+    )(orbitals, wide)
     overlaps = [overlap] + [swapped(overlap, flip) for flip in range(1, groups)]
     images = [wide] + [swapped(wide, flip) for flip in range(1, near)]
     for grid in range(1, grids):
@@ -310,11 +326,8 @@
         images += [across] + [swapped(across, flip) for flip in range(1, near)]
     cells = lines * groups * points
 
-    def factor(*refs):
-        factor_kernel(cells, *refs)
-
     intersection, weights = call(
-        factor,
+        functools.partial(factor_kernel, cells),
         "factor",
         [shape((members, members), F32), shape((2 * CAP * span, LANES), BF16)],
         FACTOR_COST,

time: 25.9 us -> 24.8 us (0.958)
  waiting for transfers between devices: 3.58 us -> 2.42 us
  starting transfers between devices: 11.7 us -> 12.2 us
  Pallas kernels: 6.94 us -> 6.5 us
    ppermute x4, waiting for transfers between devices: 2.11 us -> 0.95 us  [exchanged(): lax.ppermute(value, 'band', [(row[turn], block) for block, row in enumera...]
    pallas_call x2 -> x3, Pallas kernels: 4.16 us -> 3.72 us  [the longest x1 2.3 us: local(): call(functools.partial(image_kernel, members), 'image', [shape((packs, po...]
    ppermute x4, starting transfers between devices: 8.1 us -> 8.36 us  [exchanged(): lax.ppermute(value, 'band', [(row[turn], block) for block, row in enumera...]
  transfers between devices with their start and end apart: 10 -> 10, of which waited for: 3 -> 4; matrix products, arithmetic and copies ran while one was open for 0% -> 0% of each run, Pallas kernels for 10% -> 11%
where the time goes in v4:
time: 24.8 us; the launch traced here: 24.5 us
  starting transfers between devices  12.2 us (49%)
  Pallas kernels  6.5 us (26%)
  local copies, waits for them, and re-layouts  2.67 us (11%)
  waiting for transfers between devices  2.42 us (10%)
  between operations  0.72 us (3%)
    ppermute x4, starting transfers between devices, exchanged(): lax.ppermute(value, 'band', [(row[turn], block) for block, row in enumera...  8.36 us
    ppermute x6, starting transfers between devices, swapped(): lax.ppermute(value, ('grid', 'ham'), [(group, group ^ flip) for group in...  3.83 us
    unnamed x13, local copies, waits for them, and re-layouts  2.67 us
    pallas_call x1, Pallas kernels, local(): call(functools.partial(image_kernel, members), 'image', [shape((packs, po...  2.3 us
    ppermute x6, waiting for transfers between devices, swapped(): lax.ppermute(value, ('grid', 'ham'), [(group, group ^ flip) for group in...  1.48 us
    pallas_call x1, Pallas kernels, local(): call(response_kernel, 'response', [shape((lines, points, padded), F32)],...  1.31 us
    pallas_call x1, Pallas kernels, local(): call(route_kernel, 'route', [shape((CAP, groups * lines, points), BF16)],...  1.23 us
    pallas_call x1, Pallas kernels, local(): call(functools.partial(factor_kernel, cells), 'factor', [shape((members,...  1.23 us
  transfers between devices with their start and end apart: 10, of which 4 were waited for; matrix products, arithmetic and copies ran while one was open for 0% of the time, Pallas kernels for 11%

profile of v4, /device:TPU:0, one launch (start us, length us, event | category | flops | bytes accessed | tf_op | source)
XLA Modules:
  0.0 24.5 jit_solution(7271709782388362922)
XLA Ops:
  0.6 0.0 copy-start
  0.6 0.9 %copy-done = bf16[16,16,192]{2,1,0:T(8,128)(2,1)S(1)} copy-done((bf16[16,16,192]{2,1,0:T(8,128)(2,1)S(1)}, bf16[16,16,192]{2,1,0:T(8,128)(2,1)}, u32[]{:S(2)}) %copy-start) | copy-done | bytes 98328
  1.5 0.2 pack.1.refs_0_
  1.8 0.0 copy-start.1
  1.8 3.1 %collective-permute-start = (bf16[2,192,128]{2,1,0:T(8,128)(2,1)S(1)}, bf16[2,192,128]{2,1,0:T(8,128)(2,1)S(1)}, u32[]{:S(2)}, u32[]{:S(2)}) collective-permute-start(bf16[2,192,128]{2,1,0:T(8,128)(2,1)S(1)} %pack.1.refs_0_), channel_id=1, source_target_pairs={{24,0},{28,4},{0,8},{4,12},{8,16},{12,20},{16,24},{20,28},{25,1},{... | collective-permute-start | bytes 294920 | tf_op jit(solution)/shard_map/ppermute | solution.py:32
  4.9 3.2 %collective-permute-start.1 = (bf16[2,192,128]{2,1,0:T(8,128)(2,1)S(1)}, bf16[2,192,128]{2,1,0:T(8,128)(2,1)S(1)}, u32[]{:S(2)}, u32[]{:S(2)}) collective-permute-start(bf16[2,192,128]{2,1,0:T(8,128)(2,1)S(1)} %pack.1.refs_0_), channel_id=1, source_target_pairs={{28,0},{8,4},{4,8},{16,12},{12,16},{24,20},{20,24},{0,28},{29,1},{... | collective-permute-start | bytes 294920 | tf_op jit(solution)/shard_map/ppermute | solution.py:32
  8.1 0.0 collective-permute-start.2
  8.1 2.1 %collective-permute-start.3 = (bf16[2,192,128]{2,1,0:T(8,128)(2,1)S(1)}, bf16[2,192,128]{2,1,0:T(8,128)(2,1)S(1)}, u32[]{:S(2)}, u32[]{:S(2)}) collective-permute-start(bf16[2,192,128]{2,1,0:T(8,128)(2,1)S(1)} %pack.1.refs_0_), channel_id=1, source_target_pairs={{8,0},{12,4},{16,8},{20,12},{24,16},{28,20},{0,24},{4,28},{9,1},{1... | collective-permute-start | bytes 294920 | tf_op jit(solution)/shard_map/ppermute | solution.py:32
  10.2 1.0 %copy-done.2 = bf16[3,192,192]{2,1,0:T(8,128)(2,1)S(1)} copy-done((bf16[3,192,192]{2,1,0:T(8,128)(2,1)S(1)}, bf16[3,192,192]{2,1,0:T(8,128)(2,1)}, u32[]{:S(2)}) %copy-start.2) | copy-done | bytes 221208
  11.1 0.7 %copy-done.3 = f32[16,192]{1,0:T(8,128)S(1)} copy-done((f32[16,192]{1,0:T(8,128)S(1)}, f32[16,192]{1,0:T(8,128)}, u32[]{:S(2)}) %copy-start.3) | copy-done | bytes 12312
  11.8 1.3 %response.1.refs_5_ = f32[16,192,256]{2,1,0:T(8,128)S(1)} custom-call(f32[16,192]{1,0:T(8,128)S(1)} %copy-done.3, bf16[3,192,192]{2,1,0:T(8,128)(2,1)S(1)} %copy-done.2), custom_call_target="tpu_custom_call" | custom-call | flops 452984832 | bytes 2359296 | tf_op jit(solution)/shard_map/response/pallas_call | solution.py:296
  13.2 0.0 collective-permute-done.refs_1_
  13.2 0.6 %collective-permute-done.1.refs_2_ = bf16[2,192,128]{2,1,0:T(8,128)(2,1)S(1)} collective-permute-done((bf16[2,192,128]{2,1,0:T(8,128)(2,1)S(1)}, bf16[2,192,128]{2,1,0:T(8,128)(2,1)S(1)}, u32[]{:S(2)}, u32[]{:S(2)}) %collective-permute-start.1) | collective-permute-done | bytes 98336 | tf_op jit(solution)/shard_map/ppermute | solution.py:32
  13.7 0.4 %collective-permute-done.2.refs_3_ = bf16[2,192,128]{2,1,0:T(8,128)(2,1)S(1)} collective-permute-done((bf16[2,192,128]{2,1,0:T(8,128)(2,1)S(1)}, bf16[2,192,128]{2,1,0:T(8,128)(2,1)S(1)}, u32[]{:S(2)}, u32[]{:S(2)}) %collective-permute-start.2) | collective-permute-done | bytes 98336 | tf_op jit(solution)/shard_map/ppermute | solution.py:32
  14.1 0.0 collective-permute-done.3.refs_4_
  14.1 2.3 %image.1 = (f32[2,192,128]{2,1,0:T(8,128)S(1)}, bf16[2,192,128]{2,1,0:T(8,128)(2,1)S(1)}) custom-call(s32[8]{0:T(128)S(1)} %copy-done.4, bf16[2,192,128]{2,1,0:T(8,128)(2,1)S(1)} %pack.1.refs_0_, bf16[2,192,128]{2,1,0:T(8,128)(2,1)S(1)} %collective-permute-done.refs_1_, bf16[2,192,128]{2,1,0:T(8,128)(2,1)S(1)} %collective-permute-done.1.refs_2_, ...), custom_call_target="tpu_custom_call" | custom-call | flops 805306368 | bytes 2359296 | tf_op jit(solution)/shard_map/image/pallas_call | solution.py:305
  16.4 1.6 %collective-permute-start.8 = (bf16[2,192,128]{2,1,0:T(8,128)(2,1)S(1)}, bf16[2,192,128]{2,1,0:T(8,128)(2,1)S(1)}, u32[]{:S(2)}, u32[]{:S(2)}) collective-permute-start(bf16[2,192,128]{2,1,0:T(8,128)(2,1)S(1)} %get-tuple-element.8), channel_id=1, source_target_pairs={{0,2},{1,3},{2,0},{3,1},{4,6},{5,7},{6,4},{7,5},{8,10},{9,11},{10,... | collective-permute-start | bytes 294920 | tf_op jit(solution)/shard_map/ppermute | solution.py:39
  18.0 0.2 overlap.1.refs_0_
  18.2 0.1 collective-permute-start.4
  18.3 0.6 %collective-permute-start.5 = (f32[16,128]{1,0:T(8,128)S(1)}, f32[16,128]{1,0:T(8,128)S(1)}, u32[]{:S(2)}, u32[]{:S(2)}) collective-permute-start(f32[16,128]{1,0:T(8,128)S(1)} %overlap.1.refs_0_), channel_id=1, source_target_pairs={{0,2},{1,3},{2,0},{3,1},{4,6},{5,7},{6,4},{7,5},{8,10},{9,11},{10,... | collective-permute-start | bytes 24584 | tf_op jit(solution)/shard_map/ppermute | solution.py:39
  18.9 1.3 %collective-permute-start.6 = (f32[16,128]{1,0:T(8,128)S(1)}, f32[16,128]{1,0:T(8,128)S(1)}, u32[]{:S(2)}, u32[]{:S(2)}) collective-permute-start(f32[16,128]{1,0:T(8,128)S(1)} %overlap.1.refs_0_), channel_id=1, source_target_pairs={{0,3},{1,2},{2,1},{3,0},{4,7},{5,6},{6,5},{7,4},{8,11},{9,10},{10,... | collective-permute-start | bytes 24584 | tf_op jit(solution)/shard_map/ppermute | solution.py:39
  20.1 0.1 copy.7.owners_ref
  20.2 0.3 %collective-permute-start.7 = (f32[2,192,128]{2,1,0:T(8,128)S(1)}, f32[2,192,128]{2,1,0:T(8,128)S(1)}, u32[]{:S(2)}, u32[]{:S(2)}) collective-permute-start(f32[2,192,128]{2,1,0:T(8,128)S(1)} %get-tuple-element.6.image_ref.refs_0_), channel_id=1, source_target_pairs={{0,1},{1,0},{2,3},{3,2},{4,5},{5,4},{6,7},{7,6},{8,9},{9,8},{10,11... | collective-permute-start | bytes 589832 | tf_op jit(solution)/shard_map/ppermute | solution.py:39
  20.5 0.6 %collective-permute-done.8.refs_2_ = bf16[2,192,128]{2,1,0:T(8,128)(2,1)S(1)} collective-permute-done((bf16[2,192,128]{2,1,0:T(8,128)(2,1)S(1)}, bf16[2,192,128]{2,1,0:T(8,128)(2,1)S(1)}, u32[]{:S(2)}, u32[]{:S(2)}) %collective-permute-start.8) | collective-permute-done | bytes 98336 | tf_op jit(solution)/shard_map/ppermute | solution.py:39
  21.1 0.0 collective-permute-start.9
  21.1 0.0 collective-permute-done.4.refs_1_
  21.1 0.9 %collective-permute-done.5.refs_2_ = f32[16,128]{1,0:T(8,128)S(1)} collective-permute-done((f32[16,128]{1,0:T(8,128)S(1)}, f32[16,128]{1,0:T(8,128)S(1)}, u32[]{:S(2)}, u32[]{:S(2)}) %collective-permute-start.5) | collective-permute-done | bytes 8224 | tf_op jit(solution)/shard_map/ppermute | solution.py:39
  22.0 0.0 collective-permute-done.6.refs_3_
  22.0 1.2 %factor.1 = (f32[16,16]{1,0:T(8,128)}, bf16[128,128]{1,0:T(8,128)(2,1)S(1)}) custom-call(s32[16,1]{1,0:T(8,128)S(1)} %copy.7.owners_ref, f32[16,128]{1,0:T(8,128)S(1)} %overlap.1.refs_0_, f32[16,128]{1,0:T(8,128)S(1)} %collective-permute-done.4.refs_1_, f32[16,128]{1,0:T(8,128)S(1)} %collective-permute-done.5.refs_2_, ...), custom_call_target="tpu_custom_call" | custom-call | flops 3000000000 | bytes 1024 | tf_op jit(solution)/shard_map/factor/pallas_call | solution.py:329
  23.3 0.0 collective-permute-done.7.refs_1_
  23.3 0.0 collective-permute-done.9.refs_3_
  23.3 1.2 %route.1 = bf16[8,64,192]{2,1,0:T(8,128)(2,1)} custom-call(bf16[128,128]{1,0:T(8,128)(2,1)S(1)} %get-tuple-element.7.weights_ref, f32[2,192,128]{2,1,0:T(8,128)S(1)} %get-tuple-element.6.image_ref.refs_0_, f32[2,192,128]{2,1,0:T(8,128)S(1)} %collective-permute-done.7.refs_1_, bf16[2,192,128]{2,1,0:T(8,128)(2,1)S(1)} %collective-permute-done.8.refs_2_, ...), custom_call_target="tpu_custom_call" | custom-call | flops 3145728 | bytes 1179648 | tf_op jit(solution)/shard_map/route/pallas_call | solution.py:337
  (7 shorter events, 0.0 us)
Async XLA Ops:
  0.6 0.9 %copy-start = (bf16[16,16,192]{2,1,0:T(8,128)(2,1)S(1)}, bf16[16,16,192]{2,1,0:T(8,128)(2,1)}, u32[]{:S(2)}) copy-start(bf16[16,16,192]{2,1,0:T(8,128)(2,1)} %orbitals_ref.3) | copy-start | bytes 294916
  1.5 12.6 %copy-start.4 = (s32[8]{0:T(128)S(1)}, s32[8]{0:T(128)}, u32[]{:S(2)}) copy-start(s32[8]{0:T(128)} %occupied_ref.1) | copy-start | bytes 100
  1.5 18.6 %copy-start.5 = (s32[16,1]{0,1:T(1,128)S(1)}, s32[16,1]{0,1:T(1,128)}, u32[]{:S(2)}) copy-start(s32[16,1]{0,1:T(1,128)} %param.8) | copy-start | bytes 196
  1.8 16.2 %copy-start.1 = (bf16[16,16,192]{2,1,0:T(8,128)(2,1)S(1)}, bf16[16,16,192]{2,1,0:T(8,128)(2,1)}, u32[]{:S(2)}) copy-start(bf16[16,16,192]{2,1,0:T(8,128)(2,1)} %orbitals_ref.3) | copy-start | bytes 294916
  1.8 11.4 %collective-permute-start = (bf16[2,192,128]{2,1,0:T(8,128)(2,1)S(1)}, bf16[2,192,128]{2,1,0:T(8,128)(2,1)S(1)}, u32[]{:S(2)}, u32[]{:S(2)}) collective-permute-start(bf16[2,192,128]{2,1,0:T(8,128)(2,1)S(1)} %pack.1.refs_0_), channel_id=1, source_target_pairs={{24,0},{28,4},{0,8},{4,12},{8,16},{12,20},{16,24},{20,28},{25,1},{... | collective-permute-start | bytes 294920 | tf_op jit(solution)/shard_map/ppermute | solution.py:32
  4.9 8.8 %collective-permute-start.1 = (bf16[2,192,128]{2,1,0:T(8,128)(2,1)S(1)}, bf16[2,192,128]{2,1,0:T(8,128)(2,1)S(1)}, u32[]{:S(2)}, u32[]{:S(2)}) collective-permute-start(bf16[2,192,128]{2,1,0:T(8,128)(2,1)S(1)} %pack.1.refs_0_), channel_id=1, source_target_pairs={{28,0},{8,4},{4,8},{16,12},{12,16},{24,20},{20,24},{0,28},{29,1},{... | collective-permute-start | bytes 294920 | tf_op jit(solution)/shard_map/ppermute | solution.py:32
  8.1 6.0 %collective-permute-start.2 = (bf16[2,192,128]{2,1,0:T(8,128)(2,1)S(1)}, bf16[2,192,128]{2,1,0:T(8,128)(2,1)S(1)}, u32[]{:S(2)}, u32[]{:S(2)}) collective-permute-start(bf16[2,192,128]{2,1,0:T(8,128)(2,1)S(1)} %pack.1.refs_0_), channel_id=1, source_target_pairs={{4,0},{0,4},{12,8},{8,12},{20,16},{16,20},{28,24},{24,28},{5,1},{1... | collective-permute-start | bytes 294920 | tf_op jit(solution)/shard_map/ppermute | solution.py:32
  8.1 6.0 %collective-permute-start.3 = (bf16[2,192,128]{2,1,0:T(8,128)(2,1)S(1)}, bf16[2,192,128]{2,1,0:T(8,128)(2,1)S(1)}, u32[]{:S(2)}, u32[]{:S(2)}) collective-permute-start(bf16[2,192,128]{2,1,0:T(8,128)(2,1)S(1)} %pack.1.refs_0_), channel_id=1, source_target_pairs={{8,0},{12,4},{16,8},{20,12},{24,16},{28,20},{0,24},{4,28},{9,1},{1... | collective-permute-start | bytes 294920 | tf_op jit(solution)/shard_map/ppermute | solution.py:32
  10.2 1.0 %copy-start.2 = (bf16[3,192,192]{2,1,0:T(8,128)(2,1)S(1)}, bf16[3,192,192]{2,1,0:T(8,128)(2,1)}, u32[]{:S(2)}) copy-start(bf16[3,192,192]{2,1,0:T(8,128)(2,1)} %constant.3.tables_ref) | copy-start | bytes 663556
  11.1 0.7 %copy-start.3 = (f32[16,192]{1,0:T(8,128)S(1)}, f32[16,192]{1,0:T(8,128)}, u32[]{:S(2)}) copy-start(f32[16,192]{1,0:T(8,128)} %coulomb_ref.1) | copy-start | bytes 36868
  16.4 4.7 %collective-permute-start.8 = (bf16[2,192,128]{2,1,0:T(8,128)(2,1)S(1)}, bf16[2,192,128]{2,1,0:T(8,128)(2,1)S(1)}, u32[]{:S(2)}, u32[]{:S(2)}) collective-permute-start(bf16[2,192,128]{2,1,0:T(8,128)(2,1)S(1)} %get-tuple-element.8), channel_id=1, source_target_pairs={{0,2},{1,3},{2,0},{3,1},{4,6},{5,7},{6,4},{7,5},{8,10},{9,11},{10,... | collective-permute-start | bytes 294920 | tf_op jit(solution)/shard_map/ppermute | solution.py:39
  18.2 2.9 %collective-permute-start.4 = (f32[16,128]{1,0:T(8,128)S(1)}, f32[16,128]{1,0:T(8,128)S(1)}, u32[]{:S(2)}, u32[]{:S(2)}) collective-permute-start(f32[16,128]{1,0:T(8,128)S(1)} %overlap.1.refs_0_), channel_id=1, source_target_pairs={{0,1},{1,0},{2,3},{3,2},{4,5},{5,4},{6,7},{7,6},{8,9},{9,8},{10,11... | collective-permute-start | bytes 24584 | tf_op jit(solution)/shard_map/ppermute | solution.py:39
  18.3 3.8 %collective-permute-start.5 = (f32[16,128]{1,0:T(8,128)S(1)}, f32[16,128]{1,0:T(8,128)S(1)}, u32[]{:S(2)}, u32[]{:S(2)}) collective-permute-start(f32[16,128]{1,0:T(8,128)S(1)} %overlap.1.refs_0_), channel_id=1, source_target_pairs={{0,2},{1,3},{2,0},{3,1},{4,6},{5,7},{6,4},{7,5},{8,10},{9,11},{10,... | collective-permute-start | bytes 24584 | tf_op jit(solution)/shard_map/ppermute | solution.py:39
  18.9 3.2 %collective-permute-start.6 = (f32[16,128]{1,0:T(8,128)S(1)}, f32[16,128]{1,0:T(8,128)S(1)}, u32[]{:S(2)}, u32[]{:S(2)}) collective-permute-start(f32[16,128]{1,0:T(8,128)S(1)} %overlap.1.refs_0_), channel_id=1, source_target_pairs={{0,3},{1,2},{2,1},{3,0},{4,7},{5,6},{6,5},{7,4},{8,11},{9,10},{10,... | collective-permute-start | bytes 24584 | tf_op jit(solution)/shard_map/ppermute | solution.py:39
  20.2 3.1 %collective-permute-start.7 = (f32[2,192,128]{2,1,0:T(8,128)S(1)}, f32[2,192,128]{2,1,0:T(8,128)S(1)}, u32[]{:S(2)}, u32[]{:S(2)}) collective-permute-start(f32[2,192,128]{2,1,0:T(8,128)S(1)} %get-tuple-element.6.image_ref.refs_0_), channel_id=1, source_target_pairs={{0,1},{1,0},{2,3},{3,2},{4,5},{5,4},{6,7},{7,6},{8,9},{9,8},{10,11... | collective-permute-start | bytes 589832 | tf_op jit(solution)/shard_map/ppermute | solution.py:39
  21.1 2.2 %collective-permute-start.9 = (bf16[2,192,128]{2,1,0:T(8,128)(2,1)S(1)}, bf16[2,192,128]{2,1,0:T(8,128)(2,1)S(1)}, u32[]{:S(2)}, u32[]{:S(2)}) collective-permute-start(bf16[2,192,128]{2,1,0:T(8,128)(2,1)S(1)} %collective-permute-done.8.refs_2_), channel_id=1, source_target_pairs={{0,1},{1,0},{2,3},{3,2},{4,5},{5,4},{6,7},{7,6},{8,9},{9,8},{10,11... | collective-permute-start | bytes 294920 | tf_op jit(solution)/shard_map/ppermute | solution.py:39

commit v5 on v4

--- a/solution.py
+++ b/solution.py
@@ -124,8 +124,9 @@
         out_ref[line, :, points:] = pad
 
 
-def image_kernel(members, occupied_ref, *refs):
-    blocks, (response_ref, wide_ref, narrow_ref) = refs[:-3], refs[-3:]
+def image_kernel(occupied_ref, orbitals_ref, *refs):
+    blocks, (response_ref, high_ref, halves_ref, cross_ref) = refs[:-4], refs[-4:]
+    members = orbitals_ref.shape[0]
     packs, points, _ = blocks[0].shape
     padded = response_ref.shape[2]
     span = LANES // members
@@ -141,46 +142,51 @@
     step = lane % (LANES // 4) // members
     apart, merged = 1, (0, 2, 3, 4)
     blank = jnp.zeros((padded - points, 2 * LANES), BF16)
-    for pack in range(packs):
-        tiles = [block[pack] for block in blocks]
-        native = jnp.concatenate([tiles[0], blank[:, :LANES]], axis=0)
-        image = jnp.zeros((points, LANES), F32)
-        for quarter in range(4):
-            here = [(q == quarter) for q in quarters]
-            together = sum(tiles[m] * here[m].astype(F32).astype(BF16) for m in merged)
-            window = jnp.concatenate([together, tiles[apart]], axis=1)
-            occupied = sum((here[m] & filled[m]).astype(F32) for m in merged)
-            beside = (here[apart] & filled[apart]).astype(F32)
-            both = jnp.concatenate([occupied, beside], axis=1)
-            steps = jnp.concatenate([step, step], axis=1)
-            masked = jnp.concatenate(
-                [window * jnp.where(steps == k, both, 0.0).astype(BF16) for k in range(per)], axis=0
-            )
-            gram = dot32(masked, jnp.concatenate([window, blank], axis=0), NT)
-            first = pack * span + quarter * per
-            response = response_ref[first : first + per].reshape(per * points, padded)
-            high, low = halves(gram * response)
-            fields = dot32(jnp.concatenate([high, low], axis=0), native)
-            for k in range(per):
-                a, b = k * points, (per + k) * points
-                field = fields[a : a + points] + fields[b : b + points]
-                image = jnp.where(own_line == quarter * per + k, field, image)
-        wide_ref[pack] = image
-        narrow_ref[pack] = image.astype(BF16)
-
-
-def overlap_kernel(orbitals_ref, image_ref, out_ref):
-    members, _, _ = orbitals_ref.shape
-    span = LANES // members
     natives = orbitals_ref[...].astype(F32)
     square = (LANES, LANES)
-    same_line = ids(square, 0) % span == lane_line(ids(square, 1), own_turn(), members)
+    same_line = ids(square, 0) % span == lane_line(ids(square, 1), turns[0], members)
+    tiles = [[block[pack] for block in blocks] for pack in range(packs)]
+
+    def weighted(pack, quarter):
+        here = [q == quarter for q in quarters]
+        together = sum(tiles[pack][m] * here[m].astype(F32).astype(BF16) for m in merged)
+        window = jnp.concatenate([together, tiles[pack][apart]], axis=1)
+        occupied = sum((here[m] & filled[m]).astype(F32) for m in merged)
+        beside = (here[apart] & filled[apart]).astype(F32)
+        both = jnp.concatenate([occupied, beside], axis=1)
+        steps = jnp.concatenate([step, step], axis=1)
+        masked = jnp.concatenate(
+            [window * jnp.where(steps == k, both, 0.0).astype(BF16) for k in range(per)], axis=0
+        )
+        gram = dot32(masked, jnp.concatenate([window, blank], axis=0), NT)
+        first = pack * span + quarter * per
+        response = response_ref[first : first + per].reshape(per * points, padded)
+        return jnp.concatenate(halves(gram * response), axis=0)
+
+    order = [(pack, quarter) for pack in range(packs) for quarter in range(4)]
+    ready = weighted(*order[0])
     cross = jnp.zeros(square, F32)
-    for pack in range(image_ref.shape[0]):
-        rows = rows_of(natives, pack, span).astype(BF16)
-        product = dot32(rows, jnp.concatenate(halves(image_ref[pack]), axis=1))
-        cross = cross + (product[:, :LANES] + product[:, LANES:])
-    out_ref[...] = jnp.where(same_line, cross, 0.0).reshape(members, span, LANES).sum(axis=1)
+    for place, (pack, quarter) in enumerate(order):
+        kernel = ready
+        if place + 1 < len(order):
+            ready = weighted(*order[place + 1])
+        native = jnp.concatenate([tiles[pack][0], blank[:, :LANES]], axis=0)
+        fields = dot32(kernel, native)
+        if quarter == 0:
+            image = jnp.zeros((points, LANES), F32)
+        for k in range(per):
+            a, b = k * points, (per + k) * points
+            field = fields[a : a + points] + fields[b : b + points]
+            image = jnp.where(own_line == quarter * per + k, field, image)
+        if quarter == 3:
+            high, low = halves(image)
+            high_ref[pack] = high
+            halves_ref[pack] = high
+            halves_ref[packs + pack] = low
+            rows = rows_of(natives, pack, span).astype(BF16)
+            product = dot32(rows, jnp.concatenate([high, low], axis=1))
+            cross = cross + (product[:, :LANES] + product[:, LANES:])
+    cross_ref[...] = jnp.where(same_line, cross, 0.0).reshape(members, span, LANES).sum(axis=1)
 
 
 def factor_kernel(cells, owners_ref, *refs):
@@ -238,29 +244,33 @@
 
 
 def route_kernel(weights_ref, *refs):
-    parts, out_ref = refs[:-1], refs[-1]
-    packs, points, _ = parts[0].shape
+    parts, (out_hbm, staged, semaphores) = refs[:-3], refs[-3:]
+    points = staged.shape[3]
     weights = weights_ref[...]
     rows = weights.shape[0] // 2
     span = rows // CAP
-    lines = packs * span
+    lines = staged.shape[2]
+    packs = lines // span
     group = lax.axis_index("grid") * lax.axis_size("ham") + lax.axis_index("ham")
+    copies = []
     for flip, part in enumerate(parts):
-        start = pl.multiple_of((group ^ flip) * lines, lines)
         sums = []
         for pack in range(packs):
-            if part.dtype == BF16:
-                both = dot32(weights, part[pack], NT)
-                result = both[:rows] + both[rows:]
-            else:
-                high, low = halves(part[pack])
-                both = dot32(weights, high, NT)
-                result = both[:rows] + (both[rows:] + dot32(weights[:rows], low, NT))
+            both = dot32(weights, part[pack], NT)
+            result = both[:rows] + both[rows:]
+            if part.shape[0] > packs:
+                result = result + dot32(weights[:rows], part[packs + pack], NT)
             sums.append(result.reshape(CAP, span, points))
-        out_ref[:, pl.ds(start, lines), :] = jnp.concatenate(sums, axis=1).astype(BF16)
-
-
-def call(kernel, name, shapes, flops, moved, scratch=(), scalars=0, operands=0):
+        staged[flip] = jnp.concatenate(sums, axis=1).astype(BF16)
+        start = pl.multiple_of((group ^ flip) * lines, lines)
+        target = out_hbm.at[:, pl.ds(start, lines), :]
+        copies.append(pltpu.make_async_copy(staged.at[flip], target, semaphores.at[flip]))
+        copies[-1].start()
+    for copy in copies:
+        copy.wait()
+
+
+def call(kernel, name, shapes, flops, moved, scratch=(), scalars=0, operands=0, remote=False):
     vmem = pl.BlockSpec(memory_space=pltpu.VMEM)
     smem = pl.BlockSpec(memory_space=pltpu.SMEM)
     return pl.pallas_call(
@@ -268,7 +278,7 @@
         name=name,
         out_shape=shapes,
         in_specs=[smem] * scalars + [vmem] * operands,
-        out_specs=[vmem] * len(shapes),
+        out_specs=[pl.BlockSpec(memory_space=pl.ANY) if remote else vmem] * len(shapes),
         scratch_shapes=list(scratch),
         compiler_params=pltpu.CompilerParams(vmem_limit_bytes=VMEM_LIMIT),
         cost_estimate=pl.CostEstimate(flops=flops, bytes_accessed=moved, transcendentals=0),
@@ -302,27 +312,25 @@
         operands=2,
     )(coulomb, tables)
     blocks = len(guests) + 1
-    wide, narrow = call(
-        functools.partial(image_kernel, members),
+    high, parts, cross = call(
+        image_kernel,
         "image",
-        [shape((packs, points, LANES), F32), shape((packs, points, LANES), BF16)],
+        [
+            shape((packs, points, LANES), BF16),
+            shape((2 * packs, points, LANES), BF16),
+            shape((members, LANES), F32),
+        ],
         2 * lines * points * padded * (4 * LANES),
         4 * lines * points**2,
         scalars=1,
-        operands=blocks + 1,
-    )(occupied, packed, *guests, response)
-    (overlap,) = call(
-        overlap_kernel,
-        "overlap",
-        [shape((members, LANES), F32)],
-        4 * packs * points * LANES**2,
-        8 * orbitals.size,
-        operands=2,
-    )(orbitals, wide)
-    overlaps = [overlap] + [swapped(overlap, flip) for flip in range(1, groups)]
-    images = [wide] + [swapped(wide, flip) for flip in range(1, near)]
+        operands=blocks + 2,
+    )(occupied, orbitals, packed, *guests, response)
+    for flip in range(near.bit_length() - 1):
+        cross = cross + swapped(cross, 1 << flip)
+    sums = [cross] + [swapped(cross, grid * near) for grid in range(1, grids)]
+    images = [parts] + [swapped(parts, flip) for flip in range(1, near)]
     for grid in range(1, grids):
-        across = swapped(narrow, grid * near)
+        across = swapped(high, grid * near)
         images += [across] + [swapped(across, flip) for flip in range(1, near)]
     cells = lines * groups * points
 
@@ -332,15 +340,20 @@
         [shape((members, members), F32), shape((2 * CAP * span, LANES), BF16)],
         FACTOR_COST,
         members**2 * 4,
-        operands=1 + groups,
-    )(owners, *overlaps)
+        operands=1 + grids,
+    )(owners, *sums)
     (routed,) = call(
         route_kernel,
         "route",
         [shape((CAP, groups * lines, points), BF16)],
         2 * CAP * members * groups * lines * points,
         6 * members * groups * lines * points,
+        scratch=[
+            pltpu.VMEM((groups, CAP, lines, points), BF16),
+            pltpu.SemaphoreType.DMA((groups,)),
+        ],
         operands=1 + groups,
+        remote=True,
     )(weights, *images)
     return routed[None, None], intersection[None]
 

time: 24.8 us -> 25.7 us (1.036)
  waiting for transfers between devices: 2.42 us -> 5.15 us
  starting transfers between devices: 12.2 us -> 10.5 us
    ppermute x6 -> x5, waiting for transfers between devices: 1.48 us -> 4.2 us  [swapped(): lax.ppermute(value, ('grid', 'ham'), [(group, group ^ flip) for group in...]
    ppermute x6 -> x5, starting transfers between devices: 3.83 us -> 2.1 us  [swapped(): lax.ppermute(value, ('grid', 'ham'), [(group, group ^ flip) for group in...]
    pallas_call x2 -> x1, Pallas kernels: 2.49 us -> 2.52 us  [local(): call(image_kernel, 'image', [shape((packs, points, LANES), BF16), shape((...]
  transfers between devices with their start and end apart: 10 -> 9, of which waited for: 4 -> 5; matrix products, arithmetic and copies ran while one was open for 0% -> 0% of each run, Pallas kernels for 11% -> 10%
where the time goes in v5:
time: 25.7 us; the launch traced here: 25.5 us
  starting transfers between devices  10.5 us (41%)
  Pallas kernels  6.48 us (25%)
  waiting for transfers between devices  5.15 us (20%)
  local copies, waits for them, and re-layouts  2.67 us (10%)
  between operations  0.71 us (3%)
    ppermute x4, starting transfers between devices, exchanged(): lax.ppermute(value, 'band', [(row[turn], block) for block, row in enumera...  8.36 us
    ppermute x5, waiting for transfers between devices, swapped(): lax.ppermute(value, ('grid', 'ham'), [(group, group ^ flip) for group in...  4.2 us
    unnamed x13, local copies, waits for them, and re-layouts  2.67 us
    pallas_call x1, Pallas kernels, local(): call(image_kernel, 'image', [shape((packs, points, LANES), BF16), shape((...  2.52 us
    ppermute x5, starting transfers between devices, swapped(): lax.ppermute(value, ('grid', 'ham'), [(group, group ^ flip) for group in...  2.1 us
    pallas_call x1, Pallas kernels, local(): call(response_kernel, 'response', [shape((lines, points, padded), F32)],...  1.3 us
    pallas_call x1, Pallas kernels, local(): call(functools.partial(factor_kernel, cells), 'factor', [shape((members,...  1.23 us
    pallas_call x1, Pallas kernels, local(): call(route_kernel, 'route', [shape((CAP, groups * lines, points), BF16)],...  1.19 us
  transfers between devices with their start and end apart: 9, of which 5 were waited for; matrix products, arithmetic and copies ran while one was open for 0% of the time, Pallas kernels for 10%

profile of v5, /device:TPU:0, one launch (start us, length us, event | category | flops | bytes accessed | tf_op | source)
XLA Modules:
  0.0 25.5 jit_solution(14197241333282139000)
XLA Ops:
  0.6 0.0 copy-start
  0.6 0.9 %copy-done = bf16[16,16,192]{2,1,0:T(8,128)(2,1)S(1)} copy-done((bf16[16,16,192]{2,1,0:T(8,128)(2,1)S(1)}, bf16[16,16,192]{2,1,0:T(8,128)(2,1)}, u32[]{:S(2)}) %copy-start) | copy-done | bytes 98328
  1.5 0.0 copy-start.1
  1.5 0.2 pack.1.refs_0_
  1.8 3.1 %collective-permute-start = (bf16[2,192,128]{2,1,0:T(8,128)(2,1)S(1)}, bf16[2,192,128]{2,1,0:T(8,128)(2,1)S(1)}, u32[]{:S(2)}, u32[]{:S(2)}) collective-permute-start(bf16[2,192,128]{2,1,0:T(8,128)(2,1)S(1)} %pack.1.refs_0_), channel_id=1, source_target_pairs={{24,0},{28,4},{0,8},{4,12},{8,16},{12,20},{16,24},{20,28},{25,1},{... | collective-permute-start | bytes 294920 | tf_op jit(solution)/shard_map/ppermute | solution.py:32
  4.9 3.2 %collective-permute-start.1 = (bf16[2,192,128]{2,1,0:T(8,128)(2,1)S(1)}, bf16[2,192,128]{2,1,0:T(8,128)(2,1)S(1)}, u32[]{:S(2)}, u32[]{:S(2)}) collective-permute-start(bf16[2,192,128]{2,1,0:T(8,128)(2,1)S(1)} %pack.1.refs_0_), channel_id=1, source_target_pairs={{28,0},{8,4},{4,8},{16,12},{12,16},{24,20},{20,24},{0,28},{29,1},{... | collective-permute-start | bytes 294920 | tf_op jit(solution)/shard_map/ppermute | solution.py:32
  8.1 0.0 collective-permute-start.2
  8.1 2.1 %collective-permute-start.3 = (bf16[2,192,128]{2,1,0:T(8,128)(2,1)S(1)}, bf16[2,192,128]{2,1,0:T(8,128)(2,1)S(1)}, u32[]{:S(2)}, u32[]{:S(2)}) collective-permute-start(bf16[2,192,128]{2,1,0:T(8,128)(2,1)S(1)} %pack.1.refs_0_), channel_id=1, source_target_pairs={{8,0},{12,4},{16,8},{20,12},{24,16},{28,20},{0,24},{4,28},{9,1},{1... | collective-permute-start | bytes 294920 | tf_op jit(solution)/shard_map/ppermute | solution.py:32
  10.1 1.0 %copy-done.2 = bf16[3,192,192]{2,1,0:T(8,128)(2,1)S(1)} copy-done((bf16[3,192,192]{2,1,0:T(8,128)(2,1)S(1)}, bf16[3,192,192]{2,1,0:T(8,128)(2,1)}, u32[]{:S(2)}) %copy-start.2) | copy-done | bytes 221208
  11.1 0.7 %copy-done.3 = f32[16,192]{1,0:T(8,128)S(1)} copy-done((f32[16,192]{1,0:T(8,128)S(1)}, f32[16,192]{1,0:T(8,128)}, u32[]{:S(2)}) %copy-start.3) | copy-done | bytes 12312
  11.8 1.3 %response.1.refs_5_ = f32[16,192,256]{2,1,0:T(8,128)S(1)} custom-call(f32[16,192]{1,0:T(8,128)S(1)} %copy-done.3, bf16[3,192,192]{2,1,0:T(8,128)(2,1)S(1)} %copy-done.2), custom_call_target="tpu_custom_call" | custom-call | flops 452984832 | bytes 2359296 | tf_op jit(solution)/shard_map/response/pallas_call | solution.py:306
  13.1 0.0 collective-permute-done.refs_1_
  13.1 0.6 %collective-permute-done.1.refs_2_ = bf16[2,192,128]{2,1,0:T(8,128)(2,1)S(1)} collective-permute-done((bf16[2,192,128]{2,1,0:T(8,128)(2,1)S(1)}, bf16[2,192,128]{2,1,0:T(8,128)(2,1)S(1)}, u32[]{:S(2)}, u32[]{:S(2)}) %collective-permute-start.1) | collective-permute-done | bytes 98336 | tf_op jit(solution)/shard_map/ppermute | solution.py:32
  13.7 0.4 %collective-permute-done.2.refs_3_ = bf16[2,192,128]{2,1,0:T(8,128)(2,1)S(1)} collective-permute-done((bf16[2,192,128]{2,1,0:T(8,128)(2,1)S(1)}, bf16[2,192,128]{2,1,0:T(8,128)(2,1)S(1)}, u32[]{:S(2)}, u32[]{:S(2)}) %collective-permute-start.2) | collective-permute-done | bytes 98336 | tf_op jit(solution)/shard_map/ppermute | solution.py:32
  14.1 0.0 collective-permute-done.3.refs_4_
  14.1 0.0 copy-done.1
  14.1 0.0 copy-done.4
  14.1 2.5 %image.1 = (bf16[2,192,128]{2,1,0:T(8,128)(2,1)S(1)}, bf16[4,192,128]{2,1,0:T(8,128)(2,1)S(1)}, f32[16,128]{1,0:T(8,128)S(1)}) custom-call(s32[8]{0:T(128)S(1)} %copy-done.4, bf16[16,16,192]{2,1,0:T(8,128)(2,1)S(1)} %copy-done.1, bf16[2,192,128]{2,1,0:T(8,128)(2,1)S(1)} %pack.1.refs_0_, bf16[2,192,128]{2,1,0:T(8,128)(2,1)S(1)} %collective-permute-done.refs_1_, ...), custom_call_target="tpu_custom_call" | custom-call | flops 805306368 | bytes 2359296 | tf_op jit(solution)/shard_map/image/pallas_call | solution.py:315
  16.6 1.6 %collective-permute-start.7 = (bf16[2,192,128]{2,1,0:T(8,128)(2,1)S(1)}, bf16[2,192,128]{2,1,0:T(8,128)(2,1)S(1)}, u32[]{:S(2)}, u32[]{:S(2)}) collective-permute-start(bf16[2,192,128]{2,1,0:T(8,128)(2,1)S(1)} %get-tuple-element.10), channel_id=1, source_target_pairs={{0,2},{1,3},{2,0},{3,1},{4,6},{5,7},{6,4},{7,5},{8,10},{9,11},{10,... | collective-permute-start | bytes 294920 | tf_op jit(solution)/shard_map/ppermute | solution.py:39
  18.2 0.0 collective-permute-start.4
  18.2 1.2 %collective-permute-done.4 = f32[16,128]{1,0:T(8,128)S(1)} collective-permute-done((f32[16,128]{1,0:T(8,128)S(1)}, f32[16,128]{1,0:T(8,128)S(1)}, u32[]{:S(2)}, u32[]{:S(2)}) %collective-permute-start.4) | collective-permute-done | bytes 8224 | tf_op jit(solution)/shard_map/ppermute | solution.py:39
  19.4 0.5 %collective-permute-start.5 = (f32[16,128]{1,0:T(8,128)S(1)}, f32[16,128]{1,0:T(8,128)S(1)}, u32[]{:S(2)}, u32[]{:S(2)}) collective-permute-start(f32[16,128]{1,0:T(8,128)S(1)} %add.3.refs_0_), channel_id=1, source_target_pairs={{0,2},{1,3},{2,0},{3,1},{4,6},{5,7},{6,4},{7,5},{8,10},{9,11},{10,... | collective-permute-start | bytes 24584 | tf_op jit(solution)/shard_map/ppermute | solution.py:39
  19.9 0.0 copy-done.5
  19.9 0.1 copy.7.owners_ref
  20.0 0.0 collective-permute-start.6
  20.0 1.3 %collective-permute-done.7.refs_2_ = bf16[2,192,128]{2,1,0:T(8,128)(2,1)S(1)} collective-permute-done((bf16[2,192,128]{2,1,0:T(8,128)(2,1)S(1)}, bf16[2,192,128]{2,1,0:T(8,128)(2,1)S(1)}, u32[]{:S(2)}, u32[]{:S(2)}) %collective-permute-start.7) | collective-permute-done | bytes 98336 | tf_op jit(solution)/shard_map/ppermute | solution.py:39
  21.3 0.0 collective-permute-start.8
  21.3 1.7 %collective-permute-done.5.refs_1_ = f32[16,128]{1,0:T(8,128)S(1)} collective-permute-done((f32[16,128]{1,0:T(8,128)S(1)}, f32[16,128]{1,0:T(8,128)S(1)}, u32[]{:S(2)}, u32[]{:S(2)}) %collective-permute-start.5) | collective-permute-done | bytes 8224 | tf_op jit(solution)/shard_map/ppermute | solution.py:39
  23.0 1.2 %factor.1 = (f32[16,16]{1,0:T(8,128)}, bf16[128,128]{1,0:T(8,128)(2,1)S(1)}) custom-call(s32[16,1]{1,0:T(8,128)S(1)} %copy.7.owners_ref, f32[16,128]{1,0:T(8,128)S(1)} %add.3.refs_0_, f32[16,128]{1,0:T(8,128)S(1)} %collective-permute-done.5.refs_1_), custom_call_target="tpu_custom_call" | custom-call | flops 3000000000 | bytes 1024 | tf_op jit(solution)/shard_map/factor/pallas_call | solution.py:337
  24.3 0.0 collective-permute-done.8.refs_3_
  24.3 0.0 collective-permute-done.6.refs_1_
  24.3 1.2 %route.1 = bf16[8,64,192]{2,1,0:T(8,128)(2,1)} custom-call(bf16[128,128]{1,0:T(8,128)(2,1)S(1)} %get-tuple-element.8.weights_ref, bf16[4,192,128]{2,1,0:T(8,128)(2,1)S(1)} %get-tuple-element.9.refs_0_, bf16[4,192,128]{2,1,0:T(8,128)(2,1)S(1)} %collective-permute-done.6.refs_1_, bf16[2,192,128]{2,1,0:T(8,128)(2,1)S(1)} %collective-permute-done.7.refs_2_, ...), custom_call_target="tpu_custom_call" | custom-call | flops 3145728 | bytes 1179648 | tf_op jit(solution)/shard_map/route/pallas_call | solution.py:345
  (5 shorter events, 0.0 us)
Async XLA Ops:
  0.6 0.9 %copy-start = (bf16[16,16,192]{2,1,0:T(8,128)(2,1)S(1)}, bf16[16,16,192]{2,1,0:T(8,128)(2,1)}, u32[]{:S(2)}) copy-start(bf16[16,16,192]{2,1,0:T(8,128)(2,1)} %orbitals_ref.3) | copy-start | bytes 294916
  1.5 12.6 %copy-start.1 = (bf16[16,16,192]{2,1,0:T(8,128)(2,1)S(1)}, bf16[16,16,192]{2,1,0:T(8,128)(2,1)}, u32[]{:S(2)}) copy-start(bf16[16,16,192]{2,1,0:T(8,128)(2,1)} %orbitals_ref.3) | copy-start | bytes 294916
  1.5 12.6 %copy-start.4 = (s32[8]{0:T(128)S(1)}, s32[8]{0:T(128)}, u32[]{:S(2)}) copy-start(s32[8]{0:T(128)} %occupied_ref.1) | copy-start | bytes 100
  1.5 18.4 %copy-start.5 = (s32[16,1]{0,1:T(1,128)S(1)}, s32[16,1]{0,1:T(1,128)}, u32[]{:S(2)}) copy-start(s32[16,1]{0,1:T(1,128)} %param.8) | copy-start | bytes 196
  1.8 11.4 %collective-permute-start = (bf16[2,192,128]{2,1,0:T(8,128)(2,1)S(1)}, bf16[2,192,128]{2,1,0:T(8,128)(2,1)S(1)}, u32[]{:S(2)}, u32[]{:S(2)}) collective-permute-start(bf16[2,192,128]{2,1,0:T(8,128)(2,1)S(1)} %pack.1.refs_0_), channel_id=1, source_target_pairs={{24,0},{28,4},{0,8},{4,12},{8,16},{12,20},{16,24},{20,28},{25,1},{... | collective-permute-start | bytes 294920 | tf_op jit(solution)/shard_map/ppermute | solution.py:32
  4.9 8.8 %collective-permute-start.1 = (bf16[2,192,128]{2,1,0:T(8,128)(2,1)S(1)}, bf16[2,192,128]{2,1,0:T(8,128)(2,1)S(1)}, u32[]{:S(2)}, u32[]{:S(2)}) collective-permute-start(bf16[2,192,128]{2,1,0:T(8,128)(2,1)S(1)} %pack.1.refs_0_), channel_id=1, source_target_pairs={{28,0},{8,4},{4,8},{16,12},{12,16},{24,20},{20,24},{0,28},{29,1},{... | collective-permute-start | bytes 294920 | tf_op jit(solution)/shard_map/ppermute | solution.py:32
  8.1 6.0 %collective-permute-start.2 = (bf16[2,192,128]{2,1,0:T(8,128)(2,1)S(1)}, bf16[2,192,128]{2,1,0:T(8,128)(2,1)S(1)}, u32[]{:S(2)}, u32[]{:S(2)}) collective-permute-start(bf16[2,192,128]{2,1,0:T(8,128)(2,1)S(1)} %pack.1.refs_0_), channel_id=1, source_target_pairs={{4,0},{0,4},{12,8},{8,12},{20,16},{16,20},{28,24},{24,28},{5,1},{1... | collective-permute-start | bytes 294920 | tf_op jit(solution)/shard_map/ppermute | solution.py:32
  8.1 6.0 %collective-permute-start.3 = (bf16[2,192,128]{2,1,0:T(8,128)(2,1)S(1)}, bf16[2,192,128]{2,1,0:T(8,128)(2,1)S(1)}, u32[]{:S(2)}, u32[]{:S(2)}) collective-permute-start(bf16[2,192,128]{2,1,0:T(8,128)(2,1)S(1)} %pack.1.refs_0_), channel_id=1, source_target_pairs={{8,0},{12,4},{16,8},{20,12},{24,16},{28,20},{0,24},{4,28},{9,1},{1... | collective-permute-start | bytes 294920 | tf_op jit(solution)/shard_map/ppermute | solution.py:32
  10.1 1.0 %copy-start.2 = (bf16[3,192,192]{2,1,0:T(8,128)(2,1)S(1)}, bf16[3,192,192]{2,1,0:T(8,128)(2,1)}, u32[]{:S(2)}) copy-start(bf16[3,192,192]{2,1,0:T(8,128)(2,1)} %constant.3.tables_ref) | copy-start | bytes 663556
  11.1 0.7 %copy-start.3 = (f32[16,192]{1,0:T(8,128)S(1)}, f32[16,192]{1,0:T(8,128)}, u32[]{:S(2)}) copy-start(f32[16,192]{1,0:T(8,128)} %coulomb_ref.1) | copy-start | bytes 36868
  16.6 4.7 %collective-permute-start.7 = (bf16[2,192,128]{2,1,0:T(8,128)(2,1)S(1)}, bf16[2,192,128]{2,1,0:T(8,128)(2,1)S(1)}, u32[]{:S(2)}, u32[]{:S(2)}) collective-permute-start(bf16[2,192,128]{2,1,0:T(8,128)(2,1)S(1)} %get-tuple-element.10), channel_id=1, source_target_pairs={{0,2},{1,3},{2,0},{3,1},{4,6},{5,7},{6,4},{7,5},{8,10},{9,11},{10,... | collective-permute-start | bytes 294920 | tf_op jit(solution)/shard_map/ppermute | solution.py:39
  18.2 1.2 %collective-permute-start.4 = (f32[16,128]{1,0:T(8,128)S(1)}, f32[16,128]{1,0:T(8,128)S(1)}, u32[]{:S(2)}, u32[]{:S(2)}) collective-permute-start(f32[16,128]{1,0:T(8,128)S(1)} %get-tuple-element.7), channel_id=1, source_target_pairs={{0,1},{1,0},{2,3},{3,2},{4,5},{5,4},{6,7},{7,6},{8,9},{9,8},{10,11... | collective-permute-start | bytes 24584 | tf_op jit(solution)/shard_map/ppermute | solution.py:39
  19.4 3.7 %collective-permute-start.5 = (f32[16,128]{1,0:T(8,128)S(1)}, f32[16,128]{1,0:T(8,128)S(1)}, u32[]{:S(2)}, u32[]{:S(2)}) collective-permute-start(f32[16,128]{1,0:T(8,128)S(1)} %add.3.refs_0_), channel_id=1, source_target_pairs={{0,2},{1,3},{2,0},{3,1},{4,6},{5,7},{6,4},{7,5},{8,10},{9,11},{10,... | collective-permute-start | bytes 24584 | tf_op jit(solution)/shard_map/ppermute | solution.py:39
  20.0 4.3 %collective-permute-start.6 = (bf16[4,192,128]{2,1,0:T(8,128)(2,1)S(1)}, bf16[4,192,128]{2,1,0:T(8,128)(2,1)S(1)}, u32[]{:S(2)}, u32[]{:S(2)}) collective-permute-start(bf16[4,192,128]{2,1,0:T(8,128)(2,1)S(1)} %get-tuple-element.9.refs_0_), channel_id=1, source_target_pairs={{0,1},{1,0},{2,3},{3,2},{4,5},{5,4},{6,7},{7,6},{8,9},{9,8},{10,11... | collective-permute-start | bytes 589832 | tf_op jit(solution)/shard_map/ppermute | solution.py:39
  21.3 2.9 %collective-permute-start.8 = (bf16[2,192,128]{2,1,0:T(8,128)(2,1)S(1)}, bf16[2,192,128]{2,1,0:T(8,128)(2,1)S(1)}, u32[]{:S(2)}, u32[]{:S(2)}) collective-permute-start(bf16[2,192,128]{2,1,0:T(8,128)(2,1)S(1)} %collective-permute-done.7.refs_2_), channel_id=1, source_target_pairs={{0,1},{1,0},{2,3},{3,2},{4,5},{5,4},{6,7},{7,6},{8,9},{9,8},{10,11... | collective-permute-start | bytes 294920 | tf_op jit(solution)/shard_map/ppermute | solution.py:39

commit v6 on v4

--- a/solution.py
+++ b/solution.py
@@ -125,7 +125,7 @@
 
 
 def image_kernel(members, occupied_ref, *refs):
-    blocks, (response_ref, wide_ref, narrow_ref) = refs[:-3], refs[-3:]
+    blocks, (response_ref, high_ref, halves_ref) = refs[:-3], refs[-3:]
     packs, points, _ = blocks[0].shape
     padded = response_ref.shape[2]
     span = LANES // members
@@ -165,20 +165,24 @@
                 a, b = k * points, (per + k) * points
                 field = fields[a : a + points] + fields[b : b + points]
                 image = jnp.where(own_line == quarter * per + k, field, image)
-        wide_ref[pack] = image
-        narrow_ref[pack] = image.astype(BF16)
-
-
-def overlap_kernel(orbitals_ref, image_ref, out_ref):
+        high, low = halves(image)
+        high_ref[pack] = high
+        halves_ref[pack] = high
+        halves_ref[packs + pack] = low
+
+
+def overlap_kernel(orbitals_ref, halves_ref, out_ref):
     members, _, _ = orbitals_ref.shape
     span = LANES // members
     natives = orbitals_ref[...].astype(F32)
     square = (LANES, LANES)
     same_line = ids(square, 0) % span == lane_line(ids(square, 1), own_turn(), members)
     cross = jnp.zeros(square, F32)
-    for pack in range(image_ref.shape[0]):
+    packs = halves_ref.shape[0] // 2
+    for pack in range(packs):
         rows = rows_of(natives, pack, span).astype(BF16)
-        product = dot32(rows, jnp.concatenate(halves(image_ref[pack]), axis=1))
+        both = jnp.concatenate([halves_ref[pack], halves_ref[packs + pack]], axis=1)
+        product = dot32(rows, both)
         cross = cross + (product[:, :LANES] + product[:, LANES:])
     out_ref[...] = jnp.where(same_line, cross, 0.0).reshape(members, span, LANES).sum(axis=1)
 
@@ -237,30 +241,36 @@
         weights_ref[place : place + rows, :] = chosen.astype(BF16)
 
 
-def route_kernel(weights_ref, *refs):
-    parts, out_ref = refs[:-1], refs[-1]
-    packs, points, _ = parts[0].shape
+def route_kernel(overlap_ref, weights_ref, *refs):
+    parts, (out_hbm, overlap_hbm, staged, semaphores) = refs[:-4], refs[-4:]
+    groups = len(parts)
+    copies = [pltpu.make_async_copy(overlap_ref, overlap_hbm, semaphores.at[groups])]
+    copies[0].start()
+    points = staged.shape[3]
     weights = weights_ref[...]
     rows = weights.shape[0] // 2
     span = rows // CAP
-    lines = packs * span
+    lines = staged.shape[2]
+    packs = lines // span
     group = lax.axis_index("grid") * lax.axis_size("ham") + lax.axis_index("ham")
     for flip, part in enumerate(parts):
-        start = pl.multiple_of((group ^ flip) * lines, lines)
         sums = []
         for pack in range(packs):
-            if part.dtype == BF16:
-                both = dot32(weights, part[pack], NT)
-                result = both[:rows] + both[rows:]
-            else:
-                high, low = halves(part[pack])
-                both = dot32(weights, high, NT)
-                result = both[:rows] + (both[rows:] + dot32(weights[:rows], low, NT))
+            both = dot32(weights, part[pack], NT)
+            result = both[:rows] + both[rows:]
+            if part.shape[0] > packs:
+                result = result + dot32(weights[:rows], part[packs + pack], NT)
             sums.append(result.reshape(CAP, span, points))
-        out_ref[:, pl.ds(start, lines), :] = jnp.concatenate(sums, axis=1).astype(BF16)
-
-
-def call(kernel, name, shapes, flops, moved, scratch=(), scalars=0, operands=0):
+        staged[flip] = jnp.concatenate(sums, axis=1).astype(BF16)
+        start = pl.multiple_of((group ^ flip) * lines, lines)
+        target = out_hbm.at[:, pl.ds(start, lines), :]
+        copies.append(pltpu.make_async_copy(staged.at[flip], target, semaphores.at[flip]))
+        copies[-1].start()
+    for copy in copies:
+        copy.wait()
+
+
+def call(kernel, name, shapes, flops, moved, scratch=(), scalars=0, operands=0, remote=False):
     vmem = pl.BlockSpec(memory_space=pltpu.VMEM)
     smem = pl.BlockSpec(memory_space=pltpu.SMEM)
     return pl.pallas_call(
@@ -268,7 +278,7 @@
         name=name,
         out_shape=shapes,
         in_specs=[smem] * scalars + [vmem] * operands,
-        out_specs=[vmem] * len(shapes),
+        out_specs=[pl.BlockSpec(memory_space=pl.ANY) if remote else vmem] * len(shapes),
         scratch_shapes=list(scratch),
         compiler_params=pltpu.CompilerParams(vmem_limit_bytes=VMEM_LIMIT),
         cost_estimate=pl.CostEstimate(flops=flops, bytes_accessed=moved, transcendentals=0),
@@ -302,10 +312,13 @@
         operands=2,
     )(coulomb, tables)
     blocks = len(guests) + 1
-    wide, narrow = call(
+    high, parts = call(
         functools.partial(image_kernel, members),
         "image",
-        [shape((packs, points, LANES), F32), shape((packs, points, LANES), BF16)],
+        [
+            shape((packs, points, LANES), BF16),
+            shape((2 * packs, points, LANES), BF16),
+        ],
         2 * lines * points * padded * (4 * LANES),
         4 * lines * points**2,
         scalars=1,
@@ -318,11 +331,11 @@
         4 * packs * points * LANES**2,
         8 * orbitals.size,
         operands=2,
-    )(orbitals, wide)
+    )(orbitals, parts)
     overlaps = [overlap] + [swapped(overlap, flip) for flip in range(1, groups)]
-    images = [wide] + [swapped(wide, flip) for flip in range(1, near)]
+    images = [parts] + [swapped(parts, flip) for flip in range(1, near)]
     for grid in range(1, grids):
-        across = swapped(narrow, grid * near)
+        across = swapped(high, grid * near)
         images += [across] + [swapped(across, flip) for flip in range(1, near)]
     cells = lines * groups * points
 
@@ -334,14 +347,19 @@
         members**2 * 4,
         operands=1 + groups,
     )(owners, *overlaps)
-    (routed,) = call(
+    routed, intersection = call(
         route_kernel,
         "route",
-        [shape((CAP, groups * lines, points), BF16)],
+        [shape((CAP, groups * lines, points), BF16), shape((members, members), F32)],
         2 * CAP * members * groups * lines * points,
         6 * members * groups * lines * points,
-        operands=1 + groups,
-    )(weights, *images)
+        scratch=[
+            pltpu.VMEM((groups, CAP, lines, points), BF16),
+            pltpu.SemaphoreType.DMA((groups + 1,)),
+        ],
+        operands=2 + groups,
+        remote=True,
+    )(intersection, weights, *images)
     return routed[None, None], intersection[None]
 
 

time: 24.8 us -> 24.7 us (level)
  no operation moved by 1% of the time
where the time goes in v6:
time: 24.7 us; the launch traced here: 24.5 us
  starting transfers between devices  12.2 us (49%)
  Pallas kernels  6.47 us (26%)
  local copies, waits for them, and re-layouts  2.67 us (11%)
  waiting for transfers between devices  2.42 us (10%)
  between operations  0.72 us (3%)
    ppermute x4, starting transfers between devices, exchanged(): lax.ppermute(value, 'band', [(row[turn], block) for block, row in enumera...  8.36 us
    ppermute x6, starting transfers between devices, swapped(): lax.ppermute(value, ('grid', 'ham'), [(group, group ^ flip) for group in...  3.84 us
    unnamed x13, local copies, waits for them, and re-layouts  2.67 us
    pallas_call x1, Pallas kernels, local(): call(functools.partial(image_kernel, members), 'image', [shape((packs, po...  2.3 us
    ppermute x6, waiting for transfers between devices, swapped(): lax.ppermute(value, ('grid', 'ham'), [(group, group ^ flip) for group in...  1.48 us
    pallas_call x1, Pallas kernels, local(): call(response_kernel, 'response', [shape((lines, points, padded), F32)],...  1.31 us
    pallas_call x1, Pallas kernels, local(): call(functools.partial(factor_kernel, cells), 'factor', [shape((members,...  1.23 us
    pallas_call x1, Pallas kernels, local(): call(route_kernel, 'route', [shape((CAP, groups * lines, points), BF16),...  1.2 us
  transfers between devices with their start and end apart: 10, of which 4 were waited for; matrix products, arithmetic and copies ran while one was open for 0% of the time, Pallas kernels for 11%

profile of v6, /device:TPU:0, one launch (start us, length us, event | category | flops | bytes accessed | tf_op | source)
XLA Modules:
  0.0 24.5 jit_solution(5374272701261776734)
XLA Ops:
  0.6 0.0 copy-start
  0.6 0.9 %copy-done = bf16[16,16,192]{2,1,0:T(8,128)(2,1)S(1)} copy-done((bf16[16,16,192]{2,1,0:T(8,128)(2,1)S(1)}, bf16[16,16,192]{2,1,0:T(8,128)(2,1)}, u32[]{:S(2)}) %copy-start) | copy-done | bytes 98328
  1.5 0.2 pack.1.refs_0_
  1.8 0.0 copy-start.1
  1.8 3.1 %collective-permute-start = (bf16[2,192,128]{2,1,0:T(8,128)(2,1)S(1)}, bf16[2,192,128]{2,1,0:T(8,128)(2,1)S(1)}, u32[]{:S(2)}, u32[]{:S(2)}) collective-permute-start(bf16[2,192,128]{2,1,0:T(8,128)(2,1)S(1)} %pack.1.refs_0_), channel_id=1, source_target_pairs={{24,0},{28,4},{0,8},{4,12},{8,16},{12,20},{16,24},{20,28},{25,1},{... | collective-permute-start | bytes 294920 | tf_op jit(solution)/shard_map/ppermute | solution.py:32
  4.9 3.2 %collective-permute-start.1 = (bf16[2,192,128]{2,1,0:T(8,128)(2,1)S(1)}, bf16[2,192,128]{2,1,0:T(8,128)(2,1)S(1)}, u32[]{:S(2)}, u32[]{:S(2)}) collective-permute-start(bf16[2,192,128]{2,1,0:T(8,128)(2,1)S(1)} %pack.1.refs_0_), channel_id=1, source_target_pairs={{28,0},{8,4},{4,8},{16,12},{12,16},{24,20},{20,24},{0,28},{29,1},{... | collective-permute-start | bytes 294920 | tf_op jit(solution)/shard_map/ppermute | solution.py:32
  8.1 0.0 collective-permute-start.2
  8.1 2.1 %collective-permute-start.3 = (bf16[2,192,128]{2,1,0:T(8,128)(2,1)S(1)}, bf16[2,192,128]{2,1,0:T(8,128)(2,1)S(1)}, u32[]{:S(2)}, u32[]{:S(2)}) collective-permute-start(bf16[2,192,128]{2,1,0:T(8,128)(2,1)S(1)} %pack.1.refs_0_), channel_id=1, source_target_pairs={{8,0},{12,4},{16,8},{20,12},{24,16},{28,20},{0,24},{4,28},{9,1},{1... | collective-permute-start | bytes 294920 | tf_op jit(solution)/shard_map/ppermute | solution.py:32
  10.2 1.0 %copy-done.2 = bf16[3,192,192]{2,1,0:T(8,128)(2,1)S(1)} copy-done((bf16[3,192,192]{2,1,0:T(8,128)(2,1)S(1)}, bf16[3,192,192]{2,1,0:T(8,128)(2,1)}, u32[]{:S(2)}) %copy-start.2) | copy-done | bytes 221208
  11.1 0.7 %copy-done.3 = f32[16,192]{1,0:T(8,128)S(1)} copy-done((f32[16,192]{1,0:T(8,128)S(1)}, f32[16,192]{1,0:T(8,128)}, u32[]{:S(2)}) %copy-start.3) | copy-done | bytes 12312
  11.8 1.3 %response.1.refs_5_ = f32[16,192,256]{2,1,0:T(8,128)S(1)} custom-call(f32[16,192]{1,0:T(8,128)S(1)} %copy-done.3, bf16[3,192,192]{2,1,0:T(8,128)(2,1)S(1)} %copy-done.2), custom_call_target="tpu_custom_call" | custom-call | flops 452984832 | bytes 2359296 | tf_op jit(solution)/shard_map/response/pallas_call | solution.py:306
  13.2 0.0 collective-permute-done.refs_1_
  13.2 0.6 %collective-permute-done.1.refs_2_ = bf16[2,192,128]{2,1,0:T(8,128)(2,1)S(1)} collective-permute-done((bf16[2,192,128]{2,1,0:T(8,128)(2,1)S(1)}, bf16[2,192,128]{2,1,0:T(8,128)(2,1)S(1)}, u32[]{:S(2)}, u32[]{:S(2)}) %collective-permute-start.1) | collective-permute-done | bytes 98336 | tf_op jit(solution)/shard_map/ppermute | solution.py:32
  13.7 0.4 %collective-permute-done.2.refs_3_ = bf16[2,192,128]{2,1,0:T(8,128)(2,1)S(1)} collective-permute-done((bf16[2,192,128]{2,1,0:T(8,128)(2,1)S(1)}, bf16[2,192,128]{2,1,0:T(8,128)(2,1)S(1)}, u32[]{:S(2)}, u32[]{:S(2)}) %collective-permute-start.2) | collective-permute-done | bytes 98336 | tf_op jit(solution)/shard_map/ppermute | solution.py:32
  14.1 0.0 collective-permute-done.3.refs_4_
  14.1 2.3 %image.1 = (bf16[2,192,128]{2,1,0:T(8,128)(2,1)S(1)}, bf16[4,192,128]{2,1,0:T(8,128)(2,1)S(1)}) custom-call(s32[8]{0:T(128)S(1)} %copy-done.4, bf16[2,192,128]{2,1,0:T(8,128)(2,1)S(1)} %pack.1.refs_0_, bf16[2,192,128]{2,1,0:T(8,128)(2,1)S(1)} %collective-permute-done.refs_1_, bf16[2,192,128]{2,1,0:T(8,128)(2,1)S(1)} %collective-permute-done.1.refs_2_, ...), custom_call_target="tpu_custom_call" | custom-call | flops 805306368 | bytes 2359296 | tf_op jit(solution)/shard_map/image/pallas_call | solution.py:315
  16.4 1.6 %collective-permute-start.8 = (bf16[2,192,128]{2,1,0:T(8,128)(2,1)S(1)}, bf16[2,192,128]{2,1,0:T(8,128)(2,1)S(1)}, u32[]{:S(2)}, u32[]{:S(2)}) collective-permute-start(bf16[2,192,128]{2,1,0:T(8,128)(2,1)S(1)} %get-tuple-element.11), channel_id=1, source_target_pairs={{0,2},{1,3},{2,0},{3,1},{4,6},{5,7},{6,4},{7,5},{8,10},{9,11},{10,... | collective-permute-start | bytes 294920 | tf_op jit(solution)/shard_map/ppermute | solution.py:39
  18.0 0.2 overlap.1.refs_0_
  18.2 0.1 collective-permute-start.4
  18.3 0.6 %collective-permute-start.5 = (f32[16,128]{1,0:T(8,128)S(1)}, f32[16,128]{1,0:T(8,128)S(1)}, u32[]{:S(2)}, u32[]{:S(2)}) collective-permute-start(f32[16,128]{1,0:T(8,128)S(1)} %overlap.1.refs_0_), channel_id=1, source_target_pairs={{0,2},{1,3},{2,0},{3,1},{4,6},{5,7},{6,4},{7,5},{8,10},{9,11},{10,... | collective-permute-start | bytes 24584 | tf_op jit(solution)/shard_map/ppermute | solution.py:39
  18.9 1.3 %collective-permute-start.6 = (f32[16,128]{1,0:T(8,128)S(1)}, f32[16,128]{1,0:T(8,128)S(1)}, u32[]{:S(2)}, u32[]{:S(2)}) collective-permute-start(f32[16,128]{1,0:T(8,128)S(1)} %overlap.1.refs_0_), channel_id=1, source_target_pairs={{0,3},{1,2},{2,1},{3,0},{4,7},{5,6},{6,5},{7,4},{8,11},{9,10},{10,... | collective-permute-start | bytes 24584 | tf_op jit(solution)/shard_map/ppermute | solution.py:39
  20.1 0.1 copy.7.owners_ref
  20.2 0.3 %collective-permute-start.7 = (bf16[4,192,128]{2,1,0:T(8,128)(2,1)S(1)}, bf16[4,192,128]{2,1,0:T(8,128)(2,1)S(1)}, u32[]{:S(2)}, u32[]{:S(2)}) collective-permute-start(bf16[4,192,128]{2,1,0:T(8,128)(2,1)S(1)} %get-tuple-element.8.halves_ref.refs_0_), channel_id=1, source_target_pairs={{0,1},{1,0},{2,3},{3,2},{4,5},{5,4},{6,7},{7,6},{8,9},{9,8},{10,11... | collective-permute-start | bytes 589832 | tf_op jit(solution)/shard_map/ppermute | solution.py:39
  20.6 0.6 %collective-permute-done.8.refs_2_ = bf16[2,192,128]{2,1,0:T(8,128)(2,1)S(1)} collective-permute-done((bf16[2,192,128]{2,1,0:T(8,128)(2,1)S(1)}, bf16[2,192,128]{2,1,0:T(8,128)(2,1)S(1)}, u32[]{:S(2)}, u32[]{:S(2)}) %collective-permute-start.8) | collective-permute-done | bytes 98336 | tf_op jit(solution)/shard_map/ppermute | solution.py:39
  21.1 0.0 collective-permute-start.9
  21.1 0.0 collective-permute-done.4.refs_1_
  21.1 0.9 %collective-permute-done.5.refs_2_ = f32[16,128]{1,0:T(8,128)S(1)} collective-permute-done((f32[16,128]{1,0:T(8,128)S(1)}, f32[16,128]{1,0:T(8,128)S(1)}, u32[]{:S(2)}, u32[]{:S(2)}) %collective-permute-start.5) | collective-permute-done | bytes 8224 | tf_op jit(solution)/shard_map/ppermute | solution.py:39
  22.0 0.0 collective-permute-done.6.refs_3_
  22.0 1.2 %factor.1 = (f32[16,16]{1,0:T(8,128)S(1)}, bf16[128,128]{1,0:T(8,128)(2,1)S(1)}) custom-call(s32[16,1]{1,0:T(8,128)S(1)} %copy.7.owners_ref, f32[16,128]{1,0:T(8,128)S(1)} %overlap.1.refs_0_, f32[16,128]{1,0:T(8,128)S(1)} %collective-permute-done.4.refs_1_, f32[16,128]{1,0:T(8,128)S(1)} %collective-permute-done.5.refs_2_, ...), custom_call_target="tpu_custom_call" | custom-call | flops 3000000000 | bytes 1024 | tf_op jit(solution)/shard_map/factor/pallas_call | solution.py:342
  23.3 0.0 collective-permute-done.7.refs_1_
  23.3 0.0 collective-permute-done.9.refs_3_
  23.3 1.2 %route.1 = (bf16[8,64,192]{2,1,0:T(8,128)(2,1)}, f32[16,16]{1,0:T(8,128)}) custom-call(f32[16,16]{1,0:T(8,128)S(1)} %get-tuple-element.9.overlap_ref, bf16[128,128]{1,0:T(8,128)(2,1)S(1)} %get-tuple-element.10.weights_ref, bf16[4,192,128]{2,1,0:T(8,128)(2,1)S(1)} %get-tuple-element.8.halves_ref.refs_0_, ...), custom_call_target="tpu_custom_call" | custom-call | flops 3145728 | bytes 1179648 | tf_op jit(solution)/shard_map/route/pallas_call | solution.py:350
  (7 shorter events, 0.0 us)
Async XLA Ops:
  0.6 0.9 %copy-start = (bf16[16,16,192]{2,1,0:T(8,128)(2,1)S(1)}, bf16[16,16,192]{2,1,0:T(8,128)(2,1)}, u32[]{:S(2)}) copy-start(bf16[16,16,192]{2,1,0:T(8,128)(2,1)} %orbitals_ref.3) | copy-start | bytes 294916
  1.5 12.6 %copy-start.4 = (s32[8]{0:T(128)S(1)}, s32[8]{0:T(128)}, u32[]{:S(2)}) copy-start(s32[8]{0:T(128)} %occupied_ref.1) | copy-start | bytes 100
  1.5 18.6 %copy-start.5 = (s32[16,1]{0,1:T(1,128)S(1)}, s32[16,1]{0,1:T(1,128)}, u32[]{:S(2)}) copy-start(s32[16,1]{0,1:T(1,128)} %param.8) | copy-start | bytes 196
  1.8 16.2 %copy-start.1 = (bf16[16,16,192]{2,1,0:T(8,128)(2,1)S(1)}, bf16[16,16,192]{2,1,0:T(8,128)(2,1)}, u32[]{:S(2)}) copy-start(bf16[16,16,192]{2,1,0:T(8,128)(2,1)} %orbitals_ref.3) | copy-start | bytes 294916
  1.8 11.4 %collective-permute-start = (bf16[2,192,128]{2,1,0:T(8,128)(2,1)S(1)}, bf16[2,192,128]{2,1,0:T(8,128)(2,1)S(1)}, u32[]{:S(2)}, u32[]{:S(2)}) collective-permute-start(bf16[2,192,128]{2,1,0:T(8,128)(2,1)S(1)} %pack.1.refs_0_), channel_id=1, source_target_pairs={{24,0},{28,4},{0,8},{4,12},{8,16},{12,20},{16,24},{20,28},{25,1},{... | collective-permute-start | bytes 294920 | tf_op jit(solution)/shard_map/ppermute | solution.py:32
  4.9 8.8 %collective-permute-start.1 = (bf16[2,192,128]{2,1,0:T(8,128)(2,1)S(1)}, bf16[2,192,128]{2,1,0:T(8,128)(2,1)S(1)}, u32[]{:S(2)}, u32[]{:S(2)}) collective-permute-start(bf16[2,192,128]{2,1,0:T(8,128)(2,1)S(1)} %pack.1.refs_0_), channel_id=1, source_target_pairs={{28,0},{8,4},{4,8},{16,12},{12,16},{24,20},{20,24},{0,28},{29,1},{... | collective-permute-start | bytes 294920 | tf_op jit(solution)/shard_map/ppermute | solution.py:32
  8.1 6.0 %collective-permute-start.2 = (bf16[2,192,128]{2,1,0:T(8,128)(2,1)S(1)}, bf16[2,192,128]{2,1,0:T(8,128)(2,1)S(1)}, u32[]{:S(2)}, u32[]{:S(2)}) collective-permute-start(bf16[2,192,128]{2,1,0:T(8,128)(2,1)S(1)} %pack.1.refs_0_), channel_id=1, source_target_pairs={{4,0},{0,4},{12,8},{8,12},{20,16},{16,20},{28,24},{24,28},{5,1},{1... | collective-permute-start | bytes 294920 | tf_op jit(solution)/shard_map/ppermute | solution.py:32
  8.1 6.0 %collective-permute-start.3 = (bf16[2,192,128]{2,1,0:T(8,128)(2,1)S(1)}, bf16[2,192,128]{2,1,0:T(8,128)(2,1)S(1)}, u32[]{:S(2)}, u32[]{:S(2)}) collective-permute-start(bf16[2,192,128]{2,1,0:T(8,128)(2,1)S(1)} %pack.1.refs_0_), channel_id=1, source_target_pairs={{8,0},{12,4},{16,8},{20,12},{24,16},{28,20},{0,24},{4,28},{9,1},{1... | collective-permute-start | bytes 294920 | tf_op jit(solution)/shard_map/ppermute | solution.py:32
  10.2 1.0 %copy-start.2 = (bf16[3,192,192]{2,1,0:T(8,128)(2,1)S(1)}, bf16[3,192,192]{2,1,0:T(8,128)(2,1)}, u32[]{:S(2)}) copy-start(bf16[3,192,192]{2,1,0:T(8,128)(2,1)} %constant.3.tables_ref) | copy-start | bytes 663556
  11.1 0.7 %copy-start.3 = (f32[16,192]{1,0:T(8,128)S(1)}, f32[16,192]{1,0:T(8,128)}, u32[]{:S(2)}) copy-start(f32[16,192]{1,0:T(8,128)} %coulomb_ref.1) | copy-start | bytes 36868
  16.4 4.7 %collective-permute-start.8 = (bf16[2,192,128]{2,1,0:T(8,128)(2,1)S(1)}, bf16[2,192,128]{2,1,0:T(8,128)(2,1)S(1)}, u32[]{:S(2)}, u32[]{:S(2)}) collective-permute-start(bf16[2,192,128]{2,1,0:T(8,128)(2,1)S(1)} %get-tuple-element.11), channel_id=1, source_target_pairs={{0,2},{1,3},{2,0},{3,1},{4,6},{5,7},{6,4},{7,5},{8,10},{9,11},{10,... | collective-permute-start | bytes 294920 | tf_op jit(solution)/shard_map/ppermute | solution.py:39
  18.2 2.9 %collective-permute-start.4 = (f32[16,128]{1,0:T(8,128)S(1)}, f32[16,128]{1,0:T(8,128)S(1)}, u32[]{:S(2)}, u32[]{:S(2)}) collective-permute-start(f32[16,128]{1,0:T(8,128)S(1)} %overlap.1.refs_0_), channel_id=1, source_target_pairs={{0,1},{1,0},{2,3},{3,2},{4,5},{5,4},{6,7},{7,6},{8,9},{9,8},{10,11... | collective-permute-start | bytes 24584 | tf_op jit(solution)/shard_map/ppermute | solution.py:39
  18.3 3.8 %collective-permute-start.5 = (f32[16,128]{1,0:T(8,128)S(1)}, f32[16,128]{1,0:T(8,128)S(1)}, u32[]{:S(2)}, u32[]{:S(2)}) collective-permute-start(f32[16,128]{1,0:T(8,128)S(1)} %overlap.1.refs_0_), channel_id=1, source_target_pairs={{0,2},{1,3},{2,0},{3,1},{4,6},{5,7},{6,4},{7,5},{8,10},{9,11},{10,... | collective-permute-start | bytes 24584 | tf_op jit(solution)/shard_map/ppermute | solution.py:39
  18.9 3.2 %collective-permute-start.6 = (f32[16,128]{1,0:T(8,128)S(1)}, f32[16,128]{1,0:T(8,128)S(1)}, u32[]{:S(2)}, u32[]{:S(2)}) collective-permute-start(f32[16,128]{1,0:T(8,128)S(1)} %overlap.1.refs_0_), channel_id=1, source_target_pairs={{0,3},{1,2},{2,1},{3,0},{4,7},{5,6},{6,5},{7,4},{8,11},{9,10},{10,... | collective-permute-start | bytes 24584 | tf_op jit(solution)/shard_map/ppermute | solution.py:39
  20.2 3.1 %collective-permute-start.7 = (bf16[4,192,128]{2,1,0:T(8,128)(2,1)S(1)}, bf16[4,192,128]{2,1,0:T(8,128)(2,1)S(1)}, u32[]{:S(2)}, u32[]{:S(2)}) collective-permute-start(bf16[4,192,128]{2,1,0:T(8,128)(2,1)S(1)} %get-tuple-element.8.halves_ref.refs_0_), channel_id=1, source_target_pairs={{0,1},{1,0},{2,3},{3,2},{4,5},{5,4},{6,7},{7,6},{8,9},{9,8},{10,11... | collective-permute-start | bytes 589832 | tf_op jit(solution)/shard_map/ppermute | solution.py:39
  21.1 2.2 %collective-permute-start.9 = (bf16[2,192,128]{2,1,0:T(8,128)(2,1)S(1)}, bf16[2,192,128]{2,1,0:T(8,128)(2,1)S(1)}, u32[]{:S(2)}, u32[]{:S(2)}) collective-permute-start(bf16[2,192,128]{2,1,0:T(8,128)(2,1)S(1)} %collective-permute-done.8.refs_2_), channel_id=1, source_target_pairs={{0,1},{1,0},{2,3},{3,2},{4,5},{5,4},{6,7},{7,6},{8,9},{9,8},{10,11... | collective-permute-start | bytes 294920 | tf_op jit(solution)/shard_map/ppermute | solution.py:39

commit v7 on v6

--- a/solution.py
+++ b/solution.py
@@ -215,30 +215,33 @@
     wide = (members, LANES)
     row = ids(wide, 0)
     upper = 0.5 * (overlap + flipped)
+    columns = [jnp.broadcast_to(upper[:, j : j + 1], wide) for j in range(members)]
     lower = (row == lane_member(ids(wide, 1), members)).astype(F32)
+    diagonal = ratio = jnp.zeros(wide, F32)
     for k in range(0, members, 2):
-        first = jnp.broadcast_to(upper[:, k : k + 1], wide)
-        second = jnp.broadcast_to(upper[:, k + 1 : k + 2], wide)
+        first, second = columns[k], columns[k + 1]
         a, b, c = first[k : k + 1], first[k + 1 : k + 2], second[k + 1 : k + 2]
+        share = b / a
+        rest = c - share * b
+        diagonal = jnp.where(row == k, a, jnp.where(row == k + 1, rest, diagonal))
+        ratio = jnp.where(row == k + 1, share, ratio)
         scale = 1.0 / (a * c - b * b)
         below = row > k + 1
         one = jnp.where(below, (first * c - second * b) * scale, 0.0)
         two = jnp.where(below, (second * a - first * b) * scale, 0.0)
         lower = lower - (one * lower[k : k + 1] + two * lower[k + 1 : k + 2])
-        one, two = one[:, :members], two[:, :members]
-        upper = upper - (one * upper[k : k + 1] + two * upper[k + 1 : k + 2])
-    diagonal = jnp.sum(upper * eye, axis=1, keepdims=True)
-    beside = (ids(square, 0) == ids(square, 1) + 1) & (ids(square, 0) % 2 == 1)
-    share = jnp.sum(jnp.where(beside, upper, 0.0), axis=1, keepdims=True)
-    previous = jnp.concatenate([diagonal[:1], diagonal[:-1]], axis=0)
-    ratio = share / previous
+        for j in range(k + 2, members):
+            column = columns[j]
+            columns[j] = column - (one * column[k : k + 1] + two * column[k + 1 : k + 2])
     above = jnp.concatenate([lower[:1], lower[:-1]], axis=0)
-    inverse = (lower - ratio * above) / jnp.sqrt(diagonal - ratio * share)
+    inverse = (lower - ratio * above) / jnp.sqrt(diagonal)
     high, low = halves(inverse)
     same_line = ids((rows, LANES), 0) % span == lane_line(ids((rows, LANES), 1), turn, members)
-    for place, half in ((0, high), (rows, low)):
-        chosen = jnp.where(same_line, dot32(placed, half), 0.0)
-        weights_ref[place : place + rows, :] = chosen.astype(BF16)
+    blank = jnp.zeros((rows, LANES), BF16)
+    chosen = [jnp.where(same_line, dot32(placed, half), 0.0).astype(BF16) for half in (high, low)]
+    for i, half in enumerate(chosen + chosen):
+        pair = [half, blank] if i < 2 else [blank, half]
+        weights_ref[i * rows : (i + 1) * rows, :] = jnp.concatenate(pair, axis=1)
 
 
 def route_kernel(overlap_ref, weights_ref, *refs):
@@ -248,19 +251,23 @@
     copies[0].start()
     points = staged.shape[3]
     weights = weights_ref[...]
-    rows = weights.shape[0] // 2
+    rows = weights.shape[0] // 4
     span = rows // CAP
     lines = staged.shape[2]
     packs = lines // span
+    highs = jnp.concatenate([weights[:rows], weights[2 * rows : 3 * rows]], axis=0)
     group = lax.axis_index("grid") * lax.axis_size("ham") + lax.axis_index("ham")
     for flip, part in enumerate(parts):
         sums = []
-        for pack in range(packs):
-            both = dot32(weights, part[pack], NT)
-            result = both[:rows] + both[rows:]
+        for pack in range(0, packs, 2):
+            field = jnp.concatenate([part[pack], part[pack + 1]], axis=1)
+            both = dot32(weights, field, NT)
+            results = [both[:rows] + both[rows : 2 * rows], both[2 * rows : 3 * rows] + both[3 * rows :]]
             if part.shape[0] > packs:
-                result = result + dot32(weights[:rows], part[packs + pack], NT)
-            sums.append(result.reshape(CAP, span, points))
+                place = packs + pack
+                rest = dot32(highs, jnp.concatenate([part[place], part[place + 1]], axis=1), NT)
+                results = [results[0] + rest[:rows], results[1] + rest[rows:]]
+            sums += [result.reshape(CAP, span, points) for result in results]
         staged[flip] = jnp.concatenate(sums, axis=1).astype(BF16)
         start = pl.multiple_of((group ^ flip) * lines, lines)
         target = out_hbm.at[:, pl.ds(start, lines), :]
@@ -292,6 +299,7 @@
     padded = -(-points // LANES) * LANES
     span = LANES // members
     packs = lines // span
+    assert packs % 2 == 0
     shape = jax.ShapeDtypeStruct
     (packed,) = call(
         pack_kernel,
@@ -342,7 +350,7 @@
     intersection, weights = call(
         functools.partial(factor_kernel, cells),
         "factor",
-        [shape((members, members), F32), shape((2 * CAP * span, LANES), BF16)],
+        [shape((members, members), F32), shape((4 * CAP * span, 2 * LANES), BF16)],
         FACTOR_COST,
         members**2 * 4,
         operands=1 + groups,

time: 24.7 us -> 23.9 us (0.968)
  Pallas kernels: 6.47 us -> 5.65 us
    pallas_call x1, Pallas kernels: 1.23 us -> 0.53 us  [local(): call(functools.partial(factor_kernel, cells), 'factor', [shape((members,...]
  transfers between devices with their start and end apart: 10 -> 10, of which waited for: 4 -> 4; matrix products, arithmetic and copies ran while one was open for 0% -> 0% of each run, Pallas kernels for 11% -> 9%
where the time goes in v7:
time: 23.9 us; the launch traced here: 23.7 us
  starting transfers between devices  12.2 us (51%)
  Pallas kernels  5.65 us (24%)
  local copies, waits for them, and re-layouts  2.67 us (11%)
  waiting for transfers between devices  2.42 us (10%)
  between operations  0.72 us (3%)
    ppermute x4, starting transfers between devices, exchanged(): lax.ppermute(value, 'band', [(row[turn], block) for block, row in enumera...  8.36 us
    ppermute x6, starting transfers between devices, swapped(): lax.ppermute(value, ('grid', 'ham'), [(group, group ^ flip) for group in...  3.84 us
    unnamed x13, local copies, waits for them, and re-layouts  2.67 us
    pallas_call x1, Pallas kernels, local(): call(functools.partial(image_kernel, members), 'image', [shape((packs, po...  2.3 us
    ppermute x6, waiting for transfers between devices, swapped(): lax.ppermute(value, ('grid', 'ham'), [(group, group ^ flip) for group in...  1.47 us
    pallas_call x1, Pallas kernels, local(): call(response_kernel, 'response', [shape((lines, points, padded), F32)],...  1.31 us
    pallas_call x1, Pallas kernels, local(): call(route_kernel, 'route', [shape((CAP, groups * lines, points), BF16),...  1.08 us
    ppermute x4, waiting for transfers between devices, exchanged(): lax.ppermute(value, 'band', [(row[turn], block) for block, row in enumera...  0.95 us
  transfers between devices with their start and end apart: 10, of which 4 were waited for; matrix products, arithmetic and copies ran while one was open for 0% of the time, Pallas kernels for 9%

profile of v7, /device:TPU:0, one launch (start us, length us, event | category | flops | bytes accessed | tf_op | source)
XLA Modules:
  0.0 23.7 jit_solution(2570789503319716188)
XLA Ops:
  0.6 0.0 copy-start
  0.6 0.9 %copy-done = bf16[16,16,192]{2,1,0:T(8,128)(2,1)S(1)} copy-done((bf16[16,16,192]{2,1,0:T(8,128)(2,1)S(1)}, bf16[16,16,192]{2,1,0:T(8,128)(2,1)}, u32[]{:S(2)}) %copy-start) | copy-done | bytes 98328
  1.5 0.2 pack.1.refs_0_
  1.8 0.0 copy-start.1
  1.8 3.1 %collective-permute-start = (bf16[2,192,128]{2,1,0:T(8,128)(2,1)S(1)}, bf16[2,192,128]{2,1,0:T(8,128)(2,1)S(1)}, u32[]{:S(2)}, u32[]{:S(2)}) collective-permute-start(bf16[2,192,128]{2,1,0:T(8,128)(2,1)S(1)} %pack.1.refs_0_), channel_id=1, source_target_pairs={{24,0},{28,4},{0,8},{4,12},{8,16},{12,20},{16,24},{20,28},{25,1},{... | collective-permute-start | bytes 294920 | tf_op jit(solution)/shard_map/ppermute | solution.py:32
  4.9 3.2 %collective-permute-start.1 = (bf16[2,192,128]{2,1,0:T(8,128)(2,1)S(1)}, bf16[2,192,128]{2,1,0:T(8,128)(2,1)S(1)}, u32[]{:S(2)}, u32[]{:S(2)}) collective-permute-start(bf16[2,192,128]{2,1,0:T(8,128)(2,1)S(1)} %pack.1.refs_0_), channel_id=1, source_target_pairs={{28,0},{8,4},{4,8},{16,12},{12,16},{24,20},{20,24},{0,28},{29,1},{... | collective-permute-start | bytes 294920 | tf_op jit(solution)/shard_map/ppermute | solution.py:32
  8.1 0.0 collective-permute-start.2
  8.1 2.1 %collective-permute-start.3 = (bf16[2,192,128]{2,1,0:T(8,128)(2,1)S(1)}, bf16[2,192,128]{2,1,0:T(8,128)(2,1)S(1)}, u32[]{:S(2)}, u32[]{:S(2)}) collective-permute-start(bf16[2,192,128]{2,1,0:T(8,128)(2,1)S(1)} %pack.1.refs_0_), channel_id=1, source_target_pairs={{8,0},{12,4},{16,8},{20,12},{24,16},{28,20},{0,24},{4,28},{9,1},{1... | collective-permute-start | bytes 294920 | tf_op jit(solution)/shard_map/ppermute | solution.py:32
  10.2 1.0 %copy-done.2 = bf16[3,192,192]{2,1,0:T(8,128)(2,1)S(1)} copy-done((bf16[3,192,192]{2,1,0:T(8,128)(2,1)S(1)}, bf16[3,192,192]{2,1,0:T(8,128)(2,1)}, u32[]{:S(2)}) %copy-start.2) | copy-done | bytes 221208
  11.1 0.7 %copy-done.3 = f32[16,192]{1,0:T(8,128)S(1)} copy-done((f32[16,192]{1,0:T(8,128)S(1)}, f32[16,192]{1,0:T(8,128)}, u32[]{:S(2)}) %copy-start.3) | copy-done | bytes 12312
  11.8 1.3 %response.1.refs_5_ = f32[16,192,256]{2,1,0:T(8,128)S(1)} custom-call(f32[16,192]{1,0:T(8,128)S(1)} %copy-done.3, bf16[3,192,192]{2,1,0:T(8,128)(2,1)S(1)} %copy-done.2), custom_call_target="tpu_custom_call" | custom-call | flops 452984832 | bytes 2359296 | tf_op jit(solution)/shard_map/response/pallas_call | solution.py:314
  13.2 0.0 collective-permute-done.refs_1_
  13.2 0.6 %collective-permute-done.1.refs_2_ = bf16[2,192,128]{2,1,0:T(8,128)(2,1)S(1)} collective-permute-done((bf16[2,192,128]{2,1,0:T(8,128)(2,1)S(1)}, bf16[2,192,128]{2,1,0:T(8,128)(2,1)S(1)}, u32[]{:S(2)}, u32[]{:S(2)}) %collective-permute-start.1) | collective-permute-done | bytes 98336 | tf_op jit(solution)/shard_map/ppermute | solution.py:32
  13.7 0.4 %collective-permute-done.2.refs_3_ = bf16[2,192,128]{2,1,0:T(8,128)(2,1)S(1)} collective-permute-done((bf16[2,192,128]{2,1,0:T(8,128)(2,1)S(1)}, bf16[2,192,128]{2,1,0:T(8,128)(2,1)S(1)}, u32[]{:S(2)}, u32[]{:S(2)}) %collective-permute-start.2) | collective-permute-done | bytes 98336 | tf_op jit(solution)/shard_map/ppermute | solution.py:32
  14.1 0.0 collective-permute-done.3.refs_4_
  14.1 2.3 %image.1 = (bf16[2,192,128]{2,1,0:T(8,128)(2,1)S(1)}, bf16[4,192,128]{2,1,0:T(8,128)(2,1)S(1)}) custom-call(s32[8]{0:T(128)S(1)} %copy-done.4, bf16[2,192,128]{2,1,0:T(8,128)(2,1)S(1)} %pack.1.refs_0_, bf16[2,192,128]{2,1,0:T(8,128)(2,1)S(1)} %collective-permute-done.refs_1_, bf16[2,192,128]{2,1,0:T(8,128)(2,1)S(1)} %collective-permute-done.1.refs_2_, ...), custom_call_target="tpu_custom_call" | custom-call | flops 805306368 | bytes 2359296 | tf_op jit(solution)/shard_map/image/pallas_call | solution.py:323
  16.4 1.6 %collective-permute-start.8 = (bf16[2,192,128]{2,1,0:T(8,128)(2,1)S(1)}, bf16[2,192,128]{2,1,0:T(8,128)(2,1)S(1)}, u32[]{:S(2)}, u32[]{:S(2)}) collective-permute-start(bf16[2,192,128]{2,1,0:T(8,128)(2,1)S(1)} %get-tuple-element.11), channel_id=1, source_target_pairs={{0,2},{1,3},{2,0},{3,1},{4,6},{5,7},{6,4},{7,5},{8,10},{9,11},{10,... | collective-permute-start | bytes 294920 | tf_op jit(solution)/shard_map/ppermute | solution.py:39
  18.0 0.2 overlap.1.refs_0_
  18.2 0.1 collective-permute-start.4
  18.3 0.6 %collective-permute-start.5 = (f32[16,128]{1,0:T(8,128)S(1)}, f32[16,128]{1,0:T(8,128)S(1)}, u32[]{:S(2)}, u32[]{:S(2)}) collective-permute-start(f32[16,128]{1,0:T(8,128)S(1)} %overlap.1.refs_0_), channel_id=1, source_target_pairs={{0,2},{1,3},{2,0},{3,1},{4,6},{5,7},{6,4},{7,5},{8,10},{9,11},{10,... | collective-permute-start | bytes 24584 | tf_op jit(solution)/shard_map/ppermute | solution.py:39
  18.9 1.3 %collective-permute-start.6 = (f32[16,128]{1,0:T(8,128)S(1)}, f32[16,128]{1,0:T(8,128)S(1)}, u32[]{:S(2)}, u32[]{:S(2)}) collective-permute-start(f32[16,128]{1,0:T(8,128)S(1)} %overlap.1.refs_0_), channel_id=1, source_target_pairs={{0,3},{1,2},{2,1},{3,0},{4,7},{5,6},{6,5},{7,4},{8,11},{9,10},{10,... | collective-permute-start | bytes 24584 | tf_op jit(solution)/shard_map/ppermute | solution.py:39
  20.1 0.1 copy.7.owners_ref
  20.2 0.3 %collective-permute-start.7 = (bf16[4,192,128]{2,1,0:T(8,128)(2,1)S(1)}, bf16[4,192,128]{2,1,0:T(8,128)(2,1)S(1)}, u32[]{:S(2)}, u32[]{:S(2)}) collective-permute-start(bf16[4,192,128]{2,1,0:T(8,128)(2,1)S(1)} %get-tuple-element.8.halves_ref.refs_0_), channel_id=1, source_target_pairs={{0,1},{1,0},{2,3},{3,2},{4,5},{5,4},{6,7},{7,6},{8,9},{9,8},{10,11... | collective-permute-start | bytes 589832 | tf_op jit(solution)/shard_map/ppermute | solution.py:39
  20.6 0.6 %collective-permute-done.8.refs_2_ = bf16[2,192,128]{2,1,0:T(8,128)(2,1)S(1)} collective-permute-done((bf16[2,192,128]{2,1,0:T(8,128)(2,1)S(1)}, bf16[2,192,128]{2,1,0:T(8,128)(2,1)S(1)}, u32[]{:S(2)}, u32[]{:S(2)}) %collective-permute-start.8) | collective-permute-done | bytes 98336 | tf_op jit(solution)/shard_map/ppermute | solution.py:39
  21.1 0.0 collective-permute-start.9
  21.1 0.0 collective-permute-done.4.refs_1_
  21.1 0.9 %collective-permute-done.5.refs_2_ = f32[16,128]{1,0:T(8,128)S(1)} collective-permute-done((f32[16,128]{1,0:T(8,128)S(1)}, f32[16,128]{1,0:T(8,128)S(1)}, u32[]{:S(2)}, u32[]{:S(2)}) %collective-permute-start.5) | collective-permute-done | bytes 8224 | tf_op jit(solution)/shard_map/ppermute | solution.py:39
  22.0 0.0 collective-permute-done.6.refs_3_
  22.0 0.5 %factor.1 = (f32[16,16]{1,0:T(8,128)S(1)}, bf16[256,256]{1,0:T(8,128)(2,1)S(1)}) custom-call(s32[16,1]{1,0:T(8,128)S(1)} %copy.7.owners_ref, f32[16,128]{1,0:T(8,128)S(1)} %overlap.1.refs_0_, f32[16,128]{1,0:T(8,128)S(1)} %collective-permute-done.4.refs_1_, f32[16,128]{1,0:T(8,128)S(1)} %collective-permute-done.5.refs_2_, ...), custom_call_target="tpu_custom_call" | custom-call | flops 3000000000 | bytes 1024 | tf_op jit(solution)/shard_map/factor/pallas_call | solution.py:350
  22.6 0.0 collective-permute-done.7.refs_1_
  22.6 0.0 collective-permute-done.9.refs_3_
  22.6 1.1 %route.1 = (bf16[8,64,192]{2,1,0:T(8,128)(2,1)}, f32[16,16]{1,0:T(8,128)}) custom-call(f32[16,16]{1,0:T(8,128)S(1)} %get-tuple-element.9.overlap_ref, bf16[256,256]{1,0:T(8,128)(2,1)S(1)} %get-tuple-element.10.weights_ref, bf16[4,192,128]{2,1,0:T(8,128)(2,1)S(1)} %get-tuple-element.8.halves_ref.refs_0_, ...), custom_call_target="tpu_custom_call" | custom-call | flops 3145728 | bytes 1179648 | tf_op jit(solution)/shard_map/route/pallas_call | solution.py:358
  (7 shorter events, 0.0 us)
Async XLA Ops:
  0.6 0.9 %copy-start = (bf16[16,16,192]{2,1,0:T(8,128)(2,1)S(1)}, bf16[16,16,192]{2,1,0:T(8,128)(2,1)}, u32[]{:S(2)}) copy-start(bf16[16,16,192]{2,1,0:T(8,128)(2,1)} %orbitals_ref.3) | copy-start | bytes 294916
  1.5 12.6 %copy-start.4 = (s32[8]{0:T(128)S(1)}, s32[8]{0:T(128)}, u32[]{:S(2)}) copy-start(s32[8]{0:T(128)} %occupied_ref.1) | copy-start | bytes 100
  1.5 18.6 %copy-start.5 = (s32[16,1]{0,1:T(1,128)S(1)}, s32[16,1]{0,1:T(1,128)}, u32[]{:S(2)}) copy-start(s32[16,1]{0,1:T(1,128)} %param.8) | copy-start | bytes 196
  1.8 16.2 %copy-start.1 = (bf16[16,16,192]{2,1,0:T(8,128)(2,1)S(1)}, bf16[16,16,192]{2,1,0:T(8,128)(2,1)}, u32[]{:S(2)}) copy-start(bf16[16,16,192]{2,1,0:T(8,128)(2,1)} %orbitals_ref.3) | copy-start | bytes 294916
  1.8 11.4 %collective-permute-start = (bf16[2,192,128]{2,1,0:T(8,128)(2,1)S(1)}, bf16[2,192,128]{2,1,0:T(8,128)(2,1)S(1)}, u32[]{:S(2)}, u32[]{:S(2)}) collective-permute-start(bf16[2,192,128]{2,1,0:T(8,128)(2,1)S(1)} %pack.1.refs_0_), channel_id=1, source_target_pairs={{24,0},{28,4},{0,8},{4,12},{8,16},{12,20},{16,24},{20,28},{25,1},{... | collective-permute-start | bytes 294920 | tf_op jit(solution)/shard_map/ppermute | solution.py:32
  4.9 8.8 %collective-permute-start.1 = (bf16[2,192,128]{2,1,0:T(8,128)(2,1)S(1)}, bf16[2,192,128]{2,1,0:T(8,128)(2,1)S(1)}, u32[]{:S(2)}, u32[]{:S(2)}) collective-permute-start(bf16[2,192,128]{2,1,0:T(8,128)(2,1)S(1)} %pack.1.refs_0_), channel_id=1, source_target_pairs={{28,0},{8,4},{4,8},{16,12},{12,16},{24,20},{20,24},{0,28},{29,1},{... | collective-permute-start | bytes 294920 | tf_op jit(solution)/shard_map/ppermute | solution.py:32
  8.1 6.0 %collective-permute-start.2 = (bf16[2,192,128]{2,1,0:T(8,128)(2,1)S(1)}, bf16[2,192,128]{2,1,0:T(8,128)(2,1)S(1)}, u32[]{:S(2)}, u32[]{:S(2)}) collective-permute-start(bf16[2,192,128]{2,1,0:T(8,128)(2,1)S(1)} %pack.1.refs_0_), channel_id=1, source_target_pairs={{4,0},{0,4},{12,8},{8,12},{20,16},{16,20},{28,24},{24,28},{5,1},{1... | collective-permute-start | bytes 294920 | tf_op jit(solution)/shard_map/ppermute | solution.py:32
  8.1 6.0 %collective-permute-start.3 = (bf16[2,192,128]{2,1,0:T(8,128)(2,1)S(1)}, bf16[2,192,128]{2,1,0:T(8,128)(2,1)S(1)}, u32[]{:S(2)}, u32[]{:S(2)}) collective-permute-start(bf16[2,192,128]{2,1,0:T(8,128)(2,1)S(1)} %pack.1.refs_0_), channel_id=1, source_target_pairs={{8,0},{12,4},{16,8},{20,12},{24,16},{28,20},{0,24},{4,28},{9,1},{1... | collective-permute-start | bytes 294920 | tf_op jit(solution)/shard_map/ppermute | solution.py:32
  10.2 1.0 %copy-start.2 = (bf16[3,192,192]{2,1,0:T(8,128)(2,1)S(1)}, bf16[3,192,192]{2,1,0:T(8,128)(2,1)}, u32[]{:S(2)}) copy-start(bf16[3,192,192]{2,1,0:T(8,128)(2,1)} %constant.3.tables_ref) | copy-start | bytes 663556
  11.1 0.7 %copy-start.3 = (f32[16,192]{1,0:T(8,128)S(1)}, f32[16,192]{1,0:T(8,128)}, u32[]{:S(2)}) copy-start(f32[16,192]{1,0:T(8,128)} %coulomb_ref.1) | copy-start | bytes 36868
  16.4 4.7 %collective-permute-start.8 = (bf16[2,192,128]{2,1,0:T(8,128)(2,1)S(1)}, bf16[2,192,128]{2,1,0:T(8,128)(2,1)S(1)}, u32[]{:S(2)}, u32[]{:S(2)}) collective-permute-start(bf16[2,192,128]{2,1,0:T(8,128)(2,1)S(1)} %get-tuple-element.11), channel_id=1, source_target_pairs={{0,2},{1,3},{2,0},{3,1},{4,6},{5,7},{6,4},{7,5},{8,10},{9,11},{10,... | collective-permute-start | bytes 294920 | tf_op jit(solution)/shard_map/ppermute | solution.py:39
  18.2 2.9 %collective-permute-start.4 = (f32[16,128]{1,0:T(8,128)S(1)}, f32[16,128]{1,0:T(8,128)S(1)}, u32[]{:S(2)}, u32[]{:S(2)}) collective-permute-start(f32[16,128]{1,0:T(8,128)S(1)} %overlap.1.refs_0_), channel_id=1, source_target_pairs={{0,1},{1,0},{2,3},{3,2},{4,5},{5,4},{6,7},{7,6},{8,9},{9,8},{10,11... | collective-permute-start | bytes 24584 | tf_op jit(solution)/shard_map/ppermute | solution.py:39
  18.3 3.8 %collective-permute-start.5 = (f32[16,128]{1,0:T(8,128)S(1)}, f32[16,128]{1,0:T(8,128)S(1)}, u32[]{:S(2)}, u32[]{:S(2)}) collective-permute-start(f32[16,128]{1,0:T(8,128)S(1)} %overlap.1.refs_0_), channel_id=1, source_target_pairs={{0,2},{1,3},{2,0},{3,1},{4,6},{5,7},{6,4},{7,5},{8,10},{9,11},{10,... | collective-permute-start | bytes 24584 | tf_op jit(solution)/shard_map/ppermute | solution.py:39
  18.9 3.2 %collective-permute-start.6 = (f32[16,128]{1,0:T(8,128)S(1)}, f32[16,128]{1,0:T(8,128)S(1)}, u32[]{:S(2)}, u32[]{:S(2)}) collective-permute-start(f32[16,128]{1,0:T(8,128)S(1)} %overlap.1.refs_0_), channel_id=1, source_target_pairs={{0,3},{1,2},{2,1},{3,0},{4,7},{5,6},{6,5},{7,4},{8,11},{9,10},{10,... | collective-permute-start | bytes 24584 | tf_op jit(solution)/shard_map/ppermute | solution.py:39
  20.2 2.4 %collective-permute-start.7 = (bf16[4,192,128]{2,1,0:T(8,128)(2,1)S(1)}, bf16[4,192,128]{2,1,0:T(8,128)(2,1)S(1)}, u32[]{:S(2)}, u32[]{:S(2)}) collective-permute-start(bf16[4,192,128]{2,1,0:T(8,128)(2,1)S(1)} %get-tuple-element.8.halves_ref.refs_0_), channel_id=1, source_target_pairs={{0,1},{1,0},{2,3},{3,2},{4,5},{5,4},{6,7},{7,6},{8,9},{9,8},{10,11... | collective-permute-start | bytes 589832 | tf_op jit(solution)/shard_map/ppermute | solution.py:39
  21.1 1.5 %collective-permute-start.9 = (bf16[2,192,128]{2,1,0:T(8,128)(2,1)S(1)}, bf16[2,192,128]{2,1,0:T(8,128)(2,1)S(1)}, u32[]{:S(2)}, u32[]{:S(2)}) collective-permute-start(bf16[2,192,128]{2,1,0:T(8,128)(2,1)S(1)} %collective-permute-done.8.refs_2_), channel_id=1, source_target_pairs={{0,1},{1,0},{2,3},{3,2},{4,5},{5,4},{6,7},{7,6},{8,9},{9,8},{10,11... | collective-permute-start | bytes 294920 | tf_op jit(solution)/shard_map/ppermute | solution.py:39

commit v8 on v7

--- a/solution.py
+++ b/solution.py
@@ -24,14 +24,11 @@
     return [(block + step + count) % count for step in steps]
 
 
-def exchanged(value):
+def arrival(value, turn):
     count = lax.axis_size("band")
     assert count % 4 == 0
-    tables = [sources(block, count) for block in range(count)]
-    return [
-        lax.ppermute(value, "band", [(row[turn], block) for block, row in enumerate(tables)])
-        for turn in range(4)
-    ]
+    pairs = [(sources(block, count)[turn], block) for block in range(count)]
+    return lax.ppermute(value, "band", pairs)
 
 
 def swapped(value, flip):
@@ -90,8 +87,8 @@
     return lane_quarter(lane, turn) * per + lane % (LANES // 4) // members
 
 
-def own_turn():
-    return lax.axis_index("band") % 4
+def own_turn(distance=0):
+    return (lax.axis_index("band") + (4 - distance)) % 4
 
 
 def rows_of(block, pack, span):
@@ -100,12 +97,12 @@
     return part.reshape(members * span, points)
 
 
-def pack_kernel(orbitals_ref, out_ref):
+def pack_kernel(distance, orbitals_ref, out_ref):
     members = orbitals_ref.shape[0]
     span = LANES // members
     block = orbitals_ref[...].astype(F32)
     row, lane = ids((LANES, LANES), 0), ids((LANES, LANES), 1)
-    source = lane_member(lane, members) * span + lane_line(lane, own_turn(), members)
+    source = lane_member(lane, members) * span + lane_line(lane, own_turn(distance), members)
     order = (row == source).astype(BF16)
     for pack in range(out_ref.shape[0]):
         rows = rows_of(block, pack, span).T.astype(BF16)
@@ -301,15 +298,20 @@
     packs = lines // span
     assert packs % 2 == 0
     shape = jax.ShapeDtypeStruct
-    (packed,) = call(
-        pack_kernel,
-        "pack",
-        [shape((packs, points, LANES), BF16)],
-        orbitals.size,
-        4 * orbitals.size,
-        operands=1,
-    )(orbitals)
-    guests = exchanged(packed)
+
+    def pack(block, distance):
+        return call(
+            functools.partial(pack_kernel, distance),
+            "pack",
+            [shape((packs, points, LANES), BF16)],
+            orbitals.size,
+            4 * orbitals.size,
+            operands=1,
+        )(block)[0]
+
+    farthest = arrival(orbitals, 0)
+    packed = pack(orbitals, 0)
+    guests = [pack(farthest, 2)] + [arrival(packed, turn) for turn in range(1, 4)]
     tables = spectral_tables(points)
     (response,) = call(
         response_kernel,

time: 23.9 us -> 24 us (level)
  waiting for transfers between devices: 2.42 us -> 2.15 us
    ppermute x4, waiting for transfers between devices: 0.95 us -> 0.67 us  [arrival(): return lax.ppermute(value, 'band', pairs)]
  transfers between devices with their start and end apart: 10 -> 10, of which waited for: 4 -> 3; matrix products, arithmetic and copies ran while one was open for 0% -> 0% of each run, Pallas kernels for 9% -> 11%
where the time goes in v8:
time: 24 us; the launch traced here: 23.7 us
  starting transfers between devices  12.3 us (51%)
  Pallas kernels  5.89 us (25%)
  local copies, waits for them, and re-layouts  2.71 us (11%)
  waiting for transfers between devices  2.15 us (9%)
  between operations  0.73 us (3%)
    ppermute x4, starting transfers between devices, arrival(): return lax.ppermute(value, 'band', pairs)  8.43 us
    ppermute x6, starting transfers between devices, swapped(): lax.ppermute(value, ('grid', 'ham'), [(group, group ^ flip) for group in...  3.84 us
    unnamed x13, local copies, waits for them, and re-layouts  2.71 us
    pallas_call x1, Pallas kernels, local(): call(functools.partial(image_kernel, members), 'image', [shape((packs, po...  2.31 us
    ppermute x6, waiting for transfers between devices, swapped(): lax.ppermute(value, ('grid', 'ham'), [(group, group ^ flip) for group in...  1.47 us
    pallas_call x1, Pallas kernels, local(): call(response_kernel, 'response', [shape((lines, points, padded), F32)],...  1.31 us
    pallas_call x1, Pallas kernels, local(): call(route_kernel, 'route', [shape((CAP, groups * lines, points), BF16),...  1.09 us
    ppermute x4, waiting for transfers between devices, arrival(): return lax.ppermute(value, 'band', pairs)  0.67 us
  transfers between devices with their start and end apart: 10, of which 3 were waited for; matrix products, arithmetic and copies ran while one was open for 0% of the time, Pallas kernels for 11%

profile of v8, /device:TPU:0, one launch (start us, length us, event | category | flops | bytes accessed | tf_op | source)
XLA Modules:
  0.0 23.7 jit_solution(12057716154377689931)
XLA Ops:
  0.6 3.1 %collective-permute-start = (bf16[16,16,192]{2,1,0:T(8,128)(2,1)}, bf16[16,16,192]{2,1,0:T(8,128)(2,1)S(1)}, u32[]{:S(2)}, u32[]{:S(2)}) collective-permute-start(bf16[16,16,192]{2,1,0:T(8,128)(2,1)} %orbitals_ref.3), channel_id=1, source_target_pairs={{24,0},{28,4},{0,8},{4,12},{8,16},{12,20},{16,24},{20,28},{25,1},{... | collective-permute-start | bytes 294920 | tf_op jit(solution)/shard_map/ppermute | solution.py:31
  3.7 0.9 %copy-done = bf16[16,16,192]{2,1,0:T(8,128)(2,1)S(1)} copy-done((bf16[16,16,192]{2,1,0:T(8,128)(2,1)S(1)}, bf16[16,16,192]{2,1,0:T(8,128)(2,1)}, u32[]{:S(2)}) %copy-start) | copy-done | bytes 98328
  4.6 0.2 pack.2.refs_0_
  4.9 0.0 copy-start.1
  4.9 3.3 %collective-permute-start.1 = (bf16[2,192,128]{2,1,0:T(8,128)(2,1)S(1)}, bf16[2,192,128]{2,1,0:T(8,128)(2,1)S(1)}, u32[]{:S(2)}, u32[]{:S(2)}) collective-permute-start(bf16[2,192,128]{2,1,0:T(8,128)(2,1)S(1)} %pack.2.refs_0_), channel_id=1, source_target_pairs={{28,0},{8,4},{4,8},{16,12},{12,16},{24,20},{20,24},{0,28},{29,1},{... | collective-permute-start | bytes 294920 | tf_op jit(solution)/shard_map/ppermute | solution.py:31
  8.2 0.0 collective-permute-start.2
  8.2 2.1 %collective-permute-start.3 = (bf16[2,192,128]{2,1,0:T(8,128)(2,1)S(1)}, bf16[2,192,128]{2,1,0:T(8,128)(2,1)S(1)}, u32[]{:S(2)}, u32[]{:S(2)}) collective-permute-start(bf16[2,192,128]{2,1,0:T(8,128)(2,1)S(1)} %pack.2.refs_0_), channel_id=1, source_target_pairs={{8,0},{12,4},{16,8},{20,12},{24,16},{28,20},{0,24},{4,28},{9,1},{1... | collective-permute-start | bytes 294920 | tf_op jit(solution)/shard_map/ppermute | solution.py:31
  10.3 1.0 %copy-done.2 = bf16[3,192,192]{2,1,0:T(8,128)(2,1)S(1)} copy-done((bf16[3,192,192]{2,1,0:T(8,128)(2,1)S(1)}, bf16[3,192,192]{2,1,0:T(8,128)(2,1)}, u32[]{:S(2)}) %copy-start.2) | copy-done | bytes 221208
  11.2 0.7 %copy-done.3 = f32[16,192]{1,0:T(8,128)S(1)} copy-done((f32[16,192]{1,0:T(8,128)S(1)}, f32[16,192]{1,0:T(8,128)}, u32[]{:S(2)}) %copy-start.3) | copy-done | bytes 12312
  11.9 1.3 %response.1.refs_5_ = f32[16,192,256]{2,1,0:T(8,128)S(1)} custom-call(f32[16,192]{1,0:T(8,128)S(1)} %copy-done.3, bf16[3,192,192]{2,1,0:T(8,128)(2,1)S(1)} %copy-done.2), custom_call_target="tpu_custom_call" | custom-call | flops 452984832 | bytes 2359296 | tf_op jit(solution)/shard_map/response/pallas_call | solution.py:316
  13.3 0.0 collective-permute-done.orbitals_ref
  13.3 0.2 pack.3.refs_1_
  13.5 0.0 collective-permute-done.1.refs_2_
  13.5 0.7 %collective-permute-done.2.refs_3_ = bf16[2,192,128]{2,1,0:T(8,128)(2,1)S(1)} collective-permute-done((bf16[2,192,128]{2,1,0:T(8,128)(2,1)S(1)}, bf16[2,192,128]{2,1,0:T(8,128)(2,1)S(1)}, u32[]{:S(2)}, u32[]{:S(2)}) %collective-permute-start.2) | collective-permute-done | bytes 98336 | tf_op jit(solution)/shard_map/ppermute | solution.py:31
  14.2 0.0 collective-permute-done.3.refs_4_
  14.2 2.3 %image.1 = (bf16[2,192,128]{2,1,0:T(8,128)(2,1)S(1)}, bf16[4,192,128]{2,1,0:T(8,128)(2,1)S(1)}) custom-call(s32[8]{0:T(128)S(1)} %copy-done.4, bf16[2,192,128]{2,1,0:T(8,128)(2,1)S(1)} %pack.2.refs_0_, bf16[2,192,128]{2,1,0:T(8,128)(2,1)S(1)} %pack.3.refs_1_, bf16[2,192,128]{2,1,0:T(8,128)(2,1)S(1)} %collective-permute-done.1.refs_2_, ...), custom_call_target="tpu_custom_call" | custom-call | flops 805306368 | bytes 2359296 | tf_op jit(solution)/shard_map/image/pallas_call | solution.py:325
  16.5 1.6 %collective-permute-start.8 = (bf16[2,192,128]{2,1,0:T(8,128)(2,1)S(1)}, bf16[2,192,128]{2,1,0:T(8,128)(2,1)S(1)}, u32[]{:S(2)}, u32[]{:S(2)}) collective-permute-start(bf16[2,192,128]{2,1,0:T(8,128)(2,1)S(1)} %get-tuple-element.11), channel_id=1, source_target_pairs={{0,2},{1,3},{2,0},{3,1},{4,6},{5,7},{6,4},{7,5},{8,10},{9,11},{10,... | collective-permute-start | bytes 294920 | tf_op jit(solution)/shard_map/ppermute | solution.py:36
  18.1 0.2 overlap.1.refs_0_
  18.2 0.1 collective-permute-start.4
  18.3 0.6 %collective-permute-start.5 = (f32[16,128]{1,0:T(8,128)S(1)}, f32[16,128]{1,0:T(8,128)S(1)}, u32[]{:S(2)}, u32[]{:S(2)}) collective-permute-start(f32[16,128]{1,0:T(8,128)S(1)} %overlap.1.refs_0_), channel_id=1, source_target_pairs={{0,2},{1,3},{2,0},{3,1},{4,6},{5,7},{6,4},{7,5},{8,10},{9,11},{10,... | collective-permute-start | bytes 24584 | tf_op jit(solution)/shard_map/ppermute | solution.py:36
  18.9 1.3 %collective-permute-start.6 = (f32[16,128]{1,0:T(8,128)S(1)}, f32[16,128]{1,0:T(8,128)S(1)}, u32[]{:S(2)}, u32[]{:S(2)}) collective-permute-start(f32[16,128]{1,0:T(8,128)S(1)} %overlap.1.refs_0_), channel_id=1, source_target_pairs={{0,3},{1,2},{2,1},{3,0},{4,7},{5,6},{6,5},{7,4},{8,11},{9,10},{10,... | collective-permute-start | bytes 24584 | tf_op jit(solution)/shard_map/ppermute | solution.py:36
  20.2 0.1 copy.7.owners_ref
  20.3 0.3 %collective-permute-start.7 = (bf16[4,192,128]{2,1,0:T(8,128)(2,1)S(1)}, bf16[4,192,128]{2,1,0:T(8,128)(2,1)S(1)}, u32[]{:S(2)}, u32[]{:S(2)}) collective-permute-start(bf16[4,192,128]{2,1,0:T(8,128)(2,1)S(1)} %get-tuple-element.8.halves_ref.refs_0_), channel_id=1, source_target_pairs={{0,1},{1,0},{2,3},{3,2},{4,5},{5,4},{6,7},{7,6},{8,9},{9,8},{10,11... | collective-permute-start | bytes 589832 | tf_op jit(solution)/shard_map/ppermute | solution.py:36
  20.6 0.6 %collective-permute-done.8.refs_2_ = bf16[2,192,128]{2,1,0:T(8,128)(2,1)S(1)} collective-permute-done((bf16[2,192,128]{2,1,0:T(8,128)(2,1)S(1)}, bf16[2,192,128]{2,1,0:T(8,128)(2,1)S(1)}, u32[]{:S(2)}, u32[]{:S(2)}) %collective-permute-start.8) | collective-permute-done | bytes 98336 | tf_op jit(solution)/shard_map/ppermute | solution.py:36
  21.2 0.0 collective-permute-start.9
  21.2 0.0 collective-permute-done.4.refs_1_
  21.2 0.9 %collective-permute-done.5.refs_2_ = f32[16,128]{1,0:T(8,128)S(1)} collective-permute-done((f32[16,128]{1,0:T(8,128)S(1)}, f32[16,128]{1,0:T(8,128)S(1)}, u32[]{:S(2)}, u32[]{:S(2)}) %collective-permute-start.5) | collective-permute-done | bytes 8224 | tf_op jit(solution)/shard_map/ppermute | solution.py:36
  22.1 0.0 collective-permute-done.6.refs_3_
  22.1 0.5 %factor.1 = (f32[16,16]{1,0:T(8,128)S(1)}, bf16[256,256]{1,0:T(8,128)(2,1)S(1)}) custom-call(s32[16,1]{1,0:T(8,128)S(1)} %copy.7.owners_ref, f32[16,128]{1,0:T(8,128)S(1)} %overlap.1.refs_0_, f32[16,128]{1,0:T(8,128)S(1)} %collective-permute-done.4.refs_1_, f32[16,128]{1,0:T(8,128)S(1)} %collective-permute-done.5.refs_2_, ...), custom_call_target="tpu_custom_call" | custom-call | flops 3000000000 | bytes 1024 | tf_op jit(solution)/shard_map/factor/pallas_call | solution.py:352
  22.6 0.0 collective-permute-done.7.refs_1_
  22.6 0.0 collective-permute-done.9.refs_3_
  22.7 1.1 %route.1 = (bf16[8,64,192]{2,1,0:T(8,128)(2,1)}, f32[16,16]{1,0:T(8,128)}) custom-call(f32[16,16]{1,0:T(8,128)S(1)} %get-tuple-element.9.overlap_ref, bf16[256,256]{1,0:T(8,128)(2,1)S(1)} %get-tuple-element.10.weights_ref, bf16[4,192,128]{2,1,0:T(8,128)(2,1)S(1)} %get-tuple-element.8.halves_ref.refs_0_, ...), custom_call_target="tpu_custom_call" | custom-call | flops 3145728 | bytes 1179648 | tf_op jit(solution)/shard_map/route/pallas_call | solution.py:360
  (8 shorter events, 0.0 us)
Async XLA Ops:
  0.6 12.6 %collective-permute-start = (bf16[16,16,192]{2,1,0:T(8,128)(2,1)}, bf16[16,16,192]{2,1,0:T(8,128)(2,1)S(1)}, u32[]{:S(2)}, u32[]{:S(2)}) collective-permute-start(bf16[16,16,192]{2,1,0:T(8,128)(2,1)} %orbitals_ref.3), channel_id=1, source_target_pairs={{24,0},{28,4},{0,8},{4,12},{8,16},{12,20},{16,24},{20,28},{25,1},{... | collective-permute-start | bytes 294920 | tf_op jit(solution)/shard_map/ppermute | solution.py:31
  3.7 0.9 %copy-start = (bf16[16,16,192]{2,1,0:T(8,128)(2,1)S(1)}, bf16[16,16,192]{2,1,0:T(8,128)(2,1)}, u32[]{:S(2)}) copy-start(bf16[16,16,192]{2,1,0:T(8,128)(2,1)} %orbitals_ref.3) | copy-start | bytes 294916
  4.6 9.5 %copy-start.4 = (s32[8]{0:T(128)S(1)}, s32[8]{0:T(128)}, u32[]{:S(2)}) copy-start(s32[8]{0:T(128)} %occupied_ref.1) | copy-start | bytes 100
  4.6 15.5 %copy-start.5 = (s32[16,1]{0,1:T(1,128)S(1)}, s32[16,1]{0,1:T(1,128)}, u32[]{:S(2)}) copy-start(s32[16,1]{0,1:T(1,128)} %param.8) | copy-start | bytes 196
  4.9 13.2 %copy-start.1 = (bf16[16,16,192]{2,1,0:T(8,128)(2,1)S(1)}, bf16[16,16,192]{2,1,0:T(8,128)(2,1)}, u32[]{:S(2)}) copy-start(bf16[16,16,192]{2,1,0:T(8,128)(2,1)} %orbitals_ref.3) | copy-start | bytes 294916
  4.9 8.6 %collective-permute-start.1 = (bf16[2,192,128]{2,1,0:T(8,128)(2,1)S(1)}, bf16[2,192,128]{2,1,0:T(8,128)(2,1)S(1)}, u32[]{:S(2)}, u32[]{:S(2)}) collective-permute-start(bf16[2,192,128]{2,1,0:T(8,128)(2,1)S(1)} %pack.2.refs_0_), channel_id=1, source_target_pairs={{28,0},{8,4},{4,8},{16,12},{12,16},{24,20},{20,24},{0,28},{29,1},{... | collective-permute-start | bytes 294920 | tf_op jit(solution)/shard_map/ppermute | solution.py:31
  8.2 6.0 %collective-permute-start.2 = (bf16[2,192,128]{2,1,0:T(8,128)(2,1)S(1)}, bf16[2,192,128]{2,1,0:T(8,128)(2,1)S(1)}, u32[]{:S(2)}, u32[]{:S(2)}) collective-permute-start(bf16[2,192,128]{2,1,0:T(8,128)(2,1)S(1)} %pack.2.refs_0_), channel_id=1, source_target_pairs={{4,0},{0,4},{12,8},{8,12},{20,16},{16,20},{28,24},{24,28},{5,1},{1... | collective-permute-start | bytes 294920 | tf_op jit(solution)/shard_map/ppermute | solution.py:31
  8.2 6.0 %collective-permute-start.3 = (bf16[2,192,128]{2,1,0:T(8,128)(2,1)S(1)}, bf16[2,192,128]{2,1,0:T(8,128)(2,1)S(1)}, u32[]{:S(2)}, u32[]{:S(2)}) collective-permute-start(bf16[2,192,128]{2,1,0:T(8,128)(2,1)S(1)} %pack.2.refs_0_), channel_id=1, source_target_pairs={{8,0},{12,4},{16,8},{20,12},{24,16},{28,20},{0,24},{4,28},{9,1},{1... | collective-permute-start | bytes 294920 | tf_op jit(solution)/shard_map/ppermute | solution.py:31
  10.3 1.0 %copy-start.2 = (bf16[3,192,192]{2,1,0:T(8,128)(2,1)S(1)}, bf16[3,192,192]{2,1,0:T(8,128)(2,1)}, u32[]{:S(2)}) copy-start(bf16[3,192,192]{2,1,0:T(8,128)(2,1)} %constant.3.tables_ref) | copy-start | bytes 663556
  11.2 0.7 %copy-start.3 = (f32[16,192]{1,0:T(8,128)S(1)}, f32[16,192]{1,0:T(8,128)}, u32[]{:S(2)}) copy-start(f32[16,192]{1,0:T(8,128)} %coulomb_ref.1) | copy-start | bytes 36868
  16.5 4.7 %collective-permute-start.8 = (bf16[2,192,128]{2,1,0:T(8,128)(2,1)S(1)}, bf16[2,192,128]{2,1,0:T(8,128)(2,1)S(1)}, u32[]{:S(2)}, u32[]{:S(2)}) collective-permute-start(bf16[2,192,128]{2,1,0:T(8,128)(2,1)S(1)} %get-tuple-element.11), channel_id=1, source_target_pairs={{0,2},{1,3},{2,0},{3,1},{4,6},{5,7},{6,4},{7,5},{8,10},{9,11},{10,... | collective-permute-start | bytes 294920 | tf_op jit(solution)/shard_map/ppermute | solution.py:36
  18.2 2.9 %collective-permute-start.4 = (f32[16,128]{1,0:T(8,128)S(1)}, f32[16,128]{1,0:T(8,128)S(1)}, u32[]{:S(2)}, u32[]{:S(2)}) collective-permute-start(f32[16,128]{1,0:T(8,128)S(1)} %overlap.1.refs_0_), channel_id=1, source_target_pairs={{0,1},{1,0},{2,3},{3,2},{4,5},{5,4},{6,7},{7,6},{8,9},{9,8},{10,11... | collective-permute-start | bytes 24584 | tf_op jit(solution)/shard_map/ppermute | solution.py:36
  18.3 3.8 %collective-permute-start.5 = (f32[16,128]{1,0:T(8,128)S(1)}, f32[16,128]{1,0:T(8,128)S(1)}, u32[]{:S(2)}, u32[]{:S(2)}) collective-permute-start(f32[16,128]{1,0:T(8,128)S(1)} %overlap.1.refs_0_), channel_id=1, source_target_pairs={{0,2},{1,3},{2,0},{3,1},{4,6},{5,7},{6,4},{7,5},{8,10},{9,11},{10,... | collective-permute-start | bytes 24584 | tf_op jit(solution)/shard_map/ppermute | solution.py:36
  18.9 3.2 %collective-permute-start.6 = (f32[16,128]{1,0:T(8,128)S(1)}, f32[16,128]{1,0:T(8,128)S(1)}, u32[]{:S(2)}, u32[]{:S(2)}) collective-permute-start(f32[16,128]{1,0:T(8,128)S(1)} %overlap.1.refs_0_), channel_id=1, source_target_pairs={{0,3},{1,2},{2,1},{3,0},{4,7},{5,6},{6,5},{7,4},{8,11},{9,10},{10,... | collective-permute-start | bytes 24584 | tf_op jit(solution)/shard_map/ppermute | solution.py:36
  20.3 2.4 %collective-permute-start.7 = (bf16[4,192,128]{2,1,0:T(8,128)(2,1)S(1)}, bf16[4,192,128]{2,1,0:T(8,128)(2,1)S(1)}, u32[]{:S(2)}, u32[]{:S(2)}) collective-permute-start(bf16[4,192,128]{2,1,0:T(8,128)(2,1)S(1)} %get-tuple-element.8.halves_ref.refs_0_), channel_id=1, source_target_pairs={{0,1},{1,0},{2,3},{3,2},{4,5},{5,4},{6,7},{7,6},{8,9},{9,8},{10,11... | collective-permute-start | bytes 589832 | tf_op jit(solution)/shard_map/ppermute | solution.py:36
  21.2 1.5 %collective-permute-start.9 = (bf16[2,192,128]{2,1,0:T(8,128)(2,1)S(1)}, bf16[2,192,128]{2,1,0:T(8,128)(2,1)S(1)}, u32[]{:S(2)}, u32[]{:S(2)}) collective-permute-start(bf16[2,192,128]{2,1,0:T(8,128)(2,1)S(1)} %collective-permute-done.8.refs_2_), channel_id=1, source_target_pairs={{0,1},{1,0},{2,3},{3,2},{4,5},{5,4},{6,7},{7,6},{8,9},{9,8},{10,11... | collective-permute-start | bytes 294920 | tf_op jit(solution)/shard_map/ppermute | solution.py:36

commit v9 on v7

--- a/solution.py
+++ b/solution.py
@@ -50,7 +50,11 @@
     mirror = np.zeros((points, points))
     mirror[frequency, ids] += 0.5
     mirror[(points - frequency) % points, ids] += 0.5
-    return jnp.asarray(np.stack([forward.T, inverse.T, mirror]).astype(np.float32)).astype(BF16)
+    rounded = [np.asarray(t, np.float32).astype(jnp.bfloat16) for t in (forward.T, inverse.T, mirror)]
+    product = rounded[0].T.astype(np.float32) * rounded[1].astype(np.float32)
+    high = product.astype(jnp.bfloat16)
+    low = (product - high.astype(np.float32)).astype(jnp.bfloat16)
+    return jnp.asarray(np.stack([*rounded, high, low]))
 
 
 def split(value):
@@ -112,20 +116,32 @@
         out_ref[pack] = dot32(rows, order).astype(BF16)
 
 
-def response_kernel(coulomb_ref, tables_ref, out_ref):
+def response_kernel(members, coulomb_ref, tables_ref, out_ref, diagonal_ref):
     points = coulomb_ref.shape[1]
+    lines = coulomb_ref.shape[0]
+    span = LANES // members
     multiplier = dot_exact(coulomb_ref[...], tables_ref[2].astype(F32))
     forward = tables_ref[0]
     inverse = tables_ref[1].astype(F32)
     pad = jnp.zeros((points, out_ref.shape[2] - points), F32)
-    for line in range(coulomb_ref.shape[0]):
+    apart = ids((points, points), 0) != ids((points, points), 1)
+    for line in range(lines):
         high, low = halves(inverse * multiplier[line : line + 1, :])
-        out_ref[line, :, :points] = dot32(high, forward) + dot32(low, forward)
+        whole = dot32(high, forward) + dot32(low, forward)
+        out_ref[line, :, :points] = jnp.where(apart, whole, 0.0)
         out_ref[line, :, points:] = pad
+    parts = halves(multiplier)
+    for pack in range(diagonal_ref.shape[0]):
+        line = ids((LANES, lines), 1) - pack * span
+        repeat = (lane_line(ids((LANES, lines), 0), own_turn(), members) == line).astype(BF16)
+        high, low = [dot32(repeat, part).astype(BF16) for part in parts]
+        diagonal_ref[pack] = dot32(tables_ref[3], high, NT) + (
+            dot32(tables_ref[3], low, NT) + dot32(tables_ref[4], high, NT)
+        )
 
 
 def image_kernel(members, occupied_ref, *refs):
-    blocks, (response_ref, high_ref, halves_ref) = refs[:-3], refs[-3:]
+    blocks, (response_ref, diagonal_ref, high_ref, halves_ref) = refs[:-4], refs[-4:]
     packs, points, _ = blocks[0].shape
     padded = response_ref.shape[2]
     span = LANES // members
@@ -139,12 +155,18 @@
     filled = [lane_member(lane, members) < occupied_ref[place] for place in places]
     quarters = [lane_quarter(lane, turn) for turn in turns]
     step = lane % (LANES // 4) // members
+    steps = jnp.concatenate([step, step], axis=1)
+    pair = (2 * LANES, LANES)
+    same_step = (
+        ids(pair, 0) % (LANES // 4) // members == ids(pair, 1) % (LANES // 4) // members
+    ).astype(BF16)
     apart, merged = 1, (0, 2, 3, 4)
     blank = jnp.zeros((padded - points, 2 * LANES), BF16)
     for pack in range(packs):
         tiles = [block[pack] for block in blocks]
         native = jnp.concatenate([tiles[0], blank[:, :LANES]], axis=0)
         image = jnp.zeros((points, LANES), F32)
+        squares = jnp.zeros((points, LANES), F32)
         for quarter in range(4):
             here = [(q == quarter) for q in quarters]
             together = sum(tiles[m] * here[m].astype(F32).astype(BF16) for m in merged)
@@ -152,19 +174,20 @@
             occupied = sum((here[m] & filled[m]).astype(F32) for m in merged)
             beside = (here[apart] & filled[apart]).astype(F32)
             both = jnp.concatenate([occupied, beside], axis=1)
-            steps = jnp.concatenate([step, step], axis=1)
+            used = window * both.astype(BF16)
+            square = dot32(used * window, same_step)
+            squares = jnp.where(own_line // per == quarter, square, squares)
             masked = jnp.concatenate(
-                [window * jnp.where(steps == k, both, 0.0).astype(BF16) for k in range(per)], axis=0
+                [used * (steps == k).astype(F32).astype(BF16) for k in range(per)], axis=0
             )
             gram = dot32(masked, jnp.concatenate([window, blank], axis=0), NT)
             first = pack * span + quarter * per
             response = response_ref[first : first + per].reshape(per * points, padded)
-            high, low = halves(gram * response)
-            fields = dot32(jnp.concatenate([high, low], axis=0), native)
+            fields = dot32((gram * response).astype(BF16), native)
             for k in range(per):
-                a, b = k * points, (per + k) * points
-                field = fields[a : a + points] + fields[b : b + points]
+                field = fields[k * points : (k + 1) * points]
                 image = jnp.where(own_line == quarter * per + k, field, image)
+        image = image + tiles[0].astype(F32) * (diagonal_ref[pack] * squares)
         high, low = halves(image)
         high_ref[pack] = high
         halves_ref[pack] = high
@@ -311,10 +334,10 @@
     )(orbitals)
     guests = exchanged(packed)
     tables = spectral_tables(points)
-    (response,) = call(
-        response_kernel,
+    response, diagonal = call(
+        functools.partial(response_kernel, members),
         "response",
-        [shape((lines, points, padded), F32)],
+        [shape((lines, points, padded), F32), shape((packs, points, LANES), F32)],
         4 * lines * points**3,
         4 * lines * points**2,
         operands=2,
@@ -327,11 +350,11 @@
             shape((packs, points, LANES), BF16),
             shape((2 * packs, points, LANES), BF16),
         ],
-        2 * lines * points * padded * (4 * LANES),
+        2 * lines * points * padded * (3 * LANES),
         4 * lines * points**2,
         scalars=1,
-        operands=blocks + 1,
-    )(occupied, packed, *guests, response)
+        operands=blocks + 2,
+    )(occupied, packed, *guests, response, diagonal)
     (overlap,) = call(
         overlap_kernel,
         "overlap",

time: 23.9 us -> 24.8 us (1.038)
  local copies, waits for them, and re-layouts: 2.67 us -> 3.39 us
  Pallas kernels: 5.65 us -> 6.15 us
  waiting for transfers between devices: 2.42 us -> 2.11 us
    unnamed x13, local copies, waits for them, and re-layouts: 2.67 us -> 3.39 us
    ppermute x4, waiting for transfers between devices: 0.95 us -> 0.64 us  [exchanged(): lax.ppermute(value, 'band', [(row[turn], block) for block, row in enumera...]
    pallas_call x1, Pallas kernels: 2.3 us -> 2.57 us  [local(): call(functools.partial(image_kernel, members), 'image', [shape((packs, po...]
where the time goes in v9:
time: 24.8 us; the launch traced here: 24.6 us
  starting transfers between devices  12.2 us (49%)
  Pallas kernels  6.15 us (25%)
  local copies, waits for them, and re-layouts  3.39 us (14%)
  waiting for transfers between devices  2.11 us (9%)
  between operations  0.72 us (3%)
    ppermute x4, starting transfers between devices, exchanged(): lax.ppermute(value, 'band', [(row[turn], block) for block, row in enumera...  8.36 us
    ppermute x6, starting transfers between devices, swapped(): lax.ppermute(value, ('grid', 'ham'), [(group, group ^ flip) for group in...  3.83 us
    unnamed x13, local copies, waits for them, and re-layouts  3.39 us
    pallas_call x1, Pallas kernels, local(): call(functools.partial(image_kernel, members), 'image', [shape((packs, po...  2.57 us
    pallas_call x1, Pallas kernels, local(): call(functools.partial(response_kernel, members), 'response', [shape((lin...  1.55 us
    ppermute x6, waiting for transfers between devices, swapped(): lax.ppermute(value, ('grid', 'ham'), [(group, group ^ flip) for group in...  1.47 us
    pallas_call x1, Pallas kernels, local(): call(route_kernel, 'route', [shape((CAP, groups * lines, points), BF16),...  1.08 us
    ppermute x4, waiting for transfers between devices, exchanged(): lax.ppermute(value, 'band', [(row[turn], block) for block, row in enumera...  0.64 us
  transfers between devices with their start and end apart: 10, of which 4 were waited for; matrix products, arithmetic and copies ran while one was open for 0% of the time, Pallas kernels for 9%

profile of v9, /device:TPU:0, one launch (start us, length us, event | category | flops | bytes accessed | tf_op | source)
XLA Modules:
  0.0 24.6 jit_solution(9805490630873627073)
XLA Ops:
  0.6 0.9 %copy-done = bf16[16,16,192]{2,1,0:T(8,128)(2,1)S(1)} copy-done((bf16[16,16,192]{2,1,0:T(8,128)(2,1)S(1)}, bf16[16,16,192]{2,1,0:T(8,128)(2,1)}, u32[]{:S(2)}) %copy-start) | copy-done | bytes 98328
  1.5 0.2 pack.1.refs_0_
  1.8 3.1 %collective-permute-start = (bf16[2,192,128]{2,1,0:T(8,128)(2,1)S(1)}, bf16[2,192,128]{2,1,0:T(8,128)(2,1)S(1)}, u32[]{:S(2)}, u32[]{:S(2)}) collective-permute-start(bf16[2,192,128]{2,1,0:T(8,128)(2,1)S(1)} %pack.1.refs_0_), channel_id=1, source_target_pairs={{24,0},{28,4},{0,8},{4,12},{8,16},{12,20},{16,24},{20,28},{25,1},{... | collective-permute-start | bytes 294920 | tf_op jit(solution)/shard_map/ppermute | solution.py:32
  4.9 3.2 %collective-permute-start.1 = (bf16[2,192,128]{2,1,0:T(8,128)(2,1)S(1)}, bf16[2,192,128]{2,1,0:T(8,128)(2,1)S(1)}, u32[]{:S(2)}, u32[]{:S(2)}) collective-permute-start(bf16[2,192,128]{2,1,0:T(8,128)(2,1)S(1)} %pack.1.refs_0_), channel_id=1, source_target_pairs={{28,0},{8,4},{4,8},{16,12},{12,16},{24,20},{20,24},{0,28},{29,1},{... | collective-permute-start | bytes 294920 | tf_op jit(solution)/shard_map/ppermute | solution.py:32
  8.1 0.0 collective-permute-start.2
  8.1 2.1 %collective-permute-start.3 = (bf16[2,192,128]{2,1,0:T(8,128)(2,1)S(1)}, bf16[2,192,128]{2,1,0:T(8,128)(2,1)S(1)}, u32[]{:S(2)}, u32[]{:S(2)}) collective-permute-start(bf16[2,192,128]{2,1,0:T(8,128)(2,1)S(1)} %pack.1.refs_0_), channel_id=1, source_target_pairs={{8,0},{12,4},{16,8},{20,12},{24,16},{28,20},{0,24},{4,28},{9,1},{1... | collective-permute-start | bytes 294920 | tf_op jit(solution)/shard_map/ppermute | solution.py:32
  10.1 0.7 %copy-done.3 = f32[16,192]{1,0:T(8,128)S(1)} copy-done((f32[16,192]{1,0:T(8,128)S(1)}, f32[16,192]{1,0:T(8,128)}, u32[]{:S(2)}) %copy-start.3) | copy-done | bytes 12312
  10.9 1.0 %copy-done.4 = bf16[5,192,192]{2,1,0:T(8,128)(2,1)S(1)} copy-done((bf16[5,192,192]{2,1,0:T(8,128)(2,1)S(1)}, bf16[5,192,192]{2,1,0:T(8,128)(2,1)}, u32[]{:S(2)}) %copy-start.4) | copy-done | bytes 368664
  11.9 1.6 %response.1 = (f32[16,192,256]{2,1,0:T(8,128)S(1)}, f32[2,192,128]{2,1,0:T(8,128)S(1)}) custom-call(f32[16,192]{1,0:T(8,128)S(1)} %copy-done.3, bf16[5,192,192]{2,1,0:T(8,128)(2,1)S(1)} %copy-done.4), custom_call_target="tpu_custom_call" | custom-call | flops 452984832 | bytes 2359296 | tf_op jit(solution)/shard_map/response/pallas_call | solution.py:337
  13.5 0.0 collective-permute-done.refs_1_
  13.5 0.2 collective-permute-done.1.refs_2_
  13.7 0.4 %collective-permute-done.2.refs_3_ = bf16[2,192,128]{2,1,0:T(8,128)(2,1)S(1)} collective-permute-done((bf16[2,192,128]{2,1,0:T(8,128)(2,1)S(1)}, bf16[2,192,128]{2,1,0:T(8,128)(2,1)S(1)}, u32[]{:S(2)}, u32[]{:S(2)}) %collective-permute-start.2) | collective-permute-done | bytes 98336 | tf_op jit(solution)/shard_map/ppermute | solution.py:32
  14.1 0.0 collective-permute-done.3.refs_4_
  14.1 0.7 %copy-done.2 = s32[8]{0:T(128)S(1)} copy-done((s32[8]{0:T(128)S(1)}, s32[8]{0:T(128)}, u32[]{:S(2)}) %copy-start.2) | copy-done | bytes 56
  14.8 2.6 %image.1 = (bf16[2,192,128]{2,1,0:T(8,128)(2,1)S(1)}, bf16[4,192,128]{2,1,0:T(8,128)(2,1)S(1)}) custom-call(s32[8]{0:T(128)S(1)} %copy-done.2, bf16[2,192,128]{2,1,0:T(8,128)(2,1)S(1)} %pack.1.refs_0_, bf16[2,192,128]{2,1,0:T(8,128)(2,1)S(1)} %collective-permute-done.refs_1_, bf16[2,192,128]{2,1,0:T(8,128)(2,1)S(1)} %collective-permute-done.1.refs_2_, ...), custom_call_target="tpu_custom_call" | custom-call | flops 603979776 | bytes 2359296 | tf_op jit(solution)/shard_map/image/pallas_call | solution.py:346
  17.3 1.6 %collective-permute-start.8 = (bf16[2,192,128]{2,1,0:T(8,128)(2,1)S(1)}, bf16[2,192,128]{2,1,0:T(8,128)(2,1)S(1)}, u32[]{:S(2)}, u32[]{:S(2)}) collective-permute-start(bf16[2,192,128]{2,1,0:T(8,128)(2,1)S(1)} %get-tuple-element.15), channel_id=1, source_target_pairs={{0,2},{1,3},{2,0},{3,1},{4,6},{5,7},{6,4},{7,5},{8,10},{9,11},{10,... | collective-permute-start | bytes 294920 | tf_op jit(solution)/shard_map/ppermute | solution.py:39
  18.9 0.0 copy-done.1
  18.9 0.2 overlap.1.refs_0_
  19.1 0.1 collective-permute-start.4
  19.2 0.6 %collective-permute-start.5 = (f32[16,128]{1,0:T(8,128)S(1)}, f32[16,128]{1,0:T(8,128)S(1)}, u32[]{:S(2)}, u32[]{:S(2)}) collective-permute-start(f32[16,128]{1,0:T(8,128)S(1)} %overlap.1.refs_0_), channel_id=1, source_target_pairs={{0,2},{1,3},{2,0},{3,1},{4,6},{5,7},{6,4},{7,5},{8,10},{9,11},{10,... | collective-permute-start | bytes 24584 | tf_op jit(solution)/shard_map/ppermute | solution.py:39
  19.8 1.3 %collective-permute-start.6 = (f32[16,128]{1,0:T(8,128)S(1)}, f32[16,128]{1,0:T(8,128)S(1)}, u32[]{:S(2)}, u32[]{:S(2)}) collective-permute-start(f32[16,128]{1,0:T(8,128)S(1)} %overlap.1.refs_0_), channel_id=1, source_target_pairs={{0,3},{1,2},{2,1},{3,0},{4,7},{5,6},{6,5},{7,4},{8,11},{9,10},{10,... | collective-permute-start | bytes 24584 | tf_op jit(solution)/shard_map/ppermute | solution.py:39
  21.0 0.1 copy.7.owners_ref
  21.1 0.3 %collective-permute-start.7 = (bf16[4,192,128]{2,1,0:T(8,128)(2,1)S(1)}, bf16[4,192,128]{2,1,0:T(8,128)(2,1)S(1)}, u32[]{:S(2)}, u32[]{:S(2)}) collective-permute-start(bf16[4,192,128]{2,1,0:T(8,128)(2,1)S(1)} %get-tuple-element.12.halves_ref.refs_0_), channel_id=1, source_target_pairs={{0,1},{1,0},{2,3},{3,2},{4,5},{5,4},{6,7},{7,6},{8,9},{9,8},{10,11... | collective-permute-start | bytes 589832 | tf_op jit(solution)/shard_map/ppermute | solution.py:39
  21.5 0.6 %collective-permute-done.8.refs_2_ = bf16[2,192,128]{2,1,0:T(8,128)(2,1)S(1)} collective-permute-done((bf16[2,192,128]{2,1,0:T(8,128)(2,1)S(1)}, bf16[2,192,128]{2,1,0:T(8,128)(2,1)S(1)}, u32[]{:S(2)}, u32[]{:S(2)}) %collective-permute-start.8) | collective-permute-done | bytes 98336 | tf_op jit(solution)/shard_map/ppermute | solution.py:39
  22.0 0.0 collective-permute-start.9
  22.0 0.0 collective-permute-done.4.refs_1_
  22.0 0.9 %collective-permute-done.5.refs_2_ = f32[16,128]{1,0:T(8,128)S(1)} collective-permute-done((f32[16,128]{1,0:T(8,128)S(1)}, f32[16,128]{1,0:T(8,128)S(1)}, u32[]{:S(2)}, u32[]{:S(2)}) %collective-permute-start.5) | collective-permute-done | bytes 8224 | tf_op jit(solution)/shard_map/ppermute | solution.py:39
  22.9 0.0 collective-permute-done.6.refs_3_
  22.9 0.5 %factor.1 = (f32[16,16]{1,0:T(8,128)S(1)}, bf16[256,256]{1,0:T(8,128)(2,1)S(1)}) custom-call(s32[16,1]{1,0:T(8,128)S(1)} %copy.7.owners_ref, f32[16,128]{1,0:T(8,128)S(1)} %overlap.1.refs_0_, f32[16,128]{1,0:T(8,128)S(1)} %collective-permute-done.4.refs_1_, f32[16,128]{1,0:T(8,128)S(1)} %collective-permute-done.5.refs_2_, ...), custom_call_target="tpu_custom_call" | custom-call | flops 3000000000 | bytes 1024 | tf_op jit(solution)/shard_map/factor/pallas_call | solution.py:373
  23.5 0.0 collective-permute-done.7.refs_1_
  23.5 0.0 collective-permute-done.9.refs_3_
  23.5 1.1 %route.1 = (bf16[8,64,192]{2,1,0:T(8,128)(2,1)}, f32[16,16]{1,0:T(8,128)}) custom-call(f32[16,16]{1,0:T(8,128)S(1)} %get-tuple-element.13.overlap_ref, bf16[256,256]{1,0:T(8,128)(2,1)S(1)} %get-tuple-element.14.weights_ref, bf16[4,192,128]{2,1,0:T(8,128)(2,1)S(1)} %get-tuple-element.12.halves_ref.refs_0_, ...), custom_call_target="tpu_custom_call" | custom-call | flops 3145728 | bytes 1179648 | tf_op jit(solution)/shard_map/route/pallas_call | solution.py:381
  (7 shorter events, 0.0 us)
Async XLA Ops:
  0.6 0.9 %copy-start = (bf16[16,16,192]{2,1,0:T(8,128)(2,1)S(1)}, bf16[16,16,192]{2,1,0:T(8,128)(2,1)}, u32[]{:S(2)}) copy-start(bf16[16,16,192]{2,1,0:T(8,128)(2,1)} %orbitals_ref.3) | copy-start | bytes 294916
  1.5 17.3 %copy-start.1 = (bf16[16,16,192]{2,1,0:T(8,128)(2,1)S(1)}, bf16[16,16,192]{2,1,0:T(8,128)(2,1)}, u32[]{:S(2)}) copy-start(bf16[16,16,192]{2,1,0:T(8,128)(2,1)} %orbitals_ref.3) | copy-start | bytes 294916
  1.5 19.5 %copy-start.5 = (s32[16,1]{0,1:T(1,128)S(1)}, s32[16,1]{0,1:T(1,128)}, u32[]{:S(2)}) copy-start(s32[16,1]{0,1:T(1,128)} %param.8) | copy-start | bytes 196
  1.8 11.7 %collective-permute-start = (bf16[2,192,128]{2,1,0:T(8,128)(2,1)S(1)}, bf16[2,192,128]{2,1,0:T(8,128)(2,1)S(1)}, u32[]{:S(2)}, u32[]{:S(2)}) collective-permute-start(bf16[2,192,128]{2,1,0:T(8,128)(2,1)S(1)} %pack.1.refs_0_), channel_id=1, source_target_pairs={{24,0},{28,4},{0,8},{4,12},{8,16},{12,20},{16,24},{20,28},{25,1},{... | collective-permute-start | bytes 294920 | tf_op jit(solution)/shard_map/ppermute | solution.py:32
  4.9 8.8 %collective-permute-start.1 = (bf16[2,192,128]{2,1,0:T(8,128)(2,1)S(1)}, bf16[2,192,128]{2,1,0:T(8,128)(2,1)S(1)}, u32[]{:S(2)}, u32[]{:S(2)}) collective-permute-start(bf16[2,192,128]{2,1,0:T(8,128)(2,1)S(1)} %pack.1.refs_0_), channel_id=1, source_target_pairs={{28,0},{8,4},{4,8},{16,12},{12,16},{24,20},{20,24},{0,28},{29,1},{... | collective-permute-start | bytes 294920 | tf_op jit(solution)/shard_map/ppermute | solution.py:32
  8.1 6.0 %collective-permute-start.2 = (bf16[2,192,128]{2,1,0:T(8,128)(2,1)S(1)}, bf16[2,192,128]{2,1,0:T(8,128)(2,1)S(1)}, u32[]{:S(2)}, u32[]{:S(2)}) collective-permute-start(bf16[2,192,128]{2,1,0:T(8,128)(2,1)S(1)} %pack.1.refs_0_), channel_id=1, source_target_pairs={{4,0},{0,4},{12,8},{8,12},{20,16},{16,20},{28,24},{24,28},{5,1},{1... | collective-permute-start | bytes 294920 | tf_op jit(solution)/shard_map/ppermute | solution.py:32
  8.1 6.0 %collective-permute-start.3 = (bf16[2,192,128]{2,1,0:T(8,128)(2,1)S(1)}, bf16[2,192,128]{2,1,0:T(8,128)(2,1)S(1)}, u32[]{:S(2)}, u32[]{:S(2)}) collective-permute-start(bf16[2,192,128]{2,1,0:T(8,128)(2,1)S(1)} %pack.1.refs_0_), channel_id=1, source_target_pairs={{8,0},{12,4},{16,8},{20,12},{24,16},{28,20},{0,24},{4,28},{9,1},{1... | collective-permute-start | bytes 294920 | tf_op jit(solution)/shard_map/ppermute | solution.py:32
  10.1 0.7 %copy-start.3 = (f32[16,192]{1,0:T(8,128)S(1)}, f32[16,192]{1,0:T(8,128)}, u32[]{:S(2)}) copy-start(f32[16,192]{1,0:T(8,128)} %coulomb_ref.1) | copy-start | bytes 36868
  10.9 1.0 %copy-start.4 = (bf16[5,192,192]{2,1,0:T(8,128)(2,1)S(1)}, bf16[5,192,192]{2,1,0:T(8,128)(2,1)}, u32[]{:S(2)}) copy-start(bf16[5,192,192]{2,1,0:T(8,128)(2,1)} %constant.2.clone.tables_ref) | copy-start | bytes 1105924
  14.1 0.7 %copy-start.2 = (s32[8]{0:T(128)S(1)}, s32[8]{0:T(128)}, u32[]{:S(2)}) copy-start(s32[8]{0:T(128)} %occupied_ref.1) | copy-start | bytes 100
  17.3 4.7 %collective-permute-start.8 = (bf16[2,192,128]{2,1,0:T(8,128)(2,1)S(1)}, bf16[2,192,128]{2,1,0:T(8,128)(2,1)S(1)}, u32[]{:S(2)}, u32[]{:S(2)}) collective-permute-start(bf16[2,192,128]{2,1,0:T(8,128)(2,1)S(1)} %get-tuple-element.15), channel_id=1, source_target_pairs={{0,2},{1,3},{2,0},{3,1},{4,6},{5,7},{6,4},{7,5},{8,10},{9,11},{10,... | collective-permute-start | bytes 294920 | tf_op jit(solution)/shard_map/ppermute | solution.py:39
  19.1 2.9 %collective-permute-start.4 = (f32[16,128]{1,0:T(8,128)S(1)}, f32[16,128]{1,0:T(8,128)S(1)}, u32[]{:S(2)}, u32[]{:S(2)}) collective-permute-start(f32[16,128]{1,0:T(8,128)S(1)} %overlap.1.refs_0_), channel_id=1, source_target_pairs={{0,1},{1,0},{2,3},{3,2},{4,5},{5,4},{6,7},{7,6},{8,9},{9,8},{10,11... | collective-permute-start | bytes 24584 | tf_op jit(solution)/shard_map/ppermute | solution.py:39
  19.2 3.8 %collective-permute-start.5 = (f32[16,128]{1,0:T(8,128)S(1)}, f32[16,128]{1,0:T(8,128)S(1)}, u32[]{:S(2)}, u32[]{:S(2)}) collective-permute-start(f32[16,128]{1,0:T(8,128)S(1)} %overlap.1.refs_0_), channel_id=1, source_target_pairs={{0,2},{1,3},{2,0},{3,1},{4,6},{5,7},{6,4},{7,5},{8,10},{9,11},{10,... | collective-permute-start | bytes 24584 | tf_op jit(solution)/shard_map/ppermute | solution.py:39
  19.8 3.2 %collective-permute-start.6 = (f32[16,128]{1,0:T(8,128)S(1)}, f32[16,128]{1,0:T(8,128)S(1)}, u32[]{:S(2)}, u32[]{:S(2)}) collective-permute-start(f32[16,128]{1,0:T(8,128)S(1)} %overlap.1.refs_0_), channel_id=1, source_target_pairs={{0,3},{1,2},{2,1},{3,0},{4,7},{5,6},{6,5},{7,4},{8,11},{9,10},{10,... | collective-permute-start | bytes 24584 | tf_op jit(solution)/shard_map/ppermute | solution.py:39
  21.1 2.4 %collective-permute-start.7 = (bf16[4,192,128]{2,1,0:T(8,128)(2,1)S(1)}, bf16[4,192,128]{2,1,0:T(8,128)(2,1)S(1)}, u32[]{:S(2)}, u32[]{:S(2)}) collective-permute-start(bf16[4,192,128]{2,1,0:T(8,128)(2,1)S(1)} %get-tuple-element.12.halves_ref.refs_0_), channel_id=1, source_target_pairs={{0,1},{1,0},{2,3},{3,2},{4,5},{5,4},{6,7},{7,6},{8,9},{9,8},{10,11... | collective-permute-start | bytes 589832 | tf_op jit(solution)/shard_map/ppermute | solution.py:39
  22.0 1.5 %collective-permute-start.9 = (bf16[2,192,128]{2,1,0:T(8,128)(2,1)S(1)}, bf16[2,192,128]{2,1,0:T(8,128)(2,1)S(1)}, u32[]{:S(2)}, u32[]{:S(2)}) collective-permute-start(bf16[2,192,128]{2,1,0:T(8,128)(2,1)S(1)} %collective-permute-done.8.refs_2_), channel_id=1, source_target_pairs={{0,1},{1,0},{2,3},{3,2},{4,5},{5,4},{6,7},{7,6},{8,9},{9,8},{10,11... | collective-permute-start | bytes 294920 | tf_op jit(solution)/shard_map/ppermute | solution.py:39

commit v10 on v7

--- a/solution.py
+++ b/solution.py
@@ -144,7 +144,7 @@
     for pack in range(packs):
         tiles = [block[pack] for block in blocks]
         native = jnp.concatenate([tiles[0], blank[:, :LANES]], axis=0)
-        image = jnp.zeros((points, LANES), F32)
+        kernels = []
         for quarter in range(4):
             here = [(q == quarter) for q in quarters]
             together = sum(tiles[m] * here[m].astype(F32).astype(BF16) for m in merged)
@@ -159,12 +159,14 @@
             gram = dot32(masked, jnp.concatenate([window, blank], axis=0), NT)
             first = pack * span + quarter * per
             response = response_ref[first : first + per].reshape(per * points, padded)
-            high, low = halves(gram * response)
-            fields = dot32(jnp.concatenate([high, low], axis=0), native)
-            for k in range(per):
-                a, b = k * points, (per + k) * points
-                field = fields[a : a + points] + fields[b : b + points]
-                image = jnp.where(own_line == quarter * per + k, field, image)
+            kernels += halves(gram * response)
+        fields = dot32(jnp.concatenate(kernels, axis=0), native)
+        image = jnp.zeros((points, LANES), F32)
+        for line in range(span):
+            a = (line // per * 2 * per + line % per) * points
+            b = a + per * points
+            field = fields[a : a + points] + fields[b : b + points]
+            image = jnp.where(own_line == line, field, image)
         high, low = halves(image)
         high_ref[pack] = high
         halves_ref[pack] = high

time: 23.9 us -> 23.8 us (level)
  no operation moved by 1% of the time
where the time goes in v10:
time: 23.8 us; the launch traced here: 23.5 us
  starting transfers between devices  12.2 us (51%)
  Pallas kernels  5.49 us (23%)
  local copies, waits for them, and re-layouts  2.67 us (11%)
  waiting for transfers between devices  2.42 us (10%)
  between operations  0.72 us (3%)
    ppermute x4, starting transfers between devices, exchanged(): lax.ppermute(value, 'band', [(row[turn], block) for block, row in enumera...  8.36 us
    ppermute x6, starting transfers between devices, swapped(): lax.ppermute(value, ('grid', 'ham'), [(group, group ^ flip) for group in...  3.84 us
    unnamed x13, local copies, waits for them, and re-layouts  2.67 us
    pallas_call x1, Pallas kernels, local(): call(functools.partial(image_kernel, members), 'image', [shape((packs, po...  2.14 us
    ppermute x6, waiting for transfers between devices, swapped(): lax.ppermute(value, ('grid', 'ham'), [(group, group ^ flip) for group in...  1.47 us
    pallas_call x1, Pallas kernels, local(): call(response_kernel, 'response', [shape((lines, points, padded), F32)],...  1.31 us
    pallas_call x1, Pallas kernels, local(): call(route_kernel, 'route', [shape((CAP, groups * lines, points), BF16),...  1.08 us
    ppermute x4, waiting for transfers between devices, exchanged(): lax.ppermute(value, 'band', [(row[turn], block) for block, row in enumera...  0.95 us
  transfers between devices with their start and end apart: 10, of which 4 were waited for; matrix products, arithmetic and copies ran while one was open for 0% of the time, Pallas kernels for 9%

profile of v10, /device:TPU:0, one launch (start us, length us, event | category | flops | bytes accessed | tf_op | source)
XLA Modules:
  0.0 23.5 jit_solution(16421640118995000897)
XLA Ops:
  0.6 0.0 copy-start
  0.6 0.9 %copy-done = bf16[16,16,192]{2,1,0:T(8,128)(2,1)S(1)} copy-done((bf16[16,16,192]{2,1,0:T(8,128)(2,1)S(1)}, bf16[16,16,192]{2,1,0:T(8,128)(2,1)}, u32[]{:S(2)}) %copy-start) | copy-done | bytes 98328
  1.5 0.2 pack.1.refs_0_
  1.8 0.0 copy-start.1
  1.8 3.1 %collective-permute-start = (bf16[2,192,128]{2,1,0:T(8,128)(2,1)S(1)}, bf16[2,192,128]{2,1,0:T(8,128)(2,1)S(1)}, u32[]{:S(2)}, u32[]{:S(2)}) collective-permute-start(bf16[2,192,128]{2,1,0:T(8,128)(2,1)S(1)} %pack.1.refs_0_), channel_id=1, source_target_pairs={{24,0},{28,4},{0,8},{4,12},{8,16},{12,20},{16,24},{20,28},{25,1},{... | collective-permute-start | bytes 294920 | tf_op jit(solution)/shard_map/ppermute | solution.py:32
  4.9 3.2 %collective-permute-start.1 = (bf16[2,192,128]{2,1,0:T(8,128)(2,1)S(1)}, bf16[2,192,128]{2,1,0:T(8,128)(2,1)S(1)}, u32[]{:S(2)}, u32[]{:S(2)}) collective-permute-start(bf16[2,192,128]{2,1,0:T(8,128)(2,1)S(1)} %pack.1.refs_0_), channel_id=1, source_target_pairs={{28,0},{8,4},{4,8},{16,12},{12,16},{24,20},{20,24},{0,28},{29,1},{... | collective-permute-start | bytes 294920 | tf_op jit(solution)/shard_map/ppermute | solution.py:32
  8.1 0.0 collective-permute-start.2
  8.1 2.1 %collective-permute-start.3 = (bf16[2,192,128]{2,1,0:T(8,128)(2,1)S(1)}, bf16[2,192,128]{2,1,0:T(8,128)(2,1)S(1)}, u32[]{:S(2)}, u32[]{:S(2)}) collective-permute-start(bf16[2,192,128]{2,1,0:T(8,128)(2,1)S(1)} %pack.1.refs_0_), channel_id=1, source_target_pairs={{8,0},{12,4},{16,8},{20,12},{24,16},{28,20},{0,24},{4,28},{9,1},{1... | collective-permute-start | bytes 294920 | tf_op jit(solution)/shard_map/ppermute | solution.py:32
  10.2 1.0 %copy-done.2 = bf16[3,192,192]{2,1,0:T(8,128)(2,1)S(1)} copy-done((bf16[3,192,192]{2,1,0:T(8,128)(2,1)S(1)}, bf16[3,192,192]{2,1,0:T(8,128)(2,1)}, u32[]{:S(2)}) %copy-start.2) | copy-done | bytes 221208
  11.1 0.7 %copy-done.3 = f32[16,192]{1,0:T(8,128)S(1)} copy-done((f32[16,192]{1,0:T(8,128)S(1)}, f32[16,192]{1,0:T(8,128)}, u32[]{:S(2)}) %copy-start.3) | copy-done | bytes 12312
  11.8 1.3 %response.1.refs_5_ = f32[16,192,256]{2,1,0:T(8,128)S(1)} custom-call(f32[16,192]{1,0:T(8,128)S(1)} %copy-done.3, bf16[3,192,192]{2,1,0:T(8,128)(2,1)S(1)} %copy-done.2), custom_call_target="tpu_custom_call" | custom-call | flops 452984832 | bytes 2359296 | tf_op jit(solution)/shard_map/response/pallas_call | solution.py:316
  13.2 0.0 collective-permute-done.refs_1_
  13.2 0.6 %collective-permute-done.1.refs_2_ = bf16[2,192,128]{2,1,0:T(8,128)(2,1)S(1)} collective-permute-done((bf16[2,192,128]{2,1,0:T(8,128)(2,1)S(1)}, bf16[2,192,128]{2,1,0:T(8,128)(2,1)S(1)}, u32[]{:S(2)}, u32[]{:S(2)}) %collective-permute-start.1) | collective-permute-done | bytes 98336 | tf_op jit(solution)/shard_map/ppermute | solution.py:32
  13.7 0.4 %collective-permute-done.2.refs_3_ = bf16[2,192,128]{2,1,0:T(8,128)(2,1)S(1)} collective-permute-done((bf16[2,192,128]{2,1,0:T(8,128)(2,1)S(1)}, bf16[2,192,128]{2,1,0:T(8,128)(2,1)S(1)}, u32[]{:S(2)}, u32[]{:S(2)}) %collective-permute-start.2) | collective-permute-done | bytes 98336 | tf_op jit(solution)/shard_map/ppermute | solution.py:32
  14.1 0.0 collective-permute-done.3.refs_4_
  14.1 2.1 %image.1 = (bf16[2,192,128]{2,1,0:T(8,128)(2,1)S(1)}, bf16[4,192,128]{2,1,0:T(8,128)(2,1)S(1)}) custom-call(s32[8]{0:T(128)S(1)} %copy-done.4, bf16[2,192,128]{2,1,0:T(8,128)(2,1)S(1)} %pack.1.refs_0_, bf16[2,192,128]{2,1,0:T(8,128)(2,1)S(1)} %collective-permute-done.refs_1_, bf16[2,192,128]{2,1,0:T(8,128)(2,1)S(1)} %collective-permute-done.1.refs_2_, ...), custom_call_target="tpu_custom_call" | custom-call | flops 805306368 | bytes 2359296 | tf_op jit(solution)/shard_map/image/pallas_call | solution.py:325
  16.3 1.6 %collective-permute-start.8 = (bf16[2,192,128]{2,1,0:T(8,128)(2,1)S(1)}, bf16[2,192,128]{2,1,0:T(8,128)(2,1)S(1)}, u32[]{:S(2)}, u32[]{:S(2)}) collective-permute-start(bf16[2,192,128]{2,1,0:T(8,128)(2,1)S(1)} %get-tuple-element.11), channel_id=1, source_target_pairs={{0,2},{1,3},{2,0},{3,1},{4,6},{5,7},{6,4},{7,5},{8,10},{9,11},{10,... | collective-permute-start | bytes 294920 | tf_op jit(solution)/shard_map/ppermute | solution.py:39
  17.8 0.2 overlap.1.refs_0_
  18.0 0.1 collective-permute-start.4
  18.1 0.6 %collective-permute-start.5 = (f32[16,128]{1,0:T(8,128)S(1)}, f32[16,128]{1,0:T(8,128)S(1)}, u32[]{:S(2)}, u32[]{:S(2)}) collective-permute-start(f32[16,128]{1,0:T(8,128)S(1)} %overlap.1.refs_0_), channel_id=1, source_target_pairs={{0,2},{1,3},{2,0},{3,1},{4,6},{5,7},{6,4},{7,5},{8,10},{9,11},{10,... | collective-permute-start | bytes 24584 | tf_op jit(solution)/shard_map/ppermute | solution.py:39
  18.7 1.3 %collective-permute-start.6 = (f32[16,128]{1,0:T(8,128)S(1)}, f32[16,128]{1,0:T(8,128)S(1)}, u32[]{:S(2)}, u32[]{:S(2)}) collective-permute-start(f32[16,128]{1,0:T(8,128)S(1)} %overlap.1.refs_0_), channel_id=1, source_target_pairs={{0,3},{1,2},{2,1},{3,0},{4,7},{5,6},{6,5},{7,4},{8,11},{9,10},{10,... | collective-permute-start | bytes 24584 | tf_op jit(solution)/shard_map/ppermute | solution.py:39
  20.0 0.1 copy.7.owners_ref
  20.0 0.3 %collective-permute-start.7 = (bf16[4,192,128]{2,1,0:T(8,128)(2,1)S(1)}, bf16[4,192,128]{2,1,0:T(8,128)(2,1)S(1)}, u32[]{:S(2)}, u32[]{:S(2)}) collective-permute-start(bf16[4,192,128]{2,1,0:T(8,128)(2,1)S(1)} %get-tuple-element.8.halves_ref.refs_0_), channel_id=1, source_target_pairs={{0,1},{1,0},{2,3},{3,2},{4,5},{5,4},{6,7},{7,6},{8,9},{9,8},{10,11... | collective-permute-start | bytes 589832 | tf_op jit(solution)/shard_map/ppermute | solution.py:39
  20.4 0.6 %collective-permute-done.8.refs_2_ = bf16[2,192,128]{2,1,0:T(8,128)(2,1)S(1)} collective-permute-done((bf16[2,192,128]{2,1,0:T(8,128)(2,1)S(1)}, bf16[2,192,128]{2,1,0:T(8,128)(2,1)S(1)}, u32[]{:S(2)}, u32[]{:S(2)}) %collective-permute-start.8) | collective-permute-done | bytes 98336 | tf_op jit(solution)/shard_map/ppermute | solution.py:39
  20.9 0.0 collective-permute-start.9
  20.9 0.0 collective-permute-done.4.refs_1_
  21.0 0.9 %collective-permute-done.5.refs_2_ = f32[16,128]{1,0:T(8,128)S(1)} collective-permute-done((f32[16,128]{1,0:T(8,128)S(1)}, f32[16,128]{1,0:T(8,128)S(1)}, u32[]{:S(2)}, u32[]{:S(2)}) %collective-permute-start.5) | collective-permute-done | bytes 8224 | tf_op jit(solution)/shard_map/ppermute | solution.py:39
  21.9 0.0 collective-permute-done.6.refs_3_
  21.9 0.5 %factor.1 = (f32[16,16]{1,0:T(8,128)S(1)}, bf16[256,256]{1,0:T(8,128)(2,1)S(1)}) custom-call(s32[16,1]{1,0:T(8,128)S(1)} %copy.7.owners_ref, f32[16,128]{1,0:T(8,128)S(1)} %overlap.1.refs_0_, f32[16,128]{1,0:T(8,128)S(1)} %collective-permute-done.4.refs_1_, f32[16,128]{1,0:T(8,128)S(1)} %collective-permute-done.5.refs_2_, ...), custom_call_target="tpu_custom_call" | custom-call | flops 3000000000 | bytes 1024 | tf_op jit(solution)/shard_map/factor/pallas_call | solution.py:352
  22.4 0.0 collective-permute-done.7.refs_1_
  22.4 0.0 collective-permute-done.9.refs_3_
  22.4 1.1 %route.1 = (bf16[8,64,192]{2,1,0:T(8,128)(2,1)}, f32[16,16]{1,0:T(8,128)}) custom-call(f32[16,16]{1,0:T(8,128)S(1)} %get-tuple-element.9.overlap_ref, bf16[256,256]{1,0:T(8,128)(2,1)S(1)} %get-tuple-element.10.weights_ref, bf16[4,192,128]{2,1,0:T(8,128)(2,1)S(1)} %get-tuple-element.8.halves_ref.refs_0_, ...), custom_call_target="tpu_custom_call" | custom-call | flops 3145728 | bytes 1179648 | tf_op jit(solution)/shard_map/route/pallas_call | solution.py:360
  (7 shorter events, 0.0 us)
Async XLA Ops:
  0.6 0.9 %copy-start = (bf16[16,16,192]{2,1,0:T(8,128)(2,1)S(1)}, bf16[16,16,192]{2,1,0:T(8,128)(2,1)}, u32[]{:S(2)}) copy-start(bf16[16,16,192]{2,1,0:T(8,128)(2,1)} %orbitals_ref.3) | copy-start | bytes 294916
  1.5 12.6 %copy-start.4 = (s32[8]{0:T(128)S(1)}, s32[8]{0:T(128)}, u32[]{:S(2)}) copy-start(s32[8]{0:T(128)} %occupied_ref.1) | copy-start | bytes 100
  1.5 18.4 %copy-start.5 = (s32[16,1]{0,1:T(1,128)S(1)}, s32[16,1]{0,1:T(1,128)}, u32[]{:S(2)}) copy-start(s32[16,1]{0,1:T(1,128)} %param.8) | copy-start | bytes 196
  1.8 16.0 %copy-start.1 = (bf16[16,16,192]{2,1,0:T(8,128)(2,1)S(1)}, bf16[16,16,192]{2,1,0:T(8,128)(2,1)}, u32[]{:S(2)}) copy-start(bf16[16,16,192]{2,1,0:T(8,128)(2,1)} %orbitals_ref.3) | copy-start | bytes 294916
  1.8 11.4 %collective-permute-start = (bf16[2,192,128]{2,1,0:T(8,128)(2,1)S(1)}, bf16[2,192,128]{2,1,0:T(8,128)(2,1)S(1)}, u32[]{:S(2)}, u32[]{:S(2)}) collective-permute-start(bf16[2,192,128]{2,1,0:T(8,128)(2,1)S(1)} %pack.1.refs_0_), channel_id=1, source_target_pairs={{24,0},{28,4},{0,8},{4,12},{8,16},{12,20},{16,24},{20,28},{25,1},{... | collective-permute-start | bytes 294920 | tf_op jit(solution)/shard_map/ppermute | solution.py:32
  4.9 8.8 %collective-permute-start.1 = (bf16[2,192,128]{2,1,0:T(8,128)(2,1)S(1)}, bf16[2,192,128]{2,1,0:T(8,128)(2,1)S(1)}, u32[]{:S(2)}, u32[]{:S(2)}) collective-permute-start(bf16[2,192,128]{2,1,0:T(8,128)(2,1)S(1)} %pack.1.refs_0_), channel_id=1, source_target_pairs={{28,0},{8,4},{4,8},{16,12},{12,16},{24,20},{20,24},{0,28},{29,1},{... | collective-permute-start | bytes 294920 | tf_op jit(solution)/shard_map/ppermute | solution.py:32
  8.1 6.0 %collective-permute-start.2 = (bf16[2,192,128]{2,1,0:T(8,128)(2,1)S(1)}, bf16[2,192,128]{2,1,0:T(8,128)(2,1)S(1)}, u32[]{:S(2)}, u32[]{:S(2)}) collective-permute-start(bf16[2,192,128]{2,1,0:T(8,128)(2,1)S(1)} %pack.1.refs_0_), channel_id=1, source_target_pairs={{4,0},{0,4},{12,8},{8,12},{20,16},{16,20},{28,24},{24,28},{5,1},{1... | collective-permute-start | bytes 294920 | tf_op jit(solution)/shard_map/ppermute | solution.py:32
  8.1 6.0 %collective-permute-start.3 = (bf16[2,192,128]{2,1,0:T(8,128)(2,1)S(1)}, bf16[2,192,128]{2,1,0:T(8,128)(2,1)S(1)}, u32[]{:S(2)}, u32[]{:S(2)}) collective-permute-start(bf16[2,192,128]{2,1,0:T(8,128)(2,1)S(1)} %pack.1.refs_0_), channel_id=1, source_target_pairs={{8,0},{12,4},{16,8},{20,12},{24,16},{28,20},{0,24},{4,28},{9,1},{1... | collective-permute-start | bytes 294920 | tf_op jit(solution)/shard_map/ppermute | solution.py:32
  10.2 1.0 %copy-start.2 = (bf16[3,192,192]{2,1,0:T(8,128)(2,1)S(1)}, bf16[3,192,192]{2,1,0:T(8,128)(2,1)}, u32[]{:S(2)}) copy-start(bf16[3,192,192]{2,1,0:T(8,128)(2,1)} %constant.3.tables_ref) | copy-start | bytes 663556
  11.1 0.7 %copy-start.3 = (f32[16,192]{1,0:T(8,128)S(1)}, f32[16,192]{1,0:T(8,128)}, u32[]{:S(2)}) copy-start(f32[16,192]{1,0:T(8,128)} %coulomb_ref.1) | copy-start | bytes 36868
  16.3 4.7 %collective-permute-start.8 = (bf16[2,192,128]{2,1,0:T(8,128)(2,1)S(1)}, bf16[2,192,128]{2,1,0:T(8,128)(2,1)S(1)}, u32[]{:S(2)}, u32[]{:S(2)}) collective-permute-start(bf16[2,192,128]{2,1,0:T(8,128)(2,1)S(1)} %get-tuple-element.11), channel_id=1, source_target_pairs={{0,2},{1,3},{2,0},{3,1},{4,6},{5,7},{6,4},{7,5},{8,10},{9,11},{10,... | collective-permute-start | bytes 294920 | tf_op jit(solution)/shard_map/ppermute | solution.py:39
  18.0 2.9 %collective-permute-start.4 = (f32[16,128]{1,0:T(8,128)S(1)}, f32[16,128]{1,0:T(8,128)S(1)}, u32[]{:S(2)}, u32[]{:S(2)}) collective-permute-start(f32[16,128]{1,0:T(8,128)S(1)} %overlap.1.refs_0_), channel_id=1, source_target_pairs={{0,1},{1,0},{2,3},{3,2},{4,5},{5,4},{6,7},{7,6},{8,9},{9,8},{10,11... | collective-permute-start | bytes 24584 | tf_op jit(solution)/shard_map/ppermute | solution.py:39
  18.1 3.8 %collective-permute-start.5 = (f32[16,128]{1,0:T(8,128)S(1)}, f32[16,128]{1,0:T(8,128)S(1)}, u32[]{:S(2)}, u32[]{:S(2)}) collective-permute-start(f32[16,128]{1,0:T(8,128)S(1)} %overlap.1.refs_0_), channel_id=1, source_target_pairs={{0,2},{1,3},{2,0},{3,1},{4,6},{5,7},{6,4},{7,5},{8,10},{9,11},{10,... | collective-permute-start | bytes 24584 | tf_op jit(solution)/shard_map/ppermute | solution.py:39
  18.7 3.2 %collective-permute-start.6 = (f32[16,128]{1,0:T(8,128)S(1)}, f32[16,128]{1,0:T(8,128)S(1)}, u32[]{:S(2)}, u32[]{:S(2)}) collective-permute-start(f32[16,128]{1,0:T(8,128)S(1)} %overlap.1.refs_0_), channel_id=1, source_target_pairs={{0,3},{1,2},{2,1},{3,0},{4,7},{5,6},{6,5},{7,4},{8,11},{9,10},{10,... | collective-permute-start | bytes 24584 | tf_op jit(solution)/shard_map/ppermute | solution.py:39
  20.0 2.4 %collective-permute-start.7 = (bf16[4,192,128]{2,1,0:T(8,128)(2,1)S(1)}, bf16[4,192,128]{2,1,0:T(8,128)(2,1)S(1)}, u32[]{:S(2)}, u32[]{:S(2)}) collective-permute-start(bf16[4,192,128]{2,1,0:T(8,128)(2,1)S(1)} %get-tuple-element.8.halves_ref.refs_0_), channel_id=1, source_target_pairs={{0,1},{1,0},{2,3},{3,2},{4,5},{5,4},{6,7},{7,6},{8,9},{9,8},{10,11... | collective-permute-start | bytes 589832 | tf_op jit(solution)/shard_map/ppermute | solution.py:39
  20.9 1.5 %collective-permute-start.9 = (bf16[2,192,128]{2,1,0:T(8,128)(2,1)S(1)}, bf16[2,192,128]{2,1,0:T(8,128)(2,1)S(1)}, u32[]{:S(2)}, u32[]{:S(2)}) collective-permute-start(bf16[2,192,128]{2,1,0:T(8,128)(2,1)S(1)} %collective-permute-done.8.refs_2_), channel_id=1, source_target_pairs={{0,1},{1,0},{2,3},{3,2},{4,5},{5,4},{6,7},{7,6},{8,9},{9,8},{10,11... | collective-permute-start | bytes 294920 | tf_op jit(solution)/shard_map/ppermute | solution.py:39

commit v11 on v10

--- a/solution.py
+++ b/solution.py
@@ -11,8 +11,10 @@
 
 CAP = 8
 LANES = 128
+PIECES = 4
 HIGHEST = lax.Precision.HIGHEST
 VMEM_LIMIT = 48 * 1024 * 1024
+PACK_LIMIT = 55040 * 1024
 FACTOR_COST = 3_000_000_000
 NT = ((1,), (1,))
 F32, BF16 = jnp.float32, jnp.bfloat16
@@ -100,15 +102,27 @@
     return part.reshape(members * span, points)
 
 
-def pack_kernel(orbitals_ref, out_ref):
+def pack_kernel(orbitals_hbm, out_ref, orbitals_ref, semaphores):
     members = orbitals_ref.shape[0]
     span = LANES // members
-    block = orbitals_ref[...].astype(F32)
     row, lane = ids((LANES, LANES), 0), ids((LANES, LANES), 1)
     source = lane_member(lane, members) * span + lane_line(lane, own_turn(), members)
     order = (row == source).astype(BF16)
+    copies = []
     for pack in range(out_ref.shape[0]):
-        rows = rows_of(block, pack, span).T.astype(BF16)
+        for part in range(PIECES):
+            size = members // PIECES
+            place = (pl.ds(part * size, size), pl.ds(pack * span, span))
+            semaphore = semaphores.at[pack * PIECES + part]
+            copies.append(
+                pltpu.make_async_copy(orbitals_hbm.at[place], orbitals_ref.at[place], semaphore)
+            )
+            copies[-1].start()
+    for pack in range(out_ref.shape[0]):
+        for copy in copies[pack * PIECES : (pack + 1) * PIECES]:
+            copy.wait()
+        block = orbitals_ref[:, pack * span : (pack + 1) * span, :].astype(F32)
+        rows = block.reshape(members * span, -1).T.astype(BF16)
         out_ref[pack] = dot32(rows, order).astype(BF16)
 
 
@@ -279,17 +293,17 @@
         copy.wait()
 
 
-def call(kernel, name, shapes, flops, moved, scratch=(), scalars=0, operands=0, remote=False):
+def call(kernel, name, shapes, flops, moved, scratch=(), scalars=0, operands=0, remote=False, distant=0, limit=VMEM_LIMIT):
     vmem = pl.BlockSpec(memory_space=pltpu.VMEM)
     smem = pl.BlockSpec(memory_space=pltpu.SMEM)
     return pl.pallas_call(
         kernel,
         name=name,
         out_shape=shapes,
-        in_specs=[smem] * scalars + [vmem] * operands,
+        in_specs=[smem] * scalars + [pl.BlockSpec(memory_space=pl.ANY)] * distant + [vmem] * operands,
         out_specs=[pl.BlockSpec(memory_space=pl.ANY) if remote else vmem] * len(shapes),
         scratch_shapes=list(scratch),
-        compiler_params=pltpu.CompilerParams(vmem_limit_bytes=VMEM_LIMIT),
+        compiler_params=pltpu.CompilerParams(vmem_limit_bytes=limit),
         cost_estimate=pl.CostEstimate(flops=flops, bytes_accessed=moved, transcendentals=0),
     )
 
@@ -309,7 +323,12 @@
         [shape((packs, points, LANES), BF16)],
         orbitals.size,
         4 * orbitals.size,
-        operands=1,
+        scratch=[
+            pltpu.VMEM(orbitals.shape, BF16),
+            pltpu.SemaphoreType.DMA((packs * PIECES,)),
+        ],
+        distant=1,
+        limit=PACK_LIMIT,
     )(orbitals)
     guests = exchanged(packed)
     tables = spectral_tables(points)

time: 23.8 us -> 24 us (level)
  Pallas kernels: 5.49 us -> 6.58 us
  local copies, waits for them, and re-layouts: 2.67 us -> 1.78 us
    pallas_call x1, Pallas kernels: 0.23 us -> 1.31 us  [local(): call(pack_kernel, 'pack', [shape((packs, points, LANES), BF16)], orbitals...]
    unnamed x13 -> x11, local copies, waits for them, and re-layouts: 2.67 us -> 1.78 us
where the time goes in v11:
time: 24 us; the launch traced here: 23.7 us
  starting transfers between devices  12.2 us (51%)
  Pallas kernels  6.58 us (27%)
  waiting for transfers between devices  2.42 us (10%)
  local copies, waits for them, and re-layouts  1.78 us (7%)
  between operations  0.73 us (3%)
    ppermute x4, starting transfers between devices, exchanged(): lax.ppermute(value, 'band', [(row[turn], block) for block, row in enumera...  8.36 us
    ppermute x6, starting transfers between devices, swapped(): lax.ppermute(value, ('grid', 'ham'), [(group, group ^ flip) for group in...  3.83 us
    pallas_call x1, Pallas kernels, local(): call(functools.partial(image_kernel, members), 'image', [shape((packs, po...  2.15 us
    unnamed x11, local copies, waits for them, and re-layouts  1.78 us
    ppermute x6, waiting for transfers between devices, swapped(): lax.ppermute(value, ('grid', 'ham'), [(group, group ^ flip) for group in...  1.48 us
    pallas_call x1, Pallas kernels, local(): call(response_kernel, 'response', [shape((lines, points, padded), F32)],...  1.32 us
    pallas_call x1, Pallas kernels, local(): call(pack_kernel, 'pack', [shape((packs, points, LANES), BF16)], orbitals...  1.31 us
    pallas_call x1, Pallas kernels, local(): call(route_kernel, 'route', [shape((CAP, groups * lines, points), BF16),...  1.09 us
  transfers between devices with their start and end apart: 10, of which 4 were waited for; matrix products, arithmetic and copies ran while one was open for 0% of the time, Pallas kernels for 9%

profile of v11, /device:TPU:0, one launch (start us, length us, event | category | flops | bytes accessed | tf_op | source)
XLA Modules:
  0.0 23.7 jit_solution(11987195907935763612)
XLA Ops:
  0.6 0.0 copy-start.3
  0.6 0.0 copy-start.4
  0.6 1.3 %pack.1.refs_0_ = bf16[2,192,128]{2,1,0:T(8,128)(2,1)S(1)} custom-call(bf16[16,16,192]{2,1,0:T(8,128)(2,1)} %orbitals_ref.1), custom_call_target="tpu_custom_call" | custom-call | flops 49152 | bytes 196608 | tf_op jit(solution)/shard_map/pack/pallas_call | solution.py:320
  2.0 0.0 copy-start
  2.0 3.1 %collective-permute-start = (bf16[2,192,128]{2,1,0:T(8,128)(2,1)S(1)}, bf16[2,192,128]{2,1,0:T(8,128)(2,1)S(1)}, u32[]{:S(2)}, u32[]{:S(2)}) collective-permute-start(bf16[2,192,128]{2,1,0:T(8,128)(2,1)S(1)} %pack.1.refs_0_), channel_id=1, source_target_pairs={{24,0},{28,4},{0,8},{4,12},{8,16},{12,20},{16,24},{20,28},{25,1},{... | collective-permute-start | bytes 294920 | tf_op jit(solution)/shard_map/ppermute | solution.py:34
  5.1 3.2 %collective-permute-start.1 = (bf16[2,192,128]{2,1,0:T(8,128)(2,1)S(1)}, bf16[2,192,128]{2,1,0:T(8,128)(2,1)S(1)}, u32[]{:S(2)}, u32[]{:S(2)}) collective-permute-start(bf16[2,192,128]{2,1,0:T(8,128)(2,1)S(1)} %pack.1.refs_0_), channel_id=1, source_target_pairs={{28,0},{8,4},{4,8},{16,12},{12,16},{24,20},{20,24},{0,28},{29,1},{... | collective-permute-start | bytes 294920 | tf_op jit(solution)/shard_map/ppermute | solution.py:34
  8.3 0.0 collective-permute-start.2
  8.3 2.1 %collective-permute-start.3 = (bf16[2,192,128]{2,1,0:T(8,128)(2,1)S(1)}, bf16[2,192,128]{2,1,0:T(8,128)(2,1)S(1)}, u32[]{:S(2)}, u32[]{:S(2)}) collective-permute-start(bf16[2,192,128]{2,1,0:T(8,128)(2,1)S(1)} %pack.1.refs_0_), channel_id=1, source_target_pairs={{8,0},{12,4},{16,8},{20,12},{24,16},{28,20},{0,24},{4,28},{9,1},{1... | collective-permute-start | bytes 294920 | tf_op jit(solution)/shard_map/ppermute | solution.py:34
  10.3 1.0 %copy-done.1 = bf16[3,192,192]{2,1,0:T(8,128)(2,1)S(1)} copy-done((bf16[3,192,192]{2,1,0:T(8,128)(2,1)S(1)}, bf16[3,192,192]{2,1,0:T(8,128)(2,1)}, u32[]{:S(2)}) %copy-start.1) | copy-done | bytes 221208
  11.3 0.7 %copy-done.2 = f32[16,192]{1,0:T(8,128)S(1)} copy-done((f32[16,192]{1,0:T(8,128)S(1)}, f32[16,192]{1,0:T(8,128)}, u32[]{:S(2)}) %copy-start.2) | copy-done | bytes 12312
  12.0 1.3 %response.1.refs_5_ = f32[16,192,256]{2,1,0:T(8,128)S(1)} custom-call(f32[16,192]{1,0:T(8,128)S(1)} %copy-done.2, bf16[3,192,192]{2,1,0:T(8,128)(2,1)S(1)} %copy-done.1), custom_call_target="tpu_custom_call" | custom-call | flops 452984832 | bytes 2359296 | tf_op jit(solution)/shard_map/response/pallas_call | solution.py:335
  13.3 0.0 collective-permute-done.refs_1_
  13.4 0.5 %collective-permute-done.1.refs_2_ = bf16[2,192,128]{2,1,0:T(8,128)(2,1)S(1)} collective-permute-done((bf16[2,192,128]{2,1,0:T(8,128)(2,1)S(1)}, bf16[2,192,128]{2,1,0:T(8,128)(2,1)S(1)}, u32[]{:S(2)}, u32[]{:S(2)}) %collective-permute-start.1) | collective-permute-done | bytes 98336 | tf_op jit(solution)/shard_map/ppermute | solution.py:34
  13.9 0.4 %collective-permute-done.2.refs_3_ = bf16[2,192,128]{2,1,0:T(8,128)(2,1)S(1)} collective-permute-done((bf16[2,192,128]{2,1,0:T(8,128)(2,1)S(1)}, bf16[2,192,128]{2,1,0:T(8,128)(2,1)S(1)}, u32[]{:S(2)}, u32[]{:S(2)}) %collective-permute-start.2) | collective-permute-done | bytes 98336 | tf_op jit(solution)/shard_map/ppermute | solution.py:34
  14.3 0.0 collective-permute-done.3.refs_4_
  14.3 2.1 %image.1 = (bf16[2,192,128]{2,1,0:T(8,128)(2,1)S(1)}, bf16[4,192,128]{2,1,0:T(8,128)(2,1)S(1)}) custom-call(s32[8]{0:T(128)S(1)} %copy-done.3, bf16[2,192,128]{2,1,0:T(8,128)(2,1)S(1)} %pack.1.refs_0_, bf16[2,192,128]{2,1,0:T(8,128)(2,1)S(1)} %collective-permute-done.refs_1_, bf16[2,192,128]{2,1,0:T(8,128)(2,1)S(1)} %collective-permute-done.1.refs_2_, ...), custom_call_target="tpu_custom_call" | custom-call | flops 805306368 | bytes 2359296 | tf_op jit(solution)/shard_map/image/pallas_call | solution.py:344
  16.5 1.6 %collective-permute-start.8 = (bf16[2,192,128]{2,1,0:T(8,128)(2,1)S(1)}, bf16[2,192,128]{2,1,0:T(8,128)(2,1)S(1)}, u32[]{:S(2)}, u32[]{:S(2)}) collective-permute-start(bf16[2,192,128]{2,1,0:T(8,128)(2,1)S(1)} %get-tuple-element.11), channel_id=1, source_target_pairs={{0,2},{1,3},{2,0},{3,1},{4,6},{5,7},{6,4},{7,5},{8,10},{9,11},{10,... | collective-permute-start | bytes 294920 | tf_op jit(solution)/shard_map/ppermute | solution.py:41
  18.0 0.2 overlap.1.refs_0_
  18.2 0.1 collective-permute-start.4
  18.3 0.6 %collective-permute-start.5 = (f32[16,128]{1,0:T(8,128)S(1)}, f32[16,128]{1,0:T(8,128)S(1)}, u32[]{:S(2)}, u32[]{:S(2)}) collective-permute-start(f32[16,128]{1,0:T(8,128)S(1)} %overlap.1.refs_0_), channel_id=1, source_target_pairs={{0,2},{1,3},{2,0},{3,1},{4,6},{5,7},{6,4},{7,5},{8,10},{9,11},{10,... | collective-permute-start | bytes 24584 | tf_op jit(solution)/shard_map/ppermute | solution.py:41
  18.9 1.3 %collective-permute-start.6 = (f32[16,128]{1,0:T(8,128)S(1)}, f32[16,128]{1,0:T(8,128)S(1)}, u32[]{:S(2)}, u32[]{:S(2)}) collective-permute-start(f32[16,128]{1,0:T(8,128)S(1)} %overlap.1.refs_0_), channel_id=1, source_target_pairs={{0,3},{1,2},{2,1},{3,0},{4,7},{5,6},{6,5},{7,4},{8,11},{9,10},{10,... | collective-permute-start | bytes 24584 | tf_op jit(solution)/shard_map/ppermute | solution.py:41
  20.1 0.1 copy.7.owners_ref
  20.2 0.3 %collective-permute-start.7 = (bf16[4,192,128]{2,1,0:T(8,128)(2,1)S(1)}, bf16[4,192,128]{2,1,0:T(8,128)(2,1)S(1)}, u32[]{:S(2)}, u32[]{:S(2)}) collective-permute-start(bf16[4,192,128]{2,1,0:T(8,128)(2,1)S(1)} %get-tuple-element.8.halves_ref.refs_0_), channel_id=1, source_target_pairs={{0,1},{1,0},{2,3},{3,2},{4,5},{5,4},{6,7},{7,6},{8,9},{9,8},{10,11... | collective-permute-start | bytes 589832 | tf_op jit(solution)/shard_map/ppermute | solution.py:41
  20.6 0.6 %collective-permute-done.8.refs_2_ = bf16[2,192,128]{2,1,0:T(8,128)(2,1)S(1)} collective-permute-done((bf16[2,192,128]{2,1,0:T(8,128)(2,1)S(1)}, bf16[2,192,128]{2,1,0:T(8,128)(2,1)S(1)}, u32[]{:S(2)}, u32[]{:S(2)}) %collective-permute-start.8) | collective-permute-done | bytes 98336 | tf_op jit(solution)/shard_map/ppermute | solution.py:41
  21.1 0.0 collective-permute-start.9
  21.1 0.0 collective-permute-done.4.refs_1_
  21.1 0.9 %collective-permute-done.5.refs_2_ = f32[16,128]{1,0:T(8,128)S(1)} collective-permute-done((f32[16,128]{1,0:T(8,128)S(1)}, f32[16,128]{1,0:T(8,128)S(1)}, u32[]{:S(2)}, u32[]{:S(2)}) %collective-permute-start.5) | collective-permute-done | bytes 8224 | tf_op jit(solution)/shard_map/ppermute | solution.py:41
  22.1 0.0 collective-permute-done.6.refs_3_
  22.1 0.5 %factor.1 = (f32[16,16]{1,0:T(8,128)S(1)}, bf16[256,256]{1,0:T(8,128)(2,1)S(1)}) custom-call(s32[16,1]{1,0:T(8,128)S(1)} %copy.7.owners_ref, f32[16,128]{1,0:T(8,128)S(1)} %overlap.1.refs_0_, f32[16,128]{1,0:T(8,128)S(1)} %collective-permute-done.4.refs_1_, f32[16,128]{1,0:T(8,128)S(1)} %collective-permute-done.5.refs_2_, ...), custom_call_target="tpu_custom_call" | custom-call | flops 3000000000 | bytes 1024 | tf_op jit(solution)/shard_map/factor/pallas_call | solution.py:371
  22.6 0.0 collective-permute-done.7.refs_1_
  22.6 0.0 collective-permute-done.9.refs_3_
  22.6 1.1 %route.1 = (bf16[8,64,192]{2,1,0:T(8,128)(2,1)}, f32[16,16]{1,0:T(8,128)}) custom-call(f32[16,16]{1,0:T(8,128)S(1)} %get-tuple-element.9.overlap_ref, bf16[256,256]{1,0:T(8,128)(2,1)S(1)} %get-tuple-element.10.weights_ref, bf16[4,192,128]{2,1,0:T(8,128)(2,1)S(1)} %get-tuple-element.8.halves_ref.refs_0_, ...), custom_call_target="tpu_custom_call" | custom-call | flops 3145728 | bytes 1179648 | tf_op jit(solution)/shard_map/route/pallas_call | solution.py:379
  (5 shorter events, 0.0 us)
Async XLA Ops:
  0.6 13.7 %copy-start.3 = (s32[8]{0:T(128)S(1)}, s32[8]{0:T(128)}, u32[]{:S(2)}) copy-start(s32[8]{0:T(128)} %occupied_ref.1) | copy-start | bytes 100
  0.6 19.5 %copy-start.4 = (s32[16,1]{0,1:T(1,128)S(1)}, s32[16,1]{0,1:T(1,128)}, u32[]{:S(2)}) copy-start(s32[16,1]{0,1:T(1,128)} %param.8) | copy-start | bytes 196
  2.0 16.0 %copy-start = (bf16[16,16,192]{2,1,0:T(8,128)(2,1)S(1)}, bf16[16,16,192]{2,1,0:T(8,128)(2,1)}, u32[]{:S(2)}) copy-start(bf16[16,16,192]{2,1,0:T(8,128)(2,1)} %orbitals_ref.1) | copy-start | bytes 294916
  2.0 11.4 %collective-permute-start = (bf16[2,192,128]{2,1,0:T(8,128)(2,1)S(1)}, bf16[2,192,128]{2,1,0:T(8,128)(2,1)S(1)}, u32[]{:S(2)}, u32[]{:S(2)}) collective-permute-start(bf16[2,192,128]{2,1,0:T(8,128)(2,1)S(1)} %pack.1.refs_0_), channel_id=1, source_target_pairs={{24,0},{28,4},{0,8},{4,12},{8,16},{12,20},{16,24},{20,28},{25,1},{... | collective-permute-start | bytes 294920 | tf_op jit(solution)/shard_map/ppermute | solution.py:34
  5.1 8.8 %collective-permute-start.1 = (bf16[2,192,128]{2,1,0:T(8,128)(2,1)S(1)}, bf16[2,192,128]{2,1,0:T(8,128)(2,1)S(1)}, u32[]{:S(2)}, u32[]{:S(2)}) collective-permute-start(bf16[2,192,128]{2,1,0:T(8,128)(2,1)S(1)} %pack.1.refs_0_), channel_id=1, source_target_pairs={{28,0},{8,4},{4,8},{16,12},{12,16},{24,20},{20,24},{0,28},{29,1},{... | collective-permute-start | bytes 294920 | tf_op jit(solution)/shard_map/ppermute | solution.py:34
  8.3 6.0 %collective-permute-start.2 = (bf16[2,192,128]{2,1,0:T(8,128)(2,1)S(1)}, bf16[2,192,128]{2,1,0:T(8,128)(2,1)S(1)}, u32[]{:S(2)}, u32[]{:S(2)}) collective-permute-start(bf16[2,192,128]{2,1,0:T(8,128)(2,1)S(1)} %pack.1.refs_0_), channel_id=1, source_target_pairs={{4,0},{0,4},{12,8},{8,12},{20,16},{16,20},{28,24},{24,28},{5,1},{1... | collective-permute-start | bytes 294920 | tf_op jit(solution)/shard_map/ppermute | solution.py:34
  8.3 6.0 %collective-permute-start.3 = (bf16[2,192,128]{2,1,0:T(8,128)(2,1)S(1)}, bf16[2,192,128]{2,1,0:T(8,128)(2,1)S(1)}, u32[]{:S(2)}, u32[]{:S(2)}) collective-permute-start(bf16[2,192,128]{2,1,0:T(8,128)(2,1)S(1)} %pack.1.refs_0_), channel_id=1, source_target_pairs={{8,0},{12,4},{16,8},{20,12},{24,16},{28,20},{0,24},{4,28},{9,1},{1... | collective-permute-start | bytes 294920 | tf_op jit(solution)/shard_map/ppermute | solution.py:34
  10.3 1.0 %copy-start.1 = (bf16[3,192,192]{2,1,0:T(8,128)(2,1)S(1)}, bf16[3,192,192]{2,1,0:T(8,128)(2,1)}, u32[]{:S(2)}) copy-start(bf16[3,192,192]{2,1,0:T(8,128)(2,1)} %constant.3.tables_ref) | copy-start | bytes 663556
  11.3 0.7 %copy-start.2 = (f32[16,192]{1,0:T(8,128)S(1)}, f32[16,192]{1,0:T(8,128)}, u32[]{:S(2)}) copy-start(f32[16,192]{1,0:T(8,128)} %coulomb_ref.1) | copy-start | bytes 36868
  16.5 4.7 %collective-permute-start.8 = (bf16[2,192,128]{2,1,0:T(8,128)(2,1)S(1)}, bf16[2,192,128]{2,1,0:T(8,128)(2,1)S(1)}, u32[]{:S(2)}, u32[]{:S(2)}) collective-permute-start(bf16[2,192,128]{2,1,0:T(8,128)(2,1)S(1)} %get-tuple-element.11), channel_id=1, source_target_pairs={{0,2},{1,3},{2,0},{3,1},{4,6},{5,7},{6,4},{7,5},{8,10},{9,11},{10,... | collective-permute-start | bytes 294920 | tf_op jit(solution)/shard_map/ppermute | solution.py:41
  18.2 2.9 %collective-permute-start.4 = (f32[16,128]{1,0:T(8,128)S(1)}, f32[16,128]{1,0:T(8,128)S(1)}, u32[]{:S(2)}, u32[]{:S(2)}) collective-permute-start(f32[16,128]{1,0:T(8,128)S(1)} %overlap.1.refs_0_), channel_id=1, source_target_pairs={{0,1},{1,0},{2,3},{3,2},{4,5},{5,4},{6,7},{7,6},{8,9},{9,8},{10,11... | collective-permute-start | bytes 24584 | tf_op jit(solution)/shard_map/ppermute | solution.py:41
  18.3 3.8 %collective-permute-start.5 = (f32[16,128]{1,0:T(8,128)S(1)}, f32[16,128]{1,0:T(8,128)S(1)}, u32[]{:S(2)}, u32[]{:S(2)}) collective-permute-start(f32[16,128]{1,0:T(8,128)S(1)} %overlap.1.refs_0_), channel_id=1, source_target_pairs={{0,2},{1,3},{2,0},{3,1},{4,6},{5,7},{6,4},{7,5},{8,10},{9,11},{10,... | collective-permute-start | bytes 24584 | tf_op jit(solution)/shard_map/ppermute | solution.py:41
  18.9 3.2 %collective-permute-start.6 = (f32[16,128]{1,0:T(8,128)S(1)}, f32[16,128]{1,0:T(8,128)S(1)}, u32[]{:S(2)}, u32[]{:S(2)}) collective-permute-start(f32[16,128]{1,0:T(8,128)S(1)} %overlap.1.refs_0_), channel_id=1, source_target_pairs={{0,3},{1,2},{2,1},{3,0},{4,7},{5,6},{6,5},{7,4},{8,11},{9,10},{10,... | collective-permute-start | bytes 24584 | tf_op jit(solution)/shard_map/ppermute | solution.py:41
  20.2 2.4 %collective-permute-start.7 = (bf16[4,192,128]{2,1,0:T(8,128)(2,1)S(1)}, bf16[4,192,128]{2,1,0:T(8,128)(2,1)S(1)}, u32[]{:S(2)}, u32[]{:S(2)}) collective-permute-start(bf16[4,192,128]{2,1,0:T(8,128)(2,1)S(1)} %get-tuple-element.8.halves_ref.refs_0_), channel_id=1, source_target_pairs={{0,1},{1,0},{2,3},{3,2},{4,5},{5,4},{6,7},{7,6},{8,9},{9,8},{10,11... | collective-permute-start | bytes 589832 | tf_op jit(solution)/shard_map/ppermute | solution.py:41
  21.1 1.5 %collective-permute-start.9 = (bf16[2,192,128]{2,1,0:T(8,128)(2,1)S(1)}, bf16[2,192,128]{2,1,0:T(8,128)(2,1)S(1)}, u32[]{:S(2)}, u32[]{:S(2)}) collective-permute-start(bf16[2,192,128]{2,1,0:T(8,128)(2,1)S(1)} %collective-permute-done.8.refs_2_), channel_id=1, source_target_pairs={{0,1},{1,0},{2,3},{3,2},{4,5},{5,4},{6,7},{7,6},{8,9},{9,8},{10,11... | collective-permute-start | bytes 294920 | tf_op jit(solution)/shard_map/ppermute | solution.py:41

commit v12 on v10

--- a/solution.py
+++ b/solution.py
@@ -18,10 +18,11 @@
 F32, BF16 = jnp.float32, jnp.bfloat16
 
 
+STEPS = (-2, -1, 1, 2)
+
+
 def sources(block, count):
-    odd = block % 2
-    steps = (-2, 2 * odd - 1, 1 - 2 * odd, 2)
-    return [(block + step + count) % count for step in steps]
+    return [(block + step + count) % count for step in STEPS]
 
 
 def exchanged(value):

time: 23.8 us -> 23.9 us (level)
  waiting for transfers between devices: 2.42 us -> 2.79 us
  starting transfers between devices: 12.2 us -> 11.9 us
    ppermute x4, waiting for transfers between devices: 0.95 us -> 1.32 us  [exchanged(): lax.ppermute(value, 'band', [(row[turn], block) for block, row in enumera...]
    ppermute x4, starting transfers between devices: 8.36 us -> 8.09 us  [exchanged(): lax.ppermute(value, 'band', [(row[turn], block) for block, row in enumera...]
where the time goes in v12:
time: 23.9 us; the launch traced here: 23.6 us
  starting transfers between devices  11.9 us (50%)
  Pallas kernels  5.48 us (23%)
  waiting for transfers between devices  2.79 us (12%)
  local copies, waits for them, and re-layouts  2.67 us (11%)
  between operations  0.72 us (3%)
    ppermute x4, starting transfers between devices, exchanged(): lax.ppermute(value, 'band', [(row[turn], block) for block, row in enumera...  8.09 us
    ppermute x6, starting transfers between devices, swapped(): lax.ppermute(value, ('grid', 'ham'), [(group, group ^ flip) for group in...  3.84 us
    unnamed x13, local copies, waits for them, and re-layouts  2.67 us
    pallas_call x1, Pallas kernels, local(): call(functools.partial(image_kernel, members), 'image', [shape((packs, po...  2.13 us
    ppermute x6, waiting for transfers between devices, swapped(): lax.ppermute(value, ('grid', 'ham'), [(group, group ^ flip) for group in...  1.47 us
    ppermute x4, waiting for transfers between devices, exchanged(): lax.ppermute(value, 'band', [(row[turn], block) for block, row in enumera...  1.32 us
    pallas_call x1, Pallas kernels, local(): call(response_kernel, 'response', [shape((lines, points, padded), F32)],...  1.31 us
    pallas_call x1, Pallas kernels, local(): call(route_kernel, 'route', [shape((CAP, groups * lines, points), BF16),...  1.08 us
  transfers between devices with their start and end apart: 10, of which 4 were waited for; matrix products, arithmetic and copies ran while one was open for 0% of the time, Pallas kernels for 9%

profile of v12, /device:TPU:0, one launch (start us, length us, event | category | flops | bytes accessed | tf_op | source)
XLA Modules:
  0.0 23.6 jit_solution(9936729324872397151)
XLA Ops:
  0.6 0.0 copy-start
  0.6 0.9 %copy-done = bf16[16,16,192]{2,1,0:T(8,128)(2,1)S(1)} copy-done((bf16[16,16,192]{2,1,0:T(8,128)(2,1)S(1)}, bf16[16,16,192]{2,1,0:T(8,128)(2,1)}, u32[]{:S(2)}) %copy-start) | copy-done | bytes 98328
  1.5 0.2 pack.1.refs_0_
  1.8 0.0 copy-start.1
  1.8 3.1 %collective-permute-start = (bf16[2,192,128]{2,1,0:T(8,128)(2,1)S(1)}, bf16[2,192,128]{2,1,0:T(8,128)(2,1)S(1)}, u32[]{:S(2)}, u32[]{:S(2)}) collective-permute-start(bf16[2,192,128]{2,1,0:T(8,128)(2,1)S(1)} %pack.1.refs_0_), channel_id=1, source_target_pairs={{24,0},{28,4},{0,8},{4,12},{8,16},{12,20},{16,24},{20,28},{25,1},{... | collective-permute-start | bytes 294920 | tf_op jit(solution)/shard_map/ppermute | solution.py:33
  4.9 1.5 %collective-permute-start.1 = (bf16[2,192,128]{2,1,0:T(8,128)(2,1)S(1)}, bf16[2,192,128]{2,1,0:T(8,128)(2,1)S(1)}, u32[]{:S(2)}, u32[]{:S(2)}) collective-permute-start(bf16[2,192,128]{2,1,0:T(8,128)(2,1)S(1)} %pack.1.refs_0_), channel_id=1, source_target_pairs={{28,0},{0,4},{4,8},{8,12},{12,16},{16,20},{20,24},{24,28},{29,1},{... | collective-permute-start | bytes 294920 | tf_op jit(solution)/shard_map/ppermute | solution.py:33
  6.4 3.2 %collective-permute-start.2 = (bf16[2,192,128]{2,1,0:T(8,128)(2,1)S(1)}, bf16[2,192,128]{2,1,0:T(8,128)(2,1)S(1)}, u32[]{:S(2)}, u32[]{:S(2)}) collective-permute-start(bf16[2,192,128]{2,1,0:T(8,128)(2,1)S(1)} %pack.1.refs_0_), channel_id=1, source_target_pairs={{4,0},{8,4},{12,8},{16,12},{20,16},{24,20},{28,24},{0,28},{5,1},{9... | collective-permute-start | bytes 294920 | tf_op jit(solution)/shard_map/ppermute | solution.py:33
  9.6 0.3 %collective-permute-start.3 = (bf16[2,192,128]{2,1,0:T(8,128)(2,1)S(1)}, bf16[2,192,128]{2,1,0:T(8,128)(2,1)S(1)}, u32[]{:S(2)}, u32[]{:S(2)}) collective-permute-start(bf16[2,192,128]{2,1,0:T(8,128)(2,1)S(1)} %pack.1.refs_0_), channel_id=1, source_target_pairs={{8,0},{12,4},{16,8},{20,12},{24,16},{28,20},{0,24},{4,28},{9,1},{1... | collective-permute-start | bytes 294920 | tf_op jit(solution)/shard_map/ppermute | solution.py:33
  9.9 1.0 %copy-done.2 = bf16[3,192,192]{2,1,0:T(8,128)(2,1)S(1)} copy-done((bf16[3,192,192]{2,1,0:T(8,128)(2,1)S(1)}, bf16[3,192,192]{2,1,0:T(8,128)(2,1)}, u32[]{:S(2)}) %copy-start.2) | copy-done | bytes 221208
  10.9 0.7 %copy-done.3 = f32[16,192]{1,0:T(8,128)S(1)} copy-done((f32[16,192]{1,0:T(8,128)S(1)}, f32[16,192]{1,0:T(8,128)}, u32[]{:S(2)}) %copy-start.3) | copy-done | bytes 12312
  11.6 1.3 %response.1.refs_5_ = f32[16,192,256]{2,1,0:T(8,128)S(1)} custom-call(f32[16,192]{1,0:T(8,128)S(1)} %copy-done.3, bf16[3,192,192]{2,1,0:T(8,128)(2,1)S(1)} %copy-done.2), custom_call_target="tpu_custom_call" | custom-call | flops 452984832 | bytes 2359296 | tf_op jit(solution)/shard_map/response/pallas_call | solution.py:317
  12.9 0.0 collective-permute-done.refs_1_
  12.9 0.8 %collective-permute-done.1.refs_2_ = bf16[2,192,128]{2,1,0:T(8,128)(2,1)S(1)} collective-permute-done((bf16[2,192,128]{2,1,0:T(8,128)(2,1)S(1)}, bf16[2,192,128]{2,1,0:T(8,128)(2,1)S(1)}, u32[]{:S(2)}, u32[]{:S(2)}) %collective-permute-start.1) | collective-permute-done | bytes 98336 | tf_op jit(solution)/shard_map/ppermute | solution.py:33
  13.7 0.0 collective-permute-done.2.refs_3_
  13.7 0.5 %collective-permute-done.3.refs_4_ = bf16[2,192,128]{2,1,0:T(8,128)(2,1)S(1)} collective-permute-done((bf16[2,192,128]{2,1,0:T(8,128)(2,1)S(1)}, bf16[2,192,128]{2,1,0:T(8,128)(2,1)S(1)}, u32[]{:S(2)}, u32[]{:S(2)}) %collective-permute-start.3) | collective-permute-done | bytes 98336 | tf_op jit(solution)/shard_map/ppermute | solution.py:33
  14.2 2.1 %image.1 = (bf16[2,192,128]{2,1,0:T(8,128)(2,1)S(1)}, bf16[4,192,128]{2,1,0:T(8,128)(2,1)S(1)}) custom-call(s32[8]{0:T(128)S(1)} %copy-done.4, bf16[2,192,128]{2,1,0:T(8,128)(2,1)S(1)} %pack.1.refs_0_, bf16[2,192,128]{2,1,0:T(8,128)(2,1)S(1)} %collective-permute-done.refs_1_, bf16[2,192,128]{2,1,0:T(8,128)(2,1)S(1)} %collective-permute-done.1.refs_2_, ...), custom_call_target="tpu_custom_call" | custom-call | flops 805306368 | bytes 2359296 | tf_op jit(solution)/shard_map/image/pallas_call | solution.py:326
  16.4 1.6 %collective-permute-start.8 = (bf16[2,192,128]{2,1,0:T(8,128)(2,1)S(1)}, bf16[2,192,128]{2,1,0:T(8,128)(2,1)S(1)}, u32[]{:S(2)}, u32[]{:S(2)}) collective-permute-start(bf16[2,192,128]{2,1,0:T(8,128)(2,1)S(1)} %get-tuple-element.11), channel_id=1, source_target_pairs={{0,2},{1,3},{2,0},{3,1},{4,6},{5,7},{6,4},{7,5},{8,10},{9,11},{10,... | collective-permute-start | bytes 294920 | tf_op jit(solution)/shard_map/ppermute | solution.py:40
  17.9 0.2 overlap.1.refs_0_
  18.1 0.1 collective-permute-start.4
  18.2 0.6 %collective-permute-start.5 = (f32[16,128]{1,0:T(8,128)S(1)}, f32[16,128]{1,0:T(8,128)S(1)}, u32[]{:S(2)}, u32[]{:S(2)}) collective-permute-start(f32[16,128]{1,0:T(8,128)S(1)} %overlap.1.refs_0_), channel_id=1, source_target_pairs={{0,2},{1,3},{2,0},{3,1},{4,6},{5,7},{6,4},{7,5},{8,10},{9,11},{10,... | collective-permute-start | bytes 24584 | tf_op jit(solution)/shard_map/ppermute | solution.py:40
  18.8 1.3 %collective-permute-start.6 = (f32[16,128]{1,0:T(8,128)S(1)}, f32[16,128]{1,0:T(8,128)S(1)}, u32[]{:S(2)}, u32[]{:S(2)}) collective-permute-start(f32[16,128]{1,0:T(8,128)S(1)} %overlap.1.refs_0_), channel_id=1, source_target_pairs={{0,3},{1,2},{2,1},{3,0},{4,7},{5,6},{6,5},{7,4},{8,11},{9,10},{10,... | collective-permute-start | bytes 24584 | tf_op jit(solution)/shard_map/ppermute | solution.py:40
  20.0 0.1 copy.7.owners_ref
  20.1 0.3 %collective-permute-start.7 = (bf16[4,192,128]{2,1,0:T(8,128)(2,1)S(1)}, bf16[4,192,128]{2,1,0:T(8,128)(2,1)S(1)}, u32[]{:S(2)}, u32[]{:S(2)}) collective-permute-start(bf16[4,192,128]{2,1,0:T(8,128)(2,1)S(1)} %get-tuple-element.8.halves_ref.refs_0_), channel_id=1, source_target_pairs={{0,1},{1,0},{2,3},{3,2},{4,5},{5,4},{6,7},{7,6},{8,9},{9,8},{10,11... | collective-permute-start | bytes 589832 | tf_op jit(solution)/shard_map/ppermute | solution.py:40
  20.5 0.6 %collective-permute-done.8.refs_2_ = bf16[2,192,128]{2,1,0:T(8,128)(2,1)S(1)} collective-permute-done((bf16[2,192,128]{2,1,0:T(8,128)(2,1)S(1)}, bf16[2,192,128]{2,1,0:T(8,128)(2,1)S(1)}, u32[]{:S(2)}, u32[]{:S(2)}) %collective-permute-start.8) | collective-permute-done | bytes 98336 | tf_op jit(solution)/shard_map/ppermute | solution.py:40
  21.0 0.0 collective-permute-start.9
  21.0 0.0 collective-permute-done.4.refs_1_
  21.0 0.9 %collective-permute-done.5.refs_2_ = f32[16,128]{1,0:T(8,128)S(1)} collective-permute-done((f32[16,128]{1,0:T(8,128)S(1)}, f32[16,128]{1,0:T(8,128)S(1)}, u32[]{:S(2)}, u32[]{:S(2)}) %collective-permute-start.5) | collective-permute-done | bytes 8224 | tf_op jit(solution)/shard_map/ppermute | solution.py:40
  21.9 0.0 collective-permute-done.6.refs_3_
  22.0 0.5 %factor.1 = (f32[16,16]{1,0:T(8,128)S(1)}, bf16[256,256]{1,0:T(8,128)(2,1)S(1)}) custom-call(s32[16,1]{1,0:T(8,128)S(1)} %copy.7.owners_ref, f32[16,128]{1,0:T(8,128)S(1)} %overlap.1.refs_0_, f32[16,128]{1,0:T(8,128)S(1)} %collective-permute-done.4.refs_1_, f32[16,128]{1,0:T(8,128)S(1)} %collective-permute-done.5.refs_2_, ...), custom_call_target="tpu_custom_call" | custom-call | flops 3000000000 | bytes 1024 | tf_op jit(solution)/shard_map/factor/pallas_call | solution.py:353
  22.5 0.0 collective-permute-done.7.refs_1_
  22.5 0.0 collective-permute-done.9.refs_3_
  22.5 1.1 %route.1 = (bf16[8,64,192]{2,1,0:T(8,128)(2,1)}, f32[16,16]{1,0:T(8,128)}) custom-call(f32[16,16]{1,0:T(8,128)S(1)} %get-tuple-element.9.overlap_ref, bf16[256,256]{1,0:T(8,128)(2,1)S(1)} %get-tuple-element.10.weights_ref, bf16[4,192,128]{2,1,0:T(8,128)(2,1)S(1)} %get-tuple-element.8.halves_ref.refs_0_, ...), custom_call_target="tpu_custom_call" | custom-call | flops 3145728 | bytes 1179648 | tf_op jit(solution)/shard_map/route/pallas_call | solution.py:361
  (7 shorter events, 0.0 us)
Async XLA Ops:
  0.6 0.9 %copy-start = (bf16[16,16,192]{2,1,0:T(8,128)(2,1)S(1)}, bf16[16,16,192]{2,1,0:T(8,128)(2,1)}, u32[]{:S(2)}) copy-start(bf16[16,16,192]{2,1,0:T(8,128)(2,1)} %orbitals_ref.3) | copy-start | bytes 294916
  1.5 12.7 %copy-start.4 = (s32[8]{0:T(128)S(1)}, s32[8]{0:T(128)}, u32[]{:S(2)}) copy-start(s32[8]{0:T(128)} %occupied_ref.1) | copy-start | bytes 100
  1.5 18.5 %copy-start.5 = (s32[16,1]{0,1:T(1,128)S(1)}, s32[16,1]{0,1:T(1,128)}, u32[]{:S(2)}) copy-start(s32[16,1]{0,1:T(1,128)} %param.8) | copy-start | bytes 196
  1.8 16.1 %copy-start.1 = (bf16[16,16,192]{2,1,0:T(8,128)(2,1)S(1)}, bf16[16,16,192]{2,1,0:T(8,128)(2,1)}, u32[]{:S(2)}) copy-start(bf16[16,16,192]{2,1,0:T(8,128)(2,1)} %orbitals_ref.3) | copy-start | bytes 294916
  1.8 11.1 %collective-permute-start = (bf16[2,192,128]{2,1,0:T(8,128)(2,1)S(1)}, bf16[2,192,128]{2,1,0:T(8,128)(2,1)S(1)}, u32[]{:S(2)}, u32[]{:S(2)}) collective-permute-start(bf16[2,192,128]{2,1,0:T(8,128)(2,1)S(1)} %pack.1.refs_0_), channel_id=1, source_target_pairs={{24,0},{28,4},{0,8},{4,12},{8,16},{12,20},{16,24},{20,28},{25,1},{... | collective-permute-start | bytes 294920 | tf_op jit(solution)/shard_map/ppermute | solution.py:33
  4.9 8.9 %collective-permute-start.1 = (bf16[2,192,128]{2,1,0:T(8,128)(2,1)S(1)}, bf16[2,192,128]{2,1,0:T(8,128)(2,1)S(1)}, u32[]{:S(2)}, u32[]{:S(2)}) collective-permute-start(bf16[2,192,128]{2,1,0:T(8,128)(2,1)S(1)} %pack.1.refs_0_), channel_id=1, source_target_pairs={{28,0},{0,4},{4,8},{8,12},{12,16},{16,20},{20,24},{24,28},{29,1},{... | collective-permute-start | bytes 294920 | tf_op jit(solution)/shard_map/ppermute | solution.py:33
  6.4 7.3 %collective-permute-start.2 = (bf16[2,192,128]{2,1,0:T(8,128)(2,1)S(1)}, bf16[2,192,128]{2,1,0:T(8,128)(2,1)S(1)}, u32[]{:S(2)}, u32[]{:S(2)}) collective-permute-start(bf16[2,192,128]{2,1,0:T(8,128)(2,1)S(1)} %pack.1.refs_0_), channel_id=1, source_target_pairs={{4,0},{8,4},{12,8},{16,12},{20,16},{24,20},{28,24},{0,28},{5,1},{9... | collective-permute-start | bytes 294920 | tf_op jit(solution)/shard_map/ppermute | solution.py:33
  9.6 4.6 %collective-permute-start.3 = (bf16[2,192,128]{2,1,0:T(8,128)(2,1)S(1)}, bf16[2,192,128]{2,1,0:T(8,128)(2,1)S(1)}, u32[]{:S(2)}, u32[]{:S(2)}) collective-permute-start(bf16[2,192,128]{2,1,0:T(8,128)(2,1)S(1)} %pack.1.refs_0_), channel_id=1, source_target_pairs={{8,0},{12,4},{16,8},{20,12},{24,16},{28,20},{0,24},{4,28},{9,1},{1... | collective-permute-start | bytes 294920 | tf_op jit(solution)/shard_map/ppermute | solution.py:33
  9.9 1.0 %copy-start.2 = (bf16[3,192,192]{2,1,0:T(8,128)(2,1)S(1)}, bf16[3,192,192]{2,1,0:T(8,128)(2,1)}, u32[]{:S(2)}) copy-start(bf16[3,192,192]{2,1,0:T(8,128)(2,1)} %constant.3.tables_ref) | copy-start | bytes 663556
  10.8 0.7 %copy-start.3 = (f32[16,192]{1,0:T(8,128)S(1)}, f32[16,192]{1,0:T(8,128)}, u32[]{:S(2)}) copy-start(f32[16,192]{1,0:T(8,128)} %coulomb_ref.1) | copy-start | bytes 36868
  16.4 4.7 %collective-permute-start.8 = (bf16[2,192,128]{2,1,0:T(8,128)(2,1)S(1)}, bf16[2,192,128]{2,1,0:T(8,128)(2,1)S(1)}, u32[]{:S(2)}, u32[]{:S(2)}) collective-permute-start(bf16[2,192,128]{2,1,0:T(8,128)(2,1)S(1)} %get-tuple-element.11), channel_id=1, source_target_pairs={{0,2},{1,3},{2,0},{3,1},{4,6},{5,7},{6,4},{7,5},{8,10},{9,11},{10,... | collective-permute-start | bytes 294920 | tf_op jit(solution)/shard_map/ppermute | solution.py:40
  18.1 2.9 %collective-permute-start.4 = (f32[16,128]{1,0:T(8,128)S(1)}, f32[16,128]{1,0:T(8,128)S(1)}, u32[]{:S(2)}, u32[]{:S(2)}) collective-permute-start(f32[16,128]{1,0:T(8,128)S(1)} %overlap.1.refs_0_), channel_id=1, source_target_pairs={{0,1},{1,0},{2,3},{3,2},{4,5},{5,4},{6,7},{7,6},{8,9},{9,8},{10,11... | collective-permute-start | bytes 24584 | tf_op jit(solution)/shard_map/ppermute | solution.py:40
  18.2 3.8 %collective-permute-start.5 = (f32[16,128]{1,0:T(8,128)S(1)}, f32[16,128]{1,0:T(8,128)S(1)}, u32[]{:S(2)}, u32[]{:S(2)}) collective-permute-start(f32[16,128]{1,0:T(8,128)S(1)} %overlap.1.refs_0_), channel_id=1, source_target_pairs={{0,2},{1,3},{2,0},{3,1},{4,6},{5,7},{6,4},{7,5},{8,10},{9,11},{10,... | collective-permute-start | bytes 24584 | tf_op jit(solution)/shard_map/ppermute | solution.py:40
  18.8 3.2 %collective-permute-start.6 = (f32[16,128]{1,0:T(8,128)S(1)}, f32[16,128]{1,0:T(8,128)S(1)}, u32[]{:S(2)}, u32[]{:S(2)}) collective-permute-start(f32[16,128]{1,0:T(8,128)S(1)} %overlap.1.refs_0_), channel_id=1, source_target_pairs={{0,3},{1,2},{2,1},{3,0},{4,7},{5,6},{6,5},{7,4},{8,11},{9,10},{10,... | collective-permute-start | bytes 24584 | tf_op jit(solution)/shard_map/ppermute | solution.py:40
  20.1 2.4 %collective-permute-start.7 = (bf16[4,192,128]{2,1,0:T(8,128)(2,1)S(1)}, bf16[4,192,128]{2,1,0:T(8,128)(2,1)S(1)}, u32[]{:S(2)}, u32[]{:S(2)}) collective-permute-start(bf16[4,192,128]{2,1,0:T(8,128)(2,1)S(1)} %get-tuple-element.8.halves_ref.refs_0_), channel_id=1, source_target_pairs={{0,1},{1,0},{2,3},{3,2},{4,5},{5,4},{6,7},{7,6},{8,9},{9,8},{10,11... | collective-permute-start | bytes 589832 | tf_op jit(solution)/shard_map/ppermute | solution.py:40
  21.0 1.5 %collective-permute-start.9 = (bf16[2,192,128]{2,1,0:T(8,128)(2,1)S(1)}, bf16[2,192,128]{2,1,0:T(8,128)(2,1)S(1)}, u32[]{:S(2)}, u32[]{:S(2)}) collective-permute-start(bf16[2,192,128]{2,1,0:T(8,128)(2,1)S(1)} %collective-permute-done.8.refs_2_), channel_id=1, source_target_pairs={{0,1},{1,0},{2,3},{3,2},{4,5},{5,4},{6,7},{7,6},{8,9},{9,8},{10,11... | collective-permute-start | bytes 294920 | tf_op jit(solution)/shard_map/ppermute | solution.py:40

commit v13 on v7

--- a/solution.py
+++ b/solution.py
@@ -140,11 +140,13 @@
     quarters = [lane_quarter(lane, turn) for turn in turns]
     step = lane % (LANES // 4) // members
     apart, merged = 1, (0, 2, 3, 4)
-    blank = jnp.zeros((padded - points, 2 * LANES), BF16)
+    spare = padded - points
+    cuts = points // spare
+    assert cuts * spare == points and LANES % spare == 0
+    blank = jnp.zeros((spare, 2 * LANES), BF16)
     for pack in range(packs):
         tiles = [block[pack] for block in blocks]
-        native = jnp.concatenate([tiles[0], blank[:, :LANES]], axis=0)
-        image = jnp.zeros((points, LANES), F32)
+        kernels = [[] for _ in range(cuts)]
         for quarter in range(4):
             here = [(q == quarter) for q in quarters]
             together = sum(tiles[m] * here[m].astype(F32).astype(BF16) for m in merged)
@@ -159,12 +161,26 @@
             gram = dot32(masked, jnp.concatenate([window, blank], axis=0), NT)
             first = pack * span + quarter * per
             response = response_ref[first : first + per].reshape(per * points, padded)
-            high, low = halves(gram * response)
-            fields = dot32(jnp.concatenate([high, low], axis=0), native)
-            for k in range(per):
-                a, b = k * points, (per + k) * points
-                field = fields[a : a + points] + fields[b : b + points]
-                image = jnp.where(own_line == quarter * per + k, field, image)
+            weighted = gram * response
+            for place in range(0, per * points, spare):
+                cut = place // spare % cuts
+                part = weighted[place : place + spare]
+                tile = cut * spare // LANES * LANES
+                _, low = split(part[:, tile : tile + LANES])
+                shift = LANES - spare - cut * spare % LANES
+                low = pltpu.roll(low, shift, axis=1) if shift else low
+                last = jnp.where(lane < LANES - spare, part[:, -LANES:], low)
+                part = jnp.concatenate([part[:, :-LANES], last], axis=1)
+                kernels[cut].append(part.astype(BF16))
+        image = []
+        for cut in range(cuts):
+            native = jnp.concatenate([tiles[0], tiles[0][cut * spare : (cut + 1) * spare]], axis=0)
+            fields = dot32(jnp.concatenate(kernels[cut], axis=0), native)
+            rows = jnp.zeros((spare, LANES), F32)
+            for line in range(span):
+                rows = jnp.where(own_line == line, fields[line * spare : (line + 1) * spare], rows)
+            image.append(rows)
+        image = jnp.concatenate(image, axis=0)
         high, low = halves(image)
         high_ref[pack] = high
         halves_ref[pack] = high

time: 23.9 us -> 23.6 us (0.987)
  Pallas kernels: 5.65 us -> 5.33 us
    pallas_call x1, Pallas kernels: 2.3 us -> 1.98 us  [local(): call(functools.partial(image_kernel, members), 'image', [shape((packs, po...]
where the time goes in v13:
time: 23.6 us; the launch traced here: 23.3 us
  starting transfers between devices  12.2 us (52%)
  Pallas kernels  5.33 us (23%)
  local copies, waits for them, and re-layouts  2.67 us (11%)
  waiting for transfers between devices  2.42 us (10%)
  between operations  0.72 us (3%)
    ppermute x4, starting transfers between devices, exchanged(): lax.ppermute(value, 'band', [(row[turn], block) for block, row in enumera...  8.36 us
    ppermute x6, starting transfers between devices, swapped(): lax.ppermute(value, ('grid', 'ham'), [(group, group ^ flip) for group in...  3.84 us
    unnamed x13, local copies, waits for them, and re-layouts  2.67 us
    pallas_call x1, Pallas kernels, local(): call(functools.partial(image_kernel, members), 'image', [shape((packs, po...  1.98 us
    ppermute x6, waiting for transfers between devices, swapped(): lax.ppermute(value, ('grid', 'ham'), [(group, group ^ flip) for group in...  1.47 us
    pallas_call x1, Pallas kernels, local(): call(response_kernel, 'response', [shape((lines, points, padded), F32)],...  1.31 us
    pallas_call x1, Pallas kernels, local(): call(route_kernel, 'route', [shape((CAP, groups * lines, points), BF16),...  1.08 us
    ppermute x4, waiting for transfers between devices, exchanged(): lax.ppermute(value, 'band', [(row[turn], block) for block, row in enumera...  0.95 us
  transfers between devices with their start and end apart: 10, of which 4 were waited for; matrix products, arithmetic and copies ran while one was open for 0% of the time, Pallas kernels for 9%

profile of v13, /device:TPU:0, one launch (start us, length us, event | category | flops | bytes accessed | tf_op | source)
XLA Modules:
  0.0 23.3 jit_solution(10078829917872842652)
XLA Ops:
  0.6 0.0 copy-start
  0.6 0.9 %copy-done = bf16[16,16,192]{2,1,0:T(8,128)(2,1)S(1)} copy-done((bf16[16,16,192]{2,1,0:T(8,128)(2,1)S(1)}, bf16[16,16,192]{2,1,0:T(8,128)(2,1)}, u32[]{:S(2)}) %copy-start) | copy-done | bytes 98328
  1.5 0.2 pack.1.refs_0_
  1.8 0.0 copy-start.1
  1.8 3.1 %collective-permute-start = (bf16[2,192,128]{2,1,0:T(8,128)(2,1)S(1)}, bf16[2,192,128]{2,1,0:T(8,128)(2,1)S(1)}, u32[]{:S(2)}, u32[]{:S(2)}) collective-permute-start(bf16[2,192,128]{2,1,0:T(8,128)(2,1)S(1)} %pack.1.refs_0_), channel_id=1, source_target_pairs={{24,0},{28,4},{0,8},{4,12},{8,16},{12,20},{16,24},{20,28},{25,1},{... | collective-permute-start | bytes 294920 | tf_op jit(solution)/shard_map/ppermute | solution.py:32
  4.9 3.2 %collective-permute-start.1 = (bf16[2,192,128]{2,1,0:T(8,128)(2,1)S(1)}, bf16[2,192,128]{2,1,0:T(8,128)(2,1)S(1)}, u32[]{:S(2)}, u32[]{:S(2)}) collective-permute-start(bf16[2,192,128]{2,1,0:T(8,128)(2,1)S(1)} %pack.1.refs_0_), channel_id=1, source_target_pairs={{28,0},{8,4},{4,8},{16,12},{12,16},{24,20},{20,24},{0,28},{29,1},{... | collective-permute-start | bytes 294920 | tf_op jit(solution)/shard_map/ppermute | solution.py:32
  8.1 0.0 collective-permute-start.2
  8.1 2.1 %collective-permute-start.3 = (bf16[2,192,128]{2,1,0:T(8,128)(2,1)S(1)}, bf16[2,192,128]{2,1,0:T(8,128)(2,1)S(1)}, u32[]{:S(2)}, u32[]{:S(2)}) collective-permute-start(bf16[2,192,128]{2,1,0:T(8,128)(2,1)S(1)} %pack.1.refs_0_), channel_id=1, source_target_pairs={{8,0},{12,4},{16,8},{20,12},{24,16},{28,20},{0,24},{4,28},{9,1},{1... | collective-permute-start | bytes 294920 | tf_op jit(solution)/shard_map/ppermute | solution.py:32
  10.2 1.0 %copy-done.2 = bf16[3,192,192]{2,1,0:T(8,128)(2,1)S(1)} copy-done((bf16[3,192,192]{2,1,0:T(8,128)(2,1)S(1)}, bf16[3,192,192]{2,1,0:T(8,128)(2,1)}, u32[]{:S(2)}) %copy-start.2) | copy-done | bytes 221208
  11.1 0.7 %copy-done.3 = f32[16,192]{1,0:T(8,128)S(1)} copy-done((f32[16,192]{1,0:T(8,128)S(1)}, f32[16,192]{1,0:T(8,128)}, u32[]{:S(2)}) %copy-start.3) | copy-done | bytes 12312
  11.8 1.3 %response.1.refs_5_ = f32[16,192,256]{2,1,0:T(8,128)S(1)} custom-call(f32[16,192]{1,0:T(8,128)S(1)} %copy-done.3, bf16[3,192,192]{2,1,0:T(8,128)(2,1)S(1)} %copy-done.2), custom_call_target="tpu_custom_call" | custom-call | flops 452984832 | bytes 2359296 | tf_op jit(solution)/shard_map/response/pallas_call | solution.py:330
  13.2 0.0 collective-permute-done.refs_1_
  13.2 0.6 %collective-permute-done.1.refs_2_ = bf16[2,192,128]{2,1,0:T(8,128)(2,1)S(1)} collective-permute-done((bf16[2,192,128]{2,1,0:T(8,128)(2,1)S(1)}, bf16[2,192,128]{2,1,0:T(8,128)(2,1)S(1)}, u32[]{:S(2)}, u32[]{:S(2)}) %collective-permute-start.1) | collective-permute-done | bytes 98336 | tf_op jit(solution)/shard_map/ppermute | solution.py:32
  13.7 0.4 %collective-permute-done.2.refs_3_ = bf16[2,192,128]{2,1,0:T(8,128)(2,1)S(1)} collective-permute-done((bf16[2,192,128]{2,1,0:T(8,128)(2,1)S(1)}, bf16[2,192,128]{2,1,0:T(8,128)(2,1)S(1)}, u32[]{:S(2)}, u32[]{:S(2)}) %collective-permute-start.2) | collective-permute-done | bytes 98336 | tf_op jit(solution)/shard_map/ppermute | solution.py:32
  14.1 0.0 collective-permute-done.3.refs_4_
  14.1 2.0 %image.1 = (bf16[2,192,128]{2,1,0:T(8,128)(2,1)S(1)}, bf16[4,192,128]{2,1,0:T(8,128)(2,1)S(1)}) custom-call(s32[8]{0:T(128)S(1)} %copy-done.4, bf16[2,192,128]{2,1,0:T(8,128)(2,1)S(1)} %pack.1.refs_0_, bf16[2,192,128]{2,1,0:T(8,128)(2,1)S(1)} %collective-permute-done.refs_1_, bf16[2,192,128]{2,1,0:T(8,128)(2,1)S(1)} %collective-permute-done.1.refs_2_, ...), custom_call_target="tpu_custom_call" | custom-call | flops 805306368 | bytes 2359296 | tf_op jit(solution)/shard_map/image/pallas_call | solution.py:339
  16.1 1.6 %collective-permute-start.8 = (bf16[2,192,128]{2,1,0:T(8,128)(2,1)S(1)}, bf16[2,192,128]{2,1,0:T(8,128)(2,1)S(1)}, u32[]{:S(2)}, u32[]{:S(2)}) collective-permute-start(bf16[2,192,128]{2,1,0:T(8,128)(2,1)S(1)} %get-tuple-element.11), channel_id=1, source_target_pairs={{0,2},{1,3},{2,0},{3,1},{4,6},{5,7},{6,4},{7,5},{8,10},{9,11},{10,... | collective-permute-start | bytes 294920 | tf_op jit(solution)/shard_map/ppermute | solution.py:39
  17.7 0.2 overlap.1.refs_0_
  17.9 0.1 collective-permute-start.4
  17.9 0.6 %collective-permute-start.5 = (f32[16,128]{1,0:T(8,128)S(1)}, f32[16,128]{1,0:T(8,128)S(1)}, u32[]{:S(2)}, u32[]{:S(2)}) collective-permute-start(f32[16,128]{1,0:T(8,128)S(1)} %overlap.1.refs_0_), channel_id=1, source_target_pairs={{0,2},{1,3},{2,0},{3,1},{4,6},{5,7},{6,4},{7,5},{8,10},{9,11},{10,... | collective-permute-start | bytes 24584 | tf_op jit(solution)/shard_map/ppermute | solution.py:39
  18.5 1.3 %collective-permute-start.6 = (f32[16,128]{1,0:T(8,128)S(1)}, f32[16,128]{1,0:T(8,128)S(1)}, u32[]{:S(2)}, u32[]{:S(2)}) collective-permute-start(f32[16,128]{1,0:T(8,128)S(1)} %overlap.1.refs_0_), channel_id=1, source_target_pairs={{0,3},{1,2},{2,1},{3,0},{4,7},{5,6},{6,5},{7,4},{8,11},{9,10},{10,... | collective-permute-start | bytes 24584 | tf_op jit(solution)/shard_map/ppermute | solution.py:39
  19.8 0.1 copy.7.owners_ref
  19.9 0.3 %collective-permute-start.7 = (bf16[4,192,128]{2,1,0:T(8,128)(2,1)S(1)}, bf16[4,192,128]{2,1,0:T(8,128)(2,1)S(1)}, u32[]{:S(2)}, u32[]{:S(2)}) collective-permute-start(bf16[4,192,128]{2,1,0:T(8,128)(2,1)S(1)} %get-tuple-element.8.halves_ref.refs_0_), channel_id=1, source_target_pairs={{0,1},{1,0},{2,3},{3,2},{4,5},{5,4},{6,7},{7,6},{8,9},{9,8},{10,11... | collective-permute-start | bytes 589832 | tf_op jit(solution)/shard_map/ppermute | solution.py:39
  20.2 0.6 %collective-permute-done.8.refs_2_ = bf16[2,192,128]{2,1,0:T(8,128)(2,1)S(1)} collective-permute-done((bf16[2,192,128]{2,1,0:T(8,128)(2,1)S(1)}, bf16[2,192,128]{2,1,0:T(8,128)(2,1)S(1)}, u32[]{:S(2)}, u32[]{:S(2)}) %collective-permute-start.8) | collective-permute-done | bytes 98336 | tf_op jit(solution)/shard_map/ppermute | solution.py:39
  20.8 0.0 collective-permute-start.9
  20.8 0.0 collective-permute-done.4.refs_1_
  20.8 0.9 %collective-permute-done.5.refs_2_ = f32[16,128]{1,0:T(8,128)S(1)} collective-permute-done((f32[16,128]{1,0:T(8,128)S(1)}, f32[16,128]{1,0:T(8,128)S(1)}, u32[]{:S(2)}, u32[]{:S(2)}) %collective-permute-start.5) | collective-permute-done | bytes 8224 | tf_op jit(solution)/shard_map/ppermute | solution.py:39
  21.7 0.0 collective-permute-done.6.refs_3_
  21.7 0.5 %factor.1 = (f32[16,16]{1,0:T(8,128)S(1)}, bf16[256,256]{1,0:T(8,128)(2,1)S(1)}) custom-call(s32[16,1]{1,0:T(8,128)S(1)} %copy.7.owners_ref, f32[16,128]{1,0:T(8,128)S(1)} %overlap.1.refs_0_, f32[16,128]{1,0:T(8,128)S(1)} %collective-permute-done.4.refs_1_, f32[16,128]{1,0:T(8,128)S(1)} %collective-permute-done.5.refs_2_, ...), custom_call_target="tpu_custom_call" | custom-call | flops 3000000000 | bytes 1024 | tf_op jit(solution)/shard_map/factor/pallas_call | solution.py:366
  22.2 0.0 collective-permute-done.7.refs_1_
  22.2 0.0 collective-permute-done.9.refs_3_
  22.3 1.1 %route.1 = (bf16[8,64,192]{2,1,0:T(8,128)(2,1)}, f32[16,16]{1,0:T(8,128)}) custom-call(f32[16,16]{1,0:T(8,128)S(1)} %get-tuple-element.9.overlap_ref, bf16[256,256]{1,0:T(8,128)(2,1)S(1)} %get-tuple-element.10.weights_ref, bf16[4,192,128]{2,1,0:T(8,128)(2,1)S(1)} %get-tuple-element.8.halves_ref.refs_0_, ...), custom_call_target="tpu_custom_call" | custom-call | flops 3145728 | bytes 1179648 | tf_op jit(solution)/shard_map/route/pallas_call | solution.py:374
  (7 shorter events, 0.0 us)
Async XLA Ops:
  0.6 0.9 %copy-start = (bf16[16,16,192]{2,1,0:T(8,128)(2,1)S(1)}, bf16[16,16,192]{2,1,0:T(8,128)(2,1)}, u32[]{:S(2)}) copy-start(bf16[16,16,192]{2,1,0:T(8,128)(2,1)} %orbitals_ref.3) | copy-start | bytes 294916
  1.5 12.6 %copy-start.4 = (s32[8]{0:T(128)S(1)}, s32[8]{0:T(128)}, u32[]{:S(2)}) copy-start(s32[8]{0:T(128)} %occupied_ref.1) | copy-start | bytes 100
  1.5 18.3 %copy-start.5 = (s32[16,1]{0,1:T(1,128)S(1)}, s32[16,1]{0,1:T(1,128)}, u32[]{:S(2)}) copy-start(s32[16,1]{0,1:T(1,128)} %param.8) | copy-start | bytes 196
  1.8 15.9 %copy-start.1 = (bf16[16,16,192]{2,1,0:T(8,128)(2,1)S(1)}, bf16[16,16,192]{2,1,0:T(8,128)(2,1)}, u32[]{:S(2)}) copy-start(bf16[16,16,192]{2,1,0:T(8,128)(2,1)} %orbitals_ref.3) | copy-start | bytes 294916
  1.8 11.4 %collective-permute-start = (bf16[2,192,128]{2,1,0:T(8,128)(2,1)S(1)}, bf16[2,192,128]{2,1,0:T(8,128)(2,1)S(1)}, u32[]{:S(2)}, u32[]{:S(2)}) collective-permute-start(bf16[2,192,128]{2,1,0:T(8,128)(2,1)S(1)} %pack.1.refs_0_), channel_id=1, source_target_pairs={{24,0},{28,4},{0,8},{4,12},{8,16},{12,20},{16,24},{20,28},{25,1},{... | collective-permute-start | bytes 294920 | tf_op jit(solution)/shard_map/ppermute | solution.py:32
  4.9 8.8 %collective-permute-start.1 = (bf16[2,192,128]{2,1,0:T(8,128)(2,1)S(1)}, bf16[2,192,128]{2,1,0:T(8,128)(2,1)S(1)}, u32[]{:S(2)}, u32[]{:S(2)}) collective-permute-start(bf16[2,192,128]{2,1,0:T(8,128)(2,1)S(1)} %pack.1.refs_0_), channel_id=1, source_target_pairs={{28,0},{8,4},{4,8},{16,12},{12,16},{24,20},{20,24},{0,28},{29,1},{... | collective-permute-start | bytes 294920 | tf_op jit(solution)/shard_map/ppermute | solution.py:32
  8.1 6.0 %collective-permute-start.2 = (bf16[2,192,128]{2,1,0:T(8,128)(2,1)S(1)}, bf16[2,192,128]{2,1,0:T(8,128)(2,1)S(1)}, u32[]{:S(2)}, u32[]{:S(2)}) collective-permute-start(bf16[2,192,128]{2,1,0:T(8,128)(2,1)S(1)} %pack.1.refs_0_), channel_id=1, source_target_pairs={{4,0},{0,4},{12,8},{8,12},{20,16},{16,20},{28,24},{24,28},{5,1},{1... | collective-permute-start | bytes 294920 | tf_op jit(solution)/shard_map/ppermute | solution.py:32
  8.1 6.0 %collective-permute-start.3 = (bf16[2,192,128]{2,1,0:T(8,128)(2,1)S(1)}, bf16[2,192,128]{2,1,0:T(8,128)(2,1)S(1)}, u32[]{:S(2)}, u32[]{:S(2)}) collective-permute-start(bf16[2,192,128]{2,1,0:T(8,128)(2,1)S(1)} %pack.1.refs_0_), channel_id=1, source_target_pairs={{8,0},{12,4},{16,8},{20,12},{24,16},{28,20},{0,24},{4,28},{9,1},{1... | collective-permute-start | bytes 294920 | tf_op jit(solution)/shard_map/ppermute | solution.py:32
  10.2 1.0 %copy-start.2 = (bf16[3,192,192]{2,1,0:T(8,128)(2,1)S(1)}, bf16[3,192,192]{2,1,0:T(8,128)(2,1)}, u32[]{:S(2)}) copy-start(bf16[3,192,192]{2,1,0:T(8,128)(2,1)} %constant.3.tables_ref) | copy-start | bytes 663556
  11.1 0.7 %copy-start.3 = (f32[16,192]{1,0:T(8,128)S(1)}, f32[16,192]{1,0:T(8,128)}, u32[]{:S(2)}) copy-start(f32[16,192]{1,0:T(8,128)} %coulomb_ref.1) | copy-start | bytes 36868
  16.1 4.7 %collective-permute-start.8 = (bf16[2,192,128]{2,1,0:T(8,128)(2,1)S(1)}, bf16[2,192,128]{2,1,0:T(8,128)(2,1)S(1)}, u32[]{:S(2)}, u32[]{:S(2)}) collective-permute-start(bf16[2,192,128]{2,1,0:T(8,128)(2,1)S(1)} %get-tuple-element.11), channel_id=1, source_target_pairs={{0,2},{1,3},{2,0},{3,1},{4,6},{5,7},{6,4},{7,5},{8,10},{9,11},{10,... | collective-permute-start | bytes 294920 | tf_op jit(solution)/shard_map/ppermute | solution.py:39
  17.9 2.9 %collective-permute-start.4 = (f32[16,128]{1,0:T(8,128)S(1)}, f32[16,128]{1,0:T(8,128)S(1)}, u32[]{:S(2)}, u32[]{:S(2)}) collective-permute-start(f32[16,128]{1,0:T(8,128)S(1)} %overlap.1.refs_0_), channel_id=1, source_target_pairs={{0,1},{1,0},{2,3},{3,2},{4,5},{5,4},{6,7},{7,6},{8,9},{9,8},{10,11... | collective-permute-start | bytes 24584 | tf_op jit(solution)/shard_map/ppermute | solution.py:39
  17.9 3.8 %collective-permute-start.5 = (f32[16,128]{1,0:T(8,128)S(1)}, f32[16,128]{1,0:T(8,128)S(1)}, u32[]{:S(2)}, u32[]{:S(2)}) collective-permute-start(f32[16,128]{1,0:T(8,128)S(1)} %overlap.1.refs_0_), channel_id=1, source_target_pairs={{0,2},{1,3},{2,0},{3,1},{4,6},{5,7},{6,4},{7,5},{8,10},{9,11},{10,... | collective-permute-start | bytes 24584 | tf_op jit(solution)/shard_map/ppermute | solution.py:39
  18.5 3.2 %collective-permute-start.6 = (f32[16,128]{1,0:T(8,128)S(1)}, f32[16,128]{1,0:T(8,128)S(1)}, u32[]{:S(2)}, u32[]{:S(2)}) collective-permute-start(f32[16,128]{1,0:T(8,128)S(1)} %overlap.1.refs_0_), channel_id=1, source_target_pairs={{0,3},{1,2},{2,1},{3,0},{4,7},{5,6},{6,5},{7,4},{8,11},{9,10},{10,... | collective-permute-start | bytes 24584 | tf_op jit(solution)/shard_map/ppermute | solution.py:39
  19.9 2.4 %collective-permute-start.7 = (bf16[4,192,128]{2,1,0:T(8,128)(2,1)S(1)}, bf16[4,192,128]{2,1,0:T(8,128)(2,1)S(1)}, u32[]{:S(2)}, u32[]{:S(2)}) collective-permute-start(bf16[4,192,128]{2,1,0:T(8,128)(2,1)S(1)} %get-tuple-element.8.halves_ref.refs_0_), channel_id=1, source_target_pairs={{0,1},{1,0},{2,3},{3,2},{4,5},{5,4},{6,7},{7,6},{8,9},{9,8},{10,11... | collective-permute-start | bytes 589832 | tf_op jit(solution)/shard_map/ppermute | solution.py:39
  20.8 1.5 %collective-permute-start.9 = (bf16[2,192,128]{2,1,0:T(8,128)(2,1)S(1)}, bf16[2,192,128]{2,1,0:T(8,128)(2,1)S(1)}, u32[]{:S(2)}, u32[]{:S(2)}) collective-permute-start(bf16[2,192,128]{2,1,0:T(8,128)(2,1)S(1)} %collective-permute-done.8.refs_2_), channel_id=1, source_target_pairs={{0,1},{1,0},{2,3},{3,2},{4,5},{5,4},{6,7},{7,6},{8,9},{9,8},{10,11... | collective-permute-start | bytes 294920 | tf_op jit(solution)/shard_map/ppermute | solution.py:39

commit v14 on v13

--- a/solution.py
+++ b/solution.py
@@ -144,9 +144,9 @@
     cuts = points // spare
     assert cuts * spare == points and LANES % spare == 0
     blank = jnp.zeros((spare, 2 * LANES), BF16)
+    kernels = [[[] for _ in range(cuts)] for _ in range(packs)]
     for pack in range(packs):
         tiles = [block[pack] for block in blocks]
-        kernels = [[] for _ in range(cuts)]
         for quarter in range(4):
             here = [(q == quarter) for q in quarters]
             together = sum(tiles[m] * here[m].astype(F32).astype(BF16) for m in merged)
@@ -171,11 +171,13 @@
                 low = pltpu.roll(low, shift, axis=1) if shift else low
                 last = jnp.where(lane < LANES - spare, part[:, -LANES:], low)
                 part = jnp.concatenate([part[:, :-LANES], last], axis=1)
-                kernels[cut].append(part.astype(BF16))
+                kernels[pack][cut].append(part.astype(BF16))
+    for pack in range(packs):
+        tile = blocks[0][pack]
         image = []
         for cut in range(cuts):
-            native = jnp.concatenate([tiles[0], tiles[0][cut * spare : (cut + 1) * spare]], axis=0)
-            fields = dot32(jnp.concatenate(kernels[cut], axis=0), native)
+            native = jnp.concatenate([tile, tile[cut * spare : (cut + 1) * spare]], axis=0)
+            fields = dot32(jnp.concatenate(kernels[pack][cut], axis=0), native)
             rows = jnp.zeros((spare, LANES), F32)
             for line in range(span):
                 rows = jnp.where(own_line == line, fields[line * spare : (line + 1) * spare], rows)

time: 23.6 us -> 23.4 us (level)
  no operation moved by 1% of the time
where the time goes in v14:
time: 23.4 us; the launch traced here: 23.1 us
  starting transfers between devices  12.2 us (52%)
  Pallas kernels  5.12 us (22%)
  local copies, waits for them, and re-layouts  2.67 us (11%)
  waiting for transfers between devices  2.42 us (10%)
  between operations  0.72 us (3%)
    ppermute x4, starting transfers between devices, exchanged(): lax.ppermute(value, 'band', [(row[turn], block) for block, row in enumera...  8.36 us
    ppermute x6, starting transfers between devices, swapped(): lax.ppermute(value, ('grid', 'ham'), [(group, group ^ flip) for group in...  3.84 us
    unnamed x13, local copies, waits for them, and re-layouts  2.67 us
    pallas_call x1, Pallas kernels, local(): call(functools.partial(image_kernel, members), 'image', [shape((packs, po...  1.77 us
    ppermute x6, waiting for transfers between devices, swapped(): lax.ppermute(value, ('grid', 'ham'), [(group, group ^ flip) for group in...  1.47 us
    pallas_call x1, Pallas kernels, local(): call(response_kernel, 'response', [shape((lines, points, padded), F32)],...  1.31 us
    pallas_call x1, Pallas kernels, local(): call(route_kernel, 'route', [shape((CAP, groups * lines, points), BF16),...  1.08 us
    ppermute x4, waiting for transfers between devices, exchanged(): lax.ppermute(value, 'band', [(row[turn], block) for block, row in enumera...  0.95 us
  transfers between devices with their start and end apart: 10, of which 4 were waited for; matrix products, arithmetic and copies ran while one was open for 0% of the time, Pallas kernels for 9%

profile of v14, /device:TPU:0, one launch (start us, length us, event | category | flops | bytes accessed | tf_op | source)
XLA Modules:
  0.0 23.1 jit_solution(15313494165139474428)
XLA Ops:
  0.6 0.0 copy-start
  0.6 0.9 %copy-done = bf16[16,16,192]{2,1,0:T(8,128)(2,1)S(1)} copy-done((bf16[16,16,192]{2,1,0:T(8,128)(2,1)S(1)}, bf16[16,16,192]{2,1,0:T(8,128)(2,1)}, u32[]{:S(2)}) %copy-start) | copy-done | bytes 98328
  1.5 0.2 pack.1.refs_0_
  1.8 0.0 copy-start.1
  1.8 3.1 %collective-permute-start = (bf16[2,192,128]{2,1,0:T(8,128)(2,1)S(1)}, bf16[2,192,128]{2,1,0:T(8,128)(2,1)S(1)}, u32[]{:S(2)}, u32[]{:S(2)}) collective-permute-start(bf16[2,192,128]{2,1,0:T(8,128)(2,1)S(1)} %pack.1.refs_0_), channel_id=1, source_target_pairs={{24,0},{28,4},{0,8},{4,12},{8,16},{12,20},{16,24},{20,28},{25,1},{... | collective-permute-start | bytes 294920 | tf_op jit(solution)/shard_map/ppermute | solution.py:32
  4.9 3.2 %collective-permute-start.1 = (bf16[2,192,128]{2,1,0:T(8,128)(2,1)S(1)}, bf16[2,192,128]{2,1,0:T(8,128)(2,1)S(1)}, u32[]{:S(2)}, u32[]{:S(2)}) collective-permute-start(bf16[2,192,128]{2,1,0:T(8,128)(2,1)S(1)} %pack.1.refs_0_), channel_id=1, source_target_pairs={{28,0},{8,4},{4,8},{16,12},{12,16},{24,20},{20,24},{0,28},{29,1},{... | collective-permute-start | bytes 294920 | tf_op jit(solution)/shard_map/ppermute | solution.py:32
  8.1 0.0 collective-permute-start.2
  8.1 2.1 %collective-permute-start.3 = (bf16[2,192,128]{2,1,0:T(8,128)(2,1)S(1)}, bf16[2,192,128]{2,1,0:T(8,128)(2,1)S(1)}, u32[]{:S(2)}, u32[]{:S(2)}) collective-permute-start(bf16[2,192,128]{2,1,0:T(8,128)(2,1)S(1)} %pack.1.refs_0_), channel_id=1, source_target_pairs={{8,0},{12,4},{16,8},{20,12},{24,16},{28,20},{0,24},{4,28},{9,1},{1... | collective-permute-start | bytes 294920 | tf_op jit(solution)/shard_map/ppermute | solution.py:32
  10.2 1.0 %copy-done.2 = bf16[3,192,192]{2,1,0:T(8,128)(2,1)S(1)} copy-done((bf16[3,192,192]{2,1,0:T(8,128)(2,1)S(1)}, bf16[3,192,192]{2,1,0:T(8,128)(2,1)}, u32[]{:S(2)}) %copy-start.2) | copy-done | bytes 221208
  11.1 0.7 %copy-done.3 = f32[16,192]{1,0:T(8,128)S(1)} copy-done((f32[16,192]{1,0:T(8,128)S(1)}, f32[16,192]{1,0:T(8,128)}, u32[]{:S(2)}) %copy-start.3) | copy-done | bytes 12312
  11.8 1.3 %response.1.refs_5_ = f32[16,192,256]{2,1,0:T(8,128)S(1)} custom-call(f32[16,192]{1,0:T(8,128)S(1)} %copy-done.3, bf16[3,192,192]{2,1,0:T(8,128)(2,1)S(1)} %copy-done.2), custom_call_target="tpu_custom_call" | custom-call | flops 452984832 | bytes 2359296 | tf_op jit(solution)/shard_map/response/pallas_call | solution.py:332
  13.2 0.0 collective-permute-done.refs_1_
  13.2 0.6 %collective-permute-done.1.refs_2_ = bf16[2,192,128]{2,1,0:T(8,128)(2,1)S(1)} collective-permute-done((bf16[2,192,128]{2,1,0:T(8,128)(2,1)S(1)}, bf16[2,192,128]{2,1,0:T(8,128)(2,1)S(1)}, u32[]{:S(2)}, u32[]{:S(2)}) %collective-permute-start.1) | collective-permute-done | bytes 98336 | tf_op jit(solution)/shard_map/ppermute | solution.py:32
  13.7 0.4 %collective-permute-done.2.refs_3_ = bf16[2,192,128]{2,1,0:T(8,128)(2,1)S(1)} collective-permute-done((bf16[2,192,128]{2,1,0:T(8,128)(2,1)S(1)}, bf16[2,192,128]{2,1,0:T(8,128)(2,1)S(1)}, u32[]{:S(2)}, u32[]{:S(2)}) %collective-permute-start.2) | collective-permute-done | bytes 98336 | tf_op jit(solution)/shard_map/ppermute | solution.py:32
  14.1 0.0 collective-permute-done.3.refs_4_
  14.1 1.8 %image.1 = (bf16[2,192,128]{2,1,0:T(8,128)(2,1)S(1)}, bf16[4,192,128]{2,1,0:T(8,128)(2,1)S(1)}) custom-call(s32[8]{0:T(128)S(1)} %copy-done.4, bf16[2,192,128]{2,1,0:T(8,128)(2,1)S(1)} %pack.1.refs_0_, bf16[2,192,128]{2,1,0:T(8,128)(2,1)S(1)} %collective-permute-done.refs_1_, bf16[2,192,128]{2,1,0:T(8,128)(2,1)S(1)} %collective-permute-done.1.refs_2_, ...), custom_call_target="tpu_custom_call" | custom-call | flops 805306368 | bytes 2359296 | tf_op jit(solution)/shard_map/image/pallas_call | solution.py:341
  15.9 1.6 %collective-permute-start.8 = (bf16[2,192,128]{2,1,0:T(8,128)(2,1)S(1)}, bf16[2,192,128]{2,1,0:T(8,128)(2,1)S(1)}, u32[]{:S(2)}, u32[]{:S(2)}) collective-permute-start(bf16[2,192,128]{2,1,0:T(8,128)(2,1)S(1)} %get-tuple-element.11), channel_id=1, source_target_pairs={{0,2},{1,3},{2,0},{3,1},{4,6},{5,7},{6,4},{7,5},{8,10},{9,11},{10,... | collective-permute-start | bytes 294920 | tf_op jit(solution)/shard_map/ppermute | solution.py:39
  17.5 0.2 overlap.1.refs_0_
  17.7 0.1 collective-permute-start.4
  17.7 0.6 %collective-permute-start.5 = (f32[16,128]{1,0:T(8,128)S(1)}, f32[16,128]{1,0:T(8,128)S(1)}, u32[]{:S(2)}, u32[]{:S(2)}) collective-permute-start(f32[16,128]{1,0:T(8,128)S(1)} %overlap.1.refs_0_), channel_id=1, source_target_pairs={{0,2},{1,3},{2,0},{3,1},{4,6},{5,7},{6,4},{7,5},{8,10},{9,11},{10,... | collective-permute-start | bytes 24584 | tf_op jit(solution)/shard_map/ppermute | solution.py:39
  18.3 1.3 %collective-permute-start.6 = (f32[16,128]{1,0:T(8,128)S(1)}, f32[16,128]{1,0:T(8,128)S(1)}, u32[]{:S(2)}, u32[]{:S(2)}) collective-permute-start(f32[16,128]{1,0:T(8,128)S(1)} %overlap.1.refs_0_), channel_id=1, source_target_pairs={{0,3},{1,2},{2,1},{3,0},{4,7},{5,6},{6,5},{7,4},{8,11},{9,10},{10,... | collective-permute-start | bytes 24584 | tf_op jit(solution)/shard_map/ppermute | solution.py:39
  19.6 0.1 copy.7.owners_ref
  19.7 0.3 %collective-permute-start.7 = (bf16[4,192,128]{2,1,0:T(8,128)(2,1)S(1)}, bf16[4,192,128]{2,1,0:T(8,128)(2,1)S(1)}, u32[]{:S(2)}, u32[]{:S(2)}) collective-permute-start(bf16[4,192,128]{2,1,0:T(8,128)(2,1)S(1)} %get-tuple-element.8.halves_ref.refs_0_), channel_id=1, source_target_pairs={{0,1},{1,0},{2,3},{3,2},{4,5},{5,4},{6,7},{7,6},{8,9},{9,8},{10,11... | collective-permute-start | bytes 589832 | tf_op jit(solution)/shard_map/ppermute | solution.py:39
  20.0 0.6 %collective-permute-done.8.refs_2_ = bf16[2,192,128]{2,1,0:T(8,128)(2,1)S(1)} collective-permute-done((bf16[2,192,128]{2,1,0:T(8,128)(2,1)S(1)}, bf16[2,192,128]{2,1,0:T(8,128)(2,1)S(1)}, u32[]{:S(2)}, u32[]{:S(2)}) %collective-permute-start.8) | collective-permute-done | bytes 98336 | tf_op jit(solution)/shard_map/ppermute | solution.py:39
  20.6 0.0 collective-permute-start.9
  20.6 0.0 collective-permute-done.4.refs_1_
  20.6 0.9 %collective-permute-done.5.refs_2_ = f32[16,128]{1,0:T(8,128)S(1)} collective-permute-done((f32[16,128]{1,0:T(8,128)S(1)}, f32[16,128]{1,0:T(8,128)S(1)}, u32[]{:S(2)}, u32[]{:S(2)}) %collective-permute-start.5) | collective-permute-done | bytes 8224 | tf_op jit(solution)/shard_map/ppermute | solution.py:39
  21.5 0.0 collective-permute-done.6.refs_3_
  21.5 0.5 %factor.1 = (f32[16,16]{1,0:T(8,128)S(1)}, bf16[256,256]{1,0:T(8,128)(2,1)S(1)}) custom-call(s32[16,1]{1,0:T(8,128)S(1)} %copy.7.owners_ref, f32[16,128]{1,0:T(8,128)S(1)} %overlap.1.refs_0_, f32[16,128]{1,0:T(8,128)S(1)} %collective-permute-done.4.refs_1_, f32[16,128]{1,0:T(8,128)S(1)} %collective-permute-done.5.refs_2_, ...), custom_call_target="tpu_custom_call" | custom-call | flops 3000000000 | bytes 1024 | tf_op jit(solution)/shard_map/factor/pallas_call | solution.py:368
  22.0 0.0 collective-permute-done.7.refs_1_
  22.0 0.0 collective-permute-done.9.refs_3_
  22.1 1.1 %route.1 = (bf16[8,64,192]{2,1,0:T(8,128)(2,1)}, f32[16,16]{1,0:T(8,128)}) custom-call(f32[16,16]{1,0:T(8,128)S(1)} %get-tuple-element.9.overlap_ref, bf16[256,256]{1,0:T(8,128)(2,1)S(1)} %get-tuple-element.10.weights_ref, bf16[4,192,128]{2,1,0:T(8,128)(2,1)S(1)} %get-tuple-element.8.halves_ref.refs_0_, ...), custom_call_target="tpu_custom_call" | custom-call | flops 3145728 | bytes 1179648 | tf_op jit(solution)/shard_map/route/pallas_call | solution.py:376
  (7 shorter events, 0.0 us)
Async XLA Ops:
  0.6 0.9 %copy-start = (bf16[16,16,192]{2,1,0:T(8,128)(2,1)S(1)}, bf16[16,16,192]{2,1,0:T(8,128)(2,1)}, u32[]{:S(2)}) copy-start(bf16[16,16,192]{2,1,0:T(8,128)(2,1)} %orbitals_ref.3) | copy-start | bytes 294916
  1.5 12.6 %copy-start.4 = (s32[8]{0:T(128)S(1)}, s32[8]{0:T(128)}, u32[]{:S(2)}) copy-start(s32[8]{0:T(128)} %occupied_ref.1) | copy-start | bytes 100
  1.5 18.1 %copy-start.5 = (s32[16,1]{0,1:T(1,128)S(1)}, s32[16,1]{0,1:T(1,128)}, u32[]{:S(2)}) copy-start(s32[16,1]{0,1:T(1,128)} %param.8) | copy-start | bytes 196
  1.8 15.7 %copy-start.1 = (bf16[16,16,192]{2,1,0:T(8,128)(2,1)S(1)}, bf16[16,16,192]{2,1,0:T(8,128)(2,1)}, u32[]{:S(2)}) copy-start(bf16[16,16,192]{2,1,0:T(8,128)(2,1)} %orbitals_ref.3) | copy-start | bytes 294916
  1.8 11.4 %collective-permute-start = (bf16[2,192,128]{2,1,0:T(8,128)(2,1)S(1)}, bf16[2,192,128]{2,1,0:T(8,128)(2,1)S(1)}, u32[]{:S(2)}, u32[]{:S(2)}) collective-permute-start(bf16[2,192,128]{2,1,0:T(8,128)(2,1)S(1)} %pack.1.refs_0_), channel_id=1, source_target_pairs={{24,0},{28,4},{0,8},{4,12},{8,16},{12,20},{16,24},{20,28},{25,1},{... | collective-permute-start | bytes 294920 | tf_op jit(solution)/shard_map/ppermute | solution.py:32
  4.9 8.8 %collective-permute-start.1 = (bf16[2,192,128]{2,1,0:T(8,128)(2,1)S(1)}, bf16[2,192,128]{2,1,0:T(8,128)(2,1)S(1)}, u32[]{:S(2)}, u32[]{:S(2)}) collective-permute-start(bf16[2,192,128]{2,1,0:T(8,128)(2,1)S(1)} %pack.1.refs_0_), channel_id=1, source_target_pairs={{28,0},{8,4},{4,8},{16,12},{12,16},{24,20},{20,24},{0,28},{29,1},{... | collective-permute-start | bytes 294920 | tf_op jit(solution)/shard_map/ppermute | solution.py:32
  8.1 6.0 %collective-permute-start.2 = (bf16[2,192,128]{2,1,0:T(8,128)(2,1)S(1)}, bf16[2,192,128]{2,1,0:T(8,128)(2,1)S(1)}, u32[]{:S(2)}, u32[]{:S(2)}) collective-permute-start(bf16[2,192,128]{2,1,0:T(8,128)(2,1)S(1)} %pack.1.refs_0_), channel_id=1, source_target_pairs={{4,0},{0,4},{12,8},{8,12},{20,16},{16,20},{28,24},{24,28},{5,1},{1... | collective-permute-start | bytes 294920 | tf_op jit(solution)/shard_map/ppermute | solution.py:32
  8.1 6.0 %collective-permute-start.3 = (bf16[2,192,128]{2,1,0:T(8,128)(2,1)S(1)}, bf16[2,192,128]{2,1,0:T(8,128)(2,1)S(1)}, u32[]{:S(2)}, u32[]{:S(2)}) collective-permute-start(bf16[2,192,128]{2,1,0:T(8,128)(2,1)S(1)} %pack.1.refs_0_), channel_id=1, source_target_pairs={{8,0},{12,4},{16,8},{20,12},{24,16},{28,20},{0,24},{4,28},{9,1},{1... | collective-permute-start | bytes 294920 | tf_op jit(solution)/shard_map/ppermute | solution.py:32
  10.2 1.0 %copy-start.2 = (bf16[3,192,192]{2,1,0:T(8,128)(2,1)S(1)}, bf16[3,192,192]{2,1,0:T(8,128)(2,1)}, u32[]{:S(2)}) copy-start(bf16[3,192,192]{2,1,0:T(8,128)(2,1)} %constant.3.tables_ref) | copy-start | bytes 663556
  11.1 0.7 %copy-start.3 = (f32[16,192]{1,0:T(8,128)S(1)}, f32[16,192]{1,0:T(8,128)}, u32[]{:S(2)}) copy-start(f32[16,192]{1,0:T(8,128)} %coulomb_ref.1) | copy-start | bytes 36868
  15.9 4.7 %collective-permute-start.8 = (bf16[2,192,128]{2,1,0:T(8,128)(2,1)S(1)}, bf16[2,192,128]{2,1,0:T(8,128)(2,1)S(1)}, u32[]{:S(2)}, u32[]{:S(2)}) collective-permute-start(bf16[2,192,128]{2,1,0:T(8,128)(2,1)S(1)} %get-tuple-element.11), channel_id=1, source_target_pairs={{0,2},{1,3},{2,0},{3,1},{4,6},{5,7},{6,4},{7,5},{8,10},{9,11},{10,... | collective-permute-start | bytes 294920 | tf_op jit(solution)/shard_map/ppermute | solution.py:39
  17.7 2.9 %collective-permute-start.4 = (f32[16,128]{1,0:T(8,128)S(1)}, f32[16,128]{1,0:T(8,128)S(1)}, u32[]{:S(2)}, u32[]{:S(2)}) collective-permute-start(f32[16,128]{1,0:T(8,128)S(1)} %overlap.1.refs_0_), channel_id=1, source_target_pairs={{0,1},{1,0},{2,3},{3,2},{4,5},{5,4},{6,7},{7,6},{8,9},{9,8},{10,11... | collective-permute-start | bytes 24584 | tf_op jit(solution)/shard_map/ppermute | solution.py:39
  17.7 3.8 %collective-permute-start.5 = (f32[16,128]{1,0:T(8,128)S(1)}, f32[16,128]{1,0:T(8,128)S(1)}, u32[]{:S(2)}, u32[]{:S(2)}) collective-permute-start(f32[16,128]{1,0:T(8,128)S(1)} %overlap.1.refs_0_), channel_id=1, source_target_pairs={{0,2},{1,3},{2,0},{3,1},{4,6},{5,7},{6,4},{7,5},{8,10},{9,11},{10,... | collective-permute-start | bytes 24584 | tf_op jit(solution)/shard_map/ppermute | solution.py:39
  18.3 3.2 %collective-permute-start.6 = (f32[16,128]{1,0:T(8,128)S(1)}, f32[16,128]{1,0:T(8,128)S(1)}, u32[]{:S(2)}, u32[]{:S(2)}) collective-permute-start(f32[16,128]{1,0:T(8,128)S(1)} %overlap.1.refs_0_), channel_id=1, source_target_pairs={{0,3},{1,2},{2,1},{3,0},{4,7},{5,6},{6,5},{7,4},{8,11},{9,10},{10,... | collective-permute-start | bytes 24584 | tf_op jit(solution)/shard_map/ppermute | solution.py:39
  19.7 2.4 %collective-permute-start.7 = (bf16[4,192,128]{2,1,0:T(8,128)(2,1)S(1)}, bf16[4,192,128]{2,1,0:T(8,128)(2,1)S(1)}, u32[]{:S(2)}, u32[]{:S(2)}) collective-permute-start(bf16[4,192,128]{2,1,0:T(8,128)(2,1)S(1)} %get-tuple-element.8.halves_ref.refs_0_), channel_id=1, source_target_pairs={{0,1},{1,0},{2,3},{3,2},{4,5},{5,4},{6,7},{7,6},{8,9},{9,8},{10,11... | collective-permute-start | bytes 589832 | tf_op jit(solution)/shard_map/ppermute | solution.py:39
  20.6 1.5 %collective-permute-start.9 = (bf16[2,192,128]{2,1,0:T(8,128)(2,1)S(1)}, bf16[2,192,128]{2,1,0:T(8,128)(2,1)S(1)}, u32[]{:S(2)}, u32[]{:S(2)}) collective-permute-start(bf16[2,192,128]{2,1,0:T(8,128)(2,1)S(1)} %collective-permute-done.8.refs_2_), channel_id=1, source_target_pairs={{0,1},{1,0},{2,3},{3,2},{4,5},{5,4},{6,7},{7,6},{8,9},{9,8},{10,11... | collective-permute-start | bytes 294920 | tf_op jit(solution)/shard_map/ppermute | solution.py:39

commit v15 on v14

--- a/solution.py
+++ b/solution.py
@@ -149,7 +149,9 @@
         tiles = [block[pack] for block in blocks]
         for quarter in range(4):
             here = [(q == quarter) for q in quarters]
-            together = sum(tiles[m] * here[m].astype(F32).astype(BF16) for m in merged)
+            together = tiles[merged[0]]
+            for m in merged[1:]:
+                together = jnp.where(here[m], tiles[m], together)
             window = jnp.concatenate([together, tiles[apart]], axis=1)
             occupied = sum((here[m] & filled[m]).astype(F32) for m in merged)
             beside = (here[apart] & filled[apart]).astype(F32)

time: 23.4 us -> 23.4 us (level)
  no operation moved by 1% of the time
where the time goes in v15:
time: 23.4 us; the launch traced here: 23.1 us
  starting transfers between devices  12.2 us (52%)
  Pallas kernels  5.12 us (22%)
  local copies, waits for them, and re-layouts  2.67 us (11%)
  waiting for transfers between devices  2.42 us (10%)
  between operations  0.72 us (3%)
    ppermute x4, starting transfers between devices, exchanged(): lax.ppermute(value, 'band', [(row[turn], block) for block, row in enumera...  8.36 us
    ppermute x6, starting transfers between devices, swapped(): lax.ppermute(value, ('grid', 'ham'), [(group, group ^ flip) for group in...  3.84 us
    unnamed x13, local copies, waits for them, and re-layouts  2.67 us
    pallas_call x1, Pallas kernels, local(): call(functools.partial(image_kernel, members), 'image', [shape((packs, po...  1.77 us
    ppermute x6, waiting for transfers between devices, swapped(): lax.ppermute(value, ('grid', 'ham'), [(group, group ^ flip) for group in...  1.48 us
    pallas_call x1, Pallas kernels, local(): call(response_kernel, 'response', [shape((lines, points, padded), F32)],...  1.31 us
    pallas_call x1, Pallas kernels, local(): call(route_kernel, 'route', [shape((CAP, groups * lines, points), BF16),...  1.09 us
    ppermute x4, waiting for transfers between devices, exchanged(): lax.ppermute(value, 'band', [(row[turn], block) for block, row in enumera...  0.95 us
  transfers between devices with their start and end apart: 10, of which 4 were waited for; matrix products, arithmetic and copies ran while one was open for 0% of the time, Pallas kernels for 9%

profile of v15, /device:TPU:0, one launch (start us, length us, event | category | flops | bytes accessed | tf_op | source)
XLA Modules:
  0.0 23.1 jit_solution(15527981665427681304)
XLA Ops:
  0.6 0.0 copy-start
  0.6 0.9 %copy-done = bf16[16,16,192]{2,1,0:T(8,128)(2,1)S(1)} copy-done((bf16[16,16,192]{2,1,0:T(8,128)(2,1)S(1)}, bf16[16,16,192]{2,1,0:T(8,128)(2,1)}, u32[]{:S(2)}) %copy-start) | copy-done | bytes 98328
  1.5 0.2 pack.1.refs_0_
  1.8 0.0 copy-start.1
  1.8 3.1 %collective-permute-start = (bf16[2,192,128]{2,1,0:T(8,128)(2,1)S(1)}, bf16[2,192,128]{2,1,0:T(8,128)(2,1)S(1)}, u32[]{:S(2)}, u32[]{:S(2)}) collective-permute-start(bf16[2,192,128]{2,1,0:T(8,128)(2,1)S(1)} %pack.1.refs_0_), channel_id=1, source_target_pairs={{24,0},{28,4},{0,8},{4,12},{8,16},{12,20},{16,24},{20,28},{25,1},{... | collective-permute-start | bytes 294920 | tf_op jit(solution)/shard_map/ppermute | solution.py:32
  4.9 3.2 %collective-permute-start.1 = (bf16[2,192,128]{2,1,0:T(8,128)(2,1)S(1)}, bf16[2,192,128]{2,1,0:T(8,128)(2,1)S(1)}, u32[]{:S(2)}, u32[]{:S(2)}) collective-permute-start(bf16[2,192,128]{2,1,0:T(8,128)(2,1)S(1)} %pack.1.refs_0_), channel_id=1, source_target_pairs={{28,0},{8,4},{4,8},{16,12},{12,16},{24,20},{20,24},{0,28},{29,1},{... | collective-permute-start | bytes 294920 | tf_op jit(solution)/shard_map/ppermute | solution.py:32
  8.1 0.0 collective-permute-start.2
  8.1 2.1 %collective-permute-start.3 = (bf16[2,192,128]{2,1,0:T(8,128)(2,1)S(1)}, bf16[2,192,128]{2,1,0:T(8,128)(2,1)S(1)}, u32[]{:S(2)}, u32[]{:S(2)}) collective-permute-start(bf16[2,192,128]{2,1,0:T(8,128)(2,1)S(1)} %pack.1.refs_0_), channel_id=1, source_target_pairs={{8,0},{12,4},{16,8},{20,12},{24,16},{28,20},{0,24},{4,28},{9,1},{1... | collective-permute-start | bytes 294920 | tf_op jit(solution)/shard_map/ppermute | solution.py:32
  10.2 1.0 %copy-done.2 = bf16[3,192,192]{2,1,0:T(8,128)(2,1)S(1)} copy-done((bf16[3,192,192]{2,1,0:T(8,128)(2,1)S(1)}, bf16[3,192,192]{2,1,0:T(8,128)(2,1)}, u32[]{:S(2)}) %copy-start.2) | copy-done | bytes 221208
  11.1 0.7 %copy-done.3 = f32[16,192]{1,0:T(8,128)S(1)} copy-done((f32[16,192]{1,0:T(8,128)S(1)}, f32[16,192]{1,0:T(8,128)}, u32[]{:S(2)}) %copy-start.3) | copy-done | bytes 12312
  11.8 1.3 %response.1.refs_5_ = f32[16,192,256]{2,1,0:T(8,128)S(1)} custom-call(f32[16,192]{1,0:T(8,128)S(1)} %copy-done.3, bf16[3,192,192]{2,1,0:T(8,128)(2,1)S(1)} %copy-done.2), custom_call_target="tpu_custom_call" | custom-call | flops 452984832 | bytes 2359296 | tf_op jit(solution)/shard_map/response/pallas_call | solution.py:334
  13.2 0.0 collective-permute-done.refs_1_
  13.2 0.6 %collective-permute-done.1.refs_2_ = bf16[2,192,128]{2,1,0:T(8,128)(2,1)S(1)} collective-permute-done((bf16[2,192,128]{2,1,0:T(8,128)(2,1)S(1)}, bf16[2,192,128]{2,1,0:T(8,128)(2,1)S(1)}, u32[]{:S(2)}, u32[]{:S(2)}) %collective-permute-start.1) | collective-permute-done | bytes 98336 | tf_op jit(solution)/shard_map/ppermute | solution.py:32
  13.7 0.4 %collective-permute-done.2.refs_3_ = bf16[2,192,128]{2,1,0:T(8,128)(2,1)S(1)} collective-permute-done((bf16[2,192,128]{2,1,0:T(8,128)(2,1)S(1)}, bf16[2,192,128]{2,1,0:T(8,128)(2,1)S(1)}, u32[]{:S(2)}, u32[]{:S(2)}) %collective-permute-start.2) | collective-permute-done | bytes 98336 | tf_op jit(solution)/shard_map/ppermute | solution.py:32
  14.1 0.0 collective-permute-done.3.refs_4_
  14.1 1.8 %image.1 = (bf16[2,192,128]{2,1,0:T(8,128)(2,1)S(1)}, bf16[4,192,128]{2,1,0:T(8,128)(2,1)S(1)}) custom-call(s32[8]{0:T(128)S(1)} %copy-done.4, bf16[2,192,128]{2,1,0:T(8,128)(2,1)S(1)} %pack.1.refs_0_, bf16[2,192,128]{2,1,0:T(8,128)(2,1)S(1)} %collective-permute-done.refs_1_, bf16[2,192,128]{2,1,0:T(8,128)(2,1)S(1)} %collective-permute-done.1.refs_2_, ...), custom_call_target="tpu_custom_call" | custom-call | flops 805306368 | bytes 2359296 | tf_op jit(solution)/shard_map/image/pallas_call | solution.py:343
  15.9 1.6 %collective-permute-start.8 = (bf16[2,192,128]{2,1,0:T(8,128)(2,1)S(1)}, bf16[2,192,128]{2,1,0:T(8,128)(2,1)S(1)}, u32[]{:S(2)}, u32[]{:S(2)}) collective-permute-start(bf16[2,192,128]{2,1,0:T(8,128)(2,1)S(1)} %get-tuple-element.11), channel_id=1, source_target_pairs={{0,2},{1,3},{2,0},{3,1},{4,6},{5,7},{6,4},{7,5},{8,10},{9,11},{10,... | collective-permute-start | bytes 294920 | tf_op jit(solution)/shard_map/ppermute | solution.py:39
  17.4 0.2 overlap.1.refs_0_
  17.6 0.1 collective-permute-start.4
  17.7 0.6 %collective-permute-start.5 = (f32[16,128]{1,0:T(8,128)S(1)}, f32[16,128]{1,0:T(8,128)S(1)}, u32[]{:S(2)}, u32[]{:S(2)}) collective-permute-start(f32[16,128]{1,0:T(8,128)S(1)} %overlap.1.refs_0_), channel_id=1, source_target_pairs={{0,2},{1,3},{2,0},{3,1},{4,6},{5,7},{6,4},{7,5},{8,10},{9,11},{10,... | collective-permute-start | bytes 24584 | tf_op jit(solution)/shard_map/ppermute | solution.py:39
  18.3 1.3 %collective-permute-start.6 = (f32[16,128]{1,0:T(8,128)S(1)}, f32[16,128]{1,0:T(8,128)S(1)}, u32[]{:S(2)}, u32[]{:S(2)}) collective-permute-start(f32[16,128]{1,0:T(8,128)S(1)} %overlap.1.refs_0_), channel_id=1, source_target_pairs={{0,3},{1,2},{2,1},{3,0},{4,7},{5,6},{6,5},{7,4},{8,11},{9,10},{10,... | collective-permute-start | bytes 24584 | tf_op jit(solution)/shard_map/ppermute | solution.py:39
  19.6 0.1 copy.7.owners_ref
  19.7 0.3 %collective-permute-start.7 = (bf16[4,192,128]{2,1,0:T(8,128)(2,1)S(1)}, bf16[4,192,128]{2,1,0:T(8,128)(2,1)S(1)}, u32[]{:S(2)}, u32[]{:S(2)}) collective-permute-start(bf16[4,192,128]{2,1,0:T(8,128)(2,1)S(1)} %get-tuple-element.8.halves_ref.refs_0_), channel_id=1, source_target_pairs={{0,1},{1,0},{2,3},{3,2},{4,5},{5,4},{6,7},{7,6},{8,9},{9,8},{10,11... | collective-permute-start | bytes 589832 | tf_op jit(solution)/shard_map/ppermute | solution.py:39
  20.0 0.6 %collective-permute-done.8.refs_2_ = bf16[2,192,128]{2,1,0:T(8,128)(2,1)S(1)} collective-permute-done((bf16[2,192,128]{2,1,0:T(8,128)(2,1)S(1)}, bf16[2,192,128]{2,1,0:T(8,128)(2,1)S(1)}, u32[]{:S(2)}, u32[]{:S(2)}) %collective-permute-start.8) | collective-permute-done | bytes 98336 | tf_op jit(solution)/shard_map/ppermute | solution.py:39
  20.6 0.0 collective-permute-start.9
  20.6 0.0 collective-permute-done.4.refs_1_
  20.6 0.9 %collective-permute-done.5.refs_2_ = f32[16,128]{1,0:T(8,128)S(1)} collective-permute-done((f32[16,128]{1,0:T(8,128)S(1)}, f32[16,128]{1,0:T(8,128)S(1)}, u32[]{:S(2)}, u32[]{:S(2)}) %collective-permute-start.5) | collective-permute-done | bytes 8224 | tf_op jit(solution)/shard_map/ppermute | solution.py:39
  21.5 0.0 collective-permute-done.6.refs_3_
  21.5 0.5 %factor.1 = (f32[16,16]{1,0:T(8,128)S(1)}, bf16[256,256]{1,0:T(8,128)(2,1)S(1)}) custom-call(s32[16,1]{1,0:T(8,128)S(1)} %copy.7.owners_ref, f32[16,128]{1,0:T(8,128)S(1)} %overlap.1.refs_0_, f32[16,128]{1,0:T(8,128)S(1)} %collective-permute-done.4.refs_1_, f32[16,128]{1,0:T(8,128)S(1)} %collective-permute-done.5.refs_2_, ...), custom_call_target="tpu_custom_call" | custom-call | flops 3000000000 | bytes 1024 | tf_op jit(solution)/shard_map/factor/pallas_call | solution.py:370
  22.0 0.0 collective-permute-done.7.refs_1_
  22.0 0.0 collective-permute-done.9.refs_3_
  22.0 1.1 %route.1 = (bf16[8,64,192]{2,1,0:T(8,128)(2,1)}, f32[16,16]{1,0:T(8,128)}) custom-call(f32[16,16]{1,0:T(8,128)S(1)} %get-tuple-element.9.overlap_ref, bf16[256,256]{1,0:T(8,128)(2,1)S(1)} %get-tuple-element.10.weights_ref, bf16[4,192,128]{2,1,0:T(8,128)(2,1)S(1)} %get-tuple-element.8.halves_ref.refs_0_, ...), custom_call_target="tpu_custom_call" | custom-call | flops 3145728 | bytes 1179648 | tf_op jit(solution)/shard_map/route/pallas_call | solution.py:378
  (7 shorter events, 0.0 us)
Async XLA Ops:
  0.6 0.9 %copy-start = (bf16[16,16,192]{2,1,0:T(8,128)(2,1)S(1)}, bf16[16,16,192]{2,1,0:T(8,128)(2,1)}, u32[]{:S(2)}) copy-start(bf16[16,16,192]{2,1,0:T(8,128)(2,1)} %orbitals_ref.3) | copy-start | bytes 294916
  1.5 12.6 %copy-start.4 = (s32[8]{0:T(128)S(1)}, s32[8]{0:T(128)}, u32[]{:S(2)}) copy-start(s32[8]{0:T(128)} %occupied_ref.1) | copy-start | bytes 100
  1.5 18.0 %copy-start.5 = (s32[16,1]{0,1:T(1,128)S(1)}, s32[16,1]{0,1:T(1,128)}, u32[]{:S(2)}) copy-start(s32[16,1]{0,1:T(1,128)} %param.8) | copy-start | bytes 196
  1.8 15.7 %copy-start.1 = (bf16[16,16,192]{2,1,0:T(8,128)(2,1)S(1)}, bf16[16,16,192]{2,1,0:T(8,128)(2,1)}, u32[]{:S(2)}) copy-start(bf16[16,16,192]{2,1,0:T(8,128)(2,1)} %orbitals_ref.3) | copy-start | bytes 294916
  1.8 11.4 %collective-permute-start = (bf16[2,192,128]{2,1,0:T(8,128)(2,1)S(1)}, bf16[2,192,128]{2,1,0:T(8,128)(2,1)S(1)}, u32[]{:S(2)}, u32[]{:S(2)}) collective-permute-start(bf16[2,192,128]{2,1,0:T(8,128)(2,1)S(1)} %pack.1.refs_0_), channel_id=1, source_target_pairs={{24,0},{28,4},{0,8},{4,12},{8,16},{12,20},{16,24},{20,28},{25,1},{... | collective-permute-start | bytes 294920 | tf_op jit(solution)/shard_map/ppermute | solution.py:32
  4.9 8.8 %collective-permute-start.1 = (bf16[2,192,128]{2,1,0:T(8,128)(2,1)S(1)}, bf16[2,192,128]{2,1,0:T(8,128)(2,1)S(1)}, u32[]{:S(2)}, u32[]{:S(2)}) collective-permute-start(bf16[2,192,128]{2,1,0:T(8,128)(2,1)S(1)} %pack.1.refs_0_), channel_id=1, source_target_pairs={{28,0},{8,4},{4,8},{16,12},{12,16},{24,20},{20,24},{0,28},{29,1},{... | collective-permute-start | bytes 294920 | tf_op jit(solution)/shard_map/ppermute | solution.py:32
  8.1 6.0 %collective-permute-start.2 = (bf16[2,192,128]{2,1,0:T(8,128)(2,1)S(1)}, bf16[2,192,128]{2,1,0:T(8,128)(2,1)S(1)}, u32[]{:S(2)}, u32[]{:S(2)}) collective-permute-start(bf16[2,192,128]{2,1,0:T(8,128)(2,1)S(1)} %pack.1.refs_0_), channel_id=1, source_target_pairs={{4,0},{0,4},{12,8},{8,12},{20,16},{16,20},{28,24},{24,28},{5,1},{1... | collective-permute-start | bytes 294920 | tf_op jit(solution)/shard_map/ppermute | solution.py:32
  8.1 6.0 %collective-permute-start.3 = (bf16[2,192,128]{2,1,0:T(8,128)(2,1)S(1)}, bf16[2,192,128]{2,1,0:T(8,128)(2,1)S(1)}, u32[]{:S(2)}, u32[]{:S(2)}) collective-permute-start(bf16[2,192,128]{2,1,0:T(8,128)(2,1)S(1)} %pack.1.refs_0_), channel_id=1, source_target_pairs={{8,0},{12,4},{16,8},{20,12},{24,16},{28,20},{0,24},{4,28},{9,1},{1... | collective-permute-start | bytes 294920 | tf_op jit(solution)/shard_map/ppermute | solution.py:32
  10.2 1.0 %copy-start.2 = (bf16[3,192,192]{2,1,0:T(8,128)(2,1)S(1)}, bf16[3,192,192]{2,1,0:T(8,128)(2,1)}, u32[]{:S(2)}) copy-start(bf16[3,192,192]{2,1,0:T(8,128)(2,1)} %constant.3.tables_ref) | copy-start | bytes 663556
  11.1 0.7 %copy-start.3 = (f32[16,192]{1,0:T(8,128)S(1)}, f32[16,192]{1,0:T(8,128)}, u32[]{:S(2)}) copy-start(f32[16,192]{1,0:T(8,128)} %coulomb_ref.1) | copy-start | bytes 36868
  15.9 4.7 %collective-permute-start.8 = (bf16[2,192,128]{2,1,0:T(8,128)(2,1)S(1)}, bf16[2,192,128]{2,1,0:T(8,128)(2,1)S(1)}, u32[]{:S(2)}, u32[]{:S(2)}) collective-permute-start(bf16[2,192,128]{2,1,0:T(8,128)(2,1)S(1)} %get-tuple-element.11), channel_id=1, source_target_pairs={{0,2},{1,3},{2,0},{3,1},{4,6},{5,7},{6,4},{7,5},{8,10},{9,11},{10,... | collective-permute-start | bytes 294920 | tf_op jit(solution)/shard_map/ppermute | solution.py:39
  17.6 2.9 %collective-permute-start.4 = (f32[16,128]{1,0:T(8,128)S(1)}, f32[16,128]{1,0:T(8,128)S(1)}, u32[]{:S(2)}, u32[]{:S(2)}) collective-permute-start(f32[16,128]{1,0:T(8,128)S(1)} %overlap.1.refs_0_), channel_id=1, source_target_pairs={{0,1},{1,0},{2,3},{3,2},{4,5},{5,4},{6,7},{7,6},{8,9},{9,8},{10,11... | collective-permute-start | bytes 24584 | tf_op jit(solution)/shard_map/ppermute | solution.py:39
  17.7 3.8 %collective-permute-start.5 = (f32[16,128]{1,0:T(8,128)S(1)}, f32[16,128]{1,0:T(8,128)S(1)}, u32[]{:S(2)}, u32[]{:S(2)}) collective-permute-start(f32[16,128]{1,0:T(8,128)S(1)} %overlap.1.refs_0_), channel_id=1, source_target_pairs={{0,2},{1,3},{2,0},{3,1},{4,6},{5,7},{6,4},{7,5},{8,10},{9,11},{10,... | collective-permute-start | bytes 24584 | tf_op jit(solution)/shard_map/ppermute | solution.py:39
  18.3 3.2 %collective-permute-start.6 = (f32[16,128]{1,0:T(8,128)S(1)}, f32[16,128]{1,0:T(8,128)S(1)}, u32[]{:S(2)}, u32[]{:S(2)}) collective-permute-start(f32[16,128]{1,0:T(8,128)S(1)} %overlap.1.refs_0_), channel_id=1, source_target_pairs={{0,3},{1,2},{2,1},{3,0},{4,7},{5,6},{6,5},{7,4},{8,11},{9,10},{10,... | collective-permute-start | bytes 24584 | tf_op jit(solution)/shard_map/ppermute | solution.py:39
  19.7 2.4 %collective-permute-start.7 = (bf16[4,192,128]{2,1,0:T(8,128)(2,1)S(1)}, bf16[4,192,128]{2,1,0:T(8,128)(2,1)S(1)}, u32[]{:S(2)}, u32[]{:S(2)}) collective-permute-start(bf16[4,192,128]{2,1,0:T(8,128)(2,1)S(1)} %get-tuple-element.8.halves_ref.refs_0_), channel_id=1, source_target_pairs={{0,1},{1,0},{2,3},{3,2},{4,5},{5,4},{6,7},{7,6},{8,9},{9,8},{10,11... | collective-permute-start | bytes 589832 | tf_op jit(solution)/shard_map/ppermute | solution.py:39
  20.6 1.5 %collective-permute-start.9 = (bf16[2,192,128]{2,1,0:T(8,128)(2,1)S(1)}, bf16[2,192,128]{2,1,0:T(8,128)(2,1)S(1)}, u32[]{:S(2)}, u32[]{:S(2)}) collective-permute-start(bf16[2,192,128]{2,1,0:T(8,128)(2,1)S(1)} %collective-permute-done.8.refs_2_), channel_id=1, source_target_pairs={{0,1},{1,0},{2,3},{3,2},{4,5},{5,4},{6,7},{7,6},{8,9},{9,8},{10,11... | collective-permute-start | bytes 294920 | tf_op jit(solution)/shard_map/ppermute | solution.py:39

commit v16 on v15

--- a/solution.py
+++ b/solution.py
@@ -18,10 +18,11 @@
 F32, BF16 = jnp.float32, jnp.bfloat16
 
 
+STEPS = (-1, -2, 2, 1)
+
+
 def sources(block, count):
-    odd = block % 2
-    steps = (-2, 2 * odd - 1, 1 - 2 * odd, 2)
-    return [(block + step + count) % count for step in steps]
+    return [(block + step + count) % count for step in STEPS]
 
 
 def exchanged(value):
@@ -139,7 +140,7 @@
     filled = [lane_member(lane, members) < occupied_ref[place] for place in places]
     quarters = [lane_quarter(lane, turn) for turn in turns]
     step = lane % (LANES // 4) // members
-    apart, merged = 1, (0, 2, 3, 4)
+    apart, merged = 2, (0, 1, 3, 4)
     spare = padded - points
     cuts = points // spare
     assert cuts * spare == points and LANES % spare == 0

time: 23.4 us -> 22.6 us (0.966)
  waiting for transfers between devices: 2.42 us -> 1.79 us
    ppermute x4, waiting for transfers between devices: 0.95 us -> 0.3 us  [exchanged(): lax.ppermute(value, 'band', [(row[turn], block) for block, row in enumera...]
  transfers between devices with their start and end apart: 10 -> 10, of which waited for: 4 -> 3; matrix products, arithmetic and copies ran while one was open for 0% -> 0% of each run, Pallas kernels for 9% -> 9%
where the time goes in v16:
time: 22.6 us; the launch traced here: 22.3 us
  starting transfers between devices  12 us (53%)
  Pallas kernels  5.1 us (23%)
  local copies, waits for them, and re-layouts  2.67 us (12%)
  waiting for transfers between devices  1.79 us (8%)
  between operations  0.73 us (3%)
    ppermute x4, starting transfers between devices, exchanged(): lax.ppermute(value, 'band', [(row[turn], block) for block, row in enumera...  8.15 us
    ppermute x6, starting transfers between devices, swapped(): lax.ppermute(value, ('grid', 'ham'), [(group, group ^ flip) for group in...  3.82 us
    unnamed x13, local copies, waits for them, and re-layouts  2.67 us
    pallas_call x1, Pallas kernels, local(): call(functools.partial(image_kernel, members), 'image', [shape((packs, po...  1.77 us
    ppermute x6, waiting for transfers between devices, swapped(): lax.ppermute(value, ('grid', 'ham'), [(group, group ^ flip) for group in...  1.49 us
    pallas_call x1, Pallas kernels, local(): call(response_kernel, 'response', [shape((lines, points, padded), F32)],...  1.3 us
    pallas_call x1, Pallas kernels, local(): call(route_kernel, 'route', [shape((CAP, groups * lines, points), BF16),...  1.08 us
    pallas_call x1, Pallas kernels, local(): call(functools.partial(factor_kernel, cells), 'factor', [shape((members,...  0.53 us
  transfers between devices with their start and end apart: 10, of which 3 were waited for; matrix products, arithmetic and copies ran while one was open for 0% of the time, Pallas kernels for 9%

profile of v16, /device:TPU:0, one launch (start us, length us, event | category | flops | bytes accessed | tf_op | source)
XLA Modules:
  0.0 22.3 jit_solution(9588403413981268090)
XLA Ops:
  0.6 0.0 copy-start
  0.6 0.9 %copy-done = bf16[16,16,192]{2,1,0:T(8,128)(2,1)S(1)} copy-done((bf16[16,16,192]{2,1,0:T(8,128)(2,1)S(1)}, bf16[16,16,192]{2,1,0:T(8,128)(2,1)}, u32[]{:S(2)}) %copy-start) | copy-done | bytes 98328
  1.5 0.2 %pack.1.refs_0_ = bf16[2,192,128]{2,1,0:T(8,128)(2,1)S(1)} custom-call(bf16[16,16,192]{2,1,0:T(8,128)(2,1)S(1)} %copy-done), custom_call_target="tpu_custom_call" | custom-call | flops 49152 | bytes 196608 | tf_op jit(solution)/shard_map/pack/pallas_call | solution.py:325
  1.8 0.0 copy-start.1
  1.8 3.0 %collective-permute-start = (bf16[2,192,128]{2,1,0:T(8,128)(2,1)S(1)}, bf16[2,192,128]{2,1,0:T(8,128)(2,1)S(1)}, u32[]{:S(2)}, u32[]{:S(2)}) collective-permute-start(bf16[2,192,128]{2,1,0:T(8,128)(2,1)S(1)} %pack.1.refs_0_), channel_id=1, source_target_pairs={{28,0},{0,4},{4,8},{8,12},{12,16},{16,20},{20,24},{24,28},{29,1},{... | collective-permute-start | bytes 294920 | tf_op jit(solution)/shard_map/ppermute | solution.py:33
  4.8 1.6 %collective-permute-start.1 = (bf16[2,192,128]{2,1,0:T(8,128)(2,1)S(1)}, bf16[2,192,128]{2,1,0:T(8,128)(2,1)S(1)}, u32[]{:S(2)}, u32[]{:S(2)}) collective-permute-start(bf16[2,192,128]{2,1,0:T(8,128)(2,1)S(1)} %pack.1.refs_0_), channel_id=1, source_target_pairs={{24,0},{28,4},{0,8},{4,12},{8,16},{12,20},{16,24},{20,28},{25,1},{... | collective-permute-start | bytes 294920 | tf_op jit(solution)/shard_map/ppermute | solution.py:33
  6.4 2.2 %collective-permute-start.2 = (bf16[2,192,128]{2,1,0:T(8,128)(2,1)S(1)}, bf16[2,192,128]{2,1,0:T(8,128)(2,1)S(1)}, u32[]{:S(2)}, u32[]{:S(2)}) collective-permute-start(bf16[2,192,128]{2,1,0:T(8,128)(2,1)S(1)} %pack.1.refs_0_), channel_id=1, source_target_pairs={{8,0},{12,4},{16,8},{20,12},{24,16},{28,20},{0,24},{4,28},{9,1},{1... | collective-permute-start | bytes 294920 | tf_op jit(solution)/shard_map/ppermute | solution.py:33
  8.6 1.3 %collective-permute-start.3 = (bf16[2,192,128]{2,1,0:T(8,128)(2,1)S(1)}, bf16[2,192,128]{2,1,0:T(8,128)(2,1)S(1)}, u32[]{:S(2)}, u32[]{:S(2)}) collective-permute-start(bf16[2,192,128]{2,1,0:T(8,128)(2,1)S(1)} %pack.1.refs_0_), channel_id=1, source_target_pairs={{4,0},{8,4},{12,8},{16,12},{20,16},{24,20},{28,24},{0,28},{5,1},{9... | collective-permute-start | bytes 294920 | tf_op jit(solution)/shard_map/ppermute | solution.py:33
  9.9 1.0 %copy-done.2 = bf16[3,192,192]{2,1,0:T(8,128)(2,1)S(1)} copy-done((bf16[3,192,192]{2,1,0:T(8,128)(2,1)S(1)}, bf16[3,192,192]{2,1,0:T(8,128)(2,1)}, u32[]{:S(2)}) %copy-start.2) | copy-done | bytes 221208
  10.9 0.7 %copy-done.3 = f32[16,192]{1,0:T(8,128)S(1)} copy-done((f32[16,192]{1,0:T(8,128)S(1)}, f32[16,192]{1,0:T(8,128)}, u32[]{:S(2)}) %copy-start.3) | copy-done | bytes 12312
  11.6 1.3 %response.1.refs_5_ = f32[16,192,256]{2,1,0:T(8,128)S(1)} custom-call(f32[16,192]{1,0:T(8,128)S(1)} %copy-done.3, bf16[3,192,192]{2,1,0:T(8,128)(2,1)S(1)} %copy-done.2), custom_call_target="tpu_custom_call" | custom-call | flops 452984832 | bytes 2359296 | tf_op jit(solution)/shard_map/response/pallas_call | solution.py:335
  12.9 0.0 collective-permute-done.refs_1_
  12.9 0.0 collective-permute-done.1.refs_2_
  13.0 0.3 %collective-permute-done.2.refs_3_ = bf16[2,192,128]{2,1,0:T(8,128)(2,1)S(1)} collective-permute-done((bf16[2,192,128]{2,1,0:T(8,128)(2,1)S(1)}, bf16[2,192,128]{2,1,0:T(8,128)(2,1)S(1)}, u32[]{:S(2)}, u32[]{:S(2)}) %collective-permute-start.2) | collective-permute-done | bytes 98336 | tf_op jit(solution)/shard_map/ppermute | solution.py:33
  13.2 0.0 collective-permute-done.3.refs_4_
  13.3 1.8 %image.1 = (bf16[2,192,128]{2,1,0:T(8,128)(2,1)S(1)}, bf16[4,192,128]{2,1,0:T(8,128)(2,1)S(1)}) custom-call(s32[8]{0:T(128)S(1)} %copy-done.4, bf16[2,192,128]{2,1,0:T(8,128)(2,1)S(1)} %pack.1.refs_0_, bf16[2,192,128]{2,1,0:T(8,128)(2,1)S(1)} %collective-permute-done.refs_1_, bf16[2,192,128]{2,1,0:T(8,128)(2,1)S(1)} %collective-permute-done.1.refs_2_, ...), custom_call_target="tpu_custom_call" | custom-call | flops 805306368 | bytes 2359296 | tf_op jit(solution)/shard_map/image/pallas_call | solution.py:344
  15.0 1.5 %collective-permute-start.8 = (bf16[2,192,128]{2,1,0:T(8,128)(2,1)S(1)}, bf16[2,192,128]{2,1,0:T(8,128)(2,1)S(1)}, u32[]{:S(2)}, u32[]{:S(2)}) collective-permute-start(bf16[2,192,128]{2,1,0:T(8,128)(2,1)S(1)} %get-tuple-element.11), channel_id=1, source_target_pairs={{0,2},{1,3},{2,0},{3,1},{4,6},{5,7},{6,4},{7,5},{8,10},{9,11},{10,... | collective-permute-start | bytes 294920 | tf_op jit(solution)/shard_map/ppermute | solution.py:40
  16.6 0.2 overlap.1.refs_0_
  16.8 0.1 collective-permute-start.4
  16.9 0.6 %collective-permute-start.5 = (f32[16,128]{1,0:T(8,128)S(1)}, f32[16,128]{1,0:T(8,128)S(1)}, u32[]{:S(2)}, u32[]{:S(2)}) collective-permute-start(f32[16,128]{1,0:T(8,128)S(1)} %overlap.1.refs_0_), channel_id=1, source_target_pairs={{0,2},{1,3},{2,0},{3,1},{4,6},{5,7},{6,4},{7,5},{8,10},{9,11},{10,... | collective-permute-start | bytes 24584 | tf_op jit(solution)/shard_map/ppermute | solution.py:40
  17.5 1.2 %collective-permute-start.6 = (f32[16,128]{1,0:T(8,128)S(1)}, f32[16,128]{1,0:T(8,128)S(1)}, u32[]{:S(2)}, u32[]{:S(2)}) collective-permute-start(f32[16,128]{1,0:T(8,128)S(1)} %overlap.1.refs_0_), channel_id=1, source_target_pairs={{0,3},{1,2},{2,1},{3,0},{4,7},{5,6},{6,5},{7,4},{8,11},{9,10},{10,... | collective-permute-start | bytes 24584 | tf_op jit(solution)/shard_map/ppermute | solution.py:40
  18.7 0.1 copy.7.owners_ref
  18.8 0.3 %collective-permute-start.7 = (bf16[4,192,128]{2,1,0:T(8,128)(2,1)S(1)}, bf16[4,192,128]{2,1,0:T(8,128)(2,1)S(1)}, u32[]{:S(2)}, u32[]{:S(2)}) collective-permute-start(bf16[4,192,128]{2,1,0:T(8,128)(2,1)S(1)} %get-tuple-element.8.halves_ref.refs_0_), channel_id=1, source_target_pairs={{0,1},{1,0},{2,3},{3,2},{4,5},{5,4},{6,7},{7,6},{8,9},{9,8},{10,11... | collective-permute-start | bytes 589832 | tf_op jit(solution)/shard_map/ppermute | solution.py:40
  19.1 0.6 %collective-permute-done.8.refs_2_ = bf16[2,192,128]{2,1,0:T(8,128)(2,1)S(1)} collective-permute-done((bf16[2,192,128]{2,1,0:T(8,128)(2,1)S(1)}, bf16[2,192,128]{2,1,0:T(8,128)(2,1)S(1)}, u32[]{:S(2)}, u32[]{:S(2)}) %collective-permute-start.8) | collective-permute-done | bytes 98336 | tf_op jit(solution)/shard_map/ppermute | solution.py:40
  19.7 0.0 collective-permute-start.9
  19.7 0.0 collective-permute-done.4.refs_1_
  19.7 0.9 %collective-permute-done.5.refs_2_ = f32[16,128]{1,0:T(8,128)S(1)} collective-permute-done((f32[16,128]{1,0:T(8,128)S(1)}, f32[16,128]{1,0:T(8,128)S(1)}, u32[]{:S(2)}, u32[]{:S(2)}) %collective-permute-start.5) | collective-permute-done | bytes 8224 | tf_op jit(solution)/shard_map/ppermute | solution.py:40
  20.6 0.0 collective-permute-done.6.refs_3_
  20.6 0.5 %factor.1 = (f32[16,16]{1,0:T(8,128)S(1)}, bf16[256,256]{1,0:T(8,128)(2,1)S(1)}) custom-call(s32[16,1]{1,0:T(8,128)S(1)} %copy.7.owners_ref, f32[16,128]{1,0:T(8,128)S(1)} %overlap.1.refs_0_, f32[16,128]{1,0:T(8,128)S(1)} %collective-permute-done.4.refs_1_, f32[16,128]{1,0:T(8,128)S(1)} %collective-permute-done.5.refs_2_, ...), custom_call_target="tpu_custom_call" | custom-call | flops 3000000000 | bytes 1024 | tf_op jit(solution)/shard_map/factor/pallas_call | solution.py:371
  21.2 0.0 collective-permute-done.7.refs_1_
  21.2 0.0 collective-permute-done.9.refs_3_
  21.2 1.1 %route.1 = (bf16[8,64,192]{2,1,0:T(8,128)(2,1)}, f32[16,16]{1,0:T(8,128)}) custom-call(f32[16,16]{1,0:T(8,128)S(1)} %get-tuple-element.9.overlap_ref, bf16[256,256]{1,0:T(8,128)(2,1)S(1)} %get-tuple-element.10.weights_ref, bf16[4,192,128]{2,1,0:T(8,128)(2,1)S(1)} %get-tuple-element.8.halves_ref.refs_0_, ...), custom_call_target="tpu_custom_call" | custom-call | flops 3145728 | bytes 1179648 | tf_op jit(solution)/shard_map/route/pallas_call | solution.py:379
  (7 shorter events, 0.0 us)
Async XLA Ops:
  0.6 0.9 %copy-start = (bf16[16,16,192]{2,1,0:T(8,128)(2,1)S(1)}, bf16[16,16,192]{2,1,0:T(8,128)(2,1)}, u32[]{:S(2)}) copy-start(bf16[16,16,192]{2,1,0:T(8,128)(2,1)} %orbitals_ref.3) | copy-start | bytes 294916
  1.5 11.7 %copy-start.4 = (s32[8]{0:T(128)S(1)}, s32[8]{0:T(128)}, u32[]{:S(2)}) copy-start(s32[8]{0:T(128)} %occupied_ref.1) | copy-start | bytes 100
  1.5 17.2 %copy-start.5 = (s32[16,1]{0,1:T(1,128)S(1)}, s32[16,1]{0,1:T(1,128)}, u32[]{:S(2)}) copy-start(s32[16,1]{0,1:T(1,128)} %param.8) | copy-start | bytes 196
  1.8 14.8 %copy-start.1 = (bf16[16,16,192]{2,1,0:T(8,128)(2,1)S(1)}, bf16[16,16,192]{2,1,0:T(8,128)(2,1)}, u32[]{:S(2)}) copy-start(bf16[16,16,192]{2,1,0:T(8,128)(2,1)} %orbitals_ref.3) | copy-start | bytes 294916
  1.8 11.1 %collective-permute-start = (bf16[2,192,128]{2,1,0:T(8,128)(2,1)S(1)}, bf16[2,192,128]{2,1,0:T(8,128)(2,1)S(1)}, u32[]{:S(2)}, u32[]{:S(2)}) collective-permute-start(bf16[2,192,128]{2,1,0:T(8,128)(2,1)S(1)} %pack.1.refs_0_), channel_id=1, source_target_pairs={{28,0},{0,4},{4,8},{8,12},{12,16},{16,20},{20,24},{24,28},{29,1},{... | collective-permute-start | bytes 294920 | tf_op jit(solution)/shard_map/ppermute | solution.py:33
  4.8 8.1 %collective-permute-start.1 = (bf16[2,192,128]{2,1,0:T(8,128)(2,1)S(1)}, bf16[2,192,128]{2,1,0:T(8,128)(2,1)S(1)}, u32[]{:S(2)}, u32[]{:S(2)}) collective-permute-start(bf16[2,192,128]{2,1,0:T(8,128)(2,1)S(1)} %pack.1.refs_0_), channel_id=1, source_target_pairs={{24,0},{28,4},{0,8},{4,12},{8,16},{12,20},{16,24},{20,28},{25,1},{... | collective-permute-start | bytes 294920 | tf_op jit(solution)/shard_map/ppermute | solution.py:33
  6.4 6.8 %collective-permute-start.2 = (bf16[2,192,128]{2,1,0:T(8,128)(2,1)S(1)}, bf16[2,192,128]{2,1,0:T(8,128)(2,1)S(1)}, u32[]{:S(2)}, u32[]{:S(2)}) collective-permute-start(bf16[2,192,128]{2,1,0:T(8,128)(2,1)S(1)} %pack.1.refs_0_), channel_id=1, source_target_pairs={{8,0},{12,4},{16,8},{20,12},{24,16},{28,20},{0,24},{4,28},{9,1},{1... | collective-permute-start | bytes 294920 | tf_op jit(solution)/shard_map/ppermute | solution.py:33
  8.6 4.6 %collective-permute-start.3 = (bf16[2,192,128]{2,1,0:T(8,128)(2,1)S(1)}, bf16[2,192,128]{2,1,0:T(8,128)(2,1)S(1)}, u32[]{:S(2)}, u32[]{:S(2)}) collective-permute-start(bf16[2,192,128]{2,1,0:T(8,128)(2,1)S(1)} %pack.1.refs_0_), channel_id=1, source_target_pairs={{4,0},{8,4},{12,8},{16,12},{20,16},{24,20},{28,24},{0,28},{5,1},{9... | collective-permute-start | bytes 294920 | tf_op jit(solution)/shard_map/ppermute | solution.py:33
  9.9 1.0 %copy-start.2 = (bf16[3,192,192]{2,1,0:T(8,128)(2,1)S(1)}, bf16[3,192,192]{2,1,0:T(8,128)(2,1)}, u32[]{:S(2)}) copy-start(bf16[3,192,192]{2,1,0:T(8,128)(2,1)} %constant.3.tables_ref) | copy-start | bytes 663556
  10.9 0.7 %copy-start.3 = (f32[16,192]{1,0:T(8,128)S(1)}, f32[16,192]{1,0:T(8,128)}, u32[]{:S(2)}) copy-start(f32[16,192]{1,0:T(8,128)} %coulomb_ref.1) | copy-start | bytes 36868
  15.0 4.7 %collective-permute-start.8 = (bf16[2,192,128]{2,1,0:T(8,128)(2,1)S(1)}, bf16[2,192,128]{2,1,0:T(8,128)(2,1)S(1)}, u32[]{:S(2)}, u32[]{:S(2)}) collective-permute-start(bf16[2,192,128]{2,1,0:T(8,128)(2,1)S(1)} %get-tuple-element.11), channel_id=1, source_target_pairs={{0,2},{1,3},{2,0},{3,1},{4,6},{5,7},{6,4},{7,5},{8,10},{9,11},{10,... | collective-permute-start | bytes 294920 | tf_op jit(solution)/shard_map/ppermute | solution.py:40
  16.8 2.9 %collective-permute-start.4 = (f32[16,128]{1,0:T(8,128)S(1)}, f32[16,128]{1,0:T(8,128)S(1)}, u32[]{:S(2)}, u32[]{:S(2)}) collective-permute-start(f32[16,128]{1,0:T(8,128)S(1)} %overlap.1.refs_0_), channel_id=1, source_target_pairs={{0,1},{1,0},{2,3},{3,2},{4,5},{5,4},{6,7},{7,6},{8,9},{9,8},{10,11... | collective-permute-start | bytes 24584 | tf_op jit(solution)/shard_map/ppermute | solution.py:40
  16.9 3.8 %collective-permute-start.5 = (f32[16,128]{1,0:T(8,128)S(1)}, f32[16,128]{1,0:T(8,128)S(1)}, u32[]{:S(2)}, u32[]{:S(2)}) collective-permute-start(f32[16,128]{1,0:T(8,128)S(1)} %overlap.1.refs_0_), channel_id=1, source_target_pairs={{0,2},{1,3},{2,0},{3,1},{4,6},{5,7},{6,4},{7,5},{8,10},{9,11},{10,... | collective-permute-start | bytes 24584 | tf_op jit(solution)/shard_map/ppermute | solution.py:40
  17.5 3.2 %collective-permute-start.6 = (f32[16,128]{1,0:T(8,128)S(1)}, f32[16,128]{1,0:T(8,128)S(1)}, u32[]{:S(2)}, u32[]{:S(2)}) collective-permute-start(f32[16,128]{1,0:T(8,128)S(1)} %overlap.1.refs_0_), channel_id=1, source_target_pairs={{0,3},{1,2},{2,1},{3,0},{4,7},{5,6},{6,5},{7,4},{8,11},{9,10},{10,... | collective-permute-start | bytes 24584 | tf_op jit(solution)/shard_map/ppermute | solution.py:40
  18.8 2.4 %collective-permute-start.7 = (bf16[4,192,128]{2,1,0:T(8,128)(2,1)S(1)}, bf16[4,192,128]{2,1,0:T(8,128)(2,1)S(1)}, u32[]{:S(2)}, u32[]{:S(2)}) collective-permute-start(bf16[4,192,128]{2,1,0:T(8,128)(2,1)S(1)} %get-tuple-element.8.halves_ref.refs_0_), channel_id=1, source_target_pairs={{0,1},{1,0},{2,3},{3,2},{4,5},{5,4},{6,7},{7,6},{8,9},{9,8},{10,11... | collective-permute-start | bytes 589832 | tf_op jit(solution)/shard_map/ppermute | solution.py:40
  19.7 1.5 %collective-permute-start.9 = (bf16[2,192,128]{2,1,0:T(8,128)(2,1)S(1)}, bf16[2,192,128]{2,1,0:T(8,128)(2,1)S(1)}, u32[]{:S(2)}, u32[]{:S(2)}) collective-permute-start(bf16[2,192,128]{2,1,0:T(8,128)(2,1)S(1)} %collective-permute-done.8.refs_2_), channel_id=1, source_target_pairs={{0,1},{1,0},{2,3},{3,2},{4,5},{5,4},{6,7},{7,6},{8,9},{9,8},{10,11... | collective-permute-start | bytes 294920 | tf_op jit(solution)/shard_map/ppermute | solution.py:40

commit v17 on v16

--- a/solution.py
+++ b/solution.py
@@ -18,7 +18,8 @@
 F32, BF16 = jnp.float32, jnp.bfloat16
 
 
-STEPS = (-1, -2, 2, 1)
+TURNS = ((2, True, False), (-1, True, True), (-2, True, True), (1, True, True), (2, False, True))
+STEPS = (2, -1, -2, 1)
 
 
 def sources(block, count):
@@ -28,11 +29,12 @@
 def exchanged(value):
     count = lax.axis_size("band")
     assert count % 4 == 0
-    tables = [sources(block, count) for block in range(count)]
-    return [
-        lax.ppermute(value, "band", [(row[turn], block) for block, row in enumerate(tables)])
-        for turn in range(4)
-    ]
+    arrivals = []
+    for step, inside, around in TURNS:
+        pairs = [((block + step) % count, block) for block in range(count)]
+        pairs = [(a, b) for a, b in pairs if (inside if a - b == step else around)]
+        arrivals.append(lax.ppermute(value, "band", pairs))
+    return arrivals
 
 
 def swapped(value, flip):
@@ -140,14 +142,15 @@
     filled = [lane_member(lane, members) < occupied_ref[place] for place in places]
     quarters = [lane_quarter(lane, turn) for turn in turns]
     step = lane % (LANES // 4) // members
-    apart, merged = 2, (0, 1, 3, 4)
+    apart, merged = 1, (0, 2, 3, 4)
     spare = padded - points
     cuts = points // spare
     assert cuts * spare == points and LANES % spare == 0
     blank = jnp.zeros((spare, 2 * LANES), BF16)
     kernels = [[[] for _ in range(cuts)] for _ in range(packs)]
     for pack in range(packs):
-        tiles = [block[pack] for block in blocks]
+        tiles = [block[pack] for block in blocks[:-1]]
+        tiles[apart] = tiles[apart] + blocks[-1][pack]
         for quarter in range(4):
             here = [(q == quarter) for q in quarters]
             together = tiles[merged[0]]

time: 22.6 us -> 26.7 us (1.18)
  starting transfers between devices: 12 us -> 16.4 us
  waiting for transfers between devices: 1.79 us -> 1.48 us
    ppermute x4 -> x5, starting transfers between devices: 8.15 us -> 12.5 us  [exchanged(): arrivals.append(lax.ppermute(value, 'band', pairs))]
    ppermute x4 -> x5, waiting for transfers between devices: 0.3 us -> 0.01 us  [exchanged(): arrivals.append(lax.ppermute(value, 'band', pairs))]
  transfers between devices with their start and end apart: 10 -> 11, of which waited for: 3 -> 2; matrix products, arithmetic and copies ran while one was open for 0% -> 0% of each run, Pallas kernels for 9% -> 8%
where the time goes in v17:
time: 26.7 us; the launch traced here: 26.4 us
  starting transfers between devices  16.4 us (61%)
  Pallas kernels  5.11 us (19%)
  local copies, waits for them, and re-layouts  2.67 us (10%)
  waiting for transfers between devices  1.48 us (6%)
  between operations  0.78 us (3%)
    ppermute x5, starting transfers between devices, exchanged(): arrivals.append(lax.ppermute(value, 'band', pairs))  12.5 us
    ppermute x6, starting transfers between devices, swapped(): lax.ppermute(value, ('grid', 'ham'), [(group, group ^ flip) for group in...  3.84 us
    unnamed x13, local copies, waits for them, and re-layouts  2.67 us
    pallas_call x1, Pallas kernels, local(): call(functools.partial(image_kernel, members), 'image', [shape((packs, po...  1.77 us
    ppermute x6, waiting for transfers between devices, swapped(): lax.ppermute(value, ('grid', 'ham'), [(group, group ^ flip) for group in...  1.47 us
    pallas_call x1, Pallas kernels, local(): call(response_kernel, 'response', [shape((lines, points, padded), F32)],...  1.31 us
    pallas_call x1, Pallas kernels, local(): call(route_kernel, 'route', [shape((CAP, groups * lines, points), BF16),...  1.08 us
  transfers between devices with their start and end apart: 11, of which 2 were waited for; matrix products, arithmetic and copies ran while one was open for 0% of the time, Pallas kernels for 8%

profile of v17, /device:TPU:0, one launch (start us, length us, event | category | flops | bytes accessed | tf_op | source)
XLA Modules:
  0.0 26.4 jit_solution(4585812687256307756)
XLA Ops:
  0.6 0.0 copy-start
  0.6 0.9 %copy-done = bf16[16,16,192]{2,1,0:T(8,128)(2,1)S(1)} copy-done((bf16[16,16,192]{2,1,0:T(8,128)(2,1)S(1)}, bf16[16,16,192]{2,1,0:T(8,128)(2,1)}, u32[]{:S(2)}) %copy-start) | copy-done | bytes 98328
  1.5 0.2 pack.1.refs_0_
  1.8 0.0 copy-start.1
  1.8 1.4 %collective-permute-start = (bf16[2,192,128]{2,1,0:T(8,128)(2,1)S(1)}, bf16[2,192,128]{2,1,0:T(8,128)(2,1)S(1)}, u32[]{:S(2)}, u32[]{:S(2)}) collective-permute-start(bf16[2,192,128]{2,1,0:T(8,128)(2,1)S(1)} %pack.1.refs_0_), channel_id=1, source_target_pairs={{8,0},{12,4},{16,8},{20,12},{24,16},{28,20},{9,1},{13,5},{17,9},{2... | collective-permute-start | bytes 294920 | tf_op jit(solution)/shard_map/ppermute | solution.py:36
  3.2 3.0 %collective-permute-start.1 = (bf16[2,192,128]{2,1,0:T(8,128)(2,1)S(1)}, bf16[2,192,128]{2,1,0:T(8,128)(2,1)S(1)}, u32[]{:S(2)}, u32[]{:S(2)}) collective-permute-start(bf16[2,192,128]{2,1,0:T(8,128)(2,1)S(1)} %pack.1.refs_0_), channel_id=1, source_target_pairs={{28,0},{0,4},{4,8},{8,12},{12,16},{16,20},{20,24},{24,28},{29,1},{... | collective-permute-start | bytes 294920 | tf_op jit(solution)/shard_map/ppermute | solution.py:36
  6.2 2.6 %collective-permute-start.2 = (bf16[2,192,128]{2,1,0:T(8,128)(2,1)S(1)}, bf16[2,192,128]{2,1,0:T(8,128)(2,1)S(1)}, u32[]{:S(2)}, u32[]{:S(2)}) collective-permute-start(bf16[2,192,128]{2,1,0:T(8,128)(2,1)S(1)} %pack.1.refs_0_), channel_id=1, source_target_pairs={{24,0},{28,4},{0,8},{4,12},{8,16},{12,20},{16,24},{20,28},{25,1},{... | collective-permute-start | bytes 294920 | tf_op jit(solution)/shard_map/ppermute | solution.py:36
  8.9 2.8 %collective-permute-start.3 = (bf16[2,192,128]{2,1,0:T(8,128)(2,1)S(1)}, bf16[2,192,128]{2,1,0:T(8,128)(2,1)S(1)}, u32[]{:S(2)}, u32[]{:S(2)}) collective-permute-start(bf16[2,192,128]{2,1,0:T(8,128)(2,1)S(1)} %pack.1.refs_0_), channel_id=1, source_target_pairs={{4,0},{8,4},{12,8},{16,12},{20,16},{24,20},{28,24},{0,28},{5,1},{9... | collective-permute-start | bytes 294920 | tf_op jit(solution)/shard_map/ppermute | solution.py:36
  11.7 2.7 %collective-permute-start.4 = (bf16[2,192,128]{2,1,0:T(8,128)(2,1)S(1)}, bf16[2,192,128]{2,1,0:T(8,128)(2,1)S(1)}, u32[]{:S(2)}, u32[]{:S(2)}) collective-permute-start(bf16[2,192,128]{2,1,0:T(8,128)(2,1)S(1)} %pack.1.refs_0_), channel_id=1, source_target_pairs={{0,24},{4,28},{1,25},{5,29},{2,26},{6,30},{3,27},{7,31}} | collective-permute-start | bytes 294920 | tf_op jit(solution)/shard_map/ppermute | solution.py:36
  14.3 0.0 copy-start.2
  14.4 1.0 %copy-done.2 = bf16[3,192,192]{2,1,0:T(8,128)(2,1)S(1)} copy-done((bf16[3,192,192]{2,1,0:T(8,128)(2,1)S(1)}, bf16[3,192,192]{2,1,0:T(8,128)(2,1)}, u32[]{:S(2)}) %copy-start.2) | copy-done | bytes 221208
  15.3 0.7 %copy-done.3 = f32[16,192]{1,0:T(8,128)S(1)} copy-done((f32[16,192]{1,0:T(8,128)S(1)}, f32[16,192]{1,0:T(8,128)}, u32[]{:S(2)}) %copy-start.3) | copy-done | bytes 12312
  16.0 1.3 %response.1.refs_6_ = f32[16,192,256]{2,1,0:T(8,128)S(1)} custom-call(f32[16,192]{1,0:T(8,128)S(1)} %copy-done.3, bf16[3,192,192]{2,1,0:T(8,128)(2,1)S(1)} %copy-done.2), custom_call_target="tpu_custom_call" | custom-call | flops 452984832 | bytes 2359296 | tf_op jit(solution)/shard_map/response/pallas_call | solution.py:338
  17.3 0.0 collective-permute-done.refs_1_
  17.4 0.0 collective-permute-done.1.refs_2_
  17.4 0.0 collective-permute-done.2.refs_3_
  17.4 0.0 collective-permute-done.4.refs_5_
  17.4 1.8 %image.1 = (bf16[2,192,128]{2,1,0:T(8,128)(2,1)S(1)}, bf16[4,192,128]{2,1,0:T(8,128)(2,1)S(1)}) custom-call(s32[8]{0:T(128)S(1)} %copy-done.4, bf16[2,192,128]{2,1,0:T(8,128)(2,1)S(1)} %pack.1.refs_0_, bf16[2,192,128]{2,1,0:T(8,128)(2,1)S(1)} %collective-permute-done.refs_1_, bf16[2,192,128]{2,1,0:T(8,128)(2,1)S(1)} %collective-permute-done.1.refs_2_, ...), custom_call_target="tpu_custom_call" | custom-call | flops 805306368 | bytes 2359296 | tf_op jit(solution)/shard_map/image/pallas_call | solution.py:347
  19.2 1.6 %collective-permute-start.9 = (bf16[2,192,128]{2,1,0:T(8,128)(2,1)S(1)}, bf16[2,192,128]{2,1,0:T(8,128)(2,1)S(1)}, u32[]{:S(2)}, u32[]{:S(2)}) collective-permute-start(bf16[2,192,128]{2,1,0:T(8,128)(2,1)S(1)} %get-tuple-element.11), channel_id=1, source_target_pairs={{0,2},{1,3},{2,0},{3,1},{4,6},{5,7},{6,4},{7,5},{8,10},{9,11},{10,... | collective-permute-start | bytes 294920 | tf_op jit(solution)/shard_map/ppermute | solution.py:42
  20.7 0.2 overlap.1.refs_0_
  20.9 0.1 collective-permute-start.5
  21.0 0.6 %collective-permute-start.6 = (f32[16,128]{1,0:T(8,128)S(1)}, f32[16,128]{1,0:T(8,128)S(1)}, u32[]{:S(2)}, u32[]{:S(2)}) collective-permute-start(f32[16,128]{1,0:T(8,128)S(1)} %overlap.1.refs_0_), channel_id=1, source_target_pairs={{0,2},{1,3},{2,0},{3,1},{4,6},{5,7},{6,4},{7,5},{8,10},{9,11},{10,... | collective-permute-start | bytes 24584 | tf_op jit(solution)/shard_map/ppermute | solution.py:42
  21.6 1.3 %collective-permute-start.7 = (f32[16,128]{1,0:T(8,128)S(1)}, f32[16,128]{1,0:T(8,128)S(1)}, u32[]{:S(2)}, u32[]{:S(2)}) collective-permute-start(f32[16,128]{1,0:T(8,128)S(1)} %overlap.1.refs_0_), channel_id=1, source_target_pairs={{0,3},{1,2},{2,1},{3,0},{4,7},{5,6},{6,5},{7,4},{8,11},{9,10},{10,... | collective-permute-start | bytes 24584 | tf_op jit(solution)/shard_map/ppermute | solution.py:42
  22.9 0.1 copy.7.owners_ref
  23.0 0.3 %collective-permute-start.8 = (bf16[4,192,128]{2,1,0:T(8,128)(2,1)S(1)}, bf16[4,192,128]{2,1,0:T(8,128)(2,1)S(1)}, u32[]{:S(2)}, u32[]{:S(2)}) collective-permute-start(bf16[4,192,128]{2,1,0:T(8,128)(2,1)S(1)} %get-tuple-element.8.halves_ref.refs_0_), channel_id=1, source_target_pairs={{0,1},{1,0},{2,3},{3,2},{4,5},{5,4},{6,7},{7,6},{8,9},{9,8},{10,11... | collective-permute-start | bytes 589832 | tf_op jit(solution)/shard_map/ppermute | solution.py:42
  23.3 0.6 %collective-permute-done.9.refs_2_ = bf16[2,192,128]{2,1,0:T(8,128)(2,1)S(1)} collective-permute-done((bf16[2,192,128]{2,1,0:T(8,128)(2,1)S(1)}, bf16[2,192,128]{2,1,0:T(8,128)(2,1)S(1)}, u32[]{:S(2)}, u32[]{:S(2)}) %collective-permute-start.9) | collective-permute-done | bytes 98336 | tf_op jit(solution)/shard_map/ppermute | solution.py:42
  23.9 0.9 %collective-permute-done.6.refs_2_ = f32[16,128]{1,0:T(8,128)S(1)} collective-permute-done((f32[16,128]{1,0:T(8,128)S(1)}, f32[16,128]{1,0:T(8,128)S(1)}, u32[]{:S(2)}, u32[]{:S(2)}) %collective-permute-start.6) | collective-permute-done | bytes 8224 | tf_op jit(solution)/shard_map/ppermute | solution.py:42
  24.8 0.0 collective-permute-done.7.refs_3_
  24.8 0.5 %factor.1 = (f32[16,16]{1,0:T(8,128)S(1)}, bf16[256,256]{1,0:T(8,128)(2,1)S(1)}) custom-call(s32[16,1]{1,0:T(8,128)S(1)} %copy.7.owners_ref, f32[16,128]{1,0:T(8,128)S(1)} %overlap.1.refs_0_, f32[16,128]{1,0:T(8,128)S(1)} %collective-permute-done.5.refs_1_, f32[16,128]{1,0:T(8,128)S(1)} %collective-permute-done.6.refs_2_, ...), custom_call_target="tpu_custom_call" | custom-call | flops 3000000000 | bytes 1024 | tf_op jit(solution)/shard_map/factor/pallas_call | solution.py:374
  25.3 0.0 collective-permute-done.8.refs_1_
  25.3 0.0 collective-permute-done.10.refs_3_
  25.3 1.1 %route.1 = (bf16[8,64,192]{2,1,0:T(8,128)(2,1)}, f32[16,16]{1,0:T(8,128)}) custom-call(f32[16,16]{1,0:T(8,128)S(1)} %get-tuple-element.9.overlap_ref, bf16[256,256]{1,0:T(8,128)(2,1)S(1)} %get-tuple-element.10.weights_ref, bf16[4,192,128]{2,1,0:T(8,128)(2,1)S(1)} %get-tuple-element.8.halves_ref.refs_0_, ...), custom_call_target="tpu_custom_call" | custom-call | flops 3145728 | bytes 1179648 | tf_op jit(solution)/shard_map/route/pallas_call | solution.py:382
  (9 shorter events, 0.0 us)
Async XLA Ops:
  0.6 0.9 %copy-start = (bf16[16,16,192]{2,1,0:T(8,128)(2,1)S(1)}, bf16[16,16,192]{2,1,0:T(8,128)(2,1)}, u32[]{:S(2)}) copy-start(bf16[16,16,192]{2,1,0:T(8,128)(2,1)} %orbitals_ref.3) | copy-start | bytes 294916
  1.5 15.9 %copy-start.4 = (s32[8]{0:T(128)S(1)}, s32[8]{0:T(128)}, u32[]{:S(2)}) copy-start(s32[8]{0:T(128)} %occupied_ref.1) | copy-start | bytes 100
  1.5 21.3 %copy-start.5 = (s32[16,1]{0,1:T(1,128)S(1)}, s32[16,1]{0,1:T(1,128)}, u32[]{:S(2)}) copy-start(s32[16,1]{0,1:T(1,128)} %param.8) | copy-start | bytes 196
  1.8 19.0 %copy-start.1 = (bf16[16,16,192]{2,1,0:T(8,128)(2,1)S(1)}, bf16[16,16,192]{2,1,0:T(8,128)(2,1)}, u32[]{:S(2)}) copy-start(bf16[16,16,192]{2,1,0:T(8,128)(2,1)} %orbitals_ref.3) | copy-start | bytes 294916
  1.8 15.6 %collective-permute-start = (bf16[2,192,128]{2,1,0:T(8,128)(2,1)S(1)}, bf16[2,192,128]{2,1,0:T(8,128)(2,1)S(1)}, u32[]{:S(2)}, u32[]{:S(2)}) collective-permute-start(bf16[2,192,128]{2,1,0:T(8,128)(2,1)S(1)} %pack.1.refs_0_), channel_id=1, source_target_pairs={{8,0},{12,4},{16,8},{20,12},{24,16},{28,20},{9,1},{13,5},{17,9},{2... | collective-permute-start | bytes 294920 | tf_op jit(solution)/shard_map/ppermute | solution.py:36
  3.2 14.1 %collective-permute-start.1 = (bf16[2,192,128]{2,1,0:T(8,128)(2,1)S(1)}, bf16[2,192,128]{2,1,0:T(8,128)(2,1)S(1)}, u32[]{:S(2)}, u32[]{:S(2)}) collective-permute-start(bf16[2,192,128]{2,1,0:T(8,128)(2,1)S(1)} %pack.1.refs_0_), channel_id=1, source_target_pairs={{28,0},{0,4},{4,8},{8,12},{12,16},{16,20},{20,24},{24,28},{29,1},{... | collective-permute-start | bytes 294920 | tf_op jit(solution)/shard_map/ppermute | solution.py:36
  6.2 11.1 %collective-permute-start.2 = (bf16[2,192,128]{2,1,0:T(8,128)(2,1)S(1)}, bf16[2,192,128]{2,1,0:T(8,128)(2,1)S(1)}, u32[]{:S(2)}, u32[]{:S(2)}) collective-permute-start(bf16[2,192,128]{2,1,0:T(8,128)(2,1)S(1)} %pack.1.refs_0_), channel_id=1, source_target_pairs={{24,0},{28,4},{0,8},{4,12},{8,16},{12,20},{16,24},{20,28},{25,1},{... | collective-permute-start | bytes 294920 | tf_op jit(solution)/shard_map/ppermute | solution.py:36
  8.9 8.5 %collective-permute-start.3 = (bf16[2,192,128]{2,1,0:T(8,128)(2,1)S(1)}, bf16[2,192,128]{2,1,0:T(8,128)(2,1)S(1)}, u32[]{:S(2)}, u32[]{:S(2)}) collective-permute-start(bf16[2,192,128]{2,1,0:T(8,128)(2,1)S(1)} %pack.1.refs_0_), channel_id=1, source_target_pairs={{4,0},{8,4},{12,8},{16,12},{20,16},{24,20},{28,24},{0,28},{5,1},{9... | collective-permute-start | bytes 294920 | tf_op jit(solution)/shard_map/ppermute | solution.py:36
  11.7 5.7 %collective-permute-start.4 = (bf16[2,192,128]{2,1,0:T(8,128)(2,1)S(1)}, bf16[2,192,128]{2,1,0:T(8,128)(2,1)S(1)}, u32[]{:S(2)}, u32[]{:S(2)}) collective-permute-start(bf16[2,192,128]{2,1,0:T(8,128)(2,1)S(1)} %pack.1.refs_0_), channel_id=1, source_target_pairs={{0,24},{4,28},{1,25},{5,29},{2,26},{6,30},{3,27},{7,31}} | collective-permute-start | bytes 294920 | tf_op jit(solution)/shard_map/ppermute | solution.py:36
  14.3 1.0 %copy-start.2 = (bf16[3,192,192]{2,1,0:T(8,128)(2,1)S(1)}, bf16[3,192,192]{2,1,0:T(8,128)(2,1)}, u32[]{:S(2)}) copy-start(bf16[3,192,192]{2,1,0:T(8,128)(2,1)} %constant.3.tables_ref) | copy-start | bytes 663556
  15.3 0.7 %copy-start.3 = (f32[16,192]{1,0:T(8,128)S(1)}, f32[16,192]{1,0:T(8,128)}, u32[]{:S(2)}) copy-start(f32[16,192]{1,0:T(8,128)} %coulomb_ref.1) | copy-start | bytes 36868
  19.2 4.7 %collective-permute-start.9 = (bf16[2,192,128]{2,1,0:T(8,128)(2,1)S(1)}, bf16[2,192,128]{2,1,0:T(8,128)(2,1)S(1)}, u32[]{:S(2)}, u32[]{:S(2)}) collective-permute-start(bf16[2,192,128]{2,1,0:T(8,128)(2,1)S(1)} %get-tuple-element.11), channel_id=1, source_target_pairs={{0,2},{1,3},{2,0},{3,1},{4,6},{5,7},{6,4},{7,5},{8,10},{9,11},{10,... | collective-permute-start | bytes 294920 | tf_op jit(solution)/shard_map/ppermute | solution.py:42
  20.9 2.9 %collective-permute-start.5 = (f32[16,128]{1,0:T(8,128)S(1)}, f32[16,128]{1,0:T(8,128)S(1)}, u32[]{:S(2)}, u32[]{:S(2)}) collective-permute-start(f32[16,128]{1,0:T(8,128)S(1)} %overlap.1.refs_0_), channel_id=1, source_target_pairs={{0,1},{1,0},{2,3},{3,2},{4,5},{5,4},{6,7},{7,6},{8,9},{9,8},{10,11... | collective-permute-start | bytes 24584 | tf_op jit(solution)/shard_map/ppermute | solution.py:42
  21.0 3.8 %collective-permute-start.6 = (f32[16,128]{1,0:T(8,128)S(1)}, f32[16,128]{1,0:T(8,128)S(1)}, u32[]{:S(2)}, u32[]{:S(2)}) collective-permute-start(f32[16,128]{1,0:T(8,128)S(1)} %overlap.1.refs_0_), channel_id=1, source_target_pairs={{0,2},{1,3},{2,0},{3,1},{4,6},{5,7},{6,4},{7,5},{8,10},{9,11},{10,... | collective-permute-start | bytes 24584 | tf_op jit(solution)/shard_map/ppermute | solution.py:42
  21.6 3.2 %collective-permute-start.7 = (f32[16,128]{1,0:T(8,128)S(1)}, f32[16,128]{1,0:T(8,128)S(1)}, u32[]{:S(2)}, u32[]{:S(2)}) collective-permute-start(f32[16,128]{1,0:T(8,128)S(1)} %overlap.1.refs_0_), channel_id=1, source_target_pairs={{0,3},{1,2},{2,1},{3,0},{4,7},{5,6},{6,5},{7,4},{8,11},{9,10},{10,... | collective-permute-start | bytes 24584 | tf_op jit(solution)/shard_map/ppermute | solution.py:42
  23.0 2.4 %collective-permute-start.8 = (bf16[4,192,128]{2,1,0:T(8,128)(2,1)S(1)}, bf16[4,192,128]{2,1,0:T(8,128)(2,1)S(1)}, u32[]{:S(2)}, u32[]{:S(2)}) collective-permute-start(bf16[4,192,128]{2,1,0:T(8,128)(2,1)S(1)} %get-tuple-element.8.halves_ref.refs_0_), channel_id=1, source_target_pairs={{0,1},{1,0},{2,3},{3,2},{4,5},{5,4},{6,7},{7,6},{8,9},{9,8},{10,11... | collective-permute-start | bytes 589832 | tf_op jit(solution)/shard_map/ppermute | solution.py:42
  23.9 1.5 %collective-permute-start.10 = (bf16[2,192,128]{2,1,0:T(8,128)(2,1)S(1)}, bf16[2,192,128]{2,1,0:T(8,128)(2,1)S(1)}, u32[]{:S(2)}, u32[]{:S(2)}) collective-permute-start(bf16[2,192,128]{2,1,0:T(8,128)(2,1)S(1)} %collective-permute-done.9.refs_2_), channel_id=1, source_target_pairs={{0,1},{1,0},{2,3},{3,2},{4,5},{5,4},{6,7},{7,6},{8,9},{9,8},{10,11... | collective-permute-start | bytes 294920 | tf_op jit(solution)/shard_map/ppermute | solution.py:42

commit v18 on v16

--- a/solution.py
+++ b/solution.py
@@ -265,11 +265,7 @@
         weights_ref[i * rows : (i + 1) * rows, :] = jnp.concatenate(pair, axis=1)
 
 
-def route_kernel(overlap_ref, weights_ref, *refs):
-    parts, (out_hbm, overlap_hbm, staged, semaphores) = refs[:-4], refs[-4:]
-    groups = len(parts)
-    copies = [pltpu.make_async_copy(overlap_ref, overlap_hbm, semaphores.at[groups])]
-    copies[0].start()
+def send_rows(flips, weights_ref, parts, out_hbm, staged, semaphores):
     points = staged.shape[3]
     weights = weights_ref[...]
     rows = weights.shape[0] // 4
@@ -278,35 +274,53 @@
     packs = lines // span
     highs = jnp.concatenate([weights[:rows], weights[2 * rows : 3 * rows]], axis=0)
     group = lax.axis_index("grid") * lax.axis_size("ham") + lax.axis_index("ham")
-    for flip, part in enumerate(parts):
+    copies = []
+    for place, (flip, part) in enumerate(zip(flips, parts)):
         sums = []
         for pack in range(0, packs, 2):
             field = jnp.concatenate([part[pack], part[pack + 1]], axis=1)
             both = dot32(weights, field, NT)
             results = [both[:rows] + both[rows : 2 * rows], both[2 * rows : 3 * rows] + both[3 * rows :]]
             if part.shape[0] > packs:
-                place = packs + pack
-                rest = dot32(highs, jnp.concatenate([part[place], part[place + 1]], axis=1), NT)
+                low = packs + pack
+                rest = dot32(highs, jnp.concatenate([part[low], part[low + 1]], axis=1), NT)
                 results = [results[0] + rest[:rows], results[1] + rest[rows:]]
             sums += [result.reshape(CAP, span, points) for result in results]
-        staged[flip] = jnp.concatenate(sums, axis=1).astype(BF16)
+        staged[place] = jnp.concatenate(sums, axis=1).astype(BF16)
         start = pl.multiple_of((group ^ flip) * lines, lines)
         target = out_hbm.at[:, pl.ds(start, lines), :]
-        copies.append(pltpu.make_async_copy(staged.at[flip], target, semaphores.at[flip]))
+        copies.append(pltpu.make_async_copy(staged.at[place], target, semaphores.at[place]))
         copies[-1].start()
+    return copies
+
+
+def early_kernel(flips, overlap_ref, weights_ref, *refs):
+    parts, (out_hbm, overlap_hbm, staged, semaphores) = refs[:-4], refs[-4:]
+    copies = [pltpu.make_async_copy(overlap_ref, overlap_hbm, semaphores.at[len(flips)])]
+    copies[0].start()
+    copies += send_rows(flips, weights_ref, parts, out_hbm, staged, semaphores)
     for copy in copies:
         copy.wait()
 
 
-def call(kernel, name, shapes, flops, moved, scratch=(), scalars=0, operands=0, remote=False):
+def late_kernel(flips, begun_hbm, weights_ref, *refs):
+    parts, (out_hbm, staged, semaphores) = refs[:-3], refs[-3:]
+    del begun_hbm
+    for copy in send_rows(flips, weights_ref, parts, out_hbm, staged, semaphores):
+        copy.wait()
+
+
+def call(kernel, name, shapes, flops, moved, scratch=(), scalars=0, operands=0, remote=False, begun=False):
     vmem = pl.BlockSpec(memory_space=pltpu.VMEM)
     smem = pl.BlockSpec(memory_space=pltpu.SMEM)
+    far = pl.BlockSpec(memory_space=pl.ANY)
     return pl.pallas_call(
         kernel,
         name=name,
         out_shape=shapes,
-        in_specs=[smem] * scalars + [vmem] * operands,
-        out_specs=[pl.BlockSpec(memory_space=pl.ANY) if remote else vmem] * len(shapes),
+        in_specs=[smem] * scalars + [far] * begun + [vmem] * operands,
+        out_specs=[far if remote else vmem] * len(shapes),
+        input_output_aliases={0: 0} if begun else {},
         scratch_shapes=list(scratch),
         compiler_params=pltpu.CompilerParams(vmem_limit_bytes=VMEM_LIMIT),
         cost_estimate=pl.CostEstimate(flops=flops, bytes_accessed=moved, transcendentals=0),
@@ -361,7 +375,8 @@
         8 * orbitals.size,
         operands=2,
     )(orbitals, parts)
-    overlaps = [overlap] + [swapped(overlap, flip) for flip in range(1, groups)]
+    others = [swapped(overlap, flip) for flip in reversed(range(1, groups))]
+    overlaps = [overlap] + others[::-1]
     images = [parts] + [swapped(parts, flip) for flip in range(1, near)]
     for grid in range(1, grids):
         across = swapped(high, grid * near)
@@ -376,19 +391,31 @@
         members**2 * 4,
         operands=1 + groups,
     )(owners, *overlaps)
-    routed, intersection = call(
-        route_kernel,
-        "route",
-        [shape((CAP, groups * lines, points), BF16), shape((members, members), F32)],
-        2 * CAP * members * groups * lines * points,
-        6 * members * groups * lines * points,
-        scratch=[
-            pltpu.VMEM((groups, CAP, lines, points), BF16),
-            pltpu.SemaphoreType.DMA((groups + 1,)),
-        ],
-        operands=2 + groups,
-        remote=True,
-    )(intersection, weights, *images)
+    direct = [flip for flip in range(groups) if flip < near or flip % near == 0]
+    passed = [flip for flip in range(groups) if flip not in direct]
+
+    def route(kernel, name, flips, shapes, **more):
+        return call(
+            functools.partial(kernel, flips),
+            name,
+            [shape((CAP, groups * lines, points), BF16)] + shapes,
+            2 * CAP * members * len(flips) * lines * points,
+            6 * members * len(flips) * lines * points,
+            scratch=[
+                pltpu.VMEM((len(flips), CAP, lines, points), BF16),
+                pltpu.SemaphoreType.DMA((len(flips) + 1,)),
+            ],
+            remote=True,
+            **more,
+        )
+
+    routed, intersection = route(
+        early_kernel, "early", direct, [shape((members, members), F32)], operands=2 + len(direct)
+    )(intersection, weights, *[images[flip] for flip in direct])
+    if passed:
+        (routed,) = route(
+            late_kernel, "late", passed, [], operands=1 + len(passed), begun=True
+        )(routed, weights, *[images[flip] for flip in passed])
     return routed[None, None], intersection[None]
 
 

time: 22.6 us -> 23.4 us (1.035)
  Pallas kernels: 5.1 us -> 5.91 us
    pallas_call x1 -> x2, Pallas kernels: 1.08 us -> 1.89 us  [the longest x1 1.03 us: local(): route(early_kernel, 'early', direct, [shape((members, members), F32)], op...]
  transfers between devices with their start and end apart: 10 -> 10, of which waited for: 3 -> 3; matrix products, arithmetic and copies ran while one was open for 0% -> 0% of each run, Pallas kernels for 9% -> 13%
where the time goes in v18:
time: 23.4 us; the launch traced here: 23.1 us
  starting transfers between devices  12 us (51%)
  Pallas kernels  5.91 us (25%)
  local copies, waits for them, and re-layouts  2.67 us (11%)
  waiting for transfers between devices  1.79 us (8%)
  between operations  0.74 us (3%)
    ppermute x4, starting transfers between devices, exchanged(): lax.ppermute(value, 'band', [(row[turn], block) for block, row in enumera...  8.15 us
    ppermute x6, starting transfers between devices, swapped(): lax.ppermute(value, ('grid', 'ham'), [(group, group ^ flip) for group in...  3.82 us
    unnamed x13, local copies, waits for them, and re-layouts  2.67 us
    pallas_call x1, Pallas kernels, local(): call(functools.partial(image_kernel, members), 'image', [shape((packs, po...  1.77 us
    ppermute x6, waiting for transfers between devices, swapped(): lax.ppermute(value, ('grid', 'ham'), [(group, group ^ flip) for group in...  1.49 us
    pallas_call x1, Pallas kernels, local(): call(response_kernel, 'response', [shape((lines, points, padded), F32)],...  1.3 us
    pallas_call x1, Pallas kernels, local(): route(early_kernel, 'early', direct, [shape((members, members), F32)], op...  1.03 us
    pallas_call x1, Pallas kernels, local(): route(late_kernel, 'late', passed, [], operands=1 + len(passed), begun=True)  0.86 us
  transfers between devices with their start and end apart: 10, of which 3 were waited for; matrix products, arithmetic and copies ran while one was open for 0% of the time, Pallas kernels for 13%

profile of v18, /device:TPU:0, one launch (start us, length us, event | category | flops | bytes accessed | tf_op | source)
XLA Modules:
  0.0 23.1 jit_solution(1199849311371359465)
XLA Ops:
  0.6 0.0 copy-start
  0.6 0.9 %copy-done = bf16[16,16,192]{2,1,0:T(8,128)(2,1)S(1)} copy-done((bf16[16,16,192]{2,1,0:T(8,128)(2,1)S(1)}, bf16[16,16,192]{2,1,0:T(8,128)(2,1)}, u32[]{:S(2)}) %copy-start) | copy-done | bytes 98328
  1.5 0.2 %pack.1.refs_0_ = bf16[2,192,128]{2,1,0:T(8,128)(2,1)S(1)} custom-call(bf16[16,16,192]{2,1,0:T(8,128)(2,1)S(1)} %copy-done), custom_call_target="tpu_custom_call" | custom-call | flops 49152 | bytes 196608 | tf_op jit(solution)/shard_map/pack/pallas_call | solution.py:339
  1.8 0.0 copy-start.1
  1.8 3.0 %collective-permute-start = (bf16[2,192,128]{2,1,0:T(8,128)(2,1)S(1)}, bf16[2,192,128]{2,1,0:T(8,128)(2,1)S(1)}, u32[]{:S(2)}, u32[]{:S(2)}) collective-permute-start(bf16[2,192,128]{2,1,0:T(8,128)(2,1)S(1)} %pack.1.refs_0_), channel_id=1, source_target_pairs={{28,0},{0,4},{4,8},{8,12},{12,16},{16,20},{20,24},{24,28},{29,1},{... | collective-permute-start | bytes 294920 | tf_op jit(solution)/shard_map/ppermute | solution.py:33
  4.8 1.6 %collective-permute-start.1 = (bf16[2,192,128]{2,1,0:T(8,128)(2,1)S(1)}, bf16[2,192,128]{2,1,0:T(8,128)(2,1)S(1)}, u32[]{:S(2)}, u32[]{:S(2)}) collective-permute-start(bf16[2,192,128]{2,1,0:T(8,128)(2,1)S(1)} %pack.1.refs_0_), channel_id=1, source_target_pairs={{24,0},{28,4},{0,8},{4,12},{8,16},{12,20},{16,24},{20,28},{25,1},{... | collective-permute-start | bytes 294920 | tf_op jit(solution)/shard_map/ppermute | solution.py:33
  6.4 2.2 %collective-permute-start.2 = (bf16[2,192,128]{2,1,0:T(8,128)(2,1)S(1)}, bf16[2,192,128]{2,1,0:T(8,128)(2,1)S(1)}, u32[]{:S(2)}, u32[]{:S(2)}) collective-permute-start(bf16[2,192,128]{2,1,0:T(8,128)(2,1)S(1)} %pack.1.refs_0_), channel_id=1, source_target_pairs={{8,0},{12,4},{16,8},{20,12},{24,16},{28,20},{0,24},{4,28},{9,1},{1... | collective-permute-start | bytes 294920 | tf_op jit(solution)/shard_map/ppermute | solution.py:33
  8.6 1.3 %collective-permute-start.3 = (bf16[2,192,128]{2,1,0:T(8,128)(2,1)S(1)}, bf16[2,192,128]{2,1,0:T(8,128)(2,1)S(1)}, u32[]{:S(2)}, u32[]{:S(2)}) collective-permute-start(bf16[2,192,128]{2,1,0:T(8,128)(2,1)S(1)} %pack.1.refs_0_), channel_id=1, source_target_pairs={{4,0},{8,4},{12,8},{16,12},{20,16},{24,20},{28,24},{0,28},{5,1},{9... | collective-permute-start | bytes 294920 | tf_op jit(solution)/shard_map/ppermute | solution.py:33
  9.9 1.0 %copy-done.2 = bf16[3,192,192]{2,1,0:T(8,128)(2,1)S(1)} copy-done((bf16[3,192,192]{2,1,0:T(8,128)(2,1)S(1)}, bf16[3,192,192]{2,1,0:T(8,128)(2,1)}, u32[]{:S(2)}) %copy-start.2) | copy-done | bytes 221208
  10.9 0.7 %copy-done.3 = f32[16,192]{1,0:T(8,128)S(1)} copy-done((f32[16,192]{1,0:T(8,128)S(1)}, f32[16,192]{1,0:T(8,128)}, u32[]{:S(2)}) %copy-start.3) | copy-done | bytes 12312
  11.6 1.3 %response.1.refs_5_ = f32[16,192,256]{2,1,0:T(8,128)S(1)} custom-call(f32[16,192]{1,0:T(8,128)S(1)} %copy-done.3, bf16[3,192,192]{2,1,0:T(8,128)(2,1)S(1)} %copy-done.2), custom_call_target="tpu_custom_call" | custom-call | flops 452984832 | bytes 2359296 | tf_op jit(solution)/shard_map/response/pallas_call | solution.py:349
  12.9 0.0 collective-permute-done.refs_1_
  13.0 0.3 %collective-permute-done.2.refs_3_ = bf16[2,192,128]{2,1,0:T(8,128)(2,1)S(1)} collective-permute-done((bf16[2,192,128]{2,1,0:T(8,128)(2,1)S(1)}, bf16[2,192,128]{2,1,0:T(8,128)(2,1)S(1)}, u32[]{:S(2)}, u32[]{:S(2)}) %collective-permute-start.2) | collective-permute-done | bytes 98336 | tf_op jit(solution)/shard_map/ppermute | solution.py:33
  13.2 0.0 collective-permute-done.3.refs_4_
  13.3 1.8 %image.1 = (bf16[2,192,128]{2,1,0:T(8,128)(2,1)S(1)}, bf16[4,192,128]{2,1,0:T(8,128)(2,1)S(1)}) custom-call(s32[8]{0:T(128)S(1)} %copy-done.4, bf16[2,192,128]{2,1,0:T(8,128)(2,1)S(1)} %pack.1.refs_0_, bf16[2,192,128]{2,1,0:T(8,128)(2,1)S(1)} %collective-permute-done.refs_1_, bf16[2,192,128]{2,1,0:T(8,128)(2,1)S(1)} %collective-permute-done.1.refs_2_, ...), custom_call_target="tpu_custom_call" | custom-call | flops 805306368 | bytes 2359296 | tf_op jit(solution)/shard_map/image/pallas_call | solution.py:358
  15.0 1.5 %collective-permute-start.8 = (bf16[2,192,128]{2,1,0:T(8,128)(2,1)S(1)}, bf16[2,192,128]{2,1,0:T(8,128)(2,1)S(1)}, u32[]{:S(2)}, u32[]{:S(2)}) collective-permute-start(bf16[2,192,128]{2,1,0:T(8,128)(2,1)S(1)} %get-tuple-element.11), channel_id=1, source_target_pairs={{0,2},{1,3},{2,0},{3,1},{4,6},{5,7},{6,4},{7,5},{8,10},{9,11},{10,... | collective-permute-start | bytes 294920 | tf_op jit(solution)/shard_map/ppermute | solution.py:40
  16.6 0.2 overlap.1.refs_0_
  16.8 0.1 collective-permute-start.4
  16.9 0.6 %collective-permute-start.5 = (f32[16,128]{1,0:T(8,128)S(1)}, f32[16,128]{1,0:T(8,128)S(1)}, u32[]{:S(2)}, u32[]{:S(2)}) collective-permute-start(f32[16,128]{1,0:T(8,128)S(1)} %overlap.1.refs_0_), channel_id=1, source_target_pairs={{0,2},{1,3},{2,0},{3,1},{4,6},{5,7},{6,4},{7,5},{8,10},{9,11},{10,... | collective-permute-start | bytes 24584 | tf_op jit(solution)/shard_map/ppermute | solution.py:40
  17.5 1.2 %collective-permute-start.6 = (f32[16,128]{1,0:T(8,128)S(1)}, f32[16,128]{1,0:T(8,128)S(1)}, u32[]{:S(2)}, u32[]{:S(2)}) collective-permute-start(f32[16,128]{1,0:T(8,128)S(1)} %overlap.1.refs_0_), channel_id=1, source_target_pairs={{0,3},{1,2},{2,1},{3,0},{4,7},{5,6},{6,5},{7,4},{8,11},{9,10},{10,... | collective-permute-start | bytes 24584 | tf_op jit(solution)/shard_map/ppermute | solution.py:40
  18.7 0.1 copy.8.owners_ref
  18.8 0.3 %collective-permute-start.7 = (bf16[4,192,128]{2,1,0:T(8,128)(2,1)S(1)}, bf16[4,192,128]{2,1,0:T(8,128)(2,1)S(1)}, u32[]{:S(2)}, u32[]{:S(2)}) collective-permute-start(bf16[4,192,128]{2,1,0:T(8,128)(2,1)S(1)} %get-tuple-element.8.halves_ref.refs_0_), channel_id=1, source_target_pairs={{0,1},{1,0},{2,3},{3,2},{4,5},{5,4},{6,7},{7,6},{8,9},{9,8},{10,11... | collective-permute-start | bytes 589832 | tf_op jit(solution)/shard_map/ppermute | solution.py:40
  19.1 0.6 %collective-permute-done.8.refs_2_ = bf16[2,192,128]{2,1,0:T(8,128)(2,1)S(1)} collective-permute-done((bf16[2,192,128]{2,1,0:T(8,128)(2,1)S(1)}, bf16[2,192,128]{2,1,0:T(8,128)(2,1)S(1)}, u32[]{:S(2)}, u32[]{:S(2)}) %collective-permute-start.8) | collective-permute-done | bytes 98336 | tf_op jit(solution)/shard_map/ppermute | solution.py:40
  19.7 0.0 collective-permute-start.9
  19.7 0.0 collective-permute-done.4.refs_1_
  19.7 0.9 %collective-permute-done.5.refs_2_ = f32[16,128]{1,0:T(8,128)S(1)} collective-permute-done((f32[16,128]{1,0:T(8,128)S(1)}, f32[16,128]{1,0:T(8,128)S(1)}, u32[]{:S(2)}, u32[]{:S(2)}) %collective-permute-start.5) | collective-permute-done | bytes 8224 | tf_op jit(solution)/shard_map/ppermute | solution.py:40
  20.6 0.0 collective-permute-done.6.refs_3_
  20.6 0.5 %factor.1 = (f32[16,16]{1,0:T(8,128)S(1)}, bf16[256,256]{1,0:T(8,128)(2,1)S(1)}) custom-call(s32[16,1]{1,0:T(8,128)S(1)} %copy.8.owners_ref, f32[16,128]{1,0:T(8,128)S(1)} %overlap.1.refs_0_, f32[16,128]{1,0:T(8,128)S(1)} %collective-permute-done.4.refs_1_, f32[16,128]{1,0:T(8,128)S(1)} %collective-permute-done.5.refs_2_, ...), custom_call_target="tpu_custom_call" | custom-call | flops 3000000000 | bytes 1024 | tf_op jit(solution)/shard_map/factor/pallas_call | solution.py:386
  21.2 0.0 collective-permute-done.7.refs_1_
  21.2 1.0 %early.1 = (bf16[8,64,192]{2,1,0:T(8,128)(2,1)}, f32[16,16]{1,0:T(8,128)}) custom-call(f32[16,16]{1,0:T(8,128)S(1)} %get-tuple-element.9.overlap_ref, bf16[256,256]{1,0:T(8,128)(2,1)S(1)} %get-tuple-element.10.weights_ref, bf16[4,192,128]{2,1,0:T(8,128)(2,1)S(1)} %get-tuple-element.8.halves_ref.refs_0_, ...), custom_call_target="tpu_custom_call" | custom-call | flops 2359296 | bytes 884736 | tf_op jit(solution)/shard_map/early/pallas_call | solution.py:412
  22.2 0.0 collective-permute-done.9.refs_0_
  22.2 0.9 %late.1 = bf16[8,64,192]{2,1,0:T(8,128)(2,1)} custom-call(bf16[8,64,192]{2,1,0:T(8,128)(2,1)} %get-tuple-element.12.begun_hbm, bf16[256,256]{1,0:T(8,128)(2,1)S(1)} %get-tuple-element.10.weights_ref, bf16[2,192,128]{2,1,0:T(8,128)(2,1)S(1)} %collective-permute-done.9.refs_0_), custom_call_target="tpu_custom_call", output_to_operand_aliasing={{}: (0, {})} | custom-call | flops 786432 | bytes 294912 | tf_op jit(solution)/shard_map/late/pallas_call | solution.py:416
  (8 shorter events, 0.0 us)
Async XLA Ops:
  0.6 0.9 %copy-start = (bf16[16,16,192]{2,1,0:T(8,128)(2,1)S(1)}, bf16[16,16,192]{2,1,0:T(8,128)(2,1)}, u32[]{:S(2)}) copy-start(bf16[16,16,192]{2,1,0:T(8,128)(2,1)} %orbitals_ref.3) | copy-start | bytes 294916
  1.5 11.7 %copy-start.4 = (s32[8]{0:T(128)S(1)}, s32[8]{0:T(128)}, u32[]{:S(2)}) copy-start(s32[8]{0:T(128)} %occupied_ref.1) | copy-start | bytes 100
  1.5 17.2 %copy-start.5 = (s32[16,1]{0,1:T(1,128)S(1)}, s32[16,1]{0,1:T(1,128)}, u32[]{:S(2)}) copy-start(s32[16,1]{0,1:T(1,128)} %param.8) | copy-start | bytes 196
  1.8 14.8 %copy-start.1 = (bf16[16,16,192]{2,1,0:T(8,128)(2,1)S(1)}, bf16[16,16,192]{2,1,0:T(8,128)(2,1)}, u32[]{:S(2)}) copy-start(bf16[16,16,192]{2,1,0:T(8,128)(2,1)} %orbitals_ref.3) | copy-start | bytes 294916
  1.8 11.1 %collective-permute-start = (bf16[2,192,128]{2,1,0:T(8,128)(2,1)S(1)}, bf16[2,192,128]{2,1,0:T(8,128)(2,1)S(1)}, u32[]{:S(2)}, u32[]{:S(2)}) collective-permute-start(bf16[2,192,128]{2,1,0:T(8,128)(2,1)S(1)} %pack.1.refs_0_), channel_id=1, source_target_pairs={{28,0},{0,4},{4,8},{8,12},{12,16},{16,20},{20,24},{24,28},{29,1},{... | collective-permute-start | bytes 294920 | tf_op jit(solution)/shard_map/ppermute | solution.py:33
  4.8 8.1 %collective-permute-start.1 = (bf16[2,192,128]{2,1,0:T(8,128)(2,1)S(1)}, bf16[2,192,128]{2,1,0:T(8,128)(2,1)S(1)}, u32[]{:S(2)}, u32[]{:S(2)}) collective-permute-start(bf16[2,192,128]{2,1,0:T(8,128)(2,1)S(1)} %pack.1.refs_0_), channel_id=1, source_target_pairs={{24,0},{28,4},{0,8},{4,12},{8,16},{12,20},{16,24},{20,28},{25,1},{... | collective-permute-start | bytes 294920 | tf_op jit(solution)/shard_map/ppermute | solution.py:33
  6.4 6.8 %collective-permute-start.2 = (bf16[2,192,128]{2,1,0:T(8,128)(2,1)S(1)}, bf16[2,192,128]{2,1,0:T(8,128)(2,1)S(1)}, u32[]{:S(2)}, u32[]{:S(2)}) collective-permute-start(bf16[2,192,128]{2,1,0:T(8,128)(2,1)S(1)} %pack.1.refs_0_), channel_id=1, source_target_pairs={{8,0},{12,4},{16,8},{20,12},{24,16},{28,20},{0,24},{4,28},{9,1},{1... | collective-permute-start | bytes 294920 | tf_op jit(solution)/shard_map/ppermute | solution.py:33
  8.6 4.6 %collective-permute-start.3 = (bf16[2,192,128]{2,1,0:T(8,128)(2,1)S(1)}, bf16[2,192,128]{2,1,0:T(8,128)(2,1)S(1)}, u32[]{:S(2)}, u32[]{:S(2)}) collective-permute-start(bf16[2,192,128]{2,1,0:T(8,128)(2,1)S(1)} %pack.1.refs_0_), channel_id=1, source_target_pairs={{4,0},{8,4},{12,8},{16,12},{20,16},{24,20},{28,24},{0,28},{5,1},{9... | collective-permute-start | bytes 294920 | tf_op jit(solution)/shard_map/ppermute | solution.py:33
  9.9 1.0 %copy-start.2 = (bf16[3,192,192]{2,1,0:T(8,128)(2,1)S(1)}, bf16[3,192,192]{2,1,0:T(8,128)(2,1)}, u32[]{:S(2)}) copy-start(bf16[3,192,192]{2,1,0:T(8,128)(2,1)} %constant.3.tables_ref) | copy-start | bytes 663556
  10.9 0.7 %copy-start.3 = (f32[16,192]{1,0:T(8,128)S(1)}, f32[16,192]{1,0:T(8,128)}, u32[]{:S(2)}) copy-start(f32[16,192]{1,0:T(8,128)} %coulomb_ref.1) | copy-start | bytes 36868
  15.0 4.7 %collective-permute-start.8 = (bf16[2,192,128]{2,1,0:T(8,128)(2,1)S(1)}, bf16[2,192,128]{2,1,0:T(8,128)(2,1)S(1)}, u32[]{:S(2)}, u32[]{:S(2)}) collective-permute-start(bf16[2,192,128]{2,1,0:T(8,128)(2,1)S(1)} %get-tuple-element.11), channel_id=1, source_target_pairs={{0,2},{1,3},{2,0},{3,1},{4,6},{5,7},{6,4},{7,5},{8,10},{9,11},{10,... | collective-permute-start | bytes 294920 | tf_op jit(solution)/shard_map/ppermute | solution.py:40
  16.8 2.9 %collective-permute-start.4 = (f32[16,128]{1,0:T(8,128)S(1)}, f32[16,128]{1,0:T(8,128)S(1)}, u32[]{:S(2)}, u32[]{:S(2)}) collective-permute-start(f32[16,128]{1,0:T(8,128)S(1)} %overlap.1.refs_0_), channel_id=1, source_target_pairs={{0,1},{1,0},{2,3},{3,2},{4,5},{5,4},{6,7},{7,6},{8,9},{9,8},{10,11... | collective-permute-start | bytes 24584 | tf_op jit(solution)/shard_map/ppermute | solution.py:40
  16.9 3.8 %collective-permute-start.5 = (f32[16,128]{1,0:T(8,128)S(1)}, f32[16,128]{1,0:T(8,128)S(1)}, u32[]{:S(2)}, u32[]{:S(2)}) collective-permute-start(f32[16,128]{1,0:T(8,128)S(1)} %overlap.1.refs_0_), channel_id=1, source_target_pairs={{0,2},{1,3},{2,0},{3,1},{4,6},{5,7},{6,4},{7,5},{8,10},{9,11},{10,... | collective-permute-start | bytes 24584 | tf_op jit(solution)/shard_map/ppermute | solution.py:40
  17.5 3.2 %collective-permute-start.6 = (f32[16,128]{1,0:T(8,128)S(1)}, f32[16,128]{1,0:T(8,128)S(1)}, u32[]{:S(2)}, u32[]{:S(2)}) collective-permute-start(f32[16,128]{1,0:T(8,128)S(1)} %overlap.1.refs_0_), channel_id=1, source_target_pairs={{0,3},{1,2},{2,1},{3,0},{4,7},{5,6},{6,5},{7,4},{8,11},{9,10},{10,... | collective-permute-start | bytes 24584 | tf_op jit(solution)/shard_map/ppermute | solution.py:40
  18.8 2.4 %collective-permute-start.7 = (bf16[4,192,128]{2,1,0:T(8,128)(2,1)S(1)}, bf16[4,192,128]{2,1,0:T(8,128)(2,1)S(1)}, u32[]{:S(2)}, u32[]{:S(2)}) collective-permute-start(bf16[4,192,128]{2,1,0:T(8,128)(2,1)S(1)} %get-tuple-element.8.halves_ref.refs_0_), channel_id=1, source_target_pairs={{0,1},{1,0},{2,3},{3,2},{4,5},{5,4},{6,7},{7,6},{8,9},{9,8},{10,11... | collective-permute-start | bytes 589832 | tf_op jit(solution)/shard_map/ppermute | solution.py:40
  19.7 2.5 %collective-permute-start.9 = (bf16[2,192,128]{2,1,0:T(8,128)(2,1)S(1)}, bf16[2,192,128]{2,1,0:T(8,128)(2,1)S(1)}, u32[]{:S(2)}, u32[]{:S(2)}) collective-permute-start(bf16[2,192,128]{2,1,0:T(8,128)(2,1)S(1)} %collective-permute-done.8.refs_2_), channel_id=1, source_target_pairs={{0,1},{1,0},{2,3},{3,2},{4,5},{5,4},{6,7},{7,6},{8,9},{9,8},{10,11... | collective-permute-start | bytes 294920 | tf_op jit(solution)/shard_map/ppermute | solution.py:40

commit v19 on v16

--- a/solution.py
+++ b/solution.py
@@ -18,7 +18,7 @@
 F32, BF16 = jnp.float32, jnp.bfloat16
 
 
-STEPS = (-1, -2, 2, 1)
+STEPS = (-2, -1, 2, 1)
 
 
 def sources(block, count):
@@ -140,7 +140,7 @@
     filled = [lane_member(lane, members) < occupied_ref[place] for place in places]
     quarters = [lane_quarter(lane, turn) for turn in turns]
     step = lane % (LANES // 4) // members
-    apart, merged = 2, (0, 1, 3, 4)
+    apart, merged = 1, (0, 2, 3, 4)
     spare = padded - points
     cuts = points // spare
     assert cuts * spare == points and LANES % spare == 0

time: 22.6 us -> 23.5 us (1.040)
  waiting for transfers between devices: 1.79 us -> 2.86 us
    ppermute x4, waiting for transfers between devices: 0.3 us -> 1.39 us  [exchanged(): lax.ppermute(value, 'band', [(row[turn], block) for block, row in enumera...]
  transfers between devices with their start and end apart: 10 -> 10, of which waited for: 3 -> 4; matrix products, arithmetic and copies ran while one was open for 0% -> 0% of each run, Pallas kernels for 9% -> 9%
where the time goes in v19:
time: 23.5 us; the launch traced here: 23.3 us
  starting transfers between devices  11.9 us (51%)
  Pallas kernels  5.09 us (22%)
  waiting for transfers between devices  2.86 us (12%)
  local copies, waits for them, and re-layouts  2.67 us (11%)
  between operations  0.72 us (3%)
    ppermute x4, starting transfers between devices, exchanged(): lax.ppermute(value, 'band', [(row[turn], block) for block, row in enumera...  8.09 us
    ppermute x6, starting transfers between devices, swapped(): lax.ppermute(value, ('grid', 'ham'), [(group, group ^ flip) for group in...  3.84 us
    unnamed x13, local copies, waits for them, and re-layouts  2.67 us
    pallas_call x1, Pallas kernels, local(): call(functools.partial(image_kernel, members), 'image', [shape((packs, po...  1.75 us
    ppermute x6, waiting for transfers between devices, swapped(): lax.ppermute(value, ('grid', 'ham'), [(group, group ^ flip) for group in...  1.47 us
    ppermute x4, waiting for transfers between devices, exchanged(): lax.ppermute(value, 'band', [(row[turn], block) for block, row in enumera...  1.39 us
    pallas_call x1, Pallas kernels, local(): call(response_kernel, 'response', [shape((lines, points, padded), F32)],...  1.31 us
    pallas_call x1, Pallas kernels, local(): call(route_kernel, 'route', [shape((CAP, groups * lines, points), BF16),...  1.08 us
  transfers between devices with their start and end apart: 10, of which 4 were waited for; matrix products, arithmetic and copies ran while one was open for 0% of the time, Pallas kernels for 9%

profile of v19, /device:TPU:0, one launch (start us, length us, event | category | flops | bytes accessed | tf_op | source)
XLA Modules:
  0.0 23.3 jit_solution(4108217346280003617)
XLA Ops:
  0.6 0.0 copy-start
  0.6 0.9 %copy-done = bf16[16,16,192]{2,1,0:T(8,128)(2,1)S(1)} copy-done((bf16[16,16,192]{2,1,0:T(8,128)(2,1)S(1)}, bf16[16,16,192]{2,1,0:T(8,128)(2,1)}, u32[]{:S(2)}) %copy-start) | copy-done | bytes 98328
  1.5 0.2 pack.1.refs_0_
  1.8 0.0 copy-start.1
  1.8 3.1 %collective-permute-start = (bf16[2,192,128]{2,1,0:T(8,128)(2,1)S(1)}, bf16[2,192,128]{2,1,0:T(8,128)(2,1)S(1)}, u32[]{:S(2)}, u32[]{:S(2)}) collective-permute-start(bf16[2,192,128]{2,1,0:T(8,128)(2,1)S(1)} %pack.1.refs_0_), channel_id=1, source_target_pairs={{24,0},{28,4},{0,8},{4,12},{8,16},{12,20},{16,24},{20,28},{25,1},{... | collective-permute-start | bytes 294920 | tf_op jit(solution)/shard_map/ppermute | solution.py:33
  4.9 1.5 %collective-permute-start.1 = (bf16[2,192,128]{2,1,0:T(8,128)(2,1)S(1)}, bf16[2,192,128]{2,1,0:T(8,128)(2,1)S(1)}, u32[]{:S(2)}, u32[]{:S(2)}) collective-permute-start(bf16[2,192,128]{2,1,0:T(8,128)(2,1)S(1)} %pack.1.refs_0_), channel_id=1, source_target_pairs={{28,0},{0,4},{4,8},{8,12},{12,16},{16,20},{20,24},{24,28},{29,1},{... | collective-permute-start | bytes 294920 | tf_op jit(solution)/shard_map/ppermute | solution.py:33
  6.4 2.2 %collective-permute-start.2 = (bf16[2,192,128]{2,1,0:T(8,128)(2,1)S(1)}, bf16[2,192,128]{2,1,0:T(8,128)(2,1)S(1)}, u32[]{:S(2)}, u32[]{:S(2)}) collective-permute-start(bf16[2,192,128]{2,1,0:T(8,128)(2,1)S(1)} %pack.1.refs_0_), channel_id=1, source_target_pairs={{8,0},{12,4},{16,8},{20,12},{24,16},{28,20},{0,24},{4,28},{9,1},{1... | collective-permute-start | bytes 294920 | tf_op jit(solution)/shard_map/ppermute | solution.py:33
  8.6 1.2 %collective-permute-start.3 = (bf16[2,192,128]{2,1,0:T(8,128)(2,1)S(1)}, bf16[2,192,128]{2,1,0:T(8,128)(2,1)S(1)}, u32[]{:S(2)}, u32[]{:S(2)}) collective-permute-start(bf16[2,192,128]{2,1,0:T(8,128)(2,1)S(1)} %pack.1.refs_0_), channel_id=1, source_target_pairs={{4,0},{8,4},{12,8},{16,12},{20,16},{24,20},{28,24},{0,28},{5,1},{9... | collective-permute-start | bytes 294920 | tf_op jit(solution)/shard_map/ppermute | solution.py:33
  9.9 1.0 %copy-done.2 = bf16[3,192,192]{2,1,0:T(8,128)(2,1)S(1)} copy-done((bf16[3,192,192]{2,1,0:T(8,128)(2,1)S(1)}, bf16[3,192,192]{2,1,0:T(8,128)(2,1)}, u32[]{:S(2)}) %copy-start.2) | copy-done | bytes 221208
  10.9 0.7 %copy-done.3 = f32[16,192]{1,0:T(8,128)S(1)} copy-done((f32[16,192]{1,0:T(8,128)S(1)}, f32[16,192]{1,0:T(8,128)}, u32[]{:S(2)}) %copy-start.3) | copy-done | bytes 12312
  11.6 1.3 %response.1.refs_5_ = f32[16,192,256]{2,1,0:T(8,128)S(1)} custom-call(f32[16,192]{1,0:T(8,128)S(1)} %copy-done.3, bf16[3,192,192]{2,1,0:T(8,128)(2,1)S(1)} %copy-done.2), custom_call_target="tpu_custom_call" | custom-call | flops 452984832 | bytes 2359296 | tf_op jit(solution)/shard_map/response/pallas_call | solution.py:335
  12.9 0.0 collective-permute-done.refs_1_
  12.9 0.8 %collective-permute-done.1.refs_2_ = bf16[2,192,128]{2,1,0:T(8,128)(2,1)S(1)} collective-permute-done((bf16[2,192,128]{2,1,0:T(8,128)(2,1)S(1)}, bf16[2,192,128]{2,1,0:T(8,128)(2,1)S(1)}, u32[]{:S(2)}, u32[]{:S(2)}) %collective-permute-start.1) | collective-permute-done | bytes 98336 | tf_op jit(solution)/shard_map/ppermute | solution.py:33
  13.7 0.0 collective-permute-done.2.refs_3_
  13.7 0.5 %collective-permute-done.3.refs_4_ = bf16[2,192,128]{2,1,0:T(8,128)(2,1)S(1)} collective-permute-done((bf16[2,192,128]{2,1,0:T(8,128)(2,1)S(1)}, bf16[2,192,128]{2,1,0:T(8,128)(2,1)S(1)}, u32[]{:S(2)}, u32[]{:S(2)}) %collective-permute-start.3) | collective-permute-done | bytes 98336 | tf_op jit(solution)/shard_map/ppermute | solution.py:33
  14.3 1.7 %image.1 = (bf16[2,192,128]{2,1,0:T(8,128)(2,1)S(1)}, bf16[4,192,128]{2,1,0:T(8,128)(2,1)S(1)}) custom-call(s32[8]{0:T(128)S(1)} %copy-done.4, bf16[2,192,128]{2,1,0:T(8,128)(2,1)S(1)} %pack.1.refs_0_, bf16[2,192,128]{2,1,0:T(8,128)(2,1)S(1)} %collective-permute-done.refs_1_, bf16[2,192,128]{2,1,0:T(8,128)(2,1)S(1)} %collective-permute-done.1.refs_2_, ...), custom_call_target="tpu_custom_call" | custom-call | flops 805306368 | bytes 2359296 | tf_op jit(solution)/shard_map/image/pallas_call | solution.py:344
  16.0 1.6 %collective-permute-start.8 = (bf16[2,192,128]{2,1,0:T(8,128)(2,1)S(1)}, bf16[2,192,128]{2,1,0:T(8,128)(2,1)S(1)}, u32[]{:S(2)}, u32[]{:S(2)}) collective-permute-start(bf16[2,192,128]{2,1,0:T(8,128)(2,1)S(1)} %get-tuple-element.11), channel_id=1, source_target_pairs={{0,2},{1,3},{2,0},{3,1},{4,6},{5,7},{6,4},{7,5},{8,10},{9,11},{10,... | collective-permute-start | bytes 294920 | tf_op jit(solution)/shard_map/ppermute | solution.py:40
  17.6 0.2 overlap.1.refs_0_
  17.8 0.1 collective-permute-start.4
  17.9 0.6 %collective-permute-start.5 = (f32[16,128]{1,0:T(8,128)S(1)}, f32[16,128]{1,0:T(8,128)S(1)}, u32[]{:S(2)}, u32[]{:S(2)}) collective-permute-start(f32[16,128]{1,0:T(8,128)S(1)} %overlap.1.refs_0_), channel_id=1, source_target_pairs={{0,2},{1,3},{2,0},{3,1},{4,6},{5,7},{6,4},{7,5},{8,10},{9,11},{10,... | collective-permute-start | bytes 24584 | tf_op jit(solution)/shard_map/ppermute | solution.py:40
  18.5 1.3 %collective-permute-start.6 = (f32[16,128]{1,0:T(8,128)S(1)}, f32[16,128]{1,0:T(8,128)S(1)}, u32[]{:S(2)}, u32[]{:S(2)}) collective-permute-start(f32[16,128]{1,0:T(8,128)S(1)} %overlap.1.refs_0_), channel_id=1, source_target_pairs={{0,3},{1,2},{2,1},{3,0},{4,7},{5,6},{6,5},{7,4},{8,11},{9,10},{10,... | collective-permute-start | bytes 24584 | tf_op jit(solution)/shard_map/ppermute | solution.py:40
  19.7 0.1 copy.7.owners_ref
  19.8 0.3 %collective-permute-start.7 = (bf16[4,192,128]{2,1,0:T(8,128)(2,1)S(1)}, bf16[4,192,128]{2,1,0:T(8,128)(2,1)S(1)}, u32[]{:S(2)}, u32[]{:S(2)}) collective-permute-start(bf16[4,192,128]{2,1,0:T(8,128)(2,1)S(1)} %get-tuple-element.8.halves_ref.refs_0_), channel_id=1, source_target_pairs={{0,1},{1,0},{2,3},{3,2},{4,5},{5,4},{6,7},{7,6},{8,9},{9,8},{10,11... | collective-permute-start | bytes 589832 | tf_op jit(solution)/shard_map/ppermute | solution.py:40
  20.2 0.5 %collective-permute-done.8.refs_2_ = bf16[2,192,128]{2,1,0:T(8,128)(2,1)S(1)} collective-permute-done((bf16[2,192,128]{2,1,0:T(8,128)(2,1)S(1)}, bf16[2,192,128]{2,1,0:T(8,128)(2,1)S(1)}, u32[]{:S(2)}, u32[]{:S(2)}) %collective-permute-start.8) | collective-permute-done | bytes 98336 | tf_op jit(solution)/shard_map/ppermute | solution.py:40
  20.7 0.0 collective-permute-start.9
  20.7 0.0 collective-permute-done.4.refs_1_
  20.7 0.9 %collective-permute-done.5.refs_2_ = f32[16,128]{1,0:T(8,128)S(1)} collective-permute-done((f32[16,128]{1,0:T(8,128)S(1)}, f32[16,128]{1,0:T(8,128)S(1)}, u32[]{:S(2)}, u32[]{:S(2)}) %collective-permute-start.5) | collective-permute-done | bytes 8224 | tf_op jit(solution)/shard_map/ppermute | solution.py:40
  21.6 0.0 collective-permute-done.6.refs_3_
  21.6 0.5 %factor.1 = (f32[16,16]{1,0:T(8,128)S(1)}, bf16[256,256]{1,0:T(8,128)(2,1)S(1)}) custom-call(s32[16,1]{1,0:T(8,128)S(1)} %copy.7.owners_ref, f32[16,128]{1,0:T(8,128)S(1)} %overlap.1.refs_0_, f32[16,128]{1,0:T(8,128)S(1)} %collective-permute-done.4.refs_1_, f32[16,128]{1,0:T(8,128)S(1)} %collective-permute-done.5.refs_2_, ...), custom_call_target="tpu_custom_call" | custom-call | flops 3000000000 | bytes 1024 | tf_op jit(solution)/shard_map/factor/pallas_call | solution.py:371
  22.2 0.0 collective-permute-done.7.refs_1_
  22.2 0.0 collective-permute-done.9.refs_3_
  22.2 1.1 %route.1 = (bf16[8,64,192]{2,1,0:T(8,128)(2,1)}, f32[16,16]{1,0:T(8,128)}) custom-call(f32[16,16]{1,0:T(8,128)S(1)} %get-tuple-element.9.overlap_ref, bf16[256,256]{1,0:T(8,128)(2,1)S(1)} %get-tuple-element.10.weights_ref, bf16[4,192,128]{2,1,0:T(8,128)(2,1)S(1)} %get-tuple-element.8.halves_ref.refs_0_, ...), custom_call_target="tpu_custom_call" | custom-call | flops 3145728 | bytes 1179648 | tf_op jit(solution)/shard_map/route/pallas_call | solution.py:379
  (7 shorter events, 0.0 us)
Async XLA Ops:
  0.6 0.9 %copy-start = (bf16[16,16,192]{2,1,0:T(8,128)(2,1)S(1)}, bf16[16,16,192]{2,1,0:T(8,128)(2,1)}, u32[]{:S(2)}) copy-start(bf16[16,16,192]{2,1,0:T(8,128)(2,1)} %orbitals_ref.3) | copy-start | bytes 294916
  1.5 12.7 %copy-start.4 = (s32[8]{0:T(128)S(1)}, s32[8]{0:T(128)}, u32[]{:S(2)}) copy-start(s32[8]{0:T(128)} %occupied_ref.1) | copy-start | bytes 100
  1.5 18.2 %copy-start.5 = (s32[16,1]{0,1:T(1,128)S(1)}, s32[16,1]{0,1:T(1,128)}, u32[]{:S(2)}) copy-start(s32[16,1]{0,1:T(1,128)} %param.8) | copy-start | bytes 196
  1.8 15.8 %copy-start.1 = (bf16[16,16,192]{2,1,0:T(8,128)(2,1)S(1)}, bf16[16,16,192]{2,1,0:T(8,128)(2,1)}, u32[]{:S(2)}) copy-start(bf16[16,16,192]{2,1,0:T(8,128)(2,1)} %orbitals_ref.3) | copy-start | bytes 294916
  1.8 11.1 %collective-permute-start = (bf16[2,192,128]{2,1,0:T(8,128)(2,1)S(1)}, bf16[2,192,128]{2,1,0:T(8,128)(2,1)S(1)}, u32[]{:S(2)}, u32[]{:S(2)}) collective-permute-start(bf16[2,192,128]{2,1,0:T(8,128)(2,1)S(1)} %pack.1.refs_0_), channel_id=1, source_target_pairs={{24,0},{28,4},{0,8},{4,12},{8,16},{12,20},{16,24},{20,28},{25,1},{... | collective-permute-start | bytes 294920 | tf_op jit(solution)/shard_map/ppermute | solution.py:33
  4.9 8.9 %collective-permute-start.1 = (bf16[2,192,128]{2,1,0:T(8,128)(2,1)S(1)}, bf16[2,192,128]{2,1,0:T(8,128)(2,1)S(1)}, u32[]{:S(2)}, u32[]{:S(2)}) collective-permute-start(bf16[2,192,128]{2,1,0:T(8,128)(2,1)S(1)} %pack.1.refs_0_), channel_id=1, source_target_pairs={{28,0},{0,4},{4,8},{8,12},{12,16},{16,20},{20,24},{24,28},{29,1},{... | collective-permute-start | bytes 294920 | tf_op jit(solution)/shard_map/ppermute | solution.py:33
  6.4 7.3 %collective-permute-start.2 = (bf16[2,192,128]{2,1,0:T(8,128)(2,1)S(1)}, bf16[2,192,128]{2,1,0:T(8,128)(2,1)S(1)}, u32[]{:S(2)}, u32[]{:S(2)}) collective-permute-start(bf16[2,192,128]{2,1,0:T(8,128)(2,1)S(1)} %pack.1.refs_0_), channel_id=1, source_target_pairs={{8,0},{12,4},{16,8},{20,12},{24,16},{28,20},{0,24},{4,28},{9,1},{1... | collective-permute-start | bytes 294920 | tf_op jit(solution)/shard_map/ppermute | solution.py:33
  8.6 5.6 %collective-permute-start.3 = (bf16[2,192,128]{2,1,0:T(8,128)(2,1)S(1)}, bf16[2,192,128]{2,1,0:T(8,128)(2,1)S(1)}, u32[]{:S(2)}, u32[]{:S(2)}) collective-permute-start(bf16[2,192,128]{2,1,0:T(8,128)(2,1)S(1)} %pack.1.refs_0_), channel_id=1, source_target_pairs={{4,0},{8,4},{12,8},{16,12},{20,16},{24,20},{28,24},{0,28},{5,1},{9... | collective-permute-start | bytes 294920 | tf_op jit(solution)/shard_map/ppermute | solution.py:33
  9.9 1.0 %copy-start.2 = (bf16[3,192,192]{2,1,0:T(8,128)(2,1)S(1)}, bf16[3,192,192]{2,1,0:T(8,128)(2,1)}, u32[]{:S(2)}) copy-start(bf16[3,192,192]{2,1,0:T(8,128)(2,1)} %constant.3.tables_ref) | copy-start | bytes 663556
  10.8 0.7 %copy-start.3 = (f32[16,192]{1,0:T(8,128)S(1)}, f32[16,192]{1,0:T(8,128)}, u32[]{:S(2)}) copy-start(f32[16,192]{1,0:T(8,128)} %coulomb_ref.1) | copy-start | bytes 36868
  16.0 4.7 %collective-permute-start.8 = (bf16[2,192,128]{2,1,0:T(8,128)(2,1)S(1)}, bf16[2,192,128]{2,1,0:T(8,128)(2,1)S(1)}, u32[]{:S(2)}, u32[]{:S(2)}) collective-permute-start(bf16[2,192,128]{2,1,0:T(8,128)(2,1)S(1)} %get-tuple-element.11), channel_id=1, source_target_pairs={{0,2},{1,3},{2,0},{3,1},{4,6},{5,7},{6,4},{7,5},{8,10},{9,11},{10,... | collective-permute-start | bytes 294920 | tf_op jit(solution)/shard_map/ppermute | solution.py:40
  17.8 2.9 %collective-permute-start.4 = (f32[16,128]{1,0:T(8,128)S(1)}, f32[16,128]{1,0:T(8,128)S(1)}, u32[]{:S(2)}, u32[]{:S(2)}) collective-permute-start(f32[16,128]{1,0:T(8,128)S(1)} %overlap.1.refs_0_), channel_id=1, source_target_pairs={{0,1},{1,0},{2,3},{3,2},{4,5},{5,4},{6,7},{7,6},{8,9},{9,8},{10,11... | collective-permute-start | bytes 24584 | tf_op jit(solution)/shard_map/ppermute | solution.py:40
  17.9 3.8 %collective-permute-start.5 = (f32[16,128]{1,0:T(8,128)S(1)}, f32[16,128]{1,0:T(8,128)S(1)}, u32[]{:S(2)}, u32[]{:S(2)}) collective-permute-start(f32[16,128]{1,0:T(8,128)S(1)} %overlap.1.refs_0_), channel_id=1, source_target_pairs={{0,2},{1,3},{2,0},{3,1},{4,6},{5,7},{6,4},{7,5},{8,10},{9,11},{10,... | collective-permute-start | bytes 24584 | tf_op jit(solution)/shard_map/ppermute | solution.py:40
  18.5 3.2 %collective-permute-start.6 = (f32[16,128]{1,0:T(8,128)S(1)}, f32[16,128]{1,0:T(8,128)S(1)}, u32[]{:S(2)}, u32[]{:S(2)}) collective-permute-start(f32[16,128]{1,0:T(8,128)S(1)} %overlap.1.refs_0_), channel_id=1, source_target_pairs={{0,3},{1,2},{2,1},{3,0},{4,7},{5,6},{6,5},{7,4},{8,11},{9,10},{10,... | collective-permute-start | bytes 24584 | tf_op jit(solution)/shard_map/ppermute | solution.py:40
  19.8 2.4 %collective-permute-start.7 = (bf16[4,192,128]{2,1,0:T(8,128)(2,1)S(1)}, bf16[4,192,128]{2,1,0:T(8,128)(2,1)S(1)}, u32[]{:S(2)}, u32[]{:S(2)}) collective-permute-start(bf16[4,192,128]{2,1,0:T(8,128)(2,1)S(1)} %get-tuple-element.8.halves_ref.refs_0_), channel_id=1, source_target_pairs={{0,1},{1,0},{2,3},{3,2},{4,5},{5,4},{6,7},{7,6},{8,9},{9,8},{10,11... | collective-permute-start | bytes 589832 | tf_op jit(solution)/shard_map/ppermute | solution.py:40
  20.7 1.5 %collective-permute-start.9 = (bf16[2,192,128]{2,1,0:T(8,128)(2,1)S(1)}, bf16[2,192,128]{2,1,0:T(8,128)(2,1)S(1)}, u32[]{:S(2)}, u32[]{:S(2)}) collective-permute-start(bf16[2,192,128]{2,1,0:T(8,128)(2,1)S(1)} %collective-permute-done.8.refs_2_), channel_id=1, source_target_pairs={{0,1},{1,0},{2,3},{3,2},{4,5},{5,4},{6,7},{7,6},{8,9},{9,8},{10,11... | collective-permute-start | bytes 294920 | tf_op jit(solution)/shard_map/ppermute | solution.py:40

commit v20 on v16

--- a/solution.py
+++ b/solution.py
@@ -362,7 +362,7 @@
         operands=2,
     )(orbitals, parts)
     overlaps = [overlap] + [swapped(overlap, flip) for flip in range(1, groups)]
-    images = [parts] + [swapped(parts, flip) for flip in range(1, near)]
+    images = [parts] + [swapped(high, flip) for flip in range(1, near)]
     for grid in range(1, grids):
         across = swapped(high, grid * near)
         images += [across] + [swapped(across, flip) for flip in range(1, near)]

time: 22.6 us -> 22.6 us (level)
  no operation moved by 1% of the time
where the time goes in v20:
time: 22.6 us; the launch traced here: 22.2 us
  starting transfers between devices  12 us (53%)
  Pallas kernels  5.05 us (22%)
  local copies, waits for them, and re-layouts  2.67 us (12%)
  waiting for transfers between devices  1.79 us (8%)
  between operations  0.73 us (3%)
    ppermute x4, starting transfers between devices, exchanged(): lax.ppermute(value, 'band', [(row[turn], block) for block, row in enumera...  8.15 us
    ppermute x6, starting transfers between devices, swapped(): lax.ppermute(value, ('grid', 'ham'), [(group, group ^ flip) for group in...  3.82 us
    unnamed x13, local copies, waits for them, and re-layouts  2.67 us
    pallas_call x1, Pallas kernels, local(): call(functools.partial(image_kernel, members), 'image', [shape((packs, po...  1.77 us
    ppermute x6, waiting for transfers between devices, swapped(): lax.ppermute(value, ('grid', 'ham'), [(group, group ^ flip) for group in...  1.49 us
    pallas_call x1, Pallas kernels, local(): call(response_kernel, 'response', [shape((lines, points, padded), F32)],...  1.3 us
    pallas_call x1, Pallas kernels, local(): call(route_kernel, 'route', [shape((CAP, groups * lines, points), BF16),...  1.03 us
    pallas_call x1, Pallas kernels, local(): call(functools.partial(factor_kernel, cells), 'factor', [shape((members,...  0.53 us
  transfers between devices with their start and end apart: 10, of which 3 were waited for; matrix products, arithmetic and copies ran while one was open for 0% of the time, Pallas kernels for 9%

profile of v20, /device:TPU:0, one launch (start us, length us, event | category | flops | bytes accessed | tf_op | source)
XLA Modules:
  0.0 22.2 jit_solution(5519228762822681188)
XLA Ops:
  0.6 0.0 copy-start
  0.6 0.9 %copy-done = bf16[16,16,192]{2,1,0:T(8,128)(2,1)S(1)} copy-done((bf16[16,16,192]{2,1,0:T(8,128)(2,1)S(1)}, bf16[16,16,192]{2,1,0:T(8,128)(2,1)}, u32[]{:S(2)}) %copy-start) | copy-done | bytes 98328
  1.5 0.2 %pack.1.refs_0_ = bf16[2,192,128]{2,1,0:T(8,128)(2,1)S(1)} custom-call(bf16[16,16,192]{2,1,0:T(8,128)(2,1)S(1)} %copy-done), custom_call_target="tpu_custom_call" | custom-call | flops 49152 | bytes 196608 | tf_op jit(solution)/shard_map/pack/pallas_call | solution.py:325
  1.8 0.0 copy-start.1
  1.8 3.0 %collective-permute-start = (bf16[2,192,128]{2,1,0:T(8,128)(2,1)S(1)}, bf16[2,192,128]{2,1,0:T(8,128)(2,1)S(1)}, u32[]{:S(2)}, u32[]{:S(2)}) collective-permute-start(bf16[2,192,128]{2,1,0:T(8,128)(2,1)S(1)} %pack.1.refs_0_), channel_id=1, source_target_pairs={{28,0},{0,4},{4,8},{8,12},{12,16},{16,20},{20,24},{24,28},{29,1},{... | collective-permute-start | bytes 294920 | tf_op jit(solution)/shard_map/ppermute | solution.py:33
  4.8 1.6 %collective-permute-start.1 = (bf16[2,192,128]{2,1,0:T(8,128)(2,1)S(1)}, bf16[2,192,128]{2,1,0:T(8,128)(2,1)S(1)}, u32[]{:S(2)}, u32[]{:S(2)}) collective-permute-start(bf16[2,192,128]{2,1,0:T(8,128)(2,1)S(1)} %pack.1.refs_0_), channel_id=1, source_target_pairs={{24,0},{28,4},{0,8},{4,12},{8,16},{12,20},{16,24},{20,28},{25,1},{... | collective-permute-start | bytes 294920 | tf_op jit(solution)/shard_map/ppermute | solution.py:33
  6.4 2.2 %collective-permute-start.2 = (bf16[2,192,128]{2,1,0:T(8,128)(2,1)S(1)}, bf16[2,192,128]{2,1,0:T(8,128)(2,1)S(1)}, u32[]{:S(2)}, u32[]{:S(2)}) collective-permute-start(bf16[2,192,128]{2,1,0:T(8,128)(2,1)S(1)} %pack.1.refs_0_), channel_id=1, source_target_pairs={{8,0},{12,4},{16,8},{20,12},{24,16},{28,20},{0,24},{4,28},{9,1},{1... | collective-permute-start | bytes 294920 | tf_op jit(solution)/shard_map/ppermute | solution.py:33
  8.6 1.3 %collective-permute-start.3 = (bf16[2,192,128]{2,1,0:T(8,128)(2,1)S(1)}, bf16[2,192,128]{2,1,0:T(8,128)(2,1)S(1)}, u32[]{:S(2)}, u32[]{:S(2)}) collective-permute-start(bf16[2,192,128]{2,1,0:T(8,128)(2,1)S(1)} %pack.1.refs_0_), channel_id=1, source_target_pairs={{4,0},{8,4},{12,8},{16,12},{20,16},{24,20},{28,24},{0,28},{5,1},{9... | collective-permute-start | bytes 294920 | tf_op jit(solution)/shard_map/ppermute | solution.py:33
  9.9 1.0 %copy-done.2 = bf16[3,192,192]{2,1,0:T(8,128)(2,1)S(1)} copy-done((bf16[3,192,192]{2,1,0:T(8,128)(2,1)S(1)}, bf16[3,192,192]{2,1,0:T(8,128)(2,1)}, u32[]{:S(2)}) %copy-start.2) | copy-done | bytes 221208
  10.9 0.7 %copy-done.3 = f32[16,192]{1,0:T(8,128)S(1)} copy-done((f32[16,192]{1,0:T(8,128)S(1)}, f32[16,192]{1,0:T(8,128)}, u32[]{:S(2)}) %copy-start.3) | copy-done | bytes 12312
  11.6 1.3 %response.1.refs_5_ = f32[16,192,256]{2,1,0:T(8,128)S(1)} custom-call(f32[16,192]{1,0:T(8,128)S(1)} %copy-done.3, bf16[3,192,192]{2,1,0:T(8,128)(2,1)S(1)} %copy-done.2), custom_call_target="tpu_custom_call" | custom-call | flops 452984832 | bytes 2359296 | tf_op jit(solution)/shard_map/response/pallas_call | solution.py:335
  12.9 0.0 collective-permute-done.refs_1_
  12.9 0.0 collective-permute-done.1.refs_2_
  13.0 0.3 %collective-permute-done.2.refs_3_ = bf16[2,192,128]{2,1,0:T(8,128)(2,1)S(1)} collective-permute-done((bf16[2,192,128]{2,1,0:T(8,128)(2,1)S(1)}, bf16[2,192,128]{2,1,0:T(8,128)(2,1)S(1)}, u32[]{:S(2)}, u32[]{:S(2)}) %collective-permute-start.2) | collective-permute-done | bytes 98336 | tf_op jit(solution)/shard_map/ppermute | solution.py:33
  13.2 0.0 collective-permute-done.3.refs_4_
  13.3 1.8 %image.1 = (bf16[2,192,128]{2,1,0:T(8,128)(2,1)S(1)}, bf16[4,192,128]{2,1,0:T(8,128)(2,1)S(1)}) custom-call(s32[8]{0:T(128)S(1)} %copy-done.4, bf16[2,192,128]{2,1,0:T(8,128)(2,1)S(1)} %pack.1.refs_0_, bf16[2,192,128]{2,1,0:T(8,128)(2,1)S(1)} %collective-permute-done.refs_1_, bf16[2,192,128]{2,1,0:T(8,128)(2,1)S(1)} %collective-permute-done.1.refs_2_, ...), custom_call_target="tpu_custom_call" | custom-call | flops 805306368 | bytes 2359296 | tf_op jit(solution)/shard_map/image/pallas_call | solution.py:344
  15.0 1.5 %collective-permute-start.8 = (bf16[2,192,128]{2,1,0:T(8,128)(2,1)S(1)}, bf16[2,192,128]{2,1,0:T(8,128)(2,1)S(1)}, u32[]{:S(2)}, u32[]{:S(2)}) collective-permute-start(bf16[2,192,128]{2,1,0:T(8,128)(2,1)S(1)} %get-tuple-element.11), channel_id=1, source_target_pairs={{0,2},{1,3},{2,0},{3,1},{4,6},{5,7},{6,4},{7,5},{8,10},{9,11},{10,... | collective-permute-start | bytes 294920 | tf_op jit(solution)/shard_map/ppermute | solution.py:40
  16.6 0.2 overlap.1.refs_0_
  16.8 0.1 collective-permute-start.4
  16.9 0.6 %collective-permute-start.5 = (f32[16,128]{1,0:T(8,128)S(1)}, f32[16,128]{1,0:T(8,128)S(1)}, u32[]{:S(2)}, u32[]{:S(2)}) collective-permute-start(f32[16,128]{1,0:T(8,128)S(1)} %overlap.1.refs_0_), channel_id=1, source_target_pairs={{0,2},{1,3},{2,0},{3,1},{4,6},{5,7},{6,4},{7,5},{8,10},{9,11},{10,... | collective-permute-start | bytes 24584 | tf_op jit(solution)/shard_map/ppermute | solution.py:40
  17.5 1.2 %collective-permute-start.6 = (f32[16,128]{1,0:T(8,128)S(1)}, f32[16,128]{1,0:T(8,128)S(1)}, u32[]{:S(2)}, u32[]{:S(2)}) collective-permute-start(f32[16,128]{1,0:T(8,128)S(1)} %overlap.1.refs_0_), channel_id=1, source_target_pairs={{0,3},{1,2},{2,1},{3,0},{4,7},{5,6},{6,5},{7,4},{8,11},{9,10},{10,... | collective-permute-start | bytes 24584 | tf_op jit(solution)/shard_map/ppermute | solution.py:40
  18.7 0.1 copy.7.owners_ref
  18.8 0.3 %collective-permute-start.7 = (bf16[2,192,128]{2,1,0:T(8,128)(2,1)S(1)}, bf16[2,192,128]{2,1,0:T(8,128)(2,1)S(1)}, u32[]{:S(2)}, u32[]{:S(2)}) collective-permute-start(bf16[2,192,128]{2,1,0:T(8,128)(2,1)S(1)} %get-tuple-element.11), channel_id=1, source_target_pairs={{0,1},{1,0},{2,3},{3,2},{4,5},{5,4},{6,7},{7,6},{8,9},{9,8},{10,11... | collective-permute-start | bytes 294920 | tf_op jit(solution)/shard_map/ppermute | solution.py:40
  19.1 0.6 %collective-permute-done.8.refs_2_ = bf16[2,192,128]{2,1,0:T(8,128)(2,1)S(1)} collective-permute-done((bf16[2,192,128]{2,1,0:T(8,128)(2,1)S(1)}, bf16[2,192,128]{2,1,0:T(8,128)(2,1)S(1)}, u32[]{:S(2)}, u32[]{:S(2)}) %collective-permute-start.8) | collective-permute-done | bytes 98336 | tf_op jit(solution)/shard_map/ppermute | solution.py:40
  19.7 0.0 collective-permute-start.9
  19.7 0.0 collective-permute-done.4.refs_1_
  19.7 0.9 %collective-permute-done.5.refs_2_ = f32[16,128]{1,0:T(8,128)S(1)} collective-permute-done((f32[16,128]{1,0:T(8,128)S(1)}, f32[16,128]{1,0:T(8,128)S(1)}, u32[]{:S(2)}, u32[]{:S(2)}) %collective-permute-start.5) | collective-permute-done | bytes 8224 | tf_op jit(solution)/shard_map/ppermute | solution.py:40
  20.6 0.0 collective-permute-done.6.refs_3_
  20.6 0.5 %factor.1 = (f32[16,16]{1,0:T(8,128)S(1)}, bf16[256,256]{1,0:T(8,128)(2,1)S(1)}) custom-call(s32[16,1]{1,0:T(8,128)S(1)} %copy.7.owners_ref, f32[16,128]{1,0:T(8,128)S(1)} %overlap.1.refs_0_, f32[16,128]{1,0:T(8,128)S(1)} %collective-permute-done.4.refs_1_, f32[16,128]{1,0:T(8,128)S(1)} %collective-permute-done.5.refs_2_, ...), custom_call_target="tpu_custom_call" | custom-call | flops 3000000000 | bytes 1024 | tf_op jit(solution)/shard_map/factor/pallas_call | solution.py:371
  21.2 0.0 collective-permute-done.7.refs_1_
  21.2 0.0 collective-permute-done.9.refs_3_
  21.2 1.0 %route.1 = (bf16[8,64,192]{2,1,0:T(8,128)(2,1)}, f32[16,16]{1,0:T(8,128)}) custom-call(f32[16,16]{1,0:T(8,128)S(1)} %get-tuple-element.9.overlap_ref, bf16[256,256]{1,0:T(8,128)(2,1)S(1)} %get-tuple-element.10.weights_ref, bf16[4,192,128]{2,1,0:T(8,128)(2,1)S(1)} %get-tuple-element.8.halves_ref.refs_0_, ...), custom_call_target="tpu_custom_call" | custom-call | flops 3145728 | bytes 1179648 | tf_op jit(solution)/shard_map/route/pallas_call | solution.py:379
  (7 shorter events, 0.0 us)
Async XLA Ops:
  0.6 0.9 %copy-start = (bf16[16,16,192]{2,1,0:T(8,128)(2,1)S(1)}, bf16[16,16,192]{2,1,0:T(8,128)(2,1)}, u32[]{:S(2)}) copy-start(bf16[16,16,192]{2,1,0:T(8,128)(2,1)} %orbitals_ref.3) | copy-start | bytes 294916
  1.5 11.7 %copy-start.4 = (s32[8]{0:T(128)S(1)}, s32[8]{0:T(128)}, u32[]{:S(2)}) copy-start(s32[8]{0:T(128)} %occupied_ref.1) | copy-start | bytes 100
  1.5 17.2 %copy-start.5 = (s32[16,1]{0,1:T(1,128)S(1)}, s32[16,1]{0,1:T(1,128)}, u32[]{:S(2)}) copy-start(s32[16,1]{0,1:T(1,128)} %param.8) | copy-start | bytes 196
  1.8 14.8 %copy-start.1 = (bf16[16,16,192]{2,1,0:T(8,128)(2,1)S(1)}, bf16[16,16,192]{2,1,0:T(8,128)(2,1)}, u32[]{:S(2)}) copy-start(bf16[16,16,192]{2,1,0:T(8,128)(2,1)} %orbitals_ref.3) | copy-start | bytes 294916
  1.8 11.1 %collective-permute-start = (bf16[2,192,128]{2,1,0:T(8,128)(2,1)S(1)}, bf16[2,192,128]{2,1,0:T(8,128)(2,1)S(1)}, u32[]{:S(2)}, u32[]{:S(2)}) collective-permute-start(bf16[2,192,128]{2,1,0:T(8,128)(2,1)S(1)} %pack.1.refs_0_), channel_id=1, source_target_pairs={{28,0},{0,4},{4,8},{8,12},{12,16},{16,20},{20,24},{24,28},{29,1},{... | collective-permute-start | bytes 294920 | tf_op jit(solution)/shard_map/ppermute | solution.py:33
  4.8 8.1 %collective-permute-start.1 = (bf16[2,192,128]{2,1,0:T(8,128)(2,1)S(1)}, bf16[2,192,128]{2,1,0:T(8,128)(2,1)S(1)}, u32[]{:S(2)}, u32[]{:S(2)}) collective-permute-start(bf16[2,192,128]{2,1,0:T(8,128)(2,1)S(1)} %pack.1.refs_0_), channel_id=1, source_target_pairs={{24,0},{28,4},{0,8},{4,12},{8,16},{12,20},{16,24},{20,28},{25,1},{... | collective-permute-start | bytes 294920 | tf_op jit(solution)/shard_map/ppermute | solution.py:33
  6.4 6.8 %collective-permute-start.2 = (bf16[2,192,128]{2,1,0:T(8,128)(2,1)S(1)}, bf16[2,192,128]{2,1,0:T(8,128)(2,1)S(1)}, u32[]{:S(2)}, u32[]{:S(2)}) collective-permute-start(bf16[2,192,128]{2,1,0:T(8,128)(2,1)S(1)} %pack.1.refs_0_), channel_id=1, source_target_pairs={{8,0},{12,4},{16,8},{20,12},{24,16},{28,20},{0,24},{4,28},{9,1},{1... | collective-permute-start | bytes 294920 | tf_op jit(solution)/shard_map/ppermute | solution.py:33
  8.6 4.6 %collective-permute-start.3 = (bf16[2,192,128]{2,1,0:T(8,128)(2,1)S(1)}, bf16[2,192,128]{2,1,0:T(8,128)(2,1)S(1)}, u32[]{:S(2)}, u32[]{:S(2)}) collective-permute-start(bf16[2,192,128]{2,1,0:T(8,128)(2,1)S(1)} %pack.1.refs_0_), channel_id=1, source_target_pairs={{4,0},{8,4},{12,8},{16,12},{20,16},{24,20},{28,24},{0,28},{5,1},{9... | collective-permute-start | bytes 294920 | tf_op jit(solution)/shard_map/ppermute | solution.py:33
  9.9 1.0 %copy-start.2 = (bf16[3,192,192]{2,1,0:T(8,128)(2,1)S(1)}, bf16[3,192,192]{2,1,0:T(8,128)(2,1)}, u32[]{:S(2)}) copy-start(bf16[3,192,192]{2,1,0:T(8,128)(2,1)} %constant.3.tables_ref) | copy-start | bytes 663556
  10.9 0.7 %copy-start.3 = (f32[16,192]{1,0:T(8,128)S(1)}, f32[16,192]{1,0:T(8,128)}, u32[]{:S(2)}) copy-start(f32[16,192]{1,0:T(8,128)} %coulomb_ref.1) | copy-start | bytes 36868
  15.0 4.7 %collective-permute-start.8 = (bf16[2,192,128]{2,1,0:T(8,128)(2,1)S(1)}, bf16[2,192,128]{2,1,0:T(8,128)(2,1)S(1)}, u32[]{:S(2)}, u32[]{:S(2)}) collective-permute-start(bf16[2,192,128]{2,1,0:T(8,128)(2,1)S(1)} %get-tuple-element.11), channel_id=1, source_target_pairs={{0,2},{1,3},{2,0},{3,1},{4,6},{5,7},{6,4},{7,5},{8,10},{9,11},{10,... | collective-permute-start | bytes 294920 | tf_op jit(solution)/shard_map/ppermute | solution.py:40
  16.8 2.9 %collective-permute-start.4 = (f32[16,128]{1,0:T(8,128)S(1)}, f32[16,128]{1,0:T(8,128)S(1)}, u32[]{:S(2)}, u32[]{:S(2)}) collective-permute-start(f32[16,128]{1,0:T(8,128)S(1)} %overlap.1.refs_0_), channel_id=1, source_target_pairs={{0,1},{1,0},{2,3},{3,2},{4,5},{5,4},{6,7},{7,6},{8,9},{9,8},{10,11... | collective-permute-start | bytes 24584 | tf_op jit(solution)/shard_map/ppermute | solution.py:40
  16.9 3.8 %collective-permute-start.5 = (f32[16,128]{1,0:T(8,128)S(1)}, f32[16,128]{1,0:T(8,128)S(1)}, u32[]{:S(2)}, u32[]{:S(2)}) collective-permute-start(f32[16,128]{1,0:T(8,128)S(1)} %overlap.1.refs_0_), channel_id=1, source_target_pairs={{0,2},{1,3},{2,0},{3,1},{4,6},{5,7},{6,4},{7,5},{8,10},{9,11},{10,... | collective-permute-start | bytes 24584 | tf_op jit(solution)/shard_map/ppermute | solution.py:40
  17.5 3.2 %collective-permute-start.6 = (f32[16,128]{1,0:T(8,128)S(1)}, f32[16,128]{1,0:T(8,128)S(1)}, u32[]{:S(2)}, u32[]{:S(2)}) collective-permute-start(f32[16,128]{1,0:T(8,128)S(1)} %overlap.1.refs_0_), channel_id=1, source_target_pairs={{0,3},{1,2},{2,1},{3,0},{4,7},{5,6},{6,5},{7,4},{8,11},{9,10},{10,... | collective-permute-start | bytes 24584 | tf_op jit(solution)/shard_map/ppermute | solution.py:40
  18.8 2.4 %collective-permute-start.7 = (bf16[2,192,128]{2,1,0:T(8,128)(2,1)S(1)}, bf16[2,192,128]{2,1,0:T(8,128)(2,1)S(1)}, u32[]{:S(2)}, u32[]{:S(2)}) collective-permute-start(bf16[2,192,128]{2,1,0:T(8,128)(2,1)S(1)} %get-tuple-element.11), channel_id=1, source_target_pairs={{0,1},{1,0},{2,3},{3,2},{4,5},{5,4},{6,7},{7,6},{8,9},{9,8},{10,11... | collective-permute-start | bytes 294920 | tf_op jit(solution)/shard_map/ppermute | solution.py:40
  19.7 1.5 %collective-permute-start.9 = (bf16[2,192,128]{2,1,0:T(8,128)(2,1)S(1)}, bf16[2,192,128]{2,1,0:T(8,128)(2,1)S(1)}, u32[]{:S(2)}, u32[]{:S(2)}) collective-permute-start(bf16[2,192,128]{2,1,0:T(8,128)(2,1)S(1)} %collective-permute-done.8.refs_2_), channel_id=1, source_target_pairs={{0,1},{1,0},{2,3},{3,2},{4,5},{5,4},{6,7},{7,6},{8,9},{9,8},{10,11... | collective-permute-start | bytes 294920 | tf_op jit(solution)/shard_map/ppermute | solution.py:40

commit v21 on v16

--- a/solution.py
+++ b/solution.py
@@ -213,7 +213,7 @@
     members = owners_ref.shape[0]
     span = LANES // members
     turn = own_turn()
-    sums = [part[...] for part in parts]
+    sums = [part[...] for part in reversed(parts)]
     while len(sums) > 1:
         sums = [a + b for a, b in zip(sums[::2], sums[1::2])]
     high, rest = split(sums[0])
@@ -361,7 +361,7 @@
         8 * orbitals.size,
         operands=2,
     )(orbitals, parts)
-    overlaps = [overlap] + [swapped(overlap, flip) for flip in range(1, groups)]
+    overlaps = [swapped(overlap, flip) for flip in reversed(range(1, groups))] + [overlap]
     images = [parts] + [swapped(parts, flip) for flip in range(1, near)]
     for grid in range(1, grids):
         across = swapped(high, grid * near)

time: 22.6 us -> 22.6 us (level)
  starting transfers between devices: 12 us -> 11.6 us
  waiting for transfers between devices: 1.79 us -> 2.09 us
    ppermute x6, starting transfers between devices: 3.82 us -> 3.47 us  [swapped(): lax.ppermute(value, ('grid', 'ham'), [(group, group ^ flip) for group in...]
    ppermute x6, waiting for transfers between devices: 1.49 us -> 1.78 us  [swapped(): lax.ppermute(value, ('grid', 'ham'), [(group, group ^ flip) for group in...]
  transfers between devices with their start and end apart: 10 -> 10, of which waited for: 3 -> 4; matrix products, arithmetic and copies ran while one was open for 0% -> 0% of each run, Pallas kernels for 9% -> 9%
where the time goes in v21:
time: 22.6 us; the launch traced here: 22.2 us
  starting transfers between devices  11.6 us (51%)
  Pallas kernels  5.11 us (23%)
  local copies, waits for them, and re-layouts  2.67 us (12%)
  waiting for transfers between devices  2.09 us (9%)
  between operations  0.73 us (3%)
    ppermute x4, starting transfers between devices, exchanged(): lax.ppermute(value, 'band', [(row[turn], block) for block, row in enumera...  8.15 us
    ppermute x6, starting transfers between devices, swapped(): lax.ppermute(value, ('grid', 'ham'), [(group, group ^ flip) for group in...  3.47 us
    unnamed x13, local copies, waits for them, and re-layouts  2.67 us
    ppermute x6, waiting for transfers between devices, swapped(): lax.ppermute(value, ('grid', 'ham'), [(group, group ^ flip) for group in...  1.78 us
    pallas_call x1, Pallas kernels, local(): call(functools.partial(image_kernel, members), 'image', [shape((packs, po...  1.77 us
    pallas_call x1, Pallas kernels, local(): call(response_kernel, 'response', [shape((lines, points, padded), F32)],...  1.3 us
    pallas_call x1, Pallas kernels, local(): call(route_kernel, 'route', [shape((CAP, groups * lines, points), BF16),...  1.09 us
    pallas_call x1, Pallas kernels, local(): call(functools.partial(factor_kernel, cells), 'factor', [shape((members,...  0.53 us
  transfers between devices with their start and end apart: 10, of which 4 were waited for; matrix products, arithmetic and copies ran while one was open for 0% of the time, Pallas kernels for 9%

profile of v21, /device:TPU:0, one launch (start us, length us, event | category | flops | bytes accessed | tf_op | source)
XLA Modules:
  0.0 22.2 jit_solution(11011463599290377098)
XLA Ops:
  0.6 0.0 copy-start
  0.6 0.9 %copy-done = bf16[16,16,192]{2,1,0:T(8,128)(2,1)S(1)} copy-done((bf16[16,16,192]{2,1,0:T(8,128)(2,1)S(1)}, bf16[16,16,192]{2,1,0:T(8,128)(2,1)}, u32[]{:S(2)}) %copy-start) | copy-done | bytes 98328
  1.5 0.2 %pack.1.refs_0_ = bf16[2,192,128]{2,1,0:T(8,128)(2,1)S(1)} custom-call(bf16[16,16,192]{2,1,0:T(8,128)(2,1)S(1)} %copy-done), custom_call_target="tpu_custom_call" | custom-call | flops 49152 | bytes 196608 | tf_op jit(solution)/shard_map/pack/pallas_call | solution.py:325
  1.8 0.0 copy-start.1
  1.8 3.0 %collective-permute-start = (bf16[2,192,128]{2,1,0:T(8,128)(2,1)S(1)}, bf16[2,192,128]{2,1,0:T(8,128)(2,1)S(1)}, u32[]{:S(2)}, u32[]{:S(2)}) collective-permute-start(bf16[2,192,128]{2,1,0:T(8,128)(2,1)S(1)} %pack.1.refs_0_), channel_id=1, source_target_pairs={{28,0},{0,4},{4,8},{8,12},{12,16},{16,20},{20,24},{24,28},{29,1},{... | collective-permute-start | bytes 294920 | tf_op jit(solution)/shard_map/ppermute | solution.py:33
  4.8 1.6 %collective-permute-start.1 = (bf16[2,192,128]{2,1,0:T(8,128)(2,1)S(1)}, bf16[2,192,128]{2,1,0:T(8,128)(2,1)S(1)}, u32[]{:S(2)}, u32[]{:S(2)}) collective-permute-start(bf16[2,192,128]{2,1,0:T(8,128)(2,1)S(1)} %pack.1.refs_0_), channel_id=1, source_target_pairs={{24,0},{28,4},{0,8},{4,12},{8,16},{12,20},{16,24},{20,28},{25,1},{... | collective-permute-start | bytes 294920 | tf_op jit(solution)/shard_map/ppermute | solution.py:33
  6.4 2.2 %collective-permute-start.2 = (bf16[2,192,128]{2,1,0:T(8,128)(2,1)S(1)}, bf16[2,192,128]{2,1,0:T(8,128)(2,1)S(1)}, u32[]{:S(2)}, u32[]{:S(2)}) collective-permute-start(bf16[2,192,128]{2,1,0:T(8,128)(2,1)S(1)} %pack.1.refs_0_), channel_id=1, source_target_pairs={{8,0},{12,4},{16,8},{20,12},{24,16},{28,20},{0,24},{4,28},{9,1},{1... | collective-permute-start | bytes 294920 | tf_op jit(solution)/shard_map/ppermute | solution.py:33
  8.6 1.3 %collective-permute-start.3 = (bf16[2,192,128]{2,1,0:T(8,128)(2,1)S(1)}, bf16[2,192,128]{2,1,0:T(8,128)(2,1)S(1)}, u32[]{:S(2)}, u32[]{:S(2)}) collective-permute-start(bf16[2,192,128]{2,1,0:T(8,128)(2,1)S(1)} %pack.1.refs_0_), channel_id=1, source_target_pairs={{4,0},{8,4},{12,8},{16,12},{20,16},{24,20},{28,24},{0,28},{5,1},{9... | collective-permute-start | bytes 294920 | tf_op jit(solution)/shard_map/ppermute | solution.py:33
  9.9 1.0 %copy-done.2 = bf16[3,192,192]{2,1,0:T(8,128)(2,1)S(1)} copy-done((bf16[3,192,192]{2,1,0:T(8,128)(2,1)S(1)}, bf16[3,192,192]{2,1,0:T(8,128)(2,1)}, u32[]{:S(2)}) %copy-start.2) | copy-done | bytes 221208
  10.9 0.7 %copy-done.3 = f32[16,192]{1,0:T(8,128)S(1)} copy-done((f32[16,192]{1,0:T(8,128)S(1)}, f32[16,192]{1,0:T(8,128)}, u32[]{:S(2)}) %copy-start.3) | copy-done | bytes 12312
  11.6 1.3 %response.1.refs_5_ = f32[16,192,256]{2,1,0:T(8,128)S(1)} custom-call(f32[16,192]{1,0:T(8,128)S(1)} %copy-done.3, bf16[3,192,192]{2,1,0:T(8,128)(2,1)S(1)} %copy-done.2), custom_call_target="tpu_custom_call" | custom-call | flops 452984832 | bytes 2359296 | tf_op jit(solution)/shard_map/response/pallas_call | solution.py:335
  12.9 0.0 collective-permute-done.refs_1_
  12.9 0.0 collective-permute-done.1.refs_2_
  13.0 0.3 %collective-permute-done.2.refs_3_ = bf16[2,192,128]{2,1,0:T(8,128)(2,1)S(1)} collective-permute-done((bf16[2,192,128]{2,1,0:T(8,128)(2,1)S(1)}, bf16[2,192,128]{2,1,0:T(8,128)(2,1)S(1)}, u32[]{:S(2)}, u32[]{:S(2)}) %collective-permute-start.2) | collective-permute-done | bytes 98336 | tf_op jit(solution)/shard_map/ppermute | solution.py:33
  13.2 0.0 collective-permute-done.3.refs_4_
  13.3 1.8 %image.1 = (bf16[2,192,128]{2,1,0:T(8,128)(2,1)S(1)}, bf16[4,192,128]{2,1,0:T(8,128)(2,1)S(1)}) custom-call(s32[8]{0:T(128)S(1)} %copy-done.4, bf16[2,192,128]{2,1,0:T(8,128)(2,1)S(1)} %pack.1.refs_0_, bf16[2,192,128]{2,1,0:T(8,128)(2,1)S(1)} %collective-permute-done.refs_1_, bf16[2,192,128]{2,1,0:T(8,128)(2,1)S(1)} %collective-permute-done.1.refs_2_, ...), custom_call_target="tpu_custom_call" | custom-call | flops 805306368 | bytes 2359296 | tf_op jit(solution)/shard_map/image/pallas_call | solution.py:344
  15.0 1.5 %collective-permute-start.8 = (bf16[2,192,128]{2,1,0:T(8,128)(2,1)S(1)}, bf16[2,192,128]{2,1,0:T(8,128)(2,1)S(1)}, u32[]{:S(2)}, u32[]{:S(2)}) collective-permute-start(bf16[2,192,128]{2,1,0:T(8,128)(2,1)S(1)} %get-tuple-element.11), channel_id=1, source_target_pairs={{0,2},{1,3},{2,0},{3,1},{4,6},{5,7},{6,4},{7,5},{8,10},{9,11},{10,... | collective-permute-start | bytes 294920 | tf_op jit(solution)/shard_map/ppermute | solution.py:40
  16.6 0.2 overlap.1.refs_3_
  16.8 0.1 collective-permute-start.4
  16.9 0.6 %collective-permute-start.5 = (f32[16,128]{1,0:T(8,128)S(1)}, f32[16,128]{1,0:T(8,128)S(1)}, u32[]{:S(2)}, u32[]{:S(2)}) collective-permute-start(f32[16,128]{1,0:T(8,128)S(1)} %overlap.1.refs_3_), channel_id=1, source_target_pairs={{0,2},{1,3},{2,0},{3,1},{4,6},{5,7},{6,4},{7,5},{8,10},{9,11},{10,... | collective-permute-start | bytes 24584 | tf_op jit(solution)/shard_map/ppermute | solution.py:40
  17.5 1.2 %collective-permute-start.6 = (f32[16,128]{1,0:T(8,128)S(1)}, f32[16,128]{1,0:T(8,128)S(1)}, u32[]{:S(2)}, u32[]{:S(2)}) collective-permute-start(f32[16,128]{1,0:T(8,128)S(1)} %overlap.1.refs_3_), channel_id=1, source_target_pairs={{0,1},{1,0},{2,3},{3,2},{4,5},{5,4},{6,7},{7,6},{8,9},{9,8},{10,11... | collective-permute-start | bytes 24584 | tf_op jit(solution)/shard_map/ppermute | solution.py:40
  18.7 0.1 copy.7.owners_ref
  18.8 0.0 collective-permute-start.7
  18.8 0.9 %collective-permute-done.8.refs_2_ = bf16[2,192,128]{2,1,0:T(8,128)(2,1)S(1)} collective-permute-done((bf16[2,192,128]{2,1,0:T(8,128)(2,1)S(1)}, bf16[2,192,128]{2,1,0:T(8,128)(2,1)S(1)}, u32[]{:S(2)}, u32[]{:S(2)}) %collective-permute-start.8) | collective-permute-done | bytes 98336 | tf_op jit(solution)/shard_map/ppermute | solution.py:40
  19.7 0.0 collective-permute-start.9
  19.7 0.2 collective-permute-done.4.refs_0_
  19.9 0.7 %collective-permute-done.5.refs_1_ = f32[16,128]{1,0:T(8,128)S(1)} collective-permute-done((f32[16,128]{1,0:T(8,128)S(1)}, f32[16,128]{1,0:T(8,128)S(1)}, u32[]{:S(2)}, u32[]{:S(2)}) %collective-permute-start.5) | collective-permute-done | bytes 8224 | tf_op jit(solution)/shard_map/ppermute | solution.py:40
  20.6 0.0 collective-permute-done.6.refs_2_
  20.6 0.5 %factor.1 = (f32[16,16]{1,0:T(8,128)S(1)}, bf16[256,256]{1,0:T(8,128)(2,1)S(1)}) custom-call(s32[16,1]{1,0:T(8,128)S(1)} %copy.7.owners_ref, f32[16,128]{1,0:T(8,128)S(1)} %collective-permute-done.4.refs_0_, f32[16,128]{1,0:T(8,128)S(1)} %collective-permute-done.5.refs_1_, f32[16,128]{1,0:T(8,128)S(1)} %collective-permute-done.6.refs_2_, ...), custom_call_target="tpu_custom_call" | custom-call | flops 3000000000 | bytes 1024 | tf_op jit(solution)/shard_map/factor/pallas_call | solution.py:371
  21.1 0.0 collective-permute-done.7.refs_1_
  21.1 0.0 collective-permute-done.9.refs_3_
  21.1 1.1 %route.1 = (bf16[8,64,192]{2,1,0:T(8,128)(2,1)}, f32[16,16]{1,0:T(8,128)}) custom-call(f32[16,16]{1,0:T(8,128)S(1)} %get-tuple-element.9.overlap_ref, bf16[256,256]{1,0:T(8,128)(2,1)S(1)} %get-tuple-element.10.weights_ref, bf16[4,192,128]{2,1,0:T(8,128)(2,1)S(1)} %get-tuple-element.8.halves_ref.refs_0_, ...), custom_call_target="tpu_custom_call" | custom-call | flops 3145728 | bytes 1179648 | tf_op jit(solution)/shard_map/route/pallas_call | solution.py:379
  (7 shorter events, 0.0 us)
Async XLA Ops:
  0.6 0.9 %copy-start = (bf16[16,16,192]{2,1,0:T(8,128)(2,1)S(1)}, bf16[16,16,192]{2,1,0:T(8,128)(2,1)}, u32[]{:S(2)}) copy-start(bf16[16,16,192]{2,1,0:T(8,128)(2,1)} %orbitals_ref.3) | copy-start | bytes 294916
  1.5 11.7 %copy-start.4 = (s32[8]{0:T(128)S(1)}, s32[8]{0:T(128)}, u32[]{:S(2)}) copy-start(s32[8]{0:T(128)} %occupied_ref.1) | copy-start | bytes 100
  1.5 17.2 %copy-start.5 = (s32[16,1]{0,1:T(1,128)S(1)}, s32[16,1]{0,1:T(1,128)}, u32[]{:S(2)}) copy-start(s32[16,1]{0,1:T(1,128)} %param.8) | copy-start | bytes 196
  1.8 14.8 %copy-start.1 = (bf16[16,16,192]{2,1,0:T(8,128)(2,1)S(1)}, bf16[16,16,192]{2,1,0:T(8,128)(2,1)}, u32[]{:S(2)}) copy-start(bf16[16,16,192]{2,1,0:T(8,128)(2,1)} %orbitals_ref.3) | copy-start | bytes 294916
  1.8 11.1 %collective-permute-start = (bf16[2,192,128]{2,1,0:T(8,128)(2,1)S(1)}, bf16[2,192,128]{2,1,0:T(8,128)(2,1)S(1)}, u32[]{:S(2)}, u32[]{:S(2)}) collective-permute-start(bf16[2,192,128]{2,1,0:T(8,128)(2,1)S(1)} %pack.1.refs_0_), channel_id=1, source_target_pairs={{28,0},{0,4},{4,8},{8,12},{12,16},{16,20},{20,24},{24,28},{29,1},{... | collective-permute-start | bytes 294920 | tf_op jit(solution)/shard_map/ppermute | solution.py:33
  4.8 8.1 %collective-permute-start.1 = (bf16[2,192,128]{2,1,0:T(8,128)(2,1)S(1)}, bf16[2,192,128]{2,1,0:T(8,128)(2,1)S(1)}, u32[]{:S(2)}, u32[]{:S(2)}) collective-permute-start(bf16[2,192,128]{2,1,0:T(8,128)(2,1)S(1)} %pack.1.refs_0_), channel_id=1, source_target_pairs={{24,0},{28,4},{0,8},{4,12},{8,16},{12,20},{16,24},{20,28},{25,1},{... | collective-permute-start | bytes 294920 | tf_op jit(solution)/shard_map/ppermute | solution.py:33
  6.4 6.8 %collective-permute-start.2 = (bf16[2,192,128]{2,1,0:T(8,128)(2,1)S(1)}, bf16[2,192,128]{2,1,0:T(8,128)(2,1)S(1)}, u32[]{:S(2)}, u32[]{:S(2)}) collective-permute-start(bf16[2,192,128]{2,1,0:T(8,128)(2,1)S(1)} %pack.1.refs_0_), channel_id=1, source_target_pairs={{8,0},{12,4},{16,8},{20,12},{24,16},{28,20},{0,24},{4,28},{9,1},{1... | collective-permute-start | bytes 294920 | tf_op jit(solution)/shard_map/ppermute | solution.py:33
  8.6 4.6 %collective-permute-start.3 = (bf16[2,192,128]{2,1,0:T(8,128)(2,1)S(1)}, bf16[2,192,128]{2,1,0:T(8,128)(2,1)S(1)}, u32[]{:S(2)}, u32[]{:S(2)}) collective-permute-start(bf16[2,192,128]{2,1,0:T(8,128)(2,1)S(1)} %pack.1.refs_0_), channel_id=1, source_target_pairs={{4,0},{8,4},{12,8},{16,12},{20,16},{24,20},{28,24},{0,28},{5,1},{9... | collective-permute-start | bytes 294920 | tf_op jit(solution)/shard_map/ppermute | solution.py:33
  9.9 1.0 %copy-start.2 = (bf16[3,192,192]{2,1,0:T(8,128)(2,1)S(1)}, bf16[3,192,192]{2,1,0:T(8,128)(2,1)}, u32[]{:S(2)}) copy-start(bf16[3,192,192]{2,1,0:T(8,128)(2,1)} %constant.3.tables_ref) | copy-start | bytes 663556
  10.9 0.7 %copy-start.3 = (f32[16,192]{1,0:T(8,128)S(1)}, f32[16,192]{1,0:T(8,128)}, u32[]{:S(2)}) copy-start(f32[16,192]{1,0:T(8,128)} %coulomb_ref.1) | copy-start | bytes 36868
  15.0 4.7 %collective-permute-start.8 = (bf16[2,192,128]{2,1,0:T(8,128)(2,1)S(1)}, bf16[2,192,128]{2,1,0:T(8,128)(2,1)S(1)}, u32[]{:S(2)}, u32[]{:S(2)}) collective-permute-start(bf16[2,192,128]{2,1,0:T(8,128)(2,1)S(1)} %get-tuple-element.11), channel_id=1, source_target_pairs={{0,2},{1,3},{2,0},{3,1},{4,6},{5,7},{6,4},{7,5},{8,10},{9,11},{10,... | collective-permute-start | bytes 294920 | tf_op jit(solution)/shard_map/ppermute | solution.py:40
  16.8 3.1 %collective-permute-start.4 = (f32[16,128]{1,0:T(8,128)S(1)}, f32[16,128]{1,0:T(8,128)S(1)}, u32[]{:S(2)}, u32[]{:S(2)}) collective-permute-start(f32[16,128]{1,0:T(8,128)S(1)} %overlap.1.refs_3_), channel_id=1, source_target_pairs={{0,3},{1,2},{2,1},{3,0},{4,7},{5,6},{6,5},{7,4},{8,11},{9,10},{10,... | collective-permute-start | bytes 24584 | tf_op jit(solution)/shard_map/ppermute | solution.py:40
  16.9 3.7 %collective-permute-start.5 = (f32[16,128]{1,0:T(8,128)S(1)}, f32[16,128]{1,0:T(8,128)S(1)}, u32[]{:S(2)}, u32[]{:S(2)}) collective-permute-start(f32[16,128]{1,0:T(8,128)S(1)} %overlap.1.refs_3_), channel_id=1, source_target_pairs={{0,2},{1,3},{2,0},{3,1},{4,6},{5,7},{6,4},{7,5},{8,10},{9,11},{10,... | collective-permute-start | bytes 24584 | tf_op jit(solution)/shard_map/ppermute | solution.py:40
  17.5 3.1 %collective-permute-start.6 = (f32[16,128]{1,0:T(8,128)S(1)}, f32[16,128]{1,0:T(8,128)S(1)}, u32[]{:S(2)}, u32[]{:S(2)}) collective-permute-start(f32[16,128]{1,0:T(8,128)S(1)} %overlap.1.refs_3_), channel_id=1, source_target_pairs={{0,1},{1,0},{2,3},{3,2},{4,5},{5,4},{6,7},{7,6},{8,9},{9,8},{10,11... | collective-permute-start | bytes 24584 | tf_op jit(solution)/shard_map/ppermute | solution.py:40
  18.8 2.3 %collective-permute-start.7 = (bf16[4,192,128]{2,1,0:T(8,128)(2,1)S(1)}, bf16[4,192,128]{2,1,0:T(8,128)(2,1)S(1)}, u32[]{:S(2)}, u32[]{:S(2)}) collective-permute-start(bf16[4,192,128]{2,1,0:T(8,128)(2,1)S(1)} %get-tuple-element.8.halves_ref.refs_0_), channel_id=1, source_target_pairs={{0,1},{1,0},{2,3},{3,2},{4,5},{5,4},{6,7},{7,6},{8,9},{9,8},{10,11... | collective-permute-start | bytes 589832 | tf_op jit(solution)/shard_map/ppermute | solution.py:40
  19.7 1.4 %collective-permute-start.9 = (bf16[2,192,128]{2,1,0:T(8,128)(2,1)S(1)}, bf16[2,192,128]{2,1,0:T(8,128)(2,1)S(1)}, u32[]{:S(2)}, u32[]{:S(2)}) collective-permute-start(bf16[2,192,128]{2,1,0:T(8,128)(2,1)S(1)} %collective-permute-done.8.refs_2_), channel_id=1, source_target_pairs={{0,1},{1,0},{2,3},{3,2},{4,5},{5,4},{6,7},{7,6},{8,9},{9,8},{10,11... | collective-permute-start | bytes 294920 | tf_op jit(solution)/shard_map/ppermute | solution.py:40

commit v22 on v21

--- a/solution.py
+++ b/solution.py
@@ -208,12 +208,12 @@
     out_ref[...] = jnp.where(same_line, cross, 0.0).reshape(members, span, LANES).sum(axis=1)
 
 
-def factor_kernel(cells, owners_ref, *refs):
+def factor_kernel(cells, turns, owners_ref, *refs):
     parts, (overlap_ref, weights_ref) = refs[:-2], refs[-2:]
     members = owners_ref.shape[0]
     span = LANES // members
     turn = own_turn()
-    sums = [part[...] for part in reversed(parts)]
+    sums = [parts[place][...] for place in [len(turns)] + [turns.index(f) for f in range(1, len(parts))]]
     while len(sums) > 1:
         sums = [a + b for a, b in zip(sums[::2], sums[1::2])]
     high, rest = split(sums[0])
@@ -361,7 +361,8 @@
         8 * orbitals.size,
         operands=2,
     )(orbitals, parts)
-    overlaps = [swapped(overlap, flip) for flip in reversed(range(1, groups))] + [overlap]
+    turns = [*range(near, groups), *range(1, near)]
+    overlaps = [swapped(overlap, flip) for flip in turns] + [overlap]
     images = [parts] + [swapped(parts, flip) for flip in range(1, near)]
     for grid in range(1, grids):
         across = swapped(high, grid * near)
@@ -369,7 +370,7 @@
     cells = lines * groups * points
 
     intersection, weights = call(
-        functools.partial(factor_kernel, cells),
+        functools.partial(factor_kernel, cells, turns),
         "factor",
         [shape((members, members), F32), shape((4 * CAP * span, 2 * LANES), BF16)],
         FACTOR_COST,

time: 22.6 us -> 22.5 us (level)
  starting transfers between devices: 11.6 us -> 11.9 us
  waiting for transfers between devices: 2.09 us -> 1.79 us
    ppermute x6, waiting for transfers between devices: 1.78 us -> 1.49 us  [swapped(): lax.ppermute(value, ('grid', 'ham'), [(group, group ^ flip) for group in...]
    ppermute x6, starting transfers between devices: 3.47 us -> 3.76 us  [swapped(): lax.ppermute(value, ('grid', 'ham'), [(group, group ^ flip) for group in...]
  transfers between devices with their start and end apart: 10 -> 10, of which waited for: 4 -> 3; matrix products, arithmetic and copies ran while one was open for 0% -> 0% of each run, Pallas kernels for 9% -> 9%
where the time goes in v22:
time: 22.5 us; the launch traced here: 22.2 us
  starting transfers between devices  11.9 us (53%)
  Pallas kernels  5.1 us (23%)
  local copies, waits for them, and re-layouts  2.67 us (12%)
  waiting for transfers between devices  1.79 us (8%)
  between operations  0.73 us (3%)
    ppermute x4, starting transfers between devices, exchanged(): lax.ppermute(value, 'band', [(row[turn], block) for block, row in enumera...  8.15 us
    ppermute x6, starting transfers between devices, swapped(): lax.ppermute(value, ('grid', 'ham'), [(group, group ^ flip) for group in...  3.76 us
    unnamed x13, local copies, waits for them, and re-layouts  2.67 us
    pallas_call x1, Pallas kernels, local(): call(functools.partial(image_kernel, members), 'image', [shape((packs, po...  1.77 us
    ppermute x6, waiting for transfers between devices, swapped(): lax.ppermute(value, ('grid', 'ham'), [(group, group ^ flip) for group in...  1.49 us
    pallas_call x1, Pallas kernels, local(): call(response_kernel, 'response', [shape((lines, points, padded), F32)],...  1.3 us
    pallas_call x1, Pallas kernels, local(): call(route_kernel, 'route', [shape((CAP, groups * lines, points), BF16),...  1.08 us
    pallas_call x1, Pallas kernels, local(): call(functools.partial(factor_kernel, cells, turns), 'factor', [shape((me...  0.53 us
  transfers between devices with their start and end apart: 10, of which 3 were waited for; matrix products, arithmetic and copies ran while one was open for 0% of the time, Pallas kernels for 9%

profile of v22, /device:TPU:0, one launch (start us, length us, event | category | flops | bytes accessed | tf_op | source)
XLA Modules:
  0.0 22.2 jit_solution(357312577428268153)
XLA Ops:
  0.6 0.0 copy-start
  0.6 0.9 %copy-done = bf16[16,16,192]{2,1,0:T(8,128)(2,1)S(1)} copy-done((bf16[16,16,192]{2,1,0:T(8,128)(2,1)S(1)}, bf16[16,16,192]{2,1,0:T(8,128)(2,1)}, u32[]{:S(2)}) %copy-start) | copy-done | bytes 98328
  1.5 0.2 %pack.1.refs_0_ = bf16[2,192,128]{2,1,0:T(8,128)(2,1)S(1)} custom-call(bf16[16,16,192]{2,1,0:T(8,128)(2,1)S(1)} %copy-done), custom_call_target="tpu_custom_call" | custom-call | flops 49152 | bytes 196608 | tf_op jit(solution)/shard_map/pack/pallas_call | solution.py:325
  1.8 0.0 copy-start.1
  1.8 3.0 %collective-permute-start = (bf16[2,192,128]{2,1,0:T(8,128)(2,1)S(1)}, bf16[2,192,128]{2,1,0:T(8,128)(2,1)S(1)}, u32[]{:S(2)}, u32[]{:S(2)}) collective-permute-start(bf16[2,192,128]{2,1,0:T(8,128)(2,1)S(1)} %pack.1.refs_0_), channel_id=1, source_target_pairs={{28,0},{0,4},{4,8},{8,12},{12,16},{16,20},{20,24},{24,28},{29,1},{... | collective-permute-start | bytes 294920 | tf_op jit(solution)/shard_map/ppermute | solution.py:33
  4.8 1.6 %collective-permute-start.1 = (bf16[2,192,128]{2,1,0:T(8,128)(2,1)S(1)}, bf16[2,192,128]{2,1,0:T(8,128)(2,1)S(1)}, u32[]{:S(2)}, u32[]{:S(2)}) collective-permute-start(bf16[2,192,128]{2,1,0:T(8,128)(2,1)S(1)} %pack.1.refs_0_), channel_id=1, source_target_pairs={{24,0},{28,4},{0,8},{4,12},{8,16},{12,20},{16,24},{20,28},{25,1},{... | collective-permute-start | bytes 294920 | tf_op jit(solution)/shard_map/ppermute | solution.py:33
  6.4 2.2 %collective-permute-start.2 = (bf16[2,192,128]{2,1,0:T(8,128)(2,1)S(1)}, bf16[2,192,128]{2,1,0:T(8,128)(2,1)S(1)}, u32[]{:S(2)}, u32[]{:S(2)}) collective-permute-start(bf16[2,192,128]{2,1,0:T(8,128)(2,1)S(1)} %pack.1.refs_0_), channel_id=1, source_target_pairs={{8,0},{12,4},{16,8},{20,12},{24,16},{28,20},{0,24},{4,28},{9,1},{1... | collective-permute-start | bytes 294920 | tf_op jit(solution)/shard_map/ppermute | solution.py:33
  8.6 1.3 %collective-permute-start.3 = (bf16[2,192,128]{2,1,0:T(8,128)(2,1)S(1)}, bf16[2,192,128]{2,1,0:T(8,128)(2,1)S(1)}, u32[]{:S(2)}, u32[]{:S(2)}) collective-permute-start(bf16[2,192,128]{2,1,0:T(8,128)(2,1)S(1)} %pack.1.refs_0_), channel_id=1, source_target_pairs={{4,0},{8,4},{12,8},{16,12},{20,16},{24,20},{28,24},{0,28},{5,1},{9... | collective-permute-start | bytes 294920 | tf_op jit(solution)/shard_map/ppermute | solution.py:33
  9.9 1.0 %copy-done.2 = bf16[3,192,192]{2,1,0:T(8,128)(2,1)S(1)} copy-done((bf16[3,192,192]{2,1,0:T(8,128)(2,1)S(1)}, bf16[3,192,192]{2,1,0:T(8,128)(2,1)}, u32[]{:S(2)}) %copy-start.2) | copy-done | bytes 221208
  10.9 0.7 %copy-done.3 = f32[16,192]{1,0:T(8,128)S(1)} copy-done((f32[16,192]{1,0:T(8,128)S(1)}, f32[16,192]{1,0:T(8,128)}, u32[]{:S(2)}) %copy-start.3) | copy-done | bytes 12312
  11.6 1.3 %response.1.refs_5_ = f32[16,192,256]{2,1,0:T(8,128)S(1)} custom-call(f32[16,192]{1,0:T(8,128)S(1)} %copy-done.3, bf16[3,192,192]{2,1,0:T(8,128)(2,1)S(1)} %copy-done.2), custom_call_target="tpu_custom_call" | custom-call | flops 452984832 | bytes 2359296 | tf_op jit(solution)/shard_map/response/pallas_call | solution.py:335
  12.9 0.0 collective-permute-done.refs_1_
  12.9 0.0 collective-permute-done.1.refs_2_
  13.0 0.3 %collective-permute-done.2.refs_3_ = bf16[2,192,128]{2,1,0:T(8,128)(2,1)S(1)} collective-permute-done((bf16[2,192,128]{2,1,0:T(8,128)(2,1)S(1)}, bf16[2,192,128]{2,1,0:T(8,128)(2,1)S(1)}, u32[]{:S(2)}, u32[]{:S(2)}) %collective-permute-start.2) | collective-permute-done | bytes 98336 | tf_op jit(solution)/shard_map/ppermute | solution.py:33
  13.2 0.0 collective-permute-done.3.refs_4_
  13.3 1.8 %image.1 = (bf16[2,192,128]{2,1,0:T(8,128)(2,1)S(1)}, bf16[4,192,128]{2,1,0:T(8,128)(2,1)S(1)}) custom-call(s32[8]{0:T(128)S(1)} %copy-done.4, bf16[2,192,128]{2,1,0:T(8,128)(2,1)S(1)} %pack.1.refs_0_, bf16[2,192,128]{2,1,0:T(8,128)(2,1)S(1)} %collective-permute-done.refs_1_, bf16[2,192,128]{2,1,0:T(8,128)(2,1)S(1)} %collective-permute-done.1.refs_2_, ...), custom_call_target="tpu_custom_call" | custom-call | flops 805306368 | bytes 2359296 | tf_op jit(solution)/shard_map/image/pallas_call | solution.py:344
  15.0 1.5 %collective-permute-start.8 = (bf16[2,192,128]{2,1,0:T(8,128)(2,1)S(1)}, bf16[2,192,128]{2,1,0:T(8,128)(2,1)S(1)}, u32[]{:S(2)}, u32[]{:S(2)}) collective-permute-start(bf16[2,192,128]{2,1,0:T(8,128)(2,1)S(1)} %get-tuple-element.11), channel_id=1, source_target_pairs={{0,2},{1,3},{2,0},{3,1},{4,6},{5,7},{6,4},{7,5},{8,10},{9,11},{10,... | collective-permute-start | bytes 294920 | tf_op jit(solution)/shard_map/ppermute | solution.py:40
  16.6 0.2 overlap.1.refs_3_
  16.8 0.6 %collective-permute-start.4 = (f32[16,128]{1,0:T(8,128)S(1)}, f32[16,128]{1,0:T(8,128)S(1)}, u32[]{:S(2)}, u32[]{:S(2)}) collective-permute-start(f32[16,128]{1,0:T(8,128)S(1)} %overlap.1.refs_3_), channel_id=1, source_target_pairs={{0,2},{1,3},{2,0},{3,1},{4,6},{5,7},{6,4},{7,5},{8,10},{9,11},{10,... | collective-permute-start | bytes 24584 | tf_op jit(solution)/shard_map/ppermute | solution.py:40
  17.4 0.0 collective-permute-start.5
  17.4 1.6 %collective-permute-start.6 = (f32[16,128]{1,0:T(8,128)S(1)}, f32[16,128]{1,0:T(8,128)S(1)}, u32[]{:S(2)}, u32[]{:S(2)}) collective-permute-start(f32[16,128]{1,0:T(8,128)S(1)} %overlap.1.refs_3_), channel_id=1, source_target_pairs={{0,1},{1,0},{2,3},{3,2},{4,5},{5,4},{6,7},{7,6},{8,9},{9,8},{10,11... | collective-permute-start | bytes 24584 | tf_op jit(solution)/shard_map/ppermute | solution.py:40
  19.0 0.1 copy.7.owners_ref
  19.1 0.0 collective-permute-start.7
  19.1 0.6 %collective-permute-done.8.refs_2_ = bf16[2,192,128]{2,1,0:T(8,128)(2,1)S(1)} collective-permute-done((bf16[2,192,128]{2,1,0:T(8,128)(2,1)S(1)}, bf16[2,192,128]{2,1,0:T(8,128)(2,1)S(1)}, u32[]{:S(2)}, u32[]{:S(2)}) %collective-permute-start.8) | collective-permute-done | bytes 98336 | tf_op jit(solution)/shard_map/ppermute | solution.py:40
  19.7 0.0 collective-permute-start.9
  19.7 0.8 %collective-permute-done.4.refs_0_ = f32[16,128]{1,0:T(8,128)S(1)} collective-permute-done((f32[16,128]{1,0:T(8,128)S(1)}, f32[16,128]{1,0:T(8,128)S(1)}, u32[]{:S(2)}, u32[]{:S(2)}) %collective-permute-start.4) | collective-permute-done | bytes 8224 | tf_op jit(solution)/shard_map/ppermute | solution.py:40
  20.6 0.0 collective-permute-done.5.refs_1_
  20.6 0.0 collective-permute-done.6.refs_2_
  20.6 0.5 %factor.1 = (f32[16,16]{1,0:T(8,128)S(1)}, bf16[256,256]{1,0:T(8,128)(2,1)S(1)}) custom-call(s32[16,1]{1,0:T(8,128)S(1)} %copy.7.owners_ref, f32[16,128]{1,0:T(8,128)S(1)} %collective-permute-done.4.refs_0_, f32[16,128]{1,0:T(8,128)S(1)} %collective-permute-done.5.refs_1_, f32[16,128]{1,0:T(8,128)S(1)} %collective-permute-done.6.refs_2_, ...), custom_call_target="tpu_custom_call" | custom-call | flops 3000000000 | bytes 1024 | tf_op jit(solution)/shard_map/factor/pallas_call | solution.py:372
  21.1 0.0 collective-permute-done.7.refs_1_
  21.1 0.0 collective-permute-done.9.refs_3_
  21.1 1.1 %route.1 = (bf16[8,64,192]{2,1,0:T(8,128)(2,1)}, f32[16,16]{1,0:T(8,128)}) custom-call(f32[16,16]{1,0:T(8,128)S(1)} %get-tuple-element.9.overlap_ref, bf16[256,256]{1,0:T(8,128)(2,1)S(1)} %get-tuple-element.10.weights_ref, bf16[4,192,128]{2,1,0:T(8,128)(2,1)S(1)} %get-tuple-element.8.halves_ref.refs_0_, ...), custom_call_target="tpu_custom_call" | custom-call | flops 3145728 | bytes 1179648 | tf_op jit(solution)/shard_map/route/pallas_call | solution.py:380
  (7 shorter events, 0.0 us)
Async XLA Ops:
  0.6 0.9 %copy-start = (bf16[16,16,192]{2,1,0:T(8,128)(2,1)S(1)}, bf16[16,16,192]{2,1,0:T(8,128)(2,1)}, u32[]{:S(2)}) copy-start(bf16[16,16,192]{2,1,0:T(8,128)(2,1)} %orbitals_ref.3) | copy-start | bytes 294916
  1.5 11.7 %copy-start.4 = (s32[8]{0:T(128)S(1)}, s32[8]{0:T(128)}, u32[]{:S(2)}) copy-start(s32[8]{0:T(128)} %occupied_ref.1) | copy-start | bytes 100
  1.5 17.4 %copy-start.5 = (s32[16,1]{0,1:T(1,128)S(1)}, s32[16,1]{0,1:T(1,128)}, u32[]{:S(2)}) copy-start(s32[16,1]{0,1:T(1,128)} %param.8) | copy-start | bytes 196
  1.8 14.8 %copy-start.1 = (bf16[16,16,192]{2,1,0:T(8,128)(2,1)S(1)}, bf16[16,16,192]{2,1,0:T(8,128)(2,1)}, u32[]{:S(2)}) copy-start(bf16[16,16,192]{2,1,0:T(8,128)(2,1)} %orbitals_ref.3) | copy-start | bytes 294916
  1.8 11.1 %collective-permute-start = (bf16[2,192,128]{2,1,0:T(8,128)(2,1)S(1)}, bf16[2,192,128]{2,1,0:T(8,128)(2,1)S(1)}, u32[]{:S(2)}, u32[]{:S(2)}) collective-permute-start(bf16[2,192,128]{2,1,0:T(8,128)(2,1)S(1)} %pack.1.refs_0_), channel_id=1, source_target_pairs={{28,0},{0,4},{4,8},{8,12},{12,16},{16,20},{20,24},{24,28},{29,1},{... | collective-permute-start | bytes 294920 | tf_op jit(solution)/shard_map/ppermute | solution.py:33
  4.8 8.1 %collective-permute-start.1 = (bf16[2,192,128]{2,1,0:T(8,128)(2,1)S(1)}, bf16[2,192,128]{2,1,0:T(8,128)(2,1)S(1)}, u32[]{:S(2)}, u32[]{:S(2)}) collective-permute-start(bf16[2,192,128]{2,1,0:T(8,128)(2,1)S(1)} %pack.1.refs_0_), channel_id=1, source_target_pairs={{24,0},{28,4},{0,8},{4,12},{8,16},{12,20},{16,24},{20,28},{25,1},{... | collective-permute-start | bytes 294920 | tf_op jit(solution)/shard_map/ppermute | solution.py:33
  6.4 6.8 %collective-permute-start.2 = (bf16[2,192,128]{2,1,0:T(8,128)(2,1)S(1)}, bf16[2,192,128]{2,1,0:T(8,128)(2,1)S(1)}, u32[]{:S(2)}, u32[]{:S(2)}) collective-permute-start(bf16[2,192,128]{2,1,0:T(8,128)(2,1)S(1)} %pack.1.refs_0_), channel_id=1, source_target_pairs={{8,0},{12,4},{16,8},{20,12},{24,16},{28,20},{0,24},{4,28},{9,1},{1... | collective-permute-start | bytes 294920 | tf_op jit(solution)/shard_map/ppermute | solution.py:33
  8.6 4.6 %collective-permute-start.3 = (bf16[2,192,128]{2,1,0:T(8,128)(2,1)S(1)}, bf16[2,192,128]{2,1,0:T(8,128)(2,1)S(1)}, u32[]{:S(2)}, u32[]{:S(2)}) collective-permute-start(bf16[2,192,128]{2,1,0:T(8,128)(2,1)S(1)} %pack.1.refs_0_), channel_id=1, source_target_pairs={{4,0},{8,4},{12,8},{16,12},{20,16},{24,20},{28,24},{0,28},{5,1},{9... | collective-permute-start | bytes 294920 | tf_op jit(solution)/shard_map/ppermute | solution.py:33
  9.9 1.0 %copy-start.2 = (bf16[3,192,192]{2,1,0:T(8,128)(2,1)S(1)}, bf16[3,192,192]{2,1,0:T(8,128)(2,1)}, u32[]{:S(2)}) copy-start(bf16[3,192,192]{2,1,0:T(8,128)(2,1)} %constant.3.tables_ref) | copy-start | bytes 663556
  10.9 0.7 %copy-start.3 = (f32[16,192]{1,0:T(8,128)S(1)}, f32[16,192]{1,0:T(8,128)}, u32[]{:S(2)}) copy-start(f32[16,192]{1,0:T(8,128)} %coulomb_ref.1) | copy-start | bytes 36868
  15.0 4.7 %collective-permute-start.8 = (bf16[2,192,128]{2,1,0:T(8,128)(2,1)S(1)}, bf16[2,192,128]{2,1,0:T(8,128)(2,1)S(1)}, u32[]{:S(2)}, u32[]{:S(2)}) collective-permute-start(bf16[2,192,128]{2,1,0:T(8,128)(2,1)S(1)} %get-tuple-element.11), channel_id=1, source_target_pairs={{0,2},{1,3},{2,0},{3,1},{4,6},{5,7},{6,4},{7,5},{8,10},{9,11},{10,... | collective-permute-start | bytes 294920 | tf_op jit(solution)/shard_map/ppermute | solution.py:40
  16.8 3.8 %collective-permute-start.4 = (f32[16,128]{1,0:T(8,128)S(1)}, f32[16,128]{1,0:T(8,128)S(1)}, u32[]{:S(2)}, u32[]{:S(2)}) collective-permute-start(f32[16,128]{1,0:T(8,128)S(1)} %overlap.1.refs_3_), channel_id=1, source_target_pairs={{0,2},{1,3},{2,0},{3,1},{4,6},{5,7},{6,4},{7,5},{8,10},{9,11},{10,... | collective-permute-start | bytes 24584 | tf_op jit(solution)/shard_map/ppermute | solution.py:40
  17.4 3.2 %collective-permute-start.5 = (f32[16,128]{1,0:T(8,128)S(1)}, f32[16,128]{1,0:T(8,128)S(1)}, u32[]{:S(2)}, u32[]{:S(2)}) collective-permute-start(f32[16,128]{1,0:T(8,128)S(1)} %overlap.1.refs_3_), channel_id=1, source_target_pairs={{0,3},{1,2},{2,1},{3,0},{4,7},{5,6},{6,5},{7,4},{8,11},{9,10},{10,... | collective-permute-start | bytes 24584 | tf_op jit(solution)/shard_map/ppermute | solution.py:40
  17.4 3.2 %collective-permute-start.6 = (f32[16,128]{1,0:T(8,128)S(1)}, f32[16,128]{1,0:T(8,128)S(1)}, u32[]{:S(2)}, u32[]{:S(2)}) collective-permute-start(f32[16,128]{1,0:T(8,128)S(1)} %overlap.1.refs_3_), channel_id=1, source_target_pairs={{0,1},{1,0},{2,3},{3,2},{4,5},{5,4},{6,7},{7,6},{8,9},{9,8},{10,11... | collective-permute-start | bytes 24584 | tf_op jit(solution)/shard_map/ppermute | solution.py:40
  19.1 2.0 %collective-permute-start.7 = (bf16[4,192,128]{2,1,0:T(8,128)(2,1)S(1)}, bf16[4,192,128]{2,1,0:T(8,128)(2,1)S(1)}, u32[]{:S(2)}, u32[]{:S(2)}) collective-permute-start(bf16[4,192,128]{2,1,0:T(8,128)(2,1)S(1)} %get-tuple-element.8.halves_ref.refs_0_), channel_id=1, source_target_pairs={{0,1},{1,0},{2,3},{3,2},{4,5},{5,4},{6,7},{7,6},{8,9},{9,8},{10,11... | collective-permute-start | bytes 589832 | tf_op jit(solution)/shard_map/ppermute | solution.py:40
  19.7 1.4 %collective-permute-start.9 = (bf16[2,192,128]{2,1,0:T(8,128)(2,1)S(1)}, bf16[2,192,128]{2,1,0:T(8,128)(2,1)S(1)}, u32[]{:S(2)}, u32[]{:S(2)}) collective-permute-start(bf16[2,192,128]{2,1,0:T(8,128)(2,1)S(1)} %collective-permute-done.8.refs_2_), channel_id=1, source_target_pairs={{0,1},{1,0},{2,3},{3,2},{4,5},{5,4},{6,7},{7,6},{8,9},{9,8},{10,11... | collective-permute-start | bytes 294920 | tf_op jit(solution)/shard_map/ppermute | solution.py:40
